TPU v7x, 32 devices: a whole 2x2x4 slice. The times are simulated.
32 devices in a mesh: dp: 16 (over z, y, core), tensor: 2 (over x).
Axes of the slice: x: 2, y: 2, z: 4, core: 2. Of those that a mesh axis runs over, the one named last changes fastest.
Arguments:
- tokens: bfloat16 [4096, 2048], P(('dp', 'tensor')), may hold values from -6 to 6
- seq_lens: int32 [16, 4], P('dp'), may hold values from 1 to 253, as said below
- norm_gains: bfloat16 [2, 2048], replicated, may hold values from 0.099609375 to 1.8984375
- w_query: bfloat16 [2048, 2048], P('dp', 'tensor'), may hold values from -0.125 to 0.125
- key_weight: bfloat16 [2048, 512], P('dp', 'tensor'), may hold values from -0.125 to 0.125
- value_weight: bfloat16 [2048, 512], P('dp', 'tensor'), may hold values from -0.125 to 0.125
- w_out: bfloat16 [2048, 2048], P('dp', 'tensor'), may hold values from -0.75 to 0.75
- w_gate: bfloat16 [2048, 8192], P('dp', 'tensor'), may hold values from -0.125 to 0.125
- w_up: bfloat16 [2048, 8192], P('dp', 'tensor'), may hold values from -0.125 to 0.125
- w_down: bfloat16 [2048, 8192], P('dp', 'tensor'), may hold values from -0.0625 to 0.0625
- cotangent: bfloat16 [4096, 2048], P(('dp', 'tensor')), may hold values from -6 to 6
Outputs:
- mixed: bfloat16 [4096, 2048], P(('dp', 'tensor'))
- grad_tokens: bfloat16 [4096, 2048], P(('dp', 'tensor'))
- grad_gains: float32 [2, 2048], replicated
- grad_query: float32 [2048, 2048], P('dp', 'tensor')
- grad_key: float32 [2048, 512], P('dp', 'tensor')
- grad_value: float32 [2048, 512], P('dp', 'tensor')
- grad_out: float32 [2048, 2048], P('dp', 'tensor')
- grad_gate: float32 [2048, 8192], P('dp', 'tensor')
- grad_up: float32 [2048, 8192], P('dp', 'tensor')
- grad_down: float32 [2048, 8192], P('dp', 'tensor')
Inputs may be any that keep to these rules, and one draw needn't show every extreme that they name: `seq_lens`: row b lists the lengths of 4 sequences packed from the first row of dp index b's 256 rows; the rows after them are unused. A row's lengths add up to 130 or more and to 256 at most; in every draw some row adds up to 256, and there its first sequence has the largest length. Rows 127 and 128 of a dp index always lie in one sequence.
All inputs are finite; a program needn't handle non-finite values.
Results may differ from a plain program's by a relative error of at most 0.014.
Values may be sent and summed in bfloat16 or wider, within the bound.
No kernel may reach another device: no remote copies, remote signals or barrier semaphores. Data moves between devices by JAX's collectives and lax.ppermute only.
A program may use at most 448 MiB of HBM per device.

v0:
```python
import math

import jax
import jax.numpy as jnp
from jax import lax
from jax.sharding import PartitionSpec as P

HEAD_WIDTH = 64


EPSILON = 1e-05
MASKED = -1e30


def matrix_product(left_side, right_side):
    return jnp.dot(left_side, right_side, preferred_element_type=jnp.float32)


def matmul_nt(left_side, right_side):
    return lax.dot_general(
        left_side, right_side, (((1,), (1,)), ((), ())), preferred_element_type=jnp.float32
    )


def matmul_tn(left_side, right_side):
    return lax.dot_general(
        left_side, right_side, (((0,), (0,)), ((), ())), preferred_element_type=jnp.float32
    )


def layout(lengths, row_count):
    finish = jnp.cumsum(lengths)
    starts = jnp.concatenate([finish - lengths, finish[-1:]])
    row_ids = jnp.arange(row_count, dtype=jnp.int32)
    segment = jnp.sum((row_ids[:, None] >= finish[None, :]).astype(jnp.int32), 1)
    chosen_slot = segment[:, None] == jnp.arange(starts.shape[0], dtype=jnp.int32)[None, :]
    first_row = jnp.sum(jnp.where(chosen_slot, starts[None, :], 0), 1)
    position = row_ids - first_row
    in_use = (segment < lengths.shape[0]).astype(jnp.float32)
    return (row_ids, segment, position, in_use)


def rope_tables(position, head_size):
    halfway = head_size // 2
    ladder = jnp.arange(halfway, dtype=jnp.float32)
    inverse = 1.0 / 500000.0 ** (ladder * 2.0 / head_size)
    wavelength = 2.0 * math.pi / inverse
    smooth = (8192.0 / wavelength - 1.0) / 3.0
    blended = (1.0 - smooth) * inverse / 32.0 + smooth * inverse
    scaled = jnp.where(
        wavelength > 8192.0, inverse / 32.0, jnp.where(wavelength < 2048.0, inverse, blended)
    )
    angles = position.astype(jnp.float32)[:, None] * scaled[None, :]
    cosine_lookup = jnp.cos(angles)
    sine_lookup = jnp.sin(angles)
    return (
        jnp.concatenate([cosine_lookup, cosine_lookup], 1),
        jnp.concatenate([sine_lookup, sine_lookup], 1),
    )


def apply_rotation(heads, cosine_lookup, sine_lookup):
    halfway = heads.shape[-1] // 2
    turned = jnp.concatenate([-heads[..., halfway:], heads[..., :halfway]], -1)
    return heads * cosine_lookup[:, None, :] + turned * sine_lookup[:, None, :]


def unrotate(grads, cosine_lookup, sine_lookup):
    halfway = grads.shape[-1] // 2
    scaled = grads * sine_lookup[:, None, :]
    return grads * cosine_lookup[:, None, :] + jnp.concatenate(
        [scaled[..., halfway:], -scaled[..., :halfway]], -1
    )


def norm_rows(operand):
    return lax.all_gather(operand, "tensor", axis=0, tiled=True)


def branch_rows(operand):
    return lax.psum_scatter(operand, "tensor", scatter_dimension=0, tiled=True)


def grad_rows(operand):
    return lax.all_gather(operand, "tensor", axis=0, tiled=True)


def back_rows(operand):
    return lax.psum_scatter(operand, "tensor", scatter_dimension=0, tiled=True)


def group_scores(rotated_query, key_rot, group_index, allowed, scaling):
    per_group = rotated_query.shape[1] // key_rot.shape[1]
    chosen = rotated_query[:, group_index * per_group : (group_index + 1) * per_group, :]
    scores = (
        jnp.einsum(
            "qhd,kd->hqk", chosen, key_rot[:, group_index, :], preferred_element_type=jnp.float32
        )
        * scaling
    )
    return (chosen, jnp.where(allowed[None], scores, MASKED))


def attend(rotated_query, key_rot, value_low, allowed, scaling):
    outputs = []
    logsums = []
    for group_index in range(key_rot.shape[1]):
        chosen, scores = group_scores(rotated_query, key_rot, group_index, allowed, scaling)
        largest = jnp.max(scores, 2, keepdims=True)
        logsum = largest + jnp.log(jnp.sum(jnp.exp(scores - largest), 2, keepdims=True))
        weights = jnp.exp(scores - logsum).astype(jnp.bfloat16)
        outputs.append(
            jnp.einsum(
                "hqk,kd->qhd",
                weights,
                value_low[:, group_index, :],
                preferred_element_type=jnp.float32,
            )
        )
        logsums.append(logsum)
    return (jnp.concatenate(outputs, 1), logsums)


def attend_back(rotated_query, key_rot, value_low, grad_heads, logsums, allowed, scaling):
    per_group = rotated_query.shape[1] // key_rot.shape[1]
    query_parts = []
    key_parts = []
    value_parts = []
    for group_index in range(key_rot.shape[1]):
        chosen, scores = group_scores(rotated_query, key_rot, group_index, allowed, scaling)
        softmax_weights = jnp.exp(scores - logsums[group_index])
        grad_group = grad_heads[:, group_index * per_group : (group_index + 1) * per_group, :]
        grad_probs = jnp.einsum(
            "qhd,kd->hqk",
            grad_group,
            value_low[:, group_index, :],
            preferred_element_type=jnp.float32,
        )
        centered = grad_probs - jnp.sum(softmax_weights * grad_probs, 2, keepdims=True)
        grad_scores = (softmax_weights * centered).astype(jnp.bfloat16)
        query_parts.append(
            jnp.einsum(
                "hqk,kd->qhd",
                grad_scores,
                key_rot[:, group_index, :],
                preferred_element_type=jnp.float32,
            )
            * scaling
        )
        key_parts.append(
            jnp.einsum("hqk,qhd->kd", grad_scores, chosen, preferred_element_type=jnp.float32)
            * scaling
        )
        value_parts.append(
            jnp.einsum(
                "hqk,qhd->kd",
                softmax_weights.astype(jnp.bfloat16),
                grad_group,
                preferred_element_type=jnp.float32,
            )
        )
    return (jnp.concatenate(query_parts, 1), jnp.stack(key_parts, 1), jnp.stack(value_parts, 1))


def on_device(
    tokens,
    seq_lens,
    norm_gains,
    w_query,
    key_weight,
    value_weight,
    w_out,
    w_gate,
    w_up,
    w_down,
    cotangent,
):
    rows_own = tokens.shape[0]
    row_count = rows_own * lax.axis_size("tensor")
    heads_query = w_query.shape[1] // HEAD_WIDTH
    heads_kv = key_weight.shape[1] // HEAD_WIDTH
    scaling = HEAD_WIDTH ** (-0.5)
    row_ids, segment, position, in_use = layout(seq_lens[0], row_count)
    in_use_own = lax.dynamic_slice_in_dim(in_use, lax.axis_index("tensor") * rows_own, rows_own, 0)
    cosine_lookup, sine_lookup = rope_tables(position, HEAD_WIDTH)
    allowed = (segment[:, None] == segment[None, :]) & (row_ids[None, :] <= row_ids[:, None])
    gain_rows = norm_gains.astype(jnp.float32)
    inputs = tokens.astype(jnp.float32)
    scale_one = lax.rsqrt(jnp.mean(inputs * inputs, 1, keepdims=True) + EPSILON)
    first_normalized = norm_rows((inputs * scale_one * gain_rows[0]).astype(jnp.bfloat16))
    query_all, key_all, value_all, out_all = (
        lax.all_gather(w_query, "dp", axis=0, tiled=True),
        lax.all_gather(key_weight, "dp", axis=0, tiled=True),
        lax.all_gather(value_weight, "dp", axis=0, tiled=True),
        lax.all_gather(w_out, "dp", axis=0, tiled=True),
    )
    query_rows = matrix_product(first_normalized, query_all).reshape(
        row_count, heads_query, HEAD_WIDTH
    )
    key_projected = matrix_product(first_normalized, key_all).reshape(
        row_count, heads_kv, HEAD_WIDTH
    )
    value_low = (
        matrix_product(first_normalized, value_all)
        .astype(jnp.bfloat16)
        .reshape(row_count, heads_kv, HEAD_WIDTH)
    )
    rotated_query = apply_rotation(query_rows, cosine_lookup, sine_lookup).astype(jnp.bfloat16)
    key_rot = apply_rotation(key_projected, cosine_lookup, sine_lookup).astype(jnp.bfloat16)
    attended, logsums = attend(rotated_query, key_rot, value_low, allowed, scaling)
    attended = attended.reshape(row_count, heads_query * HEAD_WIDTH).astype(jnp.bfloat16)
    state = inputs + branch_rows(matmul_nt(attended, out_all))
    scale_two = lax.rsqrt(jnp.mean(state * state, 1, keepdims=True) + EPSILON)
    normed_two = norm_rows((state * scale_two * gain_rows[1]).astype(jnp.bfloat16))
    width_ff = w_gate.shape[1]
    pieces = (
        lax.all_gather(w_gate, "dp", axis=0, tiled=True),
        lax.all_gather(w_up, "dp", axis=0, tiled=True),
    )
    columns = normed_two
    gate = matrix_product(columns, pieces[0])
    up_proj = matrix_product(columns, pieces[1])
    sigmoid_gate = jax.nn.sigmoid(gate)
    silu_gate = gate * sigmoid_gate
    hidden = (silu_gate * up_proj).astype(jnp.bfloat16)
    ffn_part = matmul_nt(hidden, lax.all_gather(w_down, "dp", axis=0, tiled=True))
    mixed = ((state + branch_rows(ffn_part)) * in_use_own[:, None]).astype(jnp.bfloat16)
    grad_mixed = cotangent.astype(jnp.float32) * in_use_own[:, None]
    grad_low = grad_rows(grad_mixed.astype(jnp.bfloat16))
    columns = grad_low
    grad_hidden = matrix_product(columns, lax.all_gather(w_down, "dp", axis=0, tiled=True))
    grad_gate_in = (
        grad_hidden * up_proj * sigmoid_gate * (1.0 + gate * (1.0 - sigmoid_gate))
    ).astype(jnp.bfloat16)
    grad_up_in = (grad_hidden * silu_gate).astype(jnp.bfloat16)
    pieces = lax.all_gather((w_gate, w_up), "dp", axis=0, tiled=True)
    grad_normed_part = matmul_nt(grad_gate_in, pieces[0]) + matmul_nt(grad_up_in, pieces[1])
    normed_cols = normed_two
    grad_cols = grad_low
    ffn_grads = lax.psum_scatter(
        jnp.concatenate(
            [
                matmul_tn(normed_cols, grad_gate_in),
                matmul_tn(normed_cols, grad_up_in),
                matmul_tn(grad_cols, hidden),
            ],
            1,
        ),
        "dp",
        scatter_dimension=0,
        tiled=True,
    )
    grad_normed_two = back_rows(grad_normed_part)
    hat_two = state * scale_two
    inner_two = grad_normed_two * gain_rows[1]
    grad_state = grad_mixed + scale_two * (
        inner_two - hat_two * jnp.mean(inner_two * hat_two, 1, keepdims=True)
    )
    gain_two = jnp.sum(grad_normed_two * hat_two, 0)
    grad_state_low = grad_rows(grad_state.astype(jnp.bfloat16))
    query_all, key_all, value_all, out_all = (
        lax.all_gather(w_query, "dp", axis=0, tiled=True),
        lax.all_gather(key_weight, "dp", axis=0, tiled=True),
        lax.all_gather(value_weight, "dp", axis=0, tiled=True),
        lax.all_gather(w_out, "dp", axis=0, tiled=True),
    )
    grad_attended = (
        matrix_product(grad_state_low, out_all)
        .astype(jnp.bfloat16)
        .reshape(row_count, heads_query, HEAD_WIDTH)
    )
    grad_query_rot, grad_key_rot, grad_values = attend_back(
        rotated_query, key_rot, value_low, grad_attended, logsums, allowed, scaling
    )
    grad_q = (
        unrotate(grad_query_rot, cosine_lookup, sine_lookup)
        .reshape(row_count, heads_query * HEAD_WIDTH)
        .astype(jnp.bfloat16)
    )
    grad_k = (
        unrotate(grad_key_rot, cosine_lookup, sine_lookup)
        .reshape(row_count, heads_kv * HEAD_WIDTH)
        .astype(jnp.bfloat16)
    )
    grad_v = grad_values.reshape(row_count, heads_kv * HEAD_WIDTH).astype(jnp.bfloat16)
    grad_first_part = (
        matmul_nt(grad_q, query_all) + matmul_nt(grad_k, key_all) + matmul_nt(grad_v, value_all)
    )
    normed_cols = first_normalized
    grad_cols = grad_state_low
    attention_grads = lax.psum_scatter(
        jnp.concatenate(
            [
                matmul_tn(normed_cols, grad_q),
                matmul_tn(normed_cols, grad_k),
                matmul_tn(normed_cols, grad_v),
                matmul_tn(grad_cols, attended),
            ],
            1,
        ),
        "dp",
        scatter_dimension=0,
        tiled=True,
    )
    grad_normed_one = back_rows(grad_first_part)
    hat_one = inputs * scale_one
    inner_one = grad_normed_one * gain_rows[0]
    grad_tokens = (
        grad_state
        + scale_one * (inner_one - hat_one * jnp.mean(inner_one * hat_one, 1, keepdims=True))
    ).astype(jnp.bfloat16)
    gain_one = jnp.sum(grad_normed_one * hat_one, 0)
    grad_gains = lax.psum(jnp.stack([gain_one, gain_two]), ("dp", "tensor"))
    width_query = w_query.shape[1]
    width_kv = key_weight.shape[1]
    grad_query = attention_grads[:, :width_query]
    grad_key = attention_grads[:, width_query : width_query + width_kv]
    grad_value = attention_grads[:, width_query + width_kv : width_query + 2 * width_kv]
    grad_out = attention_grads[:, width_query + 2 * width_kv :]
    grad_gate = ffn_grads[:, :width_ff]
    grad_up = ffn_grads[:, width_ff : 2 * width_ff]
    grad_down = ffn_grads[:, 2 * width_ff :]
    return (
        mixed,
        grad_tokens,
        grad_gains,
        grad_query,
        grad_key,
        grad_value,
        grad_out,
        grad_gate,
        grad_up,
        grad_down,
    )


def solution(mesh):
    in_specs = (
        P(("dp", "tensor"), None),
        P("dp", None),
        P(),
        P("dp", "tensor"),
        P("dp", "tensor"),
        P("dp", "tensor"),
        P("dp", "tensor"),
        P("dp", "tensor"),
        P("dp", "tensor"),
        P("dp", "tensor"),
        P(("dp", "tensor"), None),
    )
    out_specs = (
        P(("dp", "tensor"), None),
        P(("dp", "tensor"), None),
        P(),
        P("dp", "tensor"),
        P("dp", "tensor"),
        P("dp", "tensor"),
        P("dp", "tensor"),
        P("dp", "tensor"),
        P("dp", "tensor"),
        P("dp", "tensor"),
    )
    return jax.shard_map(
        on_device, mesh=mesh, in_specs=in_specs, out_specs=out_specs, check_vma=False
    )
```

profile of v0, /device:TPU:0, one launch (start us, length us, event | category | flops | bytes accessed | tf_op | source)
XLA Modules:
  0.0 2738.3 jit_solution(4895292713138647162)
XLA Ops:
  17.4 18.1 all-gather.12.cloned.1.call-done
  35.5 40.1 %all-gather.16.cloned.1.call-done = bf16[2048,256]{1,0:T(8,128)(2,1)} async-done(((bf16[128,256]{1,0:T(8,128)(2,1)}), bf16[2048,256]{1,0:T(8,128)(2,1)}) %all-gather.16.cloned.1.call-update) | async-done | bytes 1048592 | tf_op jit(solution)/shard_map/all_gather | solution.py:193
  77.8 36.9 %all-gather.14.cloned.1.call-done = bf16[2048,256]{1,0:T(8,128)(2,1)} async-done(((bf16[128,256]{1,0:T(8,128)(2,1)}), bf16[2048,256]{1,0:T(8,128)(2,1)}) %all-gather.14.cloned.1.call-update) | async-done | bytes 1048592 | tf_op jit(solution)/shard_map/all_gather | solution.py:194
  116.7 49.5 %all-gather.18.cloned.1.call-done = bf16[2048,1024]{1,0:T(8,128)(2,1)} async-done(((bf16[128,1024]{1,0:T(8,128)(2,1)}), bf16[2048,1024]{1,0:T(8,128)(2,1)}) %all-gather.18.cloned.1.call-update) | async-done | bytes 4194320 | tf_op jit(solution)/shard_map/all_gather | solution.py:192
  176.4 40.9 %all-gather.20.cloned.1.call-done = bf16[2048,1024]{1,0:T(8,128)(2,1)} async-done(((bf16[128,1024]{1,0:T(8,128)(2,1)}), bf16[2048,1024]{1,0:T(8,128)(2,1)}) %all-gather.20.cloned.1.call-update) | async-done | bytes 4194320 | tf_op jit(solution)/shard_map/all_gather | solution.py:195
  217.3 5.0 fusion.96
  222.3 30.4 %reduce-scatter.6.cloned.1.call-done = f32[128,2048]{1,0:T(8,128)} async-done(((f32[256,2048]{1,0:T(8,128)}), f32[128,2048]{1,0:T(8,128)}) %reduce-scatter.6.cloned.1.call-update) | async-done | bytes 1048592 | tf_op jit(solution)/shard_map/reduce_scatter | solution.py:81
  262.2 15.6 all-gather.22.cloned.1.call-done
  277.8 129.3 %all-gather.24.cloned.1.call-done = bf16[2048,4096]{1,0:T(8,128)(2,1)} async-done(((bf16[128,4096]{1,0:T(8,128)(2,1)}), bf16[2048,4096]{1,0:T(8,128)(2,1)}) %all-gather.24.cloned.1.call-update) | async-done | bytes 16777232 | tf_op jit(solution)/shard_map/all_gather | solution.py:217
  407.1 12.5 fusion.97
  419.7 114.9 %all-gather.26.cloned.1.call-done = bf16[2048,4096]{1,0:T(8,128)(2,1)} async-done(((bf16[128,4096]{1,0:T(8,128)(2,1)}), bf16[2048,4096]{1,0:T(8,128)(2,1)}) %all-gather.26.cloned.1.call-update) | async-done | bytes 16777232 | tf_op jit(solution)/shard_map/all_gather | solution.py:218
  534.5 12.6 fusion.98
  547.1 9.0 all-gather.30.cloned.1.call-done
  556.1 129.3 %all-gather.28.cloned.1.call-done = bf16[2048,4096]{1,0:T(8,128)(2,1)} async-done(((bf16[128,4096]{1,0:T(8,128)(2,1)}), bf16[2048,4096]{1,0:T(8,128)(2,1)}) %all-gather.28.cloned.1.call-update) | async-done | bytes 16777232 | tf_op jit(solution)/shard_map/all_gather | solution.py:226
  685.4 13.4 multiply_convert_fusion
  698.9 12.3 fusion.100
  711.2 12.9 convolution_add_fusion.2
  724.0 11.8 reduce-scatter.8.cloned.1.call-start
  735.9 12.4 fusion.99
  748.3 5.9 reduce-scatter.10.cloned.1.call-done
  757.2 31.1 %reduce-scatter.8.cloned.1.call-done = f32[128,2048]{1,0:T(8,128)} async-done(((f32[256,2048]{1,0:T(8,128)}), f32[128,2048]{1,0:T(8,128)}) %reduce-scatter.8.cloned.1.call-update) | async-done | bytes 1048592 | tf_op jit(solution)/shard_map/reduce_scatter | solution.py:81
  792.2 21.4 all-gather.32.cloned.1.call-done
  813.6 4.6 convolution_convert_fusion
  838.2 9.3 pad_maximum_fusion.1
  847.8 17.9 fusion.104
  865.7 15.7 fusion.103
  881.5 19.7 fusion.102
  901.2 66.8 %pad_maximum_fusion = f32[2048,12288]{1,0:T(8,128)} fusion(f32[2048,4096]{1,0:T(8,128)} %fusion.104, f32[2048,4096]{1,0:T(8,128)} %fusion.103, f32[2048,4096]{1,0:T(8,128)} %fusion.102), kind=kLoop, calls=%fused_computation | loop fusion | flops 50331648 | bytes 201326592 | tf_op jit(solution)/shard_map/concatenate | solution.py:241
  971.5 42.2 %psum.7 = f32[2,2048]{1,0:T(2,128)} all-reduce(f32[2,2048]{1,0:T(2,128)S(1)} %pad_maximum_fusion.8), channel_id=1, replica_groups=mesh['dp'=16,'tensor'=2] {'dp','tensor'}, use_global_device_ids=true, to_apply=%region_25.26 | all-reduce | flops 4096 | bytes 32768 | tf_op jit(solution)/shard_map/psum | solution.py:313
  1016.2 65.8 %reduce-scatter.14.cloned.1.call-done = f32[128,2560]{0,1:T(8,128)} async-done(((f32[2048,2560]{0,1:T(8,128)}), f32[128,2560]{0,1:T(8,128)}) %reduce-scatter.14.cloned.1.call-update) | async-done | bytes 1310736 | tf_op jit(solution)/shard_map/reduce_scatter | solution.py:291
  1087.7 1636.9 %all-reduce.3.cloned.1.call-done = f32[2048,12288]{1,0:T(8,128)} async-done(((f32[2048,12288]{1,0:T(8,128)}), f32[2048,12288]{1,0:T(8,128)}) %all-reduce.3.cloned.1.call-update) | async-done | bytes 100663312
  2724.6 6.8 fusion.84
  (196 shorter events, 71.6 us)
Async XLA Ops:
  7.2 28.3 %all-gather.12.cloned.1.call-start = ((), (), s32[]{:S(2)}) async-start(), calls=%async_computation.5 | async-start | bytes 1572864 | tf_op jit(solution)/shard_map/all_gather | solution.py:77
  8.0 9.3 copy-start.18
  9.3 8.1 copy-start.28
  11.3 64.3 %all-gather.16.cloned.1.call-start = ((), (), s32[]{:S(2)}) async-start(), calls=%async_computation.7 | async-start | bytes 1114112 | tf_op jit(solution)/shard_map/all_gather | solution.py:193
  12.1 102.6 %all-gather.14.cloned.1.call-start = ((), (), s32[]{:S(2)}) async-start(), calls=%async_computation.6 | async-start | bytes 1114112 | tf_op jit(solution)/shard_map/all_gather | solution.py:194
  12.8 153.4 %all-gather.18.cloned.1.call-start = ((), (), s32[]{:S(2)}) async-start(), calls=%async_computation.8 | async-start | bytes 4456448 | tf_op jit(solution)/shard_map/all_gather | solution.py:192
  13.4 203.9 %all-gather.20.cloned.1.call-start = ((), (), s32[]{:S(2)}) async-start(), calls=%async_computation.9 | async-start | bytes 4456448 | tf_op jit(solution)/shard_map/all_gather | solution.py:195
  14.0 238.8 %reduce-scatter.6.cloned.1.call-start = ((), (), s32[]{:S(2)}) async-start(), calls=%async_computation.10 | async-start | bytes 3145728 | tf_op jit(solution)/shard_map/reduce_scatter | solution.py:81
  16.9 60.8 %copy-start.27 = (s32[256]{0:T(256)}, s32[256]{0:T(256)S(1)}, u32[]{:S(2)}) copy-start(s32[256]{0:T(256)S(1)} %convert_reduce_fusion) | copy-start | bytes 3076
  17.4 153.1 %copy-start.24 = (pred[256,256]{0,1:T(8,128)(4,1)}, pred[256,256]{0,1:T(8,128)(4,1)S(1)}, u32[]{:S(2)}) copy-start(pred[256,256]{0,1:T(8,128)(4,1)S(1)} %fusion.57) | copy-start | bytes 196612
  35.5 130.7 %copy-start = (bf16[256,2048]{1,0:T(8,128)(2,1)S(1)}, bf16[256,2048]{1,0:T(8,128)(2,1)}, u32[]{:S(2)}) copy-start(bf16[256,2048]{1,0:T(8,128)(2,1)} %all-gather.12.cloned.1.call-done) | copy-start | bytes 3145732
  170.4 3.6 copy-start.15
  222.3 55.5 %all-gather.22.cloned.1.call-start = ((), (), s32[]{:S(2)}) async-start(), calls=%async_computation.11 | async-start | bytes 1572864 | tf_op jit(solution)/shard_map/all_gather | solution.py:77
  256.3 150.8 %all-gather.24.cloned.1.call-start = ((), (), s32[]{:S(2)}) async-start(), calls=%async_computation.12 | async-start | bytes 17825792 | tf_op jit(solution)/shard_map/all_gather | solution.py:217
  257.1 277.5 %all-gather.26.cloned.1.call-start = ((), (), s32[]{:S(2)}) async-start(), calls=%async_computation.13 | async-start | bytes 17825792 | tf_op jit(solution)/shard_map/all_gather | solution.py:218
  257.8 298.3 %all-gather.30.cloned.1.call-start = ((), (), s32[]{:S(2)}) async-start(), calls=%async_computation.16 | async-start | bytes 1572864 | tf_op jit(solution)/shard_map/all_gather | solution.py:85
  261.2 424.2 %all-gather.28.cloned.1.call-start = ((), (), s32[]{:S(2)}) async-start(), calls=%async_computation.14 | async-start | bytes 17825792 | tf_op jit(solution)/shard_map/all_gather | solution.py:226
  261.9 492.3 %reduce-scatter.10.cloned.1.call-start = ((), (), s32[]{:S(2)}) async-start(), calls=%async_computation.17 | async-start | bytes 3145728 | tf_op jit(solution)/shard_map/reduce_scatter | solution.py:89
  724.0 64.2 %reduce-scatter.8.cloned.1.call-start = ((), (), s32[]{:S(2)}) async-start(), calls=%async_computation.15 | async-start | bytes 3145728 | tf_op jit(solution)/shard_map/reduce_scatter | solution.py:81
  748.2 65.3 %all-gather.32.cloned.1.call-start = ((), (), s32[]{:S(2)}) async-start(), calls=%async_computation.18 | async-start | bytes 1572864 | tf_op jit(solution)/shard_map/all_gather | solution.py:85
  792.1 177.7 %reduce-scatter.12.cloned.1.call-start = ((), (), s32[]{:S(2)}) async-start(), calls=%async_computation.19 | async-start | bytes 3145728 | tf_op jit(solution)/shard_map/reduce_scatter | solution.py:89
  818.1 4.7 copy-start.21
  818.1 5.1 copy-start.23
  820.2 3.0 copy-start.4
  828.2 3.1 copy-start.10
  834.3 247.6 %reduce-scatter.14.cloned.1.call-start = ((), (), s32[]{:S(2)}) async-start(), calls=%async_computation.20 | async-start | bytes 22282240 | tf_op jit(solution)/shard_map/reduce_scatter | solution.py:291
  847.5 18.2 copy-start.7
  847.5 18.2 copy-start.14
  847.5 1877.0 %all-reduce.3.cloned.1.call-start = ((), (), s32[]{:S(2)}) async-start(), calls=%async_computation.21 | async-start | bytes 201326592
  865.7 15.7 copy-start.13
  968.0 3.5 copy-start.26
  968.0 45.8 %copy-start.9 = (f32[128,2048]{1,0:T(8,128)S(1)}, f32[128,2048]{1,0:T(8,128)}, u32[]{:S(2)}) copy-start(f32[128,2048]{1,0:T(8,128)} %get-tuple-element.55) | copy-start | bytes 3145732
  (19 other events, 28.6 us)
Sparse Core Ops, SparseCore 0:
  11.4 23.9 all-gather.11
  37.6 37.9 all-gather.15
  77.8 36.8 all-gather.13
  116.7 49.4 all-gather.17
  168.2 49.0 all-gather.19
  222.4 30.2 reduce-scatter.5
  256.4 21.3 all-gather.21
  280.2 126.8 all-gather.23
  409.5 124.9 all-gather.25
  536.6 19.4 all-gather.29
  558.5 126.8 all-gather.27
  724.2 29.9 reduce-scatter.9
  756.4 31.8 reduce-scatter.7
  792.2 21.2 all-gather.31
  834.5 31.8 reduce-scatter.11
  870.3 211.6 reduce-scatter.13
  1086.1 1638.4 all-reduce.2
where the time goes:
time: 2750 us; the launch traced here: 2740 us
  waiting for transfers between devices  2380 us (87%)
  matrix products  165 us (6%)
  other arithmetic  101 us (4%)
  blocking collectives  42.2 us (2%)
    unnamed x18, waiting for transfers between devices  1640 us
    all_gather x1, waiting for transfers between devices, on_device(): lax.all_gather(w_down, 'dp', axis=0, tiled=True)  129 us
    all_gather x1, waiting for transfers between devices, on_device(): lax.all_gather(w_gate, 'dp', axis=0, tiled=True)  129 us
    all_gather x1, waiting for transfers between devices, on_device(): lax.all_gather(w_up, 'dp', axis=0, tiled=True)  115 us
    concatenate x1, other arithmetic, on_device(): jnp.concatenate([matmul_tn(normed_cols, grad_gate_in), matmul_tn(normed_c...  66.8 us
    reduce_scatter x1, waiting for transfers between devices, on_device(): lax.psum_scatter(jnp.concatenate([matmul_tn(normed_cols, grad_q), matmul_...  65.8 us
    reduce_scatter x2, waiting for transfers between devices, branch_rows(): return lax.psum_scatter(operand, 'tensor', scatter_dimension=0, tiled=True)  61.5 us
    dot_general x7, matrix products, matmul_tn(): lax.dot_general(left_side, right_side, (((0,), (0,)), ((), ())), preferre...  56.8 us
  transfers between devices with their start and end apart: 17, of which 16 were waited for; matrix products, arithmetic and copies ran while one was open for 7% of the time, Pallas kernels for 0%

commit v1 on v0

--- a/solution.py
+++ b/solution.py
@@ -6,10 +6,10 @@
 from jax.sharding import PartitionSpec as P
 
 HEAD_WIDTH = 64
-
-
 EPSILON = 1e-05
 MASKED = -1e30
+CORES = 2
+PLANES = 4
 
 
 def matrix_product(left_side, right_side):
@@ -26,6 +26,10 @@
     return lax.dot_general(
         left_side, right_side, (((0,), (0,)), ((), ())), preferred_element_type=jnp.float32
     )
+
+
+def after(value, *earlier):
+    return lax.optimization_barrier((value, *earlier))[0]
 
 
 def layout(lengths, row_count):
@@ -71,22 +75,6 @@
     return grads * cosine_lookup[:, None, :] + jnp.concatenate(
         [scaled[..., halfway:], -scaled[..., :halfway]], -1
     )
-
-
-def norm_rows(operand):
-    return lax.all_gather(operand, "tensor", axis=0, tiled=True)
-
-
-def branch_rows(operand):
-    return lax.psum_scatter(operand, "tensor", scatter_dimension=0, tiled=True)
-
-
-def grad_rows(operand):
-    return lax.all_gather(operand, "tensor", axis=0, tiled=True)
-
-
-def back_rows(operand):
-    return lax.psum_scatter(operand, "tensor", scatter_dimension=0, tiled=True)
 
 
 def group_scores(rotated_query, key_rot, group_index, allowed, scaling):
@@ -162,6 +150,161 @@
     return (jnp.concatenate(query_parts, 1), jnp.stack(key_parts, 1), jnp.stack(value_parts, 1))
 
 
+class Places:
+    def __init__(self, dp):
+        self.dp = dp
+        self.planes = PLANES
+        self.rows = dp // (PLANES * CORES)
+        self.chips = dp // CORES
+        index = lax.axis_index("dp")
+        self.z = index // (self.rows * CORES)
+        self.y = (index // CORES) % self.rows
+        self.core = index % CORES
+        self.x = lax.axis_index("tensor")
+        chip = index // CORES
+        self.ring_place = jnp.where(chip % 2 == 0, chip // 2, self.chips - 1 - chip // 2)
+
+    def move(self, value, target):
+        return lax.ppermute(value, "dp", [(d, target(d)) for d in range(self.dp)])
+
+    def along_z(self, value, steps):
+        stride = self.rows * CORES
+        return self.move(value, lambda d: (d + steps * stride) % self.dp)
+
+    def along_y(self, value, steps):
+        def target(d):
+            y = (d // CORES) % self.rows
+            return d + ((y + steps) % self.rows - y) * CORES
+
+        return self.move(value, target)
+
+    def other_core(self, value):
+        return self.move(value, lambda d: d ^ 1)
+
+    def other_x(self, value):
+        return lax.ppermute(value, "tensor", [(0, 1), (1, 0)])
+
+    def ring_chip(self, place):
+        place = place % self.chips
+        half = self.chips // 2
+        return jnp.where(place < half, 2 * place, 2 * (self.chips - 1 - place) + 1)
+
+    def along_ring(self, value, steps):
+        half = self.chips // 2
+        cycle = [2 * p if p < half else 2 * (self.chips - 1 - p) + 1 for p in range(self.chips)]
+        place_of = {chip: p for p, chip in enumerate(cycle)}
+
+        def target(d):
+            chip = cycle[(place_of[d // CORES] + steps) % self.chips]
+            return chip * CORES + d % CORES
+
+        return self.move(value, target)
+
+
+def ring_gather(at, clockwise, counter):
+    currents = [clockwise, counter]
+    buffers = [
+        jnp.zeros((at.chips, CORES) + part.shape, part.dtype) for part in (clockwise, counter)
+    ]
+    for step in range(at.chips):
+        for way, sign in ((0, 1), (1, -1)):
+            block = currents[way]
+            chip = at.ring_chip(at.ring_place - sign * step)
+            if step < at.chips - 1:
+                currents[way] = at.along_ring(block, sign)
+            twin = at.other_core(block)
+            buffers[way] = lax.dynamic_update_slice(
+                buffers[way], block[None, None], (chip, at.core, 0, 0)
+            )
+            buffers[way] = lax.dynamic_update_slice(
+                buffers[way], twin[None, None], (chip, 1 - at.core, 0, 0)
+            )
+    return [buffer.reshape(-1, buffer.shape[-1]) for buffer in buffers]
+
+
+def ring_scatter(at, clockwise, counter):
+    locals_ = []
+    for part in (clockwise, counter):
+        blocks = part.reshape(at.chips, CORES, -1, part.shape[-1])
+        away = lax.dynamic_index_in_dim(blocks, 1 - at.core, 1, keepdims=False)
+        mine = lax.dynamic_index_in_dim(blocks, at.core, 1, keepdims=False)
+        locals_.append((mine.astype(jnp.float32) + at.other_core(away)).astype(jnp.bfloat16))
+
+    def local(way, place):
+        return lax.dynamic_index_in_dim(locals_[way], at.ring_chip(place), 0, keepdims=False)
+
+    totals = [local(way, at.ring_place - sign) for way, sign in ((0, 1), (1, -1))]
+    for step in range(1, at.chips):
+        for way, sign in ((0, 1), (1, -1)):
+            arrived = at.along_ring(totals[way], sign).astype(jnp.float32)
+            total = arrived + local(way, at.ring_place - sign * (step + 1)).astype(jnp.float32)
+            totals[way] = total if step == at.chips - 1 else total.astype(jnp.bfloat16)
+    return totals
+
+
+def quarter_gather(at, parts, quarter):
+    count, own_rows, _ = parts.shape
+    buffer = jnp.zeros((count, at.planes, at.rows, CORES, own_rows, quarter), parts.dtype)
+    for k in (2, 1, 3, 0):
+        wanted = ((at.z + k) % at.planes) * quarter
+        block = lax.dynamic_slice(parts, (0, 0, wanted), (count, own_rows, quarter))
+        if k:
+            block = at.along_z(block, k)
+        plane = (at.z - k) % at.planes
+        for j in range(at.rows):
+            other = at.along_y(block, j) if j else block
+            row = (at.y - j) % at.rows
+            for core, piece in ((at.core, other), (1 - at.core, at.other_core(other))):
+                buffer = lax.dynamic_update_slice(
+                    buffer, piece[:, None, None, None], (0, plane, row, core, 0, 0)
+                )
+    return buffer.reshape(count, -1, quarter)
+
+
+def quarter_scatter(at, grads):
+    columns = grads.shape[-1]
+    blocks = grads.reshape(at.planes, at.rows, CORES, -1, columns)
+    away = lax.dynamic_index_in_dim(blocks, 1 - at.core, 2, keepdims=False)
+    mine = lax.dynamic_index_in_dim(blocks, at.core, 2, keepdims=False)
+    blocks = (mine.astype(jnp.float32) + at.other_core(away)).astype(jnp.bfloat16)
+    total = lax.dynamic_index_in_dim(blocks, at.y, 1, keepdims=False).astype(jnp.float32)
+    for j in range(1, at.rows):
+        away = lax.dynamic_index_in_dim(blocks, (at.y + j) % at.rows, 1, keepdims=False)
+        total = total + at.along_y(away, j)
+    result = jnp.zeros((total.shape[1], at.planes * columns), jnp.float32)
+    low = total.astype(jnp.bfloat16)
+    for k in (2, 1, 3, 0):
+        if k:
+            piece = at.along_z(
+                lax.dynamic_index_in_dim(low, (at.z + k) % at.planes, 0, keepdims=False), k
+            )
+        else:
+            piece = lax.dynamic_index_in_dim(total, at.z, 0, keepdims=False)
+        result = lax.dynamic_update_slice(
+            result, piece.astype(jnp.float32), (0, ((at.z - k) % at.planes) * columns)
+        )
+    return result
+
+
+def token_gather(at, own):
+    blocks = []
+    for k in range(at.planes):
+        block = at.along_z(own, k) if k else own
+        blocks += [block, at.other_x(block)]
+    return jnp.concatenate(blocks, 0)
+
+
+def token_scatter(at, part_of, rows_own):
+    total = None
+    for k in (2, 1, 3, 0):
+        part = part_of(k)
+        mine = part[:rows_own] + at.other_x(part[rows_own:].astype(jnp.bfloat16))
+        if k:
+            mine = at.along_z(mine.astype(jnp.bfloat16), -k)
+        total = mine.astype(jnp.float32) if total is None else total + mine
+    return total
+
+
 def on_device(
     tokens,
     seq_lens,
@@ -175,31 +318,50 @@
     w_down,
     cotangent,
 ):
+    at = Places(lax.axis_size("dp"))
     rows_own = tokens.shape[0]
     row_count = rows_own * lax.axis_size("tensor")
-    heads_query = w_query.shape[1] // HEAD_WIDTH
-    heads_kv = key_weight.shape[1] // HEAD_WIDTH
+    width_query = w_query.shape[1]
+    width_kv = key_weight.shape[1]
+    heads_query = width_query // HEAD_WIDTH
+    heads_kv = width_kv // HEAD_WIDTH
+    width_quarter = w_gate.shape[1] // at.planes
     scaling = HEAD_WIDTH ** (-0.5)
+
+    def both_x(own, other):
+        first = jnp.where(at.x == 0, own, other)
+        second = jnp.where(at.x == 0, other, own)
+        return jnp.concatenate([first, second], 0)
+
+    def sum_x(part):
+        other = lax.dynamic_slice_in_dim(part, (1 - at.x) * rows_own, rows_own, 0)
+        mine = lax.dynamic_slice_in_dim(part, at.x * rows_own, rows_own, 0)
+        return mine + at.other_x(other.astype(jnp.bfloat16))
+
     row_ids, segment, position, in_use = layout(seq_lens[0], row_count)
-    in_use_own = lax.dynamic_slice_in_dim(in_use, lax.axis_index("tensor") * rows_own, rows_own, 0)
+    in_use_own = lax.dynamic_slice_in_dim(in_use, at.x * rows_own, rows_own, 0)
     cosine_lookup, sine_lookup = rope_tables(position, HEAD_WIDTH)
     allowed = (segment[:, None] == segment[None, :]) & (row_ids[None, :] <= row_ids[:, None])
     gain_rows = norm_gains.astype(jnp.float32)
     inputs = tokens.astype(jnp.float32)
     scale_one = lax.rsqrt(jnp.mean(inputs * inputs, 1, keepdims=True) + EPSILON)
-    first_normalized = norm_rows((inputs * scale_one * gain_rows[0]).astype(jnp.bfloat16))
-    query_all, key_all, value_all, out_all = (
-        lax.all_gather(w_query, "dp", axis=0, tiled=True),
-        lax.all_gather(key_weight, "dp", axis=0, tiled=True),
-        lax.all_gather(value_weight, "dp", axis=0, tiled=True),
-        lax.all_gather(w_out, "dp", axis=0, tiled=True),
-    )
-    query_rows = matrix_product(first_normalized, query_all).reshape(
-        row_count, heads_query, HEAD_WIDTH
-    )
-    key_projected = matrix_product(first_normalized, key_all).reshape(
-        row_count, heads_kv, HEAD_WIDTH
-    )
+    normed_own = (inputs * scale_one * gain_rows[0]).astype(jnp.bfloat16)
+    first_normalized = both_x(normed_own, at.other_x(normed_own))
+    grad_mixed = cotangent.astype(jnp.float32) * in_use_own[:, None]
+    grad_low_own = grad_mixed.astype(jnp.bfloat16)
+
+    qk_all, vo_all = ring_gather(
+        at,
+        jnp.concatenate([w_query, key_weight], 1),
+        jnp.concatenate([value_weight, w_out], 1),
+    )
+    value_all, out_all = vo_all[:, :width_kv], vo_all[:, width_kv:]
+    ffn_own = after(jnp.stack([w_gate, w_up, w_down]), qk_all, vo_all)
+    gate_all, up_all, down_all = quarter_gather(at, ffn_own, width_quarter)
+
+    qk_rows = matrix_product(first_normalized, qk_all)
+    query_rows = qk_rows[:, :width_query].reshape(row_count, heads_query, HEAD_WIDTH)
+    key_projected = qk_rows[:, width_query:].reshape(row_count, heads_kv, HEAD_WIDTH)
     value_low = (
         matrix_product(first_normalized, value_all)
         .astype(jnp.bfloat16)
@@ -209,61 +371,47 @@
     key_rot = apply_rotation(key_projected, cosine_lookup, sine_lookup).astype(jnp.bfloat16)
     attended, logsums = attend(rotated_query, key_rot, value_low, allowed, scaling)
     attended = attended.reshape(row_count, heads_query * HEAD_WIDTH).astype(jnp.bfloat16)
-    state = inputs + branch_rows(matmul_nt(attended, out_all))
+    state = inputs + sum_x(matmul_nt(attended, out_all))
     scale_two = lax.rsqrt(jnp.mean(state * state, 1, keepdims=True) + EPSILON)
-    normed_two = norm_rows((state * scale_two * gain_rows[1]).astype(jnp.bfloat16))
-    width_ff = w_gate.shape[1]
-    pieces = (
-        lax.all_gather(w_gate, "dp", axis=0, tiled=True),
-        lax.all_gather(w_up, "dp", axis=0, tiled=True),
-    )
-    columns = normed_two
-    gate = matrix_product(columns, pieces[0])
-    up_proj = matrix_product(columns, pieces[1])
+    normed_two = token_gather(at, (state * scale_two * gain_rows[1]).astype(jnp.bfloat16))
+    grad_low = token_gather(at, after(grad_low_own, normed_two))
+
+    gate = matrix_product(normed_two, gate_all)
+    up_proj = matrix_product(normed_two, up_all)
     sigmoid_gate = jax.nn.sigmoid(gate)
     silu_gate = gate * sigmoid_gate
     hidden = (silu_gate * up_proj).astype(jnp.bfloat16)
-    ffn_part = matmul_nt(hidden, lax.all_gather(w_down, "dp", axis=0, tiled=True))
-    mixed = ((state + branch_rows(ffn_part)) * in_use_own[:, None]).astype(jnp.bfloat16)
-    grad_mixed = cotangent.astype(jnp.float32) * in_use_own[:, None]
-    grad_low = grad_rows(grad_mixed.astype(jnp.bfloat16))
-    columns = grad_low
-    grad_hidden = matrix_product(columns, lax.all_gather(w_down, "dp", axis=0, tiled=True))
+    grad_hidden = matrix_product(grad_low, down_all)
     grad_gate_in = (
         grad_hidden * up_proj * sigmoid_gate * (1.0 + gate * (1.0 - sigmoid_gate))
     ).astype(jnp.bfloat16)
     grad_up_in = (grad_hidden * silu_gate).astype(jnp.bfloat16)
-    pieces = lax.all_gather((w_gate, w_up), "dp", axis=0, tiled=True)
-    grad_normed_part = matmul_nt(grad_gate_in, pieces[0]) + matmul_nt(grad_up_in, pieces[1])
-    normed_cols = normed_two
-    grad_cols = grad_low
-    ffn_grads = lax.psum_scatter(
-        jnp.concatenate(
-            [
-                matmul_tn(normed_cols, grad_gate_in),
-                matmul_tn(normed_cols, grad_up_in),
-                matmul_tn(grad_cols, hidden),
-            ],
-            1,
-        ),
-        "dp",
-        scatter_dimension=0,
-        tiled=True,
-    )
-    grad_normed_two = back_rows(grad_normed_part)
+
+    def rows_of(value, k):
+        return value[k * row_count : (k + 1) * row_count]
+
+    grad_normed_two = token_scatter(
+        at,
+        lambda k: matmul_nt(rows_of(grad_gate_in, k), gate_all)
+        + matmul_nt(rows_of(grad_up_in, k), up_all),
+        rows_own,
+    )
+    hidden_late = after(hidden, grad_normed_two)
+    ffn_out = token_scatter(at, lambda k: matmul_nt(rows_of(hidden_late, k), down_all), rows_own)
+    mixed = ((state + ffn_out) * in_use_own[:, None]).astype(jnp.bfloat16)
     hat_two = state * scale_two
     inner_two = grad_normed_two * gain_rows[1]
     grad_state = grad_mixed + scale_two * (
         inner_two - hat_two * jnp.mean(inner_two * hat_two, 1, keepdims=True)
     )
     gain_two = jnp.sum(grad_normed_two * hat_two, 0)
-    grad_state_low = grad_rows(grad_state.astype(jnp.bfloat16))
-    query_all, key_all, value_all, out_all = (
-        lax.all_gather(w_query, "dp", axis=0, tiled=True),
-        lax.all_gather(key_weight, "dp", axis=0, tiled=True),
-        lax.all_gather(value_weight, "dp", axis=0, tiled=True),
-        lax.all_gather(w_out, "dp", axis=0, tiled=True),
-    )
+    grad_state_own = grad_state.astype(jnp.bfloat16)
+    grad_state_low = both_x(grad_state_own, at.other_x(grad_state_own))
+
+    grad_gate = quarter_scatter(at, matmul_tn(normed_two, grad_gate_in).astype(jnp.bfloat16))
+    grad_up = quarter_scatter(at, matmul_tn(normed_two, grad_up_in).astype(jnp.bfloat16))
+    grad_down = quarter_scatter(at, matmul_tn(grad_low, hidden).astype(jnp.bfloat16))
+
     grad_attended = (
         matrix_product(grad_state_low, out_all)
         .astype(jnp.bfloat16)
@@ -283,26 +431,18 @@
         .astype(jnp.bfloat16)
     )
     grad_v = grad_values.reshape(row_count, heads_kv * HEAD_WIDTH).astype(jnp.bfloat16)
-    grad_first_part = (
-        matmul_nt(grad_q, query_all) + matmul_nt(grad_k, key_all) + matmul_nt(grad_v, value_all)
-    )
-    normed_cols = first_normalized
-    grad_cols = grad_state_low
-    attention_grads = lax.psum_scatter(
-        jnp.concatenate(
-            [
-                matmul_tn(normed_cols, grad_q),
-                matmul_tn(normed_cols, grad_k),
-                matmul_tn(normed_cols, grad_v),
-                matmul_tn(grad_cols, attended),
-            ],
-            1,
-        ),
-        "dp",
-        scatter_dimension=0,
-        tiled=True,
-    )
-    grad_normed_one = back_rows(grad_first_part)
+    grad_qk = jnp.concatenate([grad_q, grad_k], 1)
+    grad_vo = jnp.concatenate(
+        [
+            matmul_tn(first_normalized, grad_v).astype(jnp.bfloat16),
+            matmul_tn(grad_state_low, attended).astype(jnp.bfloat16),
+        ],
+        1,
+    )
+    sum_qk, sum_vo = ring_scatter(
+        at, matmul_tn(first_normalized, grad_qk).astype(jnp.bfloat16), grad_vo
+    )
+    grad_normed_one = sum_x(matmul_nt(grad_qk, qk_all) + matmul_nt(grad_v, value_all))
     hat_one = inputs * scale_one
     inner_one = grad_normed_one * gain_rows[0]
     grad_tokens = (
@@ -310,24 +450,20 @@
         + scale_one * (inner_one - hat_one * jnp.mean(inner_one * hat_one, 1, keepdims=True))
     ).astype(jnp.bfloat16)
     gain_one = jnp.sum(grad_normed_one * hat_one, 0)
-    grad_gains = lax.psum(jnp.stack([gain_one, gain_two]), ("dp", "tensor"))
-    width_query = w_query.shape[1]
-    width_kv = key_weight.shape[1]
-    grad_query = attention_grads[:, :width_query]
-    grad_key = attention_grads[:, width_query : width_query + width_kv]
-    grad_value = attention_grads[:, width_query + width_kv : width_query + 2 * width_kv]
-    grad_out = attention_grads[:, width_query + 2 * width_kv :]
-    grad_gate = ffn_grads[:, :width_ff]
-    grad_up = ffn_grads[:, width_ff : 2 * width_ff]
-    grad_down = ffn_grads[:, 2 * width_ff :]
+    grad_gains = jnp.stack([gain_one, gain_two])
+    grad_gains = grad_gains + at.other_x(grad_gains)
+    bit = 1
+    while bit < at.dp:
+        grad_gains = grad_gains + at.move(grad_gains, lambda d: d ^ bit)
+        bit *= 2
     return (
         mixed,
         grad_tokens,
         grad_gains,
-        grad_query,
-        grad_key,
-        grad_value,
-        grad_out,
+        sum_qk[:, :width_query],
+        sum_qk[:, width_query:],
+        sum_vo[:, :width_kv],
+        sum_vo[:, width_kv:],
         grad_gate,
         grad_up,
         grad_down,

time: 2750 us -> 790 us (0.29)
  waiting for transfers between devices: 2380 us -> 346 us
  starting transfers between devices: 12.9 us -> 143 us
  local copies, waits for them, and re-layouts: 21.6 us -> 145 us
  other arithmetic: 101 us -> 37.8 us
  matrix products: 165 us -> 108 us
  blocking collectives: 42.2 us -> 0 us
    unnamed x18 -> x0, waiting for transfers between devices: 1640 us -> none
    all_gather x11 -> x0, waiting for transfers between devices: 605 us -> none  [the longest x1 129 us: on_device(): lax.all_gather(w_down, 'dp', axis=0, tiled=True)]
    ppermute x0 -> x113, waiting for transfers between devices: none -> 346 us  [the longest x92 258 us: move(): return lax.ppermute(value, 'dp', [(d, target(d)) for d in range(self.dp)])]
    ppermute x0 -> x113, starting transfers between devices: none -> 143 us  [the longest x92 117 us: move(): return lax.ppermute(value, 'dp', [(d, target(d)) for d in range(self.dp)])]
    reduce_scatter x5 -> x0, waiting for transfers between devices: 133 us -> none  [the longest x1 65.8 us: on_device(): lax.psum_scatter(jnp.concatenate([matmul_tn(normed_cols, grad_q), matmul_...]
    concatenate x2 -> x1, other arithmetic: 76 us -> 2.73 us  [on_device(): jnp.concatenate([matmul_tn(first_normalized, grad_v).astype(jnp.bfloat16)...]
    dynamic_update_slice x0 -> x51, local copies, waits for them, and re-layouts: none -> 45.6 us  [the longest x16 18.3 us: quarter_gather(): lax.dynamic_update_slice(buffer, piece[:, None, None, None], (0, plane, r...]
    psum x1 -> x0, blocking collectives: 42.2 us -> none  [on_device(): grad_gains = lax.psum(jnp.stack([gain_one, gain_two]), ('dp', 'tensor'))]
  transfers between devices with their start and end apart: 17 -> 113, of which waited for: 16 -> 55; matrix products, arithmetic and copies ran while one was open for 7% -> 28% of each run, Pallas kernels for 0% -> 0%
where the time goes in v1:
time: 790 us; the launch traced here: 783 us
  waiting for transfers between devices  346 us (44%)
  local copies, waits for them, and re-layouts  145 us (18%)
  starting transfers between devices  143 us (18%)
  matrix products  108 us (14%)
  other arithmetic  37.8 us (5%)
    ppermute x92, waiting for transfers between devices, move(): return lax.ppermute(value, 'dp', [(d, target(d)) for d in range(self.dp)])  258 us
    ppermute x92, starting transfers between devices, move(): return lax.ppermute(value, 'dp', [(d, target(d)) for d in range(self.dp)])  117 us
    ppermute x21, waiting for transfers between devices, other_x(): return lax.ppermute(value, 'tensor', [(0, 1), (1, 0)])  88 us
    dot_general x15, matrix products, matmul_nt(): lax.dot_general(left_side, right_side, (((1,), (1,)), ((), ())), preferre...  33.5 us
    dot_general x6, matrix products, matrix_product(): return jnp.dot(left_side, right_side, preferred_element_type=jnp.float32)  32 us
    dot_general x6, matrix products, matmul_tn(): lax.dot_general(left_side, right_side, (((0,), (0,)), ((), ())), preferre...  27.6 us
    unnamed x164, local copies, waits for them, and re-layouts  27 us
    ppermute x21, starting transfers between devices, other_x(): return lax.ppermute(value, 'tensor', [(0, 1), (1, 0)])  25.6 us
  transfers between devices with their start and end apart: 113, of which 55 were waited for; matrix products, arithmetic and copies ran while one was open for 28% of the time, Pallas kernels for 0%

profile of v1, /device:TPU:0, one launch (start us, length us, event | category | flops | bytes accessed | tf_op | source)
XLA Modules:
  0.0 783.1 jit_solution(10640300572195374684)
XLA Ops:
  116.6 9.3 %collective-permute-done.31 = bf16[128,2048]{1,0:T(8,128)(2,1)S(1)} collective-permute-done((bf16[128,2048]{1,0:T(8,128)(2,1)S(1)}, bf16[128,2048]{1,0:T(8,128)(2,1)S(1)}, u32[]{:S(2)}, u32[]{:S(2)}) %collective-permute-start.31) | collective-permute-done | bytes 524320 | tf_op jit(solution)/shard_map/ppermute | solution.py:185
  134.7 57.2 %collective-permute-done.39 = bf16[3,128,1024]{2,1,0:T(8,128)(2,1)} collective-permute-done((bf16[3,128,1024]{2,1,0:T(8,128)(2,1)}, bf16[3,128,1024]{2,1,0:T(8,128)(2,1)}, u32[]{:S(2)}, u32[]{:S(2)}) %collective-permute-start.39) | collective-permute-done | bytes 786464 | tf_op jit(solution)/shard_map/ppermute | solution.py:168
  193.3 6.2 broadcast_in_dim.280
  222.6 7.8 collective-permute-done.47
  237.0 11.0 %collective-permute-done.54 = bf16[128,2048]{1,0:T(8,128)(2,1)S(1)} collective-permute-done((bf16[128,2048]{1,0:T(8,128)(2,1)S(1)}, bf16[128,2048]{1,0:T(8,128)(2,1)S(1)}, u32[]{:S(2)}, u32[]{:S(2)}) %collective-permute-start.54) | collective-permute-done | bytes 524320 | tf_op jit(solution)/shard_map/ppermute | solution.py:185
  260.5 6.7 collective-permute-done.49
  267.4 20.4 %collective-permute-done.57 = bf16[128,2048]{1,0:T(8,128)(2,1)S(1)} collective-permute-done((bf16[128,2048]{1,0:T(8,128)(2,1)S(1)}, bf16[128,2048]{1,0:T(8,128)(2,1)S(1)}, u32[]{:S(2)}, u32[]{:S(2)}) %collective-permute-start.57) | collective-permute-done | bytes 524320 | tf_op jit(solution)/shard_map/ppermute | solution.py:168
  302.7 11.1 %collective-permute-done.58 = bf16[128,2048]{1,0:T(8,128)(2,1)S(1)} collective-permute-done((bf16[128,2048]{1,0:T(8,128)(2,1)S(1)}, bf16[128,2048]{1,0:T(8,128)(2,1)S(1)}, u32[]{:S(2)}, u32[]{:S(2)}) %collective-permute-start.58) | collective-permute-done | bytes 524320 | tf_op jit(solution)/shard_map/ppermute | solution.py:185
  315.8 8.3 %collective-permute-done.60 = bf16[128,2048]{1,0:T(8,128)(2,1)S(1)} collective-permute-done((bf16[128,2048]{1,0:T(8,128)(2,1)S(1)}, bf16[128,2048]{1,0:T(8,128)(2,1)S(1)}, u32[]{:S(2)}, u32[]{:S(2)}) %collective-permute-start.60) | collective-permute-done | bytes 524320 | tf_op jit(solution)/shard_map/ppermute | solution.py:185
  345.8 9.8 %multiply_convert_fusion.1 = (bf16[1024,1024]{1,0:T(8,128)(2,1)S(1)}, bf16[1024,1024]{1,0:T(8,128)(2,1)S(1)}, bf16[1024,1024]{1,0:T(8,128)(2,1)}) fusion(f32[1024,1024]{1,0:T(8,128)} %fusion.161, f32[1024,1024]{1,0:T(8,128)} %fusion.160, bf16[1024,2048]{1,0:T(8,128)(2,1)S(1)} %copy-done.67, bf16[2048,1024]{1,0:T(8,128)(2,1)S(1)} %bitcast.440), kind=kOutput, calls=%fused_computation.13 | convolution fusion | flops 4310695936 | bytes 23068672 | tf_op jit(solution)/shard_map/dot_general | solution.py:16
  355.6 8.2 %convolution_convert_fusion.3 = bf16[2048,1024]{1,0:T(8,128)(2,1)S(1)} fusion(bf16[1024,2048]{1,0:T(8,128)(2,1)} %constant_dynamic-update-slice_fusion.4, bf16[1024,1024]{1,0:T(8,128)(2,1)S(1)} %get-tuple-element.39), kind=kOutput, calls=%fused_computation.19 | convolution fusion | flops 4297064448 | bytes 10485760 | tf_op jit(solution)/shard_map/dot_general | solution.py:26
  370.0 7.0 convolution_convert_fusion.4
  386.9 6.4 collective-permute-done.61
  393.4 6.6 collective-permute-start.62
  404.7 12.8 %collective-permute-start.64 = (bf16[128,2048]{1,0:T(8,128)(2,1)S(1)}, bf16[128,2048]{1,0:T(8,128)(2,1)S(1)}, u32[]{:S(2)}, u32[]{:S(2)}) collective-permute-start(bf16[128,2048]{1,0:T(8,128)(2,1)S(1)} %fusion.66), channel_id=1, source_target_pairs={{0,24},{2,26},{4,28},{6,30},{8,0},{10,2},{12,4},{14,6},{16,8},{18,... | collective-permute-start | bytes 1572872 | tf_op jit(solution)/shard_map/ppermute | solution.py:168
  418.4 8.3 %collective-permute-start.66 = (bf16[128,2048]{1,0:T(8,128)(2,1)}, bf16[128,2048]{1,0:T(8,128)(2,1)S(1)}, u32[]{:S(2)}, u32[]{:S(2)}) collective-permute-start(bf16[128,2048]{1,0:T(8,128)(2,1)} %fusion.65), channel_id=1, source_target_pairs={{0,8},{2,10},{4,12},{6,14},{8,16},{10,18},{12,20},{14,22},{16,24},... | collective-permute-start | bytes 1572872 | tf_op jit(solution)/shard_map/ppermute | solution.py:168
  426.7 7.2 convolution_convert_fusion.2
  456.1 8.2 %collective-permute-done.68 = bf16[128,2048]{1,0:T(8,128)(2,1)S(1)} collective-permute-done((bf16[128,2048]{1,0:T(8,128)(2,1)S(1)}, bf16[128,2048]{1,0:T(8,128)(2,1)S(1)}, u32[]{:S(2)}, u32[]{:S(2)}) %collective-permute-start.68) | collective-permute-done | bytes 524320 | tf_op jit(solution)/shard_map/ppermute | solution.py:185
  467.2 8.4 %collective-permute-done.70 = bf16[128,2048]{1,0:T(8,128)(2,1)S(1)} collective-permute-done((bf16[128,2048]{1,0:T(8,128)(2,1)S(1)}, bf16[128,2048]{1,0:T(8,128)(2,1)S(1)}, u32[]{:S(2)}, u32[]{:S(2)}) %collective-permute-start.70) | collective-permute-done | bytes 524320 | tf_op jit(solution)/shard_map/ppermute | solution.py:185
  477.2 9.6 %collective-permute-done.72 = bf16[128,2048]{1,0:T(8,128)(2,1)S(1)} collective-permute-done((bf16[128,2048]{1,0:T(8,128)(2,1)S(1)}, bf16[128,2048]{1,0:T(8,128)(2,1)S(1)}, u32[]{:S(2)}, u32[]{:S(2)}) %collective-permute-start.72) | collective-permute-done | bytes 524320 | tf_op jit(solution)/shard_map/ppermute | solution.py:185
  486.8 7.4 collective-permute-start.69
  501.8 26.2 %collective-permute-done.69 = bf16[128,2048]{1,0:T(8,128)(2,1)S(1)} collective-permute-done((bf16[128,2048]{1,0:T(8,128)(2,1)S(1)}, bf16[128,2048]{1,0:T(8,128)(2,1)S(1)}, u32[]{:S(2)}, u32[]{:S(2)}) %collective-permute-start.69) | collective-permute-done | bytes 524320 | tf_op jit(solution)/shard_map/ppermute | solution.py:168
  567.1 9.7 %reshape.275 = bf16[8,2,128,1280]{2,1,0,3:T(2,128)(2,1)} reshape(bf16[2048,1280]{0,1:T(8,128)(2,1)} %pad_maximum_fusion) | data formatting | bytes 10485760 | tf_op jit(solution)/shard_map/reshape | solution.py:228
  576.9 13.6 %constant_dynamic-slice_fusion.1 = (bf16[8,1,128,1280]{2,1,0,3:T(2,128)(2,1)}, bf16[8,1,128,1280]{2,1,0,3:T(2,128)(2,1)}) fusion(bf16[8,2,128,1280]{2,1,0,3:T(2,128)(2,1)} %reshape.275, s32[]{:T(128)S(6)} %select_n.622, s32[]{:T(128)S(6)} %select_n.623), kind=kLoop, calls=%fused_computation.370 | loop fusion | bytes 10485768 | tf_op jit(solution)/shard_map/jit(dynamic_index_in_dim)/dynamic_slice | solution.py:230
  590.5 11.1 %copy.93 = bf16[8,1,128,1280]{3,2,0,1:T(8,128)(2,1)} copy(bf16[8,1,128,1280]{2,1,0,3:T(2,128)(2,1)} %get-tuple-element.42) | data formatting | bytes 5242880 | tf_op jit(solution)/shard_map/jit(dynamic_index_in_dim)/dynamic_slice | solution.py:229
  601.6 9.6 %copy.111 = bf16[8,1,128,1280]{3,2,0,1:T(8,128)(2,1)S(1)} copy(bf16[8,1,128,1280]{2,1,0,3:T(2,128)(2,1)} %get-tuple-element.41) | data formatting | bytes 5242880
  624.9 13.3 %collective-permute-start.110 = (bf16[128,1024]{1,0:T(8,128)(2,1)S(1)}, bf16[128,1024]{1,0:T(8,128)(2,1)S(1)}, u32[]{:S(2)}, u32[]{:S(2)}) collective-permute-start(bf16[128,1024]{1,0:T(8,128)(2,1)S(1)} %get-tuple-element.49), channel_id=1, source_target_pairs={{0,16},{2,18},{4,20},{6,22},{8,24},{10,26},{12,28},{14,30},{16,0},... | collective-permute-start | bytes 786440 | tf_op jit(solution)/shard_map/ppermute | solution.py:168
  644.3 9.2 %collective-permute-start.105 = (bf16[128,1024]{1,0:T(8,128)(2,1)S(1)}, bf16[128,1024]{1,0:T(8,128)(2,1)S(1)}, u32[]{:S(2)}, u32[]{:S(2)}) collective-permute-start(bf16[128,1024]{1,0:T(8,128)(2,1)S(1)} %get-tuple-element.52), channel_id=1, source_target_pairs={{0,16},{2,18},{4,20},{6,22},{8,24},{10,26},{12,28},{14,30},{16,0},... | collective-permute-start | bytes 786440 | tf_op jit(solution)/shard_map/ppermute | solution.py:168
  680.2 11.2 %collective-permute-done.106 = bf16[128,1024]{1,0:T(8,128)(2,1)S(1)} collective-permute-done((bf16[128,1024]{1,0:T(8,128)(2,1)S(1)}, bf16[128,1024]{1,0:T(8,128)(2,1)S(1)}, u32[]{:S(2)}, u32[]{:S(2)}) %collective-permute-start.106) | collective-permute-done | bytes 262176 | tf_op jit(solution)/shard_map/ppermute | solution.py:168
  697.2 14.9 %collective-permute-done.100 = bf16[128,1024]{1,0:T(8,128)(2,1)S(1)} collective-permute-done((bf16[128,1024]{1,0:T(8,128)(2,1)S(1)}, bf16[128,1024]{1,0:T(8,128)(2,1)S(1)}, u32[]{:S(2)}, u32[]{:S(2)}) %collective-permute-start.100) | collective-permute-done | bytes 262176 | tf_op jit(solution)/shard_map/ppermute | solution.py:168
  754.4 6.2 collective-permute-done.95
  764.3 7.0 collective-permute-done.96
  (604 shorter events, 410.1 us)
Async XLA Ops:
  114.1 77.8 %collective-permute-start.39 = (bf16[3,128,1024]{2,1,0:T(8,128)(2,1)}, bf16[3,128,1024]{2,1,0:T(8,128)(2,1)}, u32[]{:S(2)}, u32[]{:S(2)}) collective-permute-start(bf16[3,128,1024]{2,1,0:T(8,128)(2,1)} %get-tuple-element.45), channel_id=1, source_target_pairs={{0,16},{2,18},{4,20},{6,22},{8,24},{10,26},{12,28},{14,30},{16,0},... | collective-permute-start | bytes 2359304 | tf_op jit(solution)/shard_map/ppermute | solution.py:168
  128.3 63.5 %collective-permute-start.33 = (bf16[128,2048]{1,0:T(8,128)(2,1)}, bf16[128,2048]{1,0:T(8,128)(2,1)}, u32[]{:S(2)}, u32[]{:S(2)}) collective-permute-start(bf16[128,2048]{1,0:T(8,128)(2,1)} %get-tuple-element.30), channel_id=1, source_target_pairs={{0,8},{2,10},{4,12},{6,14},{8,16},{10,18},{12,20},{14,22},{16,24},... | collective-permute-start | bytes 1572872 | tf_op jit(solution)/shard_map/ppermute | solution.py:168
  130.1 71.6 %collective-permute-start.32 = (bf16[128,2048]{1,0:T(8,128)(2,1)}, bf16[128,2048]{1,0:T(8,128)(2,1)S(1)}, u32[]{:S(2)}, u32[]{:S(2)}) collective-permute-start(bf16[128,2048]{1,0:T(8,128)(2,1)} %get-tuple-element.30), channel_id=1, source_target_pairs={{0,1},{1,0},{2,3},{3,2},{4,5},{5,4},{6,7},{7,6},{8,9},{9,8},{10,11... | collective-permute-start | bytes 1572872 | tf_op jit(solution)/shard_map/ppermute | solution.py:185
  130.7 72.7 %collective-permute-start.35 = (bf16[128,2048]{1,0:T(8,128)(2,1)}, bf16[128,2048]{1,0:T(8,128)(2,1)}, u32[]{:S(2)}, u32[]{:S(2)}) collective-permute-start(bf16[128,2048]{1,0:T(8,128)(2,1)} %get-tuple-element.30), channel_id=1, source_target_pairs={{0,16},{2,18},{4,20},{6,22},{8,24},{10,26},{12,28},{14,30},{16,0},... | collective-permute-start | bytes 1572872 | tf_op jit(solution)/shard_map/ppermute | solution.py:168
  134.3 85.0 %collective-permute-start.43 = (bf16[3,128,1024]{2,1,0:T(8,128)(2,1)}, bf16[3,128,1024]{2,1,0:T(8,128)(2,1)S(1)}, u32[]{:S(2)}, u32[]{:S(2)}) collective-permute-start(bf16[3,128,1024]{2,1,0:T(8,128)(2,1)} %get-tuple-element.44), channel_id=1, source_target_pairs={{0,8},{2,10},{4,12},{6,14},{8,16},{10,18},{12,20},{14,22},{16,24},... | collective-permute-start | bytes 2359304 | tf_op jit(solution)/shard_map/ppermute | solution.py:168
  202.4 27.9 %collective-permute-start.47 = (bf16[3,128,1024]{2,1,0:T(8,128)(2,1)S(1)}, bf16[3,128,1024]{2,1,0:T(8,128)(2,1)S(1)}, u32[]{:S(2)}, u32[]{:S(2)}) collective-permute-start(bf16[3,128,1024]{2,1,0:T(8,128)(2,1)S(1)} %copy-done.46), channel_id=1, source_target_pairs={{0,24},{2,26},{4,28},{6,30},{8,0},{10,2},{12,4},{14,6},{16,8},{18,... | collective-permute-start | bytes 2359304 | tf_op jit(solution)/shard_map/ppermute | solution.py:168
  219.3 37.3 %collective-permute-start.44 = (bf16[3,128,1024]{2,1,0:T(8,128)(2,1)S(1)}, bf16[3,128,1024]{2,1,0:T(8,128)(2,1)S(1)}, u32[]{:S(2)}, u32[]{:S(2)}) collective-permute-start(bf16[3,128,1024]{2,1,0:T(8,128)(2,1)S(1)} %collective-permute-done.43), channel_id=1, source_target_pairs={{0,2},{2,0},{4,6},{6,4},{8,10},{10,8},{12,14},{14,12},{16,18},{18,... | collective-permute-start | bytes 2359304 | tf_op jit(solution)/shard_map/ppermute | solution.py:168
  230.6 61.1 %collective-permute-start.48 = (bf16[3,128,1024]{2,1,0:T(8,128)(2,1)S(1)}, bf16[3,128,1024]{2,1,0:T(8,128)(2,1)S(1)}, u32[]{:S(2)}, u32[]{:S(2)}) collective-permute-start(bf16[3,128,1024]{2,1,0:T(8,128)(2,1)S(1)} %collective-permute-done.47), channel_id=1, source_target_pairs={{0,2},{2,0},{4,6},{6,4},{8,10},{10,8},{12,14},{14,12},{16,18},{18,... | collective-permute-start | bytes 2359304 | tf_op jit(solution)/shard_map/ppermute | solution.py:168
  254.8 34.5 %collective-permute-start.46 = (bf16[3,128,1024]{2,1,0:T(8,128)(2,1)S(1)}, bf16[3,128,1024]{2,1,0:T(8,128)(2,1)S(1)}, u32[]{:S(2)}, u32[]{:S(2)}) collective-permute-start(bf16[3,128,1024]{2,1,0:T(8,128)(2,1)S(1)} %collective-permute-done.45), channel_id=1, source_target_pairs={{0,2},{2,0},{4,6},{6,4},{8,10},{10,8},{12,14},{14,12},{16,18},{18,... | collective-permute-start | bytes 2359304 | tf_op jit(solution)/shard_map/ppermute | solution.py:168
  256.7 31.1 %collective-permute-start.57 = (bf16[128,2048]{1,0:T(8,128)(2,1)S(1)}, bf16[128,2048]{1,0:T(8,128)(2,1)S(1)}, u32[]{:S(2)}, u32[]{:S(2)}) collective-permute-start(bf16[128,2048]{1,0:T(8,128)(2,1)S(1)} %fusion.71), channel_id=1, source_target_pairs={{0,16},{2,18},{4,20},{6,22},{8,24},{10,26},{12,28},{14,30},{16,0},... | collective-permute-start | bytes 1572872 | tf_op jit(solution)/shard_map/ppermute | solution.py:168
  267.1 30.1 %collective-permute-start.59 = (bf16[128,2048]{1,0:T(8,128)(2,1)S(1)}, bf16[128,2048]{1,0:T(8,128)(2,1)S(1)}, u32[]{:S(2)}, u32[]{:S(2)}) collective-permute-start(bf16[128,2048]{1,0:T(8,128)(2,1)S(1)} %fusion.71), channel_id=1, source_target_pairs={{0,24},{2,26},{4,28},{6,30},{8,0},{10,2},{12,4},{14,6},{16,8},{18,... | collective-permute-start | bytes 1572872 | tf_op jit(solution)/shard_map/ppermute | solution.py:168
  267.4 26.2 %collective-permute-start.50 = (bf16[3,128,1024]{2,1,0:T(8,128)(2,1)S(1)}, bf16[3,128,1024]{2,1,0:T(8,128)(2,1)S(1)}, u32[]{:S(2)}, u32[]{:S(2)}) collective-permute-start(bf16[3,128,1024]{2,1,0:T(8,128)(2,1)S(1)} %collective-permute-done.49), channel_id=1, source_target_pairs={{0,2},{2,0},{4,6},{6,4},{8,10},{10,8},{12,14},{14,12},{16,18},{18,... | collective-permute-start | bytes 2359304 | tf_op jit(solution)/shard_map/ppermute | solution.py:168
  297.2 26.9 %collective-permute-start.60 = (bf16[128,2048]{1,0:T(8,128)(2,1)S(1)}, bf16[128,2048]{1,0:T(8,128)(2,1)S(1)}, u32[]{:S(2)}, u32[]{:S(2)}) collective-permute-start(bf16[128,2048]{1,0:T(8,128)(2,1)S(1)} %collective-permute-done.59), channel_id=1, source_target_pairs={{0,1},{1,0},{2,3},{3,2},{4,5},{5,4},{6,7},{7,6},{8,9},{9,8},{10,11... | collective-permute-start | bytes 1572872 | tf_op jit(solution)/shard_map/ppermute | solution.py:185
  298.9 25.3 %collective-permute-start.51 = (bf16[3,128,1024]{2,1,0:T(8,128)(2,1)S(1)}, bf16[3,128,1024]{2,1,0:T(8,128)(2,1)S(1)}, u32[]{:S(2)}, u32[]{:S(2)}) collective-permute-start(bf16[3,128,1024]{2,1,0:T(8,128)(2,1)S(1)} %get-tuple-element.34), channel_id=1, source_target_pairs={{0,2},{2,0},{4,6},{6,4},{8,10},{10,8},{12,14},{14,12},{16,18},{18,... | collective-permute-start | bytes 2359304 | tf_op jit(solution)/shard_map/ppermute | solution.py:168
  383.4 34.1 %collective-permute-start.65 = (bf16[128,2048]{1,0:T(8,128)(2,1)S(1)}, bf16[128,2048]{1,0:T(8,128)(2,1)S(1)}, u32[]{:S(2)}, u32[]{:S(2)}) collective-permute-start(bf16[128,2048]{1,0:T(8,128)(2,1)S(1)} %slice.480), channel_id=1, source_target_pairs={{0,1},{1,0},{2,3},{3,2},{4,5},{5,4},{6,7},{7,6},{8,9},{9,8},{10,11... | collective-permute-start | bytes 1572872 | tf_op jit(solution)/shard_map/ppermute | solution.py:185
  386.3 48.5 %collective-permute-start.67 = (bf16[128,2048]{1,0:T(8,128)(2,1)S(1)}, bf16[128,2048]{1,0:T(8,128)(2,1)S(1)}, u32[]{:S(2)}, u32[]{:S(2)}) collective-permute-start(bf16[128,2048]{1,0:T(8,128)(2,1)S(1)} %slice.479), channel_id=1, source_target_pairs={{0,1},{1,0},{2,3},{3,2},{4,5},{5,4},{6,7},{7,6},{8,9},{9,8},{10,11... | collective-permute-start | bytes 1572872 | tf_op jit(solution)/shard_map/ppermute | solution.py:185
  393.4 41.9 %collective-permute-start.62 = (bf16[128,2048]{1,0:T(8,128)(2,1)S(1)}, bf16[128,2048]{1,0:T(8,128)(2,1)S(1)}, u32[]{:S(2)}, u32[]{:S(2)}) collective-permute-start(bf16[128,2048]{1,0:T(8,128)(2,1)S(1)} %fusion.67), channel_id=1, source_target_pairs={{0,16},{2,18},{4,20},{6,22},{8,24},{10,26},{12,28},{14,30},{16,0},... | collective-permute-start | bytes 1572872 | tf_op jit(solution)/shard_map/ppermute | solution.py:168
  404.7 32.8 %collective-permute-start.64 = (bf16[128,2048]{1,0:T(8,128)(2,1)S(1)}, bf16[128,2048]{1,0:T(8,128)(2,1)S(1)}, u32[]{:S(2)}, u32[]{:S(2)}) collective-permute-start(bf16[128,2048]{1,0:T(8,128)(2,1)S(1)} %fusion.66), channel_id=1, source_target_pairs={{0,24},{2,26},{4,28},{6,30},{8,0},{10,2},{12,4},{14,6},{16,8},{18,... | collective-permute-start | bytes 1572872 | tf_op jit(solution)/shard_map/ppermute | solution.py:168
  434.1 60.2 %collective-permute-start.108 = (bf16[4,2,128,1024]{3,2,1,0:T(8,128)(2,1)S(1)}, bf16[4,2,128,1024]{3,2,1,0:T(8,128)(2,1)S(1)}, u32[]{:S(2)}, u32[]{:S(2)}) collective-permute-start(bf16[4,2,128,1024]{3,2,1,0:T(8,128)(2,1)S(1)} %dynamic-slice_bitcast_fusion.1), channel_id=1, source_target_pairs={{0,2},{2,0},{4,6},{6,4},{8,10},{10,8},{12,14},{14,12},{16,18},{18,... | collective-permute-start | bytes 6291464 | tf_op jit(solution)/shard_map/ppermute | solution.py:168
  434.8 60.7 %collective-permute-start.103 = (bf16[4,2,128,1024]{3,2,1,0:T(8,128)(2,1)S(1)}, bf16[4,2,128,1024]{3,2,1,0:T(8,128)(2,1)S(1)}, u32[]{:S(2)}, u32[]{:S(2)}) collective-permute-start(bf16[4,2,128,1024]{3,2,1,0:T(8,128)(2,1)S(1)} %dynamic-slice_bitcast_fusion.2), channel_id=1, source_target_pairs={{0,2},{2,0},{4,6},{6,4},{8,10},{10,8},{12,14},{14,12},{16,18},{18,... | collective-permute-start | bytes 6291464 | tf_op jit(solution)/shard_map/ppermute | solution.py:168
  435.3 98.0 %collective-permute-start.98 = (bf16[4,2,128,1024]{3,2,1,0:T(8,128)(2,1)S(1)}, bf16[4,2,128,1024]{3,2,1,0:T(8,128)(2,1)S(1)}, u32[]{:S(2)}, u32[]{:S(2)}) collective-permute-start(bf16[4,2,128,1024]{3,2,1,0:T(8,128)(2,1)S(1)} %dynamic-slice_bitcast_fusion.3), channel_id=1, source_target_pairs={{0,2},{2,0},{4,6},{6,4},{8,10},{10,8},{12,14},{14,12},{16,18},{18,... | collective-permute-start | bytes 6291464 | tf_op jit(solution)/shard_map/ppermute | solution.py:168
  475.6 25.4 %collective-permute-start.74 = (bf16[128,2048]{1,0:T(8,128)(2,1)S(1)}, bf16[128,2048]{1,0:T(8,128)(2,1)S(1)}, u32[]{:S(2)}, u32[]{:S(2)}) collective-permute-start(bf16[128,2048]{1,0:T(8,128)(2,1)S(1)} %slice.475), channel_id=1, source_target_pairs={{0,1},{1,0},{2,3},{3,2},{4,5},{5,4},{6,7},{7,6},{8,9},{9,8},{10,11... | collective-permute-start | bytes 1572872 | tf_op jit(solution)/shard_map/ppermute | solution.py:185
  486.8 41.2 %collective-permute-start.69 = (bf16[128,2048]{1,0:T(8,128)(2,1)S(1)}, bf16[128,2048]{1,0:T(8,128)(2,1)S(1)}, u32[]{:S(2)}, u32[]{:S(2)}) collective-permute-start(bf16[128,2048]{1,0:T(8,128)(2,1)S(1)} %fusion.63), channel_id=1, source_target_pairs={{0,16},{2,18},{4,20},{6,22},{8,24},{10,26},{12,28},{14,30},{16,0},... | collective-permute-start | bytes 1572872 | tf_op jit(solution)/shard_map/ppermute | solution.py:168
  494.3 33.6 %collective-permute-start.71 = (bf16[128,2048]{1,0:T(8,128)(2,1)S(1)}, bf16[128,2048]{1,0:T(8,128)(2,1)S(1)}, u32[]{:S(2)}, u32[]{:S(2)}) collective-permute-start(bf16[128,2048]{1,0:T(8,128)(2,1)S(1)} %fusion.62), channel_id=1, source_target_pairs={{0,24},{2,26},{4,28},{6,30},{8,0},{10,2},{12,4},{14,6},{16,8},{18,... | collective-permute-start | bytes 1572872 | tf_op jit(solution)/shard_map/ppermute | solution.py:168
  495.5 32.5 %collective-permute-start.73 = (bf16[128,2048]{1,0:T(8,128)(2,1)S(1)}, bf16[128,2048]{1,0:T(8,128)(2,1)S(1)}, u32[]{:S(2)}, u32[]{:S(2)}) collective-permute-start(bf16[128,2048]{1,0:T(8,128)(2,1)S(1)} %fusion.61), channel_id=1, source_target_pairs={{0,8},{2,10},{4,12},{6,14},{8,16},{10,18},{12,20},{14,22},{16,24},... | collective-permute-start | bytes 1572872 | tf_op jit(solution)/shard_map/ppermute | solution.py:168
  501.0 120.6 %collective-permute-start.109 = (bf16[4,128,1024]{2,1,0:T(8,128)(2,1)}, bf16[4,128,1024]{2,1,0:T(8,128)(2,1)}, u32[]{:S(2)}, u32[]{:S(2)}) collective-permute-start(bf16[4,128,1024]{2,1,0:T(8,128)(2,1)} %dynamic-slice_bitcast_fusion.4), channel_id=1, source_target_pairs={{0,4},{2,6},{4,0},{6,2},{8,12},{10,14},{12,8},{14,10},{16,20},{18,... | collective-permute-start | bytes 3145736 | tf_op jit(solution)/shard_map/ppermute | solution.py:168
  532.5 92.4 %collective-permute-start.104 = (bf16[4,128,1024]{2,1,0:T(8,128)(2,1)}, bf16[4,128,1024]{2,1,0:T(8,128)(2,1)}, u32[]{:S(2)}, u32[]{:S(2)}) collective-permute-start(bf16[4,128,1024]{2,1,0:T(8,128)(2,1)} %dynamic-slice_bitcast_fusion.5), channel_id=1, source_target_pairs={{0,4},{2,6},{4,0},{6,2},{8,12},{10,14},{12,8},{14,10},{16,20},{18,... | collective-permute-start | bytes 3145736 | tf_op jit(solution)/shard_map/ppermute | solution.py:168
  535.4 118.0 %collective-permute-start.99 = (bf16[4,128,1024]{2,1,0:T(8,128)(2,1)}, bf16[4,128,1024]{2,1,0:T(8,128)(2,1)}, u32[]{:S(2)}, u32[]{:S(2)}) collective-permute-start(bf16[4,128,1024]{2,1,0:T(8,128)(2,1)} %dynamic-slice_bitcast_fusion.6), channel_id=1, source_target_pairs={{0,4},{2,6},{4,0},{6,2},{8,12},{10,14},{12,8},{14,10},{16,20},{18,... | collective-permute-start | bytes 3145736 | tf_op jit(solution)/shard_map/ppermute | solution.py:168
  601.6 111.1 %collective-permute-start.90 = (bf16[8,128,1280]{2,1,0:T(8,128)(2,1)}, bf16[8,128,1280]{2,1,0:T(8,128)(2,1)}, u32[]{:S(2)}, u32[]{:S(2)}) collective-permute-start(bf16[8,128,1280]{2,1,0:T(8,128)(2,1)} %bitcast.132), channel_id=1, source_target_pairs={{0,2},{2,0},{4,6},{6,4},{8,10},{10,8},{12,14},{14,12},{16,18},{18,... | collective-permute-start | bytes 7864328 | tf_op jit(solution)/shard_map/ppermute | solution.py:168
  614.8 103.8 %collective-permute-start.82 = (bf16[8,128,1280]{2,1,0:T(8,128)(2,1)S(1)}, bf16[8,128,1280]{2,1,0:T(8,128)(2,1)S(1)}, u32[]{:S(2)}, u32[]{:S(2)}) collective-permute-start(bf16[8,128,1280]{2,1,0:T(8,128)(2,1)S(1)} %dynamic-slice_bitcast_fusion), channel_id=1, source_target_pairs={{0,2},{2,0},{4,6},{6,4},{8,10},{10,8},{12,14},{14,12},{16,18},{18,... | collective-permute-start | bytes 7864328 | tf_op jit(solution)/shard_map/ppermute | solution.py:168
  624.9 44.8 %collective-permute-start.110 = (bf16[128,1024]{1,0:T(8,128)(2,1)S(1)}, bf16[128,1024]{1,0:T(8,128)(2,1)S(1)}, u32[]{:S(2)}, u32[]{:S(2)}) collective-permute-start(bf16[128,1024]{1,0:T(8,128)(2,1)S(1)} %get-tuple-element.49), channel_id=1, source_target_pairs={{0,16},{2,18},{4,20},{6,22},{8,24},{10,26},{12,28},{14,30},{16,0},... | collective-permute-start | bytes 786440 | tf_op jit(solution)/shard_map/ppermute | solution.py:168
  644.3 29.6 %collective-permute-start.105 = (bf16[128,1024]{1,0:T(8,128)(2,1)S(1)}, bf16[128,1024]{1,0:T(8,128)(2,1)S(1)}, u32[]{:S(2)}, u32[]{:S(2)}) collective-permute-start(bf16[128,1024]{1,0:T(8,128)(2,1)S(1)} %get-tuple-element.52), channel_id=1, source_target_pairs={{0,16},{2,18},{4,20},{6,22},{8,24},{10,26},{12,28},{14,30},{16,0},... | collective-permute-start | bytes 786440 | tf_op jit(solution)/shard_map/ppermute | solution.py:168
  (155 other events, 2550.2 us)

commit v2 on v1

--- a/solution.py
+++ b/solution.py
@@ -1,8 +1,12 @@
+import functools
 import math
 
 import jax
 import jax.numpy as jnp
 from jax import lax
+from jax.experimental import pallas as pl
+from jax.experimental.layout import Layout, with_layout_constraint
+from jax.experimental.pallas import tpu as pltpu
 from jax.sharding import PartitionSpec as P
 
 HEAD_WIDTH = 64
@@ -30,6 +34,10 @@
 
 def after(value, *earlier):
     return lax.optimization_barrier((value, *earlier))[0]
+
+
+def row_major(value):
+    return with_layout_constraint(value, Layout(major_to_minor=(0, 1)))
 
 
 def layout(lengths, row_count):
@@ -163,13 +171,15 @@
         self.x = lax.axis_index("tensor")
         chip = index // CORES
         self.ring_place = jnp.where(chip % 2 == 0, chip // 2, self.chips - 1 - chip // 2)
+        stride = self.rows * CORES
+        self.columns = [[z * stride + i for z in range(PLANES)] for i in range(stride)]
 
     def move(self, value, target):
         return lax.ppermute(value, "dp", [(d, target(d)) for d in range(self.dp)])
 
-    def along_z(self, value, steps):
+    def across_z(self, value, mask):
         stride = self.rows * CORES
-        return self.move(value, lambda d: (d + steps * stride) % self.dp)
+        return self.move(value, lambda d: d ^ (mask * stride))
 
     def along_y(self, value, steps):
         def target(d):
@@ -184,6 +194,11 @@
     def other_x(self, value):
         return lax.ppermute(value, "tensor", [(0, 1), (1, 0)])
 
+    def by_core(self, own, other, axis):
+        first = jnp.where(self.core == 0, own, other)
+        second = jnp.where(self.core == 0, other, own)
+        return jnp.stack([first, second], axis)
+
     def ring_chip(self, place):
         place = place % self.chips
         half = self.chips // 2
@@ -201,25 +216,25 @@
         return self.move(value, target)
 
 
-def ring_gather(at, clockwise, counter):
+def ring_gather(at, clockwise, counter, beside):
     currents = [clockwise, counter]
-    buffers = [
-        jnp.zeros((at.chips, CORES) + part.shape, part.dtype) for part in (clockwise, counter)
-    ]
+    buffers = [jnp.zeros((at.chips,) + part.shape, part.dtype) for part in currents]
+    steps = []
     for step in range(at.chips):
+        if step == at.chips // 2:
+            extra = beside(tuple(currents))
+        if step == at.chips - 2:
+            currents = list(after(tuple(currents), *extra))
+        else:
+            currents = list(lax.optimization_barrier(tuple(currents)))
         for way, sign in ((0, 1), (1, -1)):
             block = currents[way]
-            chip = at.ring_chip(at.ring_place - sign * step)
             if step < at.chips - 1:
                 currents[way] = at.along_ring(block, sign)
-            twin = at.other_core(block)
-            buffers[way] = lax.dynamic_update_slice(
-                buffers[way], block[None, None], (chip, at.core, 0, 0)
-            )
-            buffers[way] = lax.dynamic_update_slice(
-                buffers[way], twin[None, None], (chip, 1 - at.core, 0, 0)
-            )
-    return [buffer.reshape(-1, buffer.shape[-1]) for buffer in buffers]
+            chip = at.ring_chip(at.ring_place - sign * step)
+            buffers[way] = lax.dynamic_update_slice(buffers[way], block[None], (chip, 0, 0))
+        steps.append(tuple(currents))
+    return buffers, steps, extra
 
 
 def ring_scatter(at, clockwise, counter):
@@ -234,75 +249,188 @@
         return lax.dynamic_index_in_dim(locals_[way], at.ring_chip(place), 0, keepdims=False)
 
     totals = [local(way, at.ring_place - sign) for way, sign in ((0, 1), (1, -1))]
+    steps = []
     for step in range(1, at.chips):
+        totals = list(lax.optimization_barrier(tuple(totals)))
         for way, sign in ((0, 1), (1, -1)):
             arrived = at.along_ring(totals[way], sign).astype(jnp.float32)
             total = arrived + local(way, at.ring_place - sign * (step + 1)).astype(jnp.float32)
             totals[way] = total if step == at.chips - 1 else total.astype(jnp.bfloat16)
-    return totals
-
-
-def quarter_gather(at, parts, quarter):
-    count, own_rows, _ = parts.shape
-    buffer = jnp.zeros((count, at.planes, at.rows, CORES, own_rows, quarter), parts.dtype)
-    for k in (2, 1, 3, 0):
-        wanted = ((at.z + k) % at.planes) * quarter
-        block = lax.dynamic_slice(parts, (0, 0, wanted), (count, own_rows, quarter))
-        if k:
-            block = at.along_z(block, k)
-        plane = (at.z - k) % at.planes
-        for j in range(at.rows):
-            other = at.along_y(block, j) if j else block
-            row = (at.y - j) % at.rows
-            for core, piece in ((at.core, other), (1 - at.core, at.other_core(other))):
-                buffer = lax.dynamic_update_slice(
-                    buffer, piece[:, None, None, None], (0, plane, row, core, 0, 0)
-                )
-    return buffer.reshape(count, -1, quarter)
-
-
-def quarter_scatter(at, grads):
-    columns = grads.shape[-1]
-    blocks = grads.reshape(at.planes, at.rows, CORES, -1, columns)
-    away = lax.dynamic_index_in_dim(blocks, 1 - at.core, 2, keepdims=False)
-    mine = lax.dynamic_index_in_dim(blocks, at.core, 2, keepdims=False)
-    blocks = (mine.astype(jnp.float32) + at.other_core(away)).astype(jnp.bfloat16)
-    total = lax.dynamic_index_in_dim(blocks, at.y, 1, keepdims=False).astype(jnp.float32)
-    for j in range(1, at.rows):
-        away = lax.dynamic_index_in_dim(blocks, (at.y + j) % at.rows, 1, keepdims=False)
-        total = total + at.along_y(away, j)
-    result = jnp.zeros((total.shape[1], at.planes * columns), jnp.float32)
-    low = total.astype(jnp.bfloat16)
-    for k in (2, 1, 3, 0):
-        if k:
-            piece = at.along_z(
-                lax.dynamic_index_in_dim(low, (at.z + k) % at.planes, 0, keepdims=False), k
-            )
-        else:
-            piece = lax.dynamic_index_in_dim(total, at.z, 0, keepdims=False)
-        result = lax.dynamic_update_slice(
-            result, piece.astype(jnp.float32), (0, ((at.z - k) % at.planes) * columns)
-        )
-    return result
-
-
-def token_gather(at, own):
-    blocks = []
-    for k in range(at.planes):
-        block = at.along_z(own, k) if k else own
-        blocks += [block, at.other_x(block)]
-    return jnp.concatenate(blocks, 0)
-
-
-def token_scatter(at, part_of, rows_own):
-    total = None
-    for k in (2, 1, 3, 0):
-        part = part_of(k)
-        mine = part[:rows_own] + at.other_x(part[rows_own:].astype(jnp.bfloat16))
-        if k:
-            mine = at.along_z(mine.astype(jnp.bfloat16), -k)
-        total = mine.astype(jnp.float32) if total is None else total + mine
-    return total
+        if step < at.chips - 1:
+            steps.append(totals[0])
+    return (*totals, steps)
+
+
+def product(left_side, right_side, contract):
+    return lax.dot_general(
+        left_side, right_side, (contract, ((), ())), preferred_element_type=jnp.float32
+    )
+
+
+NN = ((1,), (0,))
+NT = ((1,), (1,))
+TN = ((0,), (0,))
+
+
+class Held:
+    def __init__(self, place, blocks, weights, which, held, sems):
+        self.z, self.y, self.core, self.rows = (place[i] for i in range(4))
+        self.blocks, self.weights, self.which = blocks, weights, which
+        self.held, self.sems = held, sems
+        for i in range(len(which)):
+            for n in range(len(blocks)):
+                self.copy(i, n).start()
+
+    def copy(self, i, n):
+        mask, back, other = self.blocks[n]
+        size = self.weights[n].shape[1]
+        chip = (self.z ^ mask) * self.rows + lax.rem(self.y + self.rows - back, self.rows)
+        start = pl.multiple_of((chip * CORES + (self.core ^ other)) * size, size)
+        return pltpu.make_async_copy(
+            self.weights[n].at[self.which[i]],
+            self.held.at[i, pl.ds(start, size)],
+            self.sems.at[i, n],
+        )
+
+    def wait(self, i):
+        for n in range(len(self.blocks)):
+            self.copy(i, n).wait()
+
+
+def held_call(at, kernel, weights, which, arrays, out_shapes):
+    blocks = list(weights)
+    sources = [weights[key] for key in blocks]
+    _, size, quarter = sources[0].shape
+    place = jnp.stack([at.z, at.y, at.core, jnp.int32(at.rows)]).astype(jnp.int32)
+    vmem = pl.BlockSpec(memory_space=pltpu.VMEM)
+    low = jnp.bfloat16
+
+    def body(place, *refs):
+        ins, refs = refs[: len(arrays)], refs[len(arrays) :]
+        sources, refs = refs[: len(blocks)], refs[len(blocks) :]
+        outs, (held, sems) = refs[: len(out_shapes)], refs[len(out_shapes) :]
+        kernel(Held(place, blocks, sources, which, held, sems), ins, outs)
+
+    return pl.pallas_call(
+        body,
+        in_specs=[pl.BlockSpec(memory_space=pltpu.SMEM)]
+        + [vmem] * len(arrays)
+        + [pl.BlockSpec(memory_space=pl.ANY)] * len(sources),
+        out_specs=[vmem] * len(out_shapes),
+        out_shape=[jax.ShapeDtypeStruct(shape, low) for shape in out_shapes],
+        scratch_shapes=[
+            pltpu.VMEM((len(which), len(blocks) * size, quarter), low),
+            pltpu.SemaphoreType.DMA((len(which), len(blocks))),
+        ],
+        compiler_params=pltpu.CompilerParams(vmem_limit_bytes=56 * 2**20),
+        cost_estimate=pl.CostEstimate(flops=1, bytes_accessed=1, transcendentals=0),
+    )(place, *arrays, *sources)
+
+
+def forward(at, weights, normed):
+    rows_own, width = normed[0].shape
+    quarter = next(iter(weights.values())).shape[-1]
+    count = len(normed) // 2
+    half = width // 2
+
+    def kernel(held, normed, outs):
+        hidden_ref, silu_ref, slope_ref, *out_refs = outs
+        for k in range(count):
+            here = slice(2 * k * rows_own, 2 * (k + 1) * rows_own)
+            own = slice(k * rows_own, (k + 1) * rows_own)
+            rows = jnp.concatenate([normed[2 * k][...], normed[2 * k + 1][...]], 0)
+            if k == 0:
+                held.wait(0)
+            gate = product(rows, held.held[0], NN)
+            if k == 0:
+                held.wait(1)
+            up = product(rows, held.held[1], NN)
+            sigmoid_gate = jax.nn.sigmoid(gate)
+            silu_gate = gate * sigmoid_gate
+            hidden = (silu_gate * up).astype(jnp.bfloat16)
+            hidden_ref[here] = hidden
+            silu_ref[here] = silu_gate.astype(jnp.bfloat16)
+            slope = up * sigmoid_gate * (1.0 + gate * (1.0 - sigmoid_gate))
+            slope_ref[here] = slope.astype(jnp.bfloat16)
+            if k == 0:
+                held.wait(2)
+            out = product(hidden, held.held[2], NT).astype(jnp.bfloat16)
+            for i in range(2):
+                columns = slice(i * half, (i + 1) * half)
+                out_refs[2 * i][own] = out[:rows_own, columns]
+                out_refs[2 * i + 1][own] = out[rows_own:, columns]
+
+    shapes = [(2 * count * rows_own, quarter)] * 3 + [(count * rows_own, half)] * 4
+    return held_call(at, kernel, weights, (0, 1, 2), normed, shapes)
+
+
+def backward(at, weights, masks, grads, silu, slope):
+    rows_own, width = grads[0].shape[1:]
+
+    def kernel(held, ins, outs):
+        mine, other, silu, slope = ins
+        gate_ref, up_ref, *back = outs
+        for k, mask in enumerate(masks):
+            here = slice(2 * k * rows_own, 2 * (k + 1) * rows_own)
+            rows = jnp.concatenate([mine[held.z ^ mask], other[held.z ^ mask]], 0)
+            if k == 0:
+                held.wait(0)
+            grad_hidden = product(rows, held.held[0], NN)
+            grad_gate = (grad_hidden * slope[here]).astype(jnp.bfloat16)
+            grad_up = (grad_hidden * silu[here]).astype(jnp.bfloat16)
+            gate_ref[here] = grad_gate
+            up_ref[here] = grad_up
+            if k == 0:
+                held.wait(1)
+            total = product(grad_gate, held.held[1], NT)
+            if k == 0:
+                held.wait(2)
+            total = (total + product(grad_up, held.held[2], NT)).astype(jnp.bfloat16)
+            back[2 * k][...] = total[:rows_own]
+            back[2 * k + 1][...] = total[rows_own:]
+
+    shapes = [silu.shape] * 2 + [(rows_own, width)] * (2 * len(masks))
+    return held_call(at, kernel, weights, (2, 0, 1), [*grads, silu, slope], shapes)
+
+
+def weight_grad_kernel(masks, by_plane, place, *refs):
+    z, core = place[0], place[1]
+    *left, right, own_ref, other_ref = refs
+    if by_plane:
+        pieces = [ref[z ^ mask] for mask in masks for ref in left]
+    else:
+        pieces = [ref[...] for ref in left]
+    total = product(jnp.concatenate(pieces, 0), right[...], TN).astype(jnp.bfloat16)
+    rows, _, own_features, quarter = own_ref.shape
+    total = total.reshape(rows, CORES, own_features, quarter)
+    own_ref[:, 0] = jnp.where(core == 0, total[:, 0], total[:, 1])
+    other_ref[:, 0] = jnp.where(core == 0, total[:, 1], total[:, 0])
+
+
+def weight_grad(at, masks, left, right, own_features):
+    by_plane = left[0].ndim == 3
+    width = left[0].shape[-1]
+    quarter = right.shape[-1]
+    share = width // at.planes
+    place = jnp.stack([at.z, at.core]).astype(jnp.int32)
+    shape = (at.rows, at.planes, own_features, quarter)
+    block = (at.rows, 1, own_features, quarter)
+    if by_plane:
+        left_spec = pl.BlockSpec(left[0].shape[:2] + (share,), lambda i, place: (0, 0, i))
+    else:
+        left_spec = pl.BlockSpec((left[0].shape[0], share), lambda i, place: (0, i))
+    return pl.pallas_call(
+        functools.partial(weight_grad_kernel, masks, by_plane),
+        grid_spec=pltpu.PrefetchScalarGridSpec(
+            num_scalar_prefetch=1,
+            grid=(at.planes,),
+            in_specs=[left_spec] * len(left) + [pl.BlockSpec(right.shape, lambda i, place: (0, 0))],
+            out_specs=[pl.BlockSpec(block, lambda i, place: (0, i, 0, 0))] * 2,
+        ),
+        out_shape=[jax.ShapeDtypeStruct(shape, jnp.bfloat16)] * 2,
+        compiler_params=pltpu.CompilerParams(vmem_limit_bytes=56 * 2**20),
+        cost_estimate=pl.CostEstimate(flops=1, bytes_accessed=1, transcendentals=0),
+    )(place, *left, right)
 
 
 def on_device(
@@ -325,7 +453,8 @@
     width_kv = key_weight.shape[1]
     heads_query = width_query // HEAD_WIDTH
     heads_kv = width_kv // HEAD_WIDTH
-    width_quarter = w_gate.shape[1] // at.planes
+    quarter = w_gate.shape[1] // at.planes
+    own_features = w_gate.shape[0]
     scaling = HEAD_WIDTH ** (-0.5)
 
     def both_x(own, other):
@@ -340,8 +469,6 @@
 
     row_ids, segment, position, in_use = layout(seq_lens[0], row_count)
     in_use_own = lax.dynamic_slice_in_dim(in_use, at.x * rows_own, rows_own, 0)
-    cosine_lookup, sine_lookup = rope_tables(position, HEAD_WIDTH)
-    allowed = (segment[:, None] == segment[None, :]) & (row_ids[None, :] <= row_ids[:, None])
     gain_rows = norm_gains.astype(jnp.float32)
     inputs = tokens.astype(jnp.float32)
     scale_one = lax.rsqrt(jnp.mean(inputs * inputs, 1, keepdims=True) + EPSILON)
@@ -349,15 +476,45 @@
     first_normalized = both_x(normed_own, at.other_x(normed_own))
     grad_mixed = cotangent.astype(jnp.float32) * in_use_own[:, None]
     grad_low_own = grad_mixed.astype(jnp.bfloat16)
-
-    qk_all, vo_all = ring_gather(
+    grad_low_mine = lax.all_gather(grad_low_own, "dp", axis_index_groups=at.columns)
+
+    weights = {}
+    shares = {}
+
+    def beside(halfway):
+        for mask in range(at.planes):
+            start = (at.z ^ mask) * quarter
+            parts = after((w_gate, w_up, w_down), *halfway)
+            shares[mask] = jnp.stack(
+                [lax.dynamic_slice_in_dim(part, start, quarter, 1) for part in parts]
+            )
+        grad_rows = at.other_x(after(grad_low_mine, *halfway))
+        return (grad_rows, at.across_z(shares[2], 2), *to_chips(0, shares[0]))
+
+    def to_chips(mask, block, *earlier):
+        weights[mask, 0, 0] = block
+        for j in range(1, at.rows):
+            weights[mask, j, 0] = at.along_y(after(block, *earlier), j)
+            earlier = (weights[mask, j, 0],)
+        return earlier
+
+    (qk_mine, vo_mine), steps, (grad_low_other, plane_two, *last) = ring_gather(
         at,
         jnp.concatenate([w_query, key_weight], 1),
         jnp.concatenate([value_weight, w_out], 1),
-    )
+        beside,
+    )
+    qk_all = at.by_core(qk_mine, at.other_core(qk_mine), 1).reshape(-1, qk_mine.shape[-1])
+    vo_all = at.by_core(vo_mine, at.other_core(vo_mine), 1).reshape(-1, vo_mine.shape[-1])
     value_all, out_all = vo_all[:, :width_kv], vo_all[:, width_kv:]
-    ffn_own = after(jnp.stack([w_gate, w_up, w_down]), qk_all, vo_all)
-    gate_all, up_all, down_all = quarter_gather(at, ffn_own, width_quarter)
+    position, segment = after((position, segment), *steps[1])
+    cosine_lookup, sine_lookup = rope_tables(position, HEAD_WIDTH)
+    allowed = (segment[:, None] == segment[None, :]) & (row_ids[None, :] <= row_ids[:, None])
+
+    ring_end = steps[-1]
+    plane_three = at.across_z(after(shares[3], *ring_end), 3)
+    plane_one = at.across_z(after(shares[1], *ring_end), 1)
+    last = to_chips(2, plane_two, *last, *ring_end)
 
     qk_rows = matrix_product(first_normalized, qk_all)
     query_rows = qk_rows[:, :width_query].reshape(row_count, heads_query, HEAD_WIDTH)
@@ -371,34 +528,122 @@
     key_rot = apply_rotation(key_projected, cosine_lookup, sine_lookup).astype(jnp.bfloat16)
     attended, logsums = attend(rotated_query, key_rot, value_low, allowed, scaling)
     attended = attended.reshape(row_count, heads_query * HEAD_WIDTH).astype(jnp.bfloat16)
-    state = inputs + sum_x(matmul_nt(attended, out_all))
+    branch = matmul_nt(after(attended, grad_low_other, plane_one, plane_three, *last), out_all)
+    state = inputs + sum_x(branch)
     scale_two = lax.rsqrt(jnp.mean(state * state, 1, keepdims=True) + EPSILON)
-    normed_two = token_gather(at, (state * scale_two * gain_rows[1]).astype(jnp.bfloat16))
-    grad_low = token_gather(at, after(grad_low_own, normed_two))
-
-    gate = matrix_product(normed_two, gate_all)
-    up_proj = matrix_product(normed_two, up_all)
-    sigmoid_gate = jax.nn.sigmoid(gate)
-    silu_gate = gate * sigmoid_gate
-    hidden = (silu_gate * up_proj).astype(jnp.bfloat16)
-    grad_hidden = matrix_product(grad_low, down_all)
-    grad_gate_in = (
-        grad_hidden * up_proj * sigmoid_gate * (1.0 + gate * (1.0 - sigmoid_gate))
-    ).astype(jnp.bfloat16)
-    grad_up_in = (grad_hidden * silu_gate).astype(jnp.bfloat16)
-
-    def rows_of(value, k):
-        return value[k * row_count : (k + 1) * row_count]
-
-    grad_normed_two = token_scatter(
-        at,
-        lambda k: matmul_nt(rows_of(grad_gate_in, k), gate_all)
-        + matmul_nt(rows_of(grad_up_in, k), up_all),
-        rows_own,
-    )
-    hidden_late = after(hidden, grad_normed_two)
-    ffn_out = token_scatter(at, lambda k: matmul_nt(rows_of(hidden_late, k), down_all), rows_own)
-    mixed = ((state + ffn_out) * in_use_own[:, None]).astype(jnp.bfloat16)
+    normed_two = (state * scale_two * gain_rows[1]).astype(jnp.bfloat16)
+
+    last = to_chips(1, plane_one, *last, branch)
+
+    def to_cores(*keys, earlier):
+        for mask, back in keys:
+            weights[mask, back, 1] = at.other_core(after(weights[mask, back, 0], *earlier))
+
+    every_row = range(at.rows)
+    to_cores(*((0, j) for j in every_row), earlier=[branch])
+    normed = {(0, 0): normed_two, (0, 1): at.other_x(normed_two)}
+    normed[2, 0] = at.across_z(normed_two, 2)
+    normed[1, 0] = at.across_z(normed_two, 1)
+    to_cores(*((2, j) for j in every_row), earlier=[normed_two])
+
+    stage = list(normed.values()) + list(last)
+    normed[3, 0] = at.across_z(after(normed[2, 0], *stage), 1)
+    normed[2, 1] = at.other_x(after(normed[2, 0], *stage))
+    last = to_chips(3, plane_three, *stage)
+    to_cores(*((1, j) for j in every_row), earlier=stage)
+
+    stage = [normed[3, 0], normed[2, 1], *last]
+    normed[3, 1] = at.other_x(after(normed[3, 0], *stage))
+    normed[1, 1] = at.across_z(after(normed[0, 1], *stage), 1)
+    to_cores(*((3, j) for j in every_row), earlier=stage)
+
+    masks = (3, 2, 1, 0)
+    normed_rows = [normed[mask, x] for mask in masks for x in range(2)]
+    grad_rows = [grad_low_mine, grad_low_other]
+    hidden, silu, slope, *outs = forward(at, weights, normed_rows)
+    def out_sums(mine, arrived):
+        total = (mine.astype(jnp.float32) + arrived).astype(jnp.bfloat16)
+        total = total.reshape(len(masks), rows_own, -1)
+        order = []
+        for z in range(at.planes):
+            slot = sum(jnp.where((at.z ^ z) == mask, i, 0) for i, mask in enumerate(masks))
+            order.append(lax.dynamic_index_in_dim(total, slot, 0))
+        return lax.psum_scatter(
+            jnp.concatenate(order, 0), "dp", scatter_dimension=0, axis_index_groups=at.columns
+        )
+
+    def of_chip(own, arrived, j):
+        y = (at.y + j) % at.rows
+        mine = lax.dynamic_index_in_dim(own, y, 0, keepdims=False)
+        theirs = lax.dynamic_index_in_dim(arrived, y, 0, keepdims=False)
+        return mine.astype(jnp.float32) + theirs
+
+    def over_cores(own, arrived):
+        half = at.planes // 2
+        away = [of_chip(own, arrived, j).astype(jnp.bfloat16) for j in range(1, at.rows)]
+        return of_chip(own, arrived, 0), [[a[:half] for a in away], [a[half:] for a in away]]
+
+    def send_chips(away, earlier):
+        return [at.along_y(after(a, *earlier), j + 1) for j, a in enumerate(away)]
+
+    def over_chips(total, lower, upper):
+        for first, second in zip(lower, upper, strict=True):
+            total = total + jnp.concatenate([first, second], 0)
+        return total
+
+    def send_planes(total, wanted, earlier):
+        low = total.astype(jnp.bfloat16)
+        sent = {}
+        for mask in wanted:
+            piece = lax.dynamic_index_in_dim(low, at.z ^ mask, 0, keepdims=False)
+            sent[mask] = at.across_z(after(piece, *earlier), mask)
+        return sent
+
+    def all_columns(total, pieces, *earlier):
+        result = jnp.zeros((own_features, at.planes * quarter), jnp.float32)
+        own = {0: lax.dynamic_index_in_dim(total, at.z, 0, keepdims=False)}
+        for mask, piece in after({**own, **pieces}, *earlier).items():
+            result = lax.dynamic_update_slice(
+                result, piece.astype(jnp.float32), (0, (at.z ^ mask) * quarter)
+            )
+        return result
+
+    grad_gate_in, grad_up_in, *back = backward(at, weights, masks, grad_rows, silu, slope)
+    out_first = at.other_x(outs[1])
+
+    def sum_of(i, arrived):
+        return back[2 * i].astype(jnp.float32) + arrived
+
+    stage = [out_first, back[0]]
+    three = at.other_x(after(back[1], *stage))
+    one = at.across_z(after(back[5], *stage), 1)
+    gate_own, gate_other = weight_grad(
+        at, masks, normed_rows, after(grad_gate_in, *stage), own_features
+    )
+    out_sums_first = out_sums(outs[0], out_first)
+
+    stage = [three, one, gate_own]
+    to_two = at.across_z(after(sum_of(0, three).astype(jnp.bfloat16), *stage), 1)
+    two = at.other_x(after(back[3], *stage))
+    gate_arrived = at.other_core(after(gate_other, *stage))
+    up_own, up_other = weight_grad(at, masks, normed_rows, after(grad_up_in, *stage), own_features)
+
+    stage = [to_two, two, gate_arrived, up_own]
+    to_zero = at.across_z(after((sum_of(1, two) + to_two).astype(jnp.bfloat16), *stage), 2)
+    other_zero = (back[7].astype(jnp.float32) + one).astype(jnp.bfloat16)
+    zero = at.other_x(after(other_zero, *stage))
+    gate_total, gate_away = over_cores(gate_own, gate_arrived)
+    gate_lower = send_chips(gate_away[0], stage)
+    up_arrived = at.other_core(after(up_other, *stage))
+    down_own, down_other = weight_grad(at, masks, grad_rows, after(hidden, *stage), own_features)
+
+    stage = [zero, *gate_lower, up_arrived, down_own]
+    from_one = at.across_z(after(back[4], *stage), 1)
+    gate_upper = send_chips(gate_away[1], stage)
+    down_arrived = at.other_core(after(down_other, *stage))
+    up_total, up_away = over_cores(up_own, up_arrived)
+
+    grad_normed_two = sum_of(3, zero) + from_one + to_zero
     hat_two = state * scale_two
     inner_two = grad_normed_two * gain_rows[1]
     grad_state = grad_mixed + scale_two * (
@@ -406,17 +651,30 @@
     )
     gain_two = jnp.sum(grad_normed_two * hat_two, 0)
     grad_state_own = grad_state.astype(jnp.bfloat16)
-    grad_state_low = both_x(grad_state_own, at.other_x(grad_state_own))
-
-    grad_gate = quarter_scatter(at, matmul_tn(normed_two, grad_gate_in).astype(jnp.bfloat16))
-    grad_up = quarter_scatter(at, matmul_tn(normed_two, grad_up_in).astype(jnp.bfloat16))
-    grad_down = quarter_scatter(at, matmul_tn(grad_low, hidden).astype(jnp.bfloat16))
+
+    stage = [grad_state_own, *gate_upper, down_arrived]
+    grad_state_other = at.other_x(after(grad_state_own, *stage))
+    up_lower = send_chips(up_away[0], stage)
+    gate_total = over_chips(gate_total, gate_lower, gate_upper)
+    gate_pieces = send_planes(gate_total, (2, 1), stage)
+    down_total, down_away = over_cores(down_own, down_arrived)
+
+    stage = [grad_state_other, *up_lower, *gate_pieces.values()]
+    grad_state_low = after(both_x(grad_state_own, grad_state_other), *stage)
+    up_upper = send_chips(up_away[1], stage)
+    gate_pieces.update(send_planes(gate_total, (3,), stage))
+    out_second = at.other_x(after(outs[3], *stage))
 
     grad_attended = (
         matrix_product(grad_state_low, out_all)
         .astype(jnp.bfloat16)
         .reshape(row_count, heads_query, HEAD_WIDTH)
     )
+    stage = [grad_attended, *up_upper, gate_pieces[3]]
+    grad_attended = after(grad_attended, *stage)
+    up_total = over_chips(up_total, up_lower, up_upper)
+    up_pieces = send_planes(up_total, (2, 1), stage)
+    down_lower = send_chips(down_away[0], stage)
     grad_query_rot, grad_key_rot, grad_values = attend_back(
         rotated_query, key_rot, value_low, grad_attended, logsums, allowed, scaling
     )
@@ -432,16 +690,33 @@
     )
     grad_v = grad_values.reshape(row_count, heads_kv * HEAD_WIDTH).astype(jnp.bfloat16)
     grad_qk = jnp.concatenate([grad_q, grad_k], 1)
-    grad_vo = jnp.concatenate(
-        [
-            matmul_tn(first_normalized, grad_v).astype(jnp.bfloat16),
-            matmul_tn(grad_state_low, attended).astype(jnp.bfloat16),
-        ],
-        1,
-    )
-    sum_qk, sum_vo = ring_scatter(
-        at, matmul_tn(first_normalized, grad_qk).astype(jnp.bfloat16), grad_vo
-    )
+    stage = [grad_qk, *up_pieces.values(), *down_lower, out_second]
+    grad_qk = after(grad_qk, *stage)
+    up_pieces.update(send_planes(up_total, (3,), stage))
+    down_upper = send_chips(down_away[1], stage)
+    out_sums_second = out_sums(after(outs[2], *stage), out_second)
+    grad_vo = row_major(
+        jnp.concatenate(
+            [
+                row_major(matmul_tn(first_normalized, grad_v).astype(jnp.bfloat16)),
+                row_major(matmul_tn(grad_state_low, attended).astype(jnp.bfloat16)),
+            ],
+            1,
+        )
+    )
+    sum_qk, sum_vo, steps = ring_scatter(
+        at, row_major(matmul_tn(first_normalized, grad_qk).astype(jnp.bfloat16)), grad_vo
+    )
+    down_total = over_chips(down_total, down_lower, down_upper)
+    down_pieces = send_planes(down_total, (2, 1), [steps[0]])
+    down_pieces.update(send_planes(down_total, (3,), [steps[2], down_pieces[2]]))
+    grad_gate = all_columns(gate_total, gate_pieces, steps[1])
+    grad_up = all_columns(up_total, up_pieces, steps[2])
+    grad_down = all_columns(down_total, down_pieces, steps[-1])
+    out_sums_first, out_sums_second = after((out_sums_first, out_sums_second), sum_qk, sum_vo)
+    ffn_out = jnp.concatenate([out_sums_first, out_sums_second], 1).astype(jnp.float32)
+    mixed = ((state + ffn_out) * in_use_own[:, None]).astype(jnp.bfloat16)
+    grad_qk, grad_v = after((grad_qk, grad_v), steps[0])
     grad_normed_one = sum_x(matmul_nt(grad_qk, qk_all) + matmul_nt(grad_v, value_all))
     hat_one = inputs * scale_one
     inner_one = grad_normed_one * gain_rows[0]
@@ -454,6 +729,8 @@
     grad_gains = grad_gains + at.other_x(grad_gains)
     bit = 1
     while bit < at.dp:
+        if steps:
+            grad_gains = after(grad_gains, steps.pop(0))
         grad_gains = grad_gains + at.move(grad_gains, lambda d: d ^ bit)
         bit *= 2
     return (

time: 790 us -> 615 us (0.78)
  local copies, waits for them, and re-layouts: 145 us -> 46.4 us
  matrix products: 108 us -> 21.7 us
  waiting for transfers between devices: 346 us -> 270 us
  Pallas kernels: 0 us -> 72.4 us
  other arithmetic: 37.8 us -> 63 us
  starting transfers between devices: 143 us -> 120 us
  between operations: 3.29 us -> 15.9 us
    pallas_call x0 -> x5, Pallas kernels: none -> 72.4 us  [the longest x2 43.9 us: held_call(): pl.pallas_call(body, in_specs=[pl.BlockSpec(memory_space=pltpu.SMEM)] + [...]
    ppermute x21 -> x14, waiting for transfers between devices: 88 us -> 26.5 us  [other_x(): return lax.ppermute(value, 'tensor', [(0, 1), (1, 0)])]
    dynamic_update_slice x51 -> x19, local copies, waits for them, and re-layouts: 45.6 us -> 13 us  [the longest x16 12.1 us: ring_gather(): lax.dynamic_update_slice(buffers[way], block[None], (chip, 0, 0))]
    dot_general x15 -> x3, matrix products: 33.5 us -> 4.61 us  [matmul_nt(): lax.dot_general(left_side, right_side, (((1,), (1,)), ((), ())), preferre...]
    dot_general x6 -> x3, matrix products: 32 us -> 5.35 us  [matrix_product(): return jnp.dot(left_side, right_side, preferred_element_type=jnp.float32)]
    dynamic_slice x3 -> x2, local copies, waits for them, and re-layouts: 26.3 us -> 0.21 us  [out_sums(): order.append(lax.dynamic_index_in_dim(total, slot, 0))]
    dot_general x6 -> x3, matrix products: 27.6 us -> 4.74 us  [matmul_tn(): lax.dot_general(left_side, right_side, (((0,), (0,)), ((), ())), preferre...]
    unnamed x164 -> x226, local copies, waits for them, and re-layouts: 27 us -> 9.78 us
  transfers between devices with their start and end apart: 113 -> 94, of which waited for: 55 -> 53; matrix products, arithmetic and copies ran while one was open for 28% -> 19% of each run, Pallas kernels for 0% -> 8%
where the time goes in v2:
time: 615 us; the launch traced here: 609 us
  waiting for transfers between devices  270 us (44%)
  starting transfers between devices  120 us (20%)
  Pallas kernels  72.4 us (12%)
  other arithmetic  63 us (10%)
  local copies, waits for them, and re-layouts  46.4 us (8%)
  matrix products  21.7 us (4%)
  between operations  15.9 us (3%)
    ppermute x77, waiting for transfers between devices, move(): return lax.ppermute(value, 'dp', [(d, target(d)) for d in range(self.dp)])  243 us
    ppermute x77, starting transfers between devices, move(): return lax.ppermute(value, 'dp', [(d, target(d)) for d in range(self.dp)])  103 us
    pallas_call x2, Pallas kernels, held_call(): pl.pallas_call(body, in_specs=[pl.BlockSpec(memory_space=pltpu.SMEM)] + [...  43.9 us
    pallas_call x3, Pallas kernels, weight_grad(): pl.pallas_call(functools.partial(weight_grad_kernel, masks, by_plane), gr...  28.5 us
    ppermute x14, waiting for transfers between devices, other_x(): return lax.ppermute(value, 'tensor', [(0, 1), (1, 0)])  26.5 us
    ppermute x14, starting transfers between devices, other_x(): return lax.ppermute(value, 'tensor', [(0, 1), (1, 0)])  16.5 us
  transfers between devices with their start and end apart: 94, of which 53 were waited for; matrix products, arithmetic and copies ran while one was open for 19% of the time, Pallas kernels for 8%

profile of v2, /device:TPU:0, one launch (start us, length us, event | category | flops | bytes accessed | tf_op | source)
XLA Modules:
  0.0 609.2 jit_solution(1871491190009913371)
XLA Ops:
  32.6 6.4 %collective-permute-done.3 = bf16[128,1280]{1,0:T(8,128)(2,1)S(1)} collective-permute-done((bf16[128,1280]{1,0:T(8,128)(2,1)}, bf16[128,1280]{1,0:T(8,128)(2,1)S(1)}, u32[]{:S(2)}, u32[]{:S(2)}) %collective-permute-start.3) | collective-permute-done | bytes 327712 | tf_op jit(solution)/shard_map/ppermute | solution.py:178
  39.0 10.0 %collective-permute-done.4 = bf16[128,1280]{1,0:T(8,128)(2,1)S(1)} collective-permute-done((bf16[128,1280]{1,0:T(8,128)(2,1)}, bf16[128,1280]{1,0:T(8,128)(2,1)S(1)}, u32[]{:S(2)}, u32[]{:S(2)}) %collective-permute-start.4) | collective-permute-done | bytes 327712 | tf_op jit(solution)/shard_map/ppermute | solution.py:178
  52.0 10.3 %collective-permute-done.5 = bf16[128,1280]{1,0:T(8,128)(2,1)S(1)} collective-permute-done((bf16[128,1280]{1,0:T(8,128)(2,1)S(1)}, bf16[128,1280]{1,0:T(8,128)(2,1)S(1)}, u32[]{:S(2)}, u32[]{:S(2)}) %collective-permute-start.5) | collective-permute-done | bytes 327712 | tf_op jit(solution)/shard_map/ppermute | solution.py:178
  62.4 11.1 %collective-permute-done.6 = bf16[128,1280]{1,0:T(8,128)(2,1)S(1)} collective-permute-done((bf16[128,1280]{1,0:T(8,128)(2,1)S(1)}, bf16[128,1280]{1,0:T(8,128)(2,1)S(1)}, u32[]{:S(2)}, u32[]{:S(2)}) %collective-permute-start.6) | collective-permute-done | bytes 327712 | tf_op jit(solution)/shard_map/ppermute | solution.py:178
  76.2 4.4 collective-permute-done.7
  93.7 20.1 %collective-permute-start.11 = (bf16[128,1280]{1,0:T(8,128)(2,1)S(1)}, bf16[128,1280]{1,0:T(8,128)(2,1)S(1)}, u32[]{:S(2)}, u32[]{:S(2)}) collective-permute-start(bf16[128,1280]{1,0:T(8,128)(2,1)S(1)} %collective-permute-done.9), channel_id=1, source_target_pairs={{0,8},{2,10},{4,0},{6,2},{8,16},{10,18},{12,4},{14,6},{16,24},{18,... | collective-permute-start | bytes 983048 | tf_op jit(solution)/shard_map/ppermute | solution.py:178
  113.9 4.6 collective-permute-done.11
  118.4 11.1 %collective-permute-done.12 = bf16[128,1280]{1,0:T(8,128)(2,1)S(1)} collective-permute-done((bf16[128,1280]{1,0:T(8,128)(2,1)S(1)}, bf16[128,1280]{1,0:T(8,128)(2,1)S(1)}, u32[]{:S(2)}, u32[]{:S(2)}) %collective-permute-start.12) | collective-permute-done | bytes 327712 | tf_op jit(solution)/shard_map/ppermute | solution.py:178
  130.1 5.0 collective-permute-start.16
  165.4 20.7 %collective-permute-done.20.refs_12_.refs_8_ = bf16[3,128,1024]{2,1,0:T(8,128)(2,1)} collective-permute-done((bf16[3,128,1024]{2,1,0:T(8,128)(2,1)}, bf16[3,128,1024]{2,1,0:T(8,128)(2,1)}, u32[]{:S(2)}, u32[]{:S(2)}) %collective-permute-start.20) | collective-permute-done | bytes 786464 | tf_op jit(solution)/shard_map/ppermute | solution.py:178
  189.2 11.1 %collective-permute-done.23 = bf16[128,2048]{1,0:T(8,128)(2,1)S(1)} collective-permute-done((bf16[128,2048]{1,0:T(8,128)(2,1)S(1)}, bf16[128,2048]{1,0:T(8,128)(2,1)S(1)}, u32[]{:S(2)}, u32[]{:S(2)}) %collective-permute-start.23) | collective-permute-done | bytes 524320 | tf_op jit(solution)/shard_map/ppermute | solution.py:195
  207.2 17.5 %collective-permute-done.24.refs_2_ = bf16[128,2048]{1,0:T(8,128)(2,1)S(1)} collective-permute-done((bf16[128,2048]{1,0:T(8,128)(2,1)S(1)}, bf16[128,2048]{1,0:T(8,128)(2,1)S(1)}, u32[]{:S(2)}, u32[]{:S(2)}) %collective-permute-start.24) | collective-permute-done | bytes 524320 | tf_op jit(solution)/shard_map/ppermute | solution.py:178
  227.7 11.2 %collective-permute-done.28.refs_0_ = bf16[128,2048]{1,0:T(8,128)(2,1)S(1)} collective-permute-done((bf16[128,2048]{1,0:T(8,128)(2,1)S(1)}, bf16[128,2048]{1,0:T(8,128)(2,1)S(1)}, u32[]{:S(2)}, u32[]{:S(2)}) %collective-permute-start.28) | collective-permute-done | bytes 524320 | tf_op jit(solution)/shard_map/ppermute | solution.py:178
  248.6 9.7 %collective-permute-done.31.refs_1_ = bf16[128,2048]{1,0:T(8,128)(2,1)S(1)} collective-permute-done((bf16[128,2048]{1,0:T(8,128)(2,1)S(1)}, bf16[128,2048]{1,0:T(8,128)(2,1)S(1)}, u32[]{:S(2)}, u32[]{:S(2)}) %collective-permute-start.31) | collective-permute-done | bytes 524320 | tf_op jit(solution)/shard_map/ppermute | solution.py:195
  261.2 21.9 %shard_map.186 = (bf16[1024,1024]{1,0:T(8,128)(2,1)}, bf16[1024,1024]{1,0:T(8,128)(2,1)}, bf16[1024,1024]{1,0:T(8,128)(2,1)}, bf16[512,1024]{1,0:T(8,128)(2,1)},...) custom-call(s32[4]{0:T(128)} %pad_add_fusion.1.place, ...), custom_call_target="tpu_custom_call" | custom-call | flops 1 | bytes 1 | tf_op jit(solution)/shard_map/pallas_call | solution.py:314
  284.3 22.0 %shard_map.187 = (bf16[1024,1024]{1,0:T(8,128)(2,1)}, bf16[1024,1024]{1,0:T(8,128)(2,1)}, bf16[128,2048]{1,0:T(8,128)(2,1)}, bf16[128,2048]{1,0:T(8,128)(2,1)}, ...) custom-call(s32[4]{0:T(128)} %pad_add_fusion.1.place, ...), custom_call_target="tpu_custom_call" | custom-call | flops 1 | bytes 1 | tf_op jit(solution)/shard_map/pallas_call | solution.py:314
  310.1 9.5 %shard_map.188 = (bf16[2,4,128,1024]{3,2,1,0:T(8,128)(2,1)}, bf16[2,4,128,1024]{3,2,1,0:T(8,128)(2,1)}) custom-call(s32[2]{0:T(128)} %pad_add_fusion.2.place, bf16[128,2048]{1,0:T(8,128)(2,1)} %copy-done.18, bf16[128,2048]{1,0:T(8,128)(2,1)} %copy-done.20, bf16[128,2048]{1,0:T(8,128)(2,1)} %copy-done.15, bf16[128,2048]{1,0:T(8,128)(2,1)} %copy-done.19, ...), custom_call_target="tpu_custom_call" | custom-call | flops 1 | bytes 1 | tf_op jit(solution)/shard_map/pallas_call | solution.py:422
  323.0 9.4 %shard_map.189 = (bf16[2,4,128,1024]{3,2,1,0:T(8,128)(2,1)}, bf16[2,4,128,1024]{3,2,1,0:T(8,128)(2,1)}) custom-call(s32[2]{0:T(128)} %pad_add_fusion.2.place, bf16[128,2048]{1,0:T(8,128)(2,1)} %copy-done.18, bf16[128,2048]{1,0:T(8,128)(2,1)} %copy-done.20, bf16[128,2048]{1,0:T(8,128)(2,1)} %copy-done.15, bf16[128,2048]{1,0:T(8,128)(2,1)} %copy-done.19, ...), custom_call_target="tpu_custom_call" | custom-call | flops 1 | bytes 1 | tf_op jit(solution)/shard_map/pallas_call | solution.py:422
  346.6 9.6 %shard_map.190 = (bf16[2,4,128,1024]{3,2,1,0:T(8,128)(2,1)}, bf16[2,4,128,1024]{3,2,1,0:T(8,128)(2,1)}) custom-call(s32[2]{0:T(128)} %pad_add_fusion.2.place, bf16[4,128,2048]{2,1,0:T(8,128)(2,1)} %bitcast.389, bf16[4,128,2048]{2,1,0:T(8,128)(2,1)} %copy-done.9, bf16[1024,1024]{1,0:T(8,128)(2,1)} %get-tuple-element.208.refs_2_), custom_call_target="tpu_custom_call" | custom-call | flops 1 | bytes 1 | tf_op jit(solution)/shard_map/pallas_call | solution.py:422
  364.3 6.6 %collective-permute-done.52 = bf16[2,128,1024]{2,1,0:T(8,128)(2,1)S(1)} collective-permute-done((bf16[2,128,1024]{2,1,0:T(8,128)(2,1)S(1)}, bf16[2,128,1024]{2,1,0:T(8,128)(2,1)S(1)}, u32[]{:S(2)}, u32[]{:S(2)}) %collective-permute-start.52) | collective-permute-done | bytes 524320 | tf_op jit(solution)/shard_map/ppermute | solution.py:178
  374.2 19.2 %collective-permute-done.51 = bf16[128,2048]{1,0:T(8,128)(2,1)S(1)} collective-permute-done((bf16[128,2048]{1,0:T(8,128)(2,1)S(1)}, bf16[128,2048]{1,0:T(8,128)(2,1)S(1)}, u32[]{:S(2)}, u32[]{:S(2)}) %collective-permute-start.51) | collective-permute-done | bytes 524320 | tf_op jit(solution)/shard_map/ppermute | solution.py:178
  405.7 9.8 %collective-permute-done.56 = bf16[128,1024]{1,0:T(8,128)(2,1)S(1)} collective-permute-done((bf16[128,1024]{1,0:T(8,128)(2,1)S(1)}, bf16[128,1024]{1,0:T(8,128)(2,1)S(1)}, u32[]{:S(2)}, u32[]{:S(2)}) %collective-permute-start.56) | collective-permute-done | bytes 262176 | tf_op jit(solution)/shard_map/ppermute | solution.py:178
  428.3 4.7 collective-permute-done.59
  454.5 4.6 collective-permute-done.60
  488.8 9.2 %collective-permute-done.66 = bf16[128,1280]{1,0:T(8,128)(2,1)S(1)} collective-permute-done((bf16[128,1280]{1,0:T(8,128)(2,1)S(1)}, bf16[128,1280]{1,0:T(8,128)(2,1)S(1)}, u32[]{:S(2)}, u32[]{:S(2)}) %collective-permute-start.66) | collective-permute-done | bytes 327712 | tf_op jit(solution)/shard_map/ppermute | solution.py:178
  498.0 8.3 %collective-permute-done.67 = bf16[128,1280]{1,0:T(8,128)(2,1)S(1)} collective-permute-done((bf16[128,1280]{1,0:T(8,128)(2,1)S(1)}, bf16[128,1280]{1,0:T(8,128)(2,1)S(1)}, u32[]{:S(2)}, u32[]{:S(2)}) %collective-permute-start.67) | collective-permute-done | bytes 327712 | tf_op jit(solution)/shard_map/ppermute | solution.py:178
  536.1 7.6 %collective-permute-done.71 = bf16[128,1280]{1,0:T(8,128)(2,1)S(1)} collective-permute-done((bf16[128,1280]{1,0:T(8,128)(2,1)S(1)}, bf16[128,1280]{1,0:T(8,128)(2,1)S(1)}, u32[]{:S(2)}, u32[]{:S(2)}) %collective-permute-start.71) | collective-permute-done | bytes 327712 | tf_op jit(solution)/shard_map/ppermute | solution.py:178
  555.4 7.1 %collective-permute-start.74 = (bf16[128,1280]{1,0:T(8,128)(2,1)S(1)}, bf16[128,1280]{1,0:T(8,128)(2,1)S(1)}, u32[]{:S(2)}, u32[]{:S(2)}) collective-permute-start(bf16[128,1280]{1,0:T(8,128)(2,1)S(1)} %fusion.68), channel_id=1, source_target_pairs={{0,8},{2,10},{4,0},{6,2},{8,16},{10,18},{12,4},{14,6},{16,24},{18,... | collective-permute-start | bytes 983048 | tf_op jit(solution)/shard_map/ppermute | solution.py:178
  570.1 5.2 collective-permute-start.76
  576.5 4.8 collective-permute-done.85
  583.8 5.2 collective-permute-done.77
  592.1 4.5 collective-permute-done.78
  (594 shorter events, 270.9 us)
Async XLA Ops:
  7.2 74.2 %all-gather.3.cloned.1.call-start = ((), (), s32[]{:S(2)}) async-start(), calls=%async_computation.4 | async-start | bytes 2621440 | tf_op jit(solution)/shard_map/all_gather | solution.py:479
  15.2 585.3 %reduce-scatter.3.cloned.1.call-start = ((), (), s32[]{:S(2)}) async-start(), calls=%async_computation.2 | async-start | bytes 1310720 | tf_op jit(solution)/shard_map/reduce_scatter | solution.py:571
  25.0 24.0 %collective-permute-start.4 = (bf16[128,1280]{1,0:T(8,128)(2,1)}, bf16[128,1280]{1,0:T(8,128)(2,1)S(1)}, u32[]{:S(2)}, u32[]{:S(2)}) collective-permute-start(bf16[128,1280]{1,0:T(8,128)(2,1)} %collective-permute-done.2), channel_id=1, source_target_pairs={{0,4},{2,6},{4,12},{6,14},{8,0},{10,2},{12,20},{14,22},{16,8},{18,... | collective-permute-start | bytes 983048 | tf_op jit(solution)/shard_map/ppermute | solution.py:178
  49.8 23.6 %collective-permute-start.6 = (bf16[128,1280]{1,0:T(8,128)(2,1)S(1)}, bf16[128,1280]{1,0:T(8,128)(2,1)S(1)}, u32[]{:S(2)}, u32[]{:S(2)}) collective-permute-start(bf16[128,1280]{1,0:T(8,128)(2,1)S(1)} %collective-permute-done.4), channel_id=1, source_target_pairs={{0,4},{2,6},{4,12},{6,14},{8,0},{10,2},{12,20},{14,22},{16,8},{18,... | collective-permute-start | bytes 983048 | tf_op jit(solution)/shard_map/ppermute | solution.py:178
  81.4 48.6 %collective-permute-start.13 = (bf16[4,128,2048]{2,1,0:T(8,128)(2,1)}, bf16[4,128,2048]{2,1,0:T(8,128)(2,1)S(1)}, u32[]{:S(2)}, u32[]{:S(2)}) collective-permute-start(bf16[4,128,2048]{2,1,0:T(8,128)(2,1)} %bitcast.387), channel_id=1, source_target_pairs={{0,1},{1,0},{2,3},{3,2},{4,5},{5,4},{6,7},{7,6},{8,9},{9,8},{10,11... | collective-permute-start | bytes 6291464 | tf_op jit(solution)/shard_map/ppermute | solution.py:195
  87.2 42.8 %collective-permute-start.14 = (bf16[3,128,1024]{2,1,0:T(8,128)(2,1)S(1)}, bf16[3,128,1024]{2,1,0:T(8,128)(2,1)}, u32[]{:S(2)}, u32[]{:S(2)}) collective-permute-start(bf16[3,128,1024]{2,1,0:T(8,128)(2,1)S(1)} %pad_maximum_fusion.8), channel_id=1, source_target_pairs={{0,16},{2,18},{4,20},{6,22},{8,24},{10,26},{12,28},{14,30},{16,0},... | collective-permute-start | bytes 2359304 | tf_op jit(solution)/shard_map/ppermute | solution.py:178
  89.6 40.4 %collective-permute-start.15 = (bf16[3,128,1024]{2,1,0:T(8,128)(2,1)S(1)}, bf16[3,128,1024]{2,1,0:T(8,128)(2,1)S(1)}, u32[]{:S(2)}, u32[]{:S(2)}) collective-permute-start(bf16[3,128,1024]{2,1,0:T(8,128)(2,1)S(1)} %pad_maximum_fusion.9.refs_8_.refs_4_), channel_id=1, source_target_pairs={{0,4},{2,6},{4,0},{6,2},{8,12},{10,14},{12,8},{14,10},{16,20},{18,... | collective-permute-start | bytes 2359304 | tf_op jit(solution)/shard_map/ppermute | solution.py:178
  93.7 24.7 %collective-permute-start.11 = (bf16[128,1280]{1,0:T(8,128)(2,1)S(1)}, bf16[128,1280]{1,0:T(8,128)(2,1)S(1)}, u32[]{:S(2)}, u32[]{:S(2)}) collective-permute-start(bf16[128,1280]{1,0:T(8,128)(2,1)S(1)} %collective-permute-done.9), channel_id=1, source_target_pairs={{0,8},{2,10},{4,0},{6,2},{8,16},{10,18},{12,4},{14,6},{16,24},{18,... | collective-permute-start | bytes 983048 | tf_op jit(solution)/shard_map/ppermute | solution.py:178
  149.5 36.6 %collective-permute-start.20 = (bf16[3,128,1024]{2,1,0:T(8,128)(2,1)}, bf16[3,128,1024]{2,1,0:T(8,128)(2,1)}, u32[]{:S(2)}, u32[]{:S(2)}) collective-permute-start(bf16[3,128,1024]{2,1,0:T(8,128)(2,1)} %pad_maximum_fusion.10), channel_id=1, source_target_pairs={{0,8},{2,10},{4,12},{6,14},{8,0},{10,2},{12,4},{14,6},{16,24},{18,... | collective-permute-start | bytes 2359304 | tf_op jit(solution)/shard_map/ppermute | solution.py:178
  150.1 36.1 %collective-permute-start.21 = (bf16[3,128,1024]{2,1,0:T(8,128)(2,1)}, bf16[3,128,1024]{2,1,0:T(8,128)(2,1)}, u32[]{:S(2)}, u32[]{:S(2)}) collective-permute-start(bf16[3,128,1024]{2,1,0:T(8,128)(2,1)} %pad_maximum_fusion.11), channel_id=1, source_target_pairs={{0,24},{2,26},{4,28},{6,30},{8,16},{10,18},{12,20},{14,22},{16,8},... | collective-permute-start | bytes 2359304 | tf_op jit(solution)/shard_map/ppermute | solution.py:178
  151.1 35.1 %collective-permute-start.22 = (bf16[3,128,1024]{2,1,0:T(8,128)(2,1)}, bf16[3,128,1024]{2,1,0:T(8,128)(2,1)}, u32[]{:S(2)}, u32[]{:S(2)}) collective-permute-start(bf16[3,128,1024]{2,1,0:T(8,128)(2,1)} %collective-permute-done.14.refs_10_.refs_6_), channel_id=1, source_target_pairs={{0,4},{2,6},{4,0},{6,2},{8,12},{10,14},{12,8},{14,10},{16,20},{18,... | collective-permute-start | bytes 2359304 | tf_op jit(solution)/shard_map/ppermute | solution.py:178
  189.2 18.0 %collective-permute-start.27 = (bf16[3,128,1024]{2,1,0:T(8,128)(2,1)}, bf16[3,128,1024]{2,1,0:T(8,128)(2,1)S(1)}, u32[]{:S(2)}, u32[]{:S(2)}) collective-permute-start(bf16[3,128,1024]{2,1,0:T(8,128)(2,1)} %collective-permute-done.20.refs_12_.refs_8_), channel_id=1, source_target_pairs={{0,4},{2,6},{4,0},{6,2},{8,12},{10,14},{12,8},{14,10},{16,20},{18,... | collective-permute-start | bytes 2359304 | tf_op jit(solution)/shard_map/ppermute | solution.py:178
  200.8 23.9 %collective-permute-start.24 = (bf16[128,2048]{1,0:T(8,128)(2,1)S(1)}, bf16[128,2048]{1,0:T(8,128)(2,1)S(1)}, u32[]{:S(2)}, u32[]{:S(2)}) collective-permute-start(bf16[128,2048]{1,0:T(8,128)(2,1)S(1)} %multiply_convert_fusion.5.refs_6_), channel_id=1, source_target_pairs={{0,16},{2,18},{4,20},{6,22},{8,24},{10,26},{12,28},{14,30},{16,0},... | collective-permute-start | bytes 1572872 | tf_op jit(solution)/shard_map/ppermute | solution.py:178
  201.3 23.4 %collective-permute-start.25 = (bf16[128,2048]{1,0:T(8,128)(2,1)S(1)}, bf16[128,2048]{1,0:T(8,128)(2,1)S(1)}, u32[]{:S(2)}, u32[]{:S(2)}) collective-permute-start(bf16[128,2048]{1,0:T(8,128)(2,1)S(1)} %multiply_convert_fusion.5.refs_6_), channel_id=1, source_target_pairs={{0,1},{1,0},{2,3},{3,2},{4,5},{5,4},{6,7},{7,6},{8,9},{9,8},{10,11... | collective-permute-start | bytes 1572872 | tf_op jit(solution)/shard_map/ppermute | solution.py:195
  203.0 22.0 %collective-permute-start.26 = (bf16[128,2048]{1,0:T(8,128)(2,1)S(1)}, bf16[128,2048]{1,0:T(8,128)(2,1)S(1)}, u32[]{:S(2)}, u32[]{:S(2)}) collective-permute-start(bf16[128,2048]{1,0:T(8,128)(2,1)S(1)} %multiply_convert_fusion.5.refs_6_), channel_id=1, source_target_pairs={{0,8},{2,10},{4,12},{6,14},{8,0},{10,2},{12,4},{14,6},{16,24},{18,... | collective-permute-start | bytes 1572872 | tf_op jit(solution)/shard_map/ppermute | solution.py:178
  225.0 18.3 %collective-permute-start.30 = (bf16[3,128,1024]{2,1,0:T(8,128)(2,1)}, bf16[3,128,1024]{2,1,0:T(8,128)(2,1)S(1)}, u32[]{:S(2)}, u32[]{:S(2)}) collective-permute-start(bf16[3,128,1024]{2,1,0:T(8,128)(2,1)} %collective-permute-done.21.refs_18_.refs_14_), channel_id=1, source_target_pairs={{0,4},{2,6},{4,0},{6,2},{8,12},{10,14},{12,8},{14,10},{16,20},{18,... | collective-permute-start | bytes 2359304 | tf_op jit(solution)/shard_map/ppermute | solution.py:178
  243.9 17.2 %collective-permute-start.40 = (bf16[3,128,1024]{2,1,0:T(8,128)(2,1)S(1)}, bf16[3,128,1024]{2,1,0:T(8,128)(2,1)}, u32[]{:S(2)}, u32[]{:S(2)}) collective-permute-start(bf16[3,128,1024]{2,1,0:T(8,128)(2,1)S(1)} %collective-permute-done.30.refs_19_.refs_15_), channel_id=1, source_target_pairs={{0,2},{2,0},{4,6},{6,4},{8,10},{10,8},{12,14},{14,12},{16,18},{18,... | collective-permute-start | bytes 2359304 | tf_op jit(solution)/shard_map/ppermute | solution.py:178
  283.1 24.7 %collective-permute-start.41 = (bf16[512,1024]{1,0:T(8,128)(2,1)}, bf16[512,1024]{1,0:T(8,128)(2,1)S(1)}, u32[]{:S(2)}, u32[]{:S(2)}) collective-permute-start(bf16[512,1024]{1,0:T(8,128)(2,1)} %get-tuple-element.180), channel_id=1, source_target_pairs={{0,1},{1,0},{2,3},{3,2},{4,5},{5,4},{6,7},{7,6},{8,9},{9,8},{10,11... | collective-permute-start | bytes 3145736 | tf_op jit(solution)/shard_map/ppermute | solution.py:195
  337.1 20.4 %collective-permute-start.49 = (bf16[2,4,128,1024]{3,2,1,0:T(8,128)(2,1)}, bf16[2,4,128,1024]{3,2,1,0:T(8,128)(2,1)}, u32[]{:S(2)}, u32[]{:S(2)}) collective-permute-start(bf16[2,4,128,1024]{3,2,1,0:T(8,128)(2,1)} %get-tuple-element.206), channel_id=1, source_target_pairs={{0,2},{2,0},{4,6},{6,4},{8,10},{10,8},{12,14},{14,12},{16,18},{18,... | collective-permute-start | bytes 6291464 | tf_op jit(solution)/shard_map/ppermute | solution.py:178
  346.5 254.0 %reduce-scatter.5.cloned.1.call-start = ((), (), s32[]{:S(2)}) async-start(), calls=%async_computation.3 | async-start | bytes 1310720 | tf_op jit(solution)/shard_map/reduce_scatter | solution.py:571
  359.3 39.1 %collective-permute-start.53 = (bf16[2,4,128,1024]{3,2,1,0:T(8,128)(2,1)}, bf16[2,4,128,1024]{3,2,1,0:T(8,128)(2,1)S(1)}, u32[]{:S(2)}, u32[]{:S(2)}) collective-permute-start(bf16[2,4,128,1024]{3,2,1,0:T(8,128)(2,1)} %get-tuple-element.215), channel_id=1, source_target_pairs={{0,2},{2,0},{4,6},{6,4},{8,10},{10,8},{12,14},{14,12},{16,18},{18,... | collective-permute-start | bytes 6291464 | tf_op jit(solution)/shard_map/ppermute | solution.py:178
  359.6 33.9 %collective-permute-start.51 = (bf16[128,2048]{1,0:T(8,128)(2,1)S(1)}, bf16[128,2048]{1,0:T(8,128)(2,1)S(1)}, u32[]{:S(2)}, u32[]{:S(2)}) collective-permute-start(bf16[128,2048]{1,0:T(8,128)(2,1)S(1)} %add_convert_fusion.5), channel_id=1, source_target_pairs={{0,16},{2,18},{4,20},{6,22},{8,24},{10,26},{12,28},{14,30},{16,0},... | collective-permute-start | bytes 1572872 | tf_op jit(solution)/shard_map/ppermute | solution.py:178
  360.7 32.8 %collective-permute-start.50 = (bf16[128,2048]{1,0:T(8,128)(2,1)S(1)}, bf16[128,2048]{1,0:T(8,128)(2,1)S(1)}, u32[]{:S(2)}, u32[]{:S(2)}) collective-permute-start(bf16[128,2048]{1,0:T(8,128)(2,1)S(1)} %copy-done.104), channel_id=1, source_target_pairs={{0,8},{2,10},{4,12},{6,14},{8,0},{10,2},{12,4},{14,6},{16,24},{18,... | collective-permute-start | bytes 1572872 | tf_op jit(solution)/shard_map/ppermute | solution.py:178
  398.4 18.2 %collective-permute-start.54 = (bf16[128,2048]{1,0:T(8,128)(2,1)S(1)}, bf16[128,2048]{1,0:T(8,128)(2,1)S(1)}, u32[]{:S(2)}, u32[]{:S(2)}) collective-permute-start(bf16[128,2048]{1,0:T(8,128)(2,1)S(1)} %get-tuple-element.216), channel_id=1, source_target_pairs={{0,1},{1,0},{2,3},{3,2},{4,5},{5,4},{6,7},{7,6},{8,9},{9,8},{10,11... | collective-permute-start | bytes 1572872 | tf_op jit(solution)/shard_map/ppermute | solution.py:195
  416.6 42.6 %collective-permute-start.63 = (bf16[512,1024]{1,0:T(8,128)(2,1)}, bf16[512,1024]{1,0:T(8,128)(2,1)}, u32[]{:S(2)}, u32[]{:S(2)}) collective-permute-start(bf16[512,1024]{1,0:T(8,128)(2,1)} %get-tuple-element.228), channel_id=1, source_target_pairs={{0,1},{1,0},{2,3},{3,2},{4,5},{5,4},{6,7},{7,6},{8,9},{9,8},{10,11... | collective-permute-start | bytes 3145736 | tf_op jit(solution)/shard_map/ppermute | solution.py:195
  454.1 21.3 %collective-permute-start.65 = (bf16[8,128,1280]{2,1,0:T(8,128)(2,1)}, bf16[8,128,1280]{2,1,0:T(8,128)(2,1)}, u32[]{:S(2)}, u32[]{:S(2)}) collective-permute-start(bf16[8,128,1280]{2,1,0:T(8,128)(2,1)} %dynamic-slice_bitcast_fusion), channel_id=1, source_target_pairs={{0,2},{2,0},{4,6},{6,4},{8,10},{10,8},{12,14},{14,12},{16,18},{18,... | collective-permute-start | bytes 7864328 | tf_op jit(solution)/shard_map/ppermute | solution.py:178
  468.9 78.4 %collective-permute-start.86 = (bf16[128,1024]{1,0:T(8,128)(2,1)}, bf16[128,1024]{1,0:T(8,128)(2,1)}, u32[]{:S(2)}, u32[]{:S(2)}) collective-permute-start(bf16[128,1024]{1,0:T(8,128)(2,1)} %get-tuple-element.257), channel_id=1, source_target_pairs={{0,24},{2,26},{4,28},{6,30},{8,16},{10,18},{12,20},{14,22},{16,8},... | collective-permute-start | bytes 786440 | tf_op jit(solution)/shard_map/ppermute | solution.py:178
  488.2 18.1 %collective-permute-start.67 = (bf16[128,1280]{1,0:T(8,128)(2,1)S(1)}, bf16[128,1280]{1,0:T(8,128)(2,1)S(1)}, u32[]{:S(2)}, u32[]{:S(2)}) collective-permute-start(bf16[128,1280]{1,0:T(8,128)(2,1)S(1)} %dynamic-slice_bitcast_fusion.5), channel_id=1, source_target_pairs={{0,4},{2,6},{4,12},{6,14},{8,0},{10,2},{12,20},{14,22},{16,8},{18,... | collective-permute-start | bytes 983048 | tf_op jit(solution)/shard_map/ppermute | solution.py:178
  513.7 77.9 %collective-permute-start.88 = (bf16[128,1024]{1,0:T(8,128)(2,1)S(1)}, bf16[128,1024]{1,0:T(8,128)(2,1)S(1)}, u32[]{:S(2)}, u32[]{:S(2)}) collective-permute-start(bf16[128,1024]{1,0:T(8,128)(2,1)S(1)} %get-tuple-element.263), channel_id=1, source_target_pairs={{0,8},{2,10},{4,12},{6,14},{8,0},{10,2},{12,4},{14,6},{16,24},{18,... | collective-permute-start | bytes 786440 | tf_op jit(solution)/shard_map/ppermute | solution.py:178
  516.9 31.1 %collective-permute-start.89 = (bf16[128,1024]{1,0:T(8,128)(2,1)S(1)}, bf16[128,1024]{1,0:T(8,128)(2,1)S(1)}, u32[]{:S(2)}, u32[]{:S(2)}) collective-permute-start(bf16[128,1024]{1,0:T(8,128)(2,1)S(1)} %get-tuple-element.264), channel_id=1, source_target_pairs={{0,16},{2,18},{4,20},{6,22},{8,24},{10,26},{12,28},{14,30},{16,0},... | collective-permute-start | bytes 786440 | tf_op jit(solution)/shard_map/ppermute | solution.py:178
  547.3 28.1 %collective-permute-start.84 = (f32[2,2048]{1,0:T(2,128)S(1)}, f32[2,2048]{1,0:T(2,128)S(1)}, u32[]{:S(2)}, u32[]{:S(2)}) collective-permute-start(f32[2,2048]{1,0:T(2,128)S(1)} %add.753), channel_id=1, source_target_pairs={{0,8},{2,10},{4,12},{6,14},{8,0},{10,2},{12,4},{14,6},{16,24},{18,... | collective-permute-start | bytes 49160 | tf_op jit(solution)/shard_map/ppermute | solution.py:178
  548.0 43.6 %collective-permute-start.90 = (bf16[128,1024]{1,0:T(8,128)(2,1)S(1)}, bf16[128,1024]{1,0:T(8,128)(2,1)S(1)}, u32[]{:S(2)}, u32[]{:S(2)}) collective-permute-start(bf16[128,1024]{1,0:T(8,128)(2,1)S(1)} %get-tuple-element.265), channel_id=1, source_target_pairs={{0,24},{2,26},{4,28},{6,30},{8,16},{10,18},{12,20},{14,22},{16,8},... | collective-permute-start | bytes 786440 | tf_op jit(solution)/shard_map/ppermute | solution.py:178
  (175 other events, 2171.8 us)
Sparse Core Ops, SparseCore 0:
  15.3 60.4 all-gather.2
  346.7 32.8 reduce-scatter.2
  475.5 32.3 reduce-scatter.4

commit v3 on v2

v3 whole, which is shorter than its diff:
```python
import functools
import math

import jax
import jax.numpy as jnp
from jax import lax
from jax.experimental import pallas as pl
from jax.experimental.pallas import tpu as pltpu
from jax.sharding import PartitionSpec as P

HEAD_WIDTH = 64
EPSILON = 1e-05
MASKED = -1e30
CORES = 2
PLANES = 4


def after(value, *earlier):
    return lax.optimization_barrier((value, *earlier))[0]


def layout(lengths, row_count):
    finish = jnp.cumsum(lengths)
    starts = jnp.concatenate([finish - lengths, finish[-1:]])
    row_ids = jnp.arange(row_count, dtype=jnp.int32)
    segment = jnp.sum((row_ids[:, None] >= finish[None, :]).astype(jnp.int32), 1)
    chosen_slot = segment[:, None] == jnp.arange(starts.shape[0], dtype=jnp.int32)[None, :]
    first_row = jnp.sum(jnp.where(chosen_slot, starts[None, :], 0), 1)
    position = row_ids - first_row
    in_use = (segment < lengths.shape[0]).astype(jnp.float32)
    return (row_ids, segment, position, in_use)


def rope_tables(position, head_size):
    halfway = head_size // 2
    ladder = jnp.arange(halfway, dtype=jnp.float32)
    inverse = 1.0 / 500000.0 ** (ladder * 2.0 / head_size)
    wavelength = 2.0 * math.pi / inverse
    smooth = (8192.0 / wavelength - 1.0) / 3.0
    blended = (1.0 - smooth) * inverse / 32.0 + smooth * inverse
    scaled = jnp.where(
        wavelength > 8192.0, inverse / 32.0, jnp.where(wavelength < 2048.0, inverse, blended)
    )
    angles = position.astype(jnp.float32)[:, None] * scaled[None, :]
    cosine_lookup = jnp.cos(angles)
    sine_lookup = jnp.sin(angles)
    return (
        jnp.concatenate([cosine_lookup, cosine_lookup], 1),
        jnp.concatenate([sine_lookup, sine_lookup], 1),
    )


class Places:
    def __init__(self, dp):
        self.dp = dp
        self.planes = PLANES
        self.rows = dp // (PLANES * CORES)
        self.chips = dp // CORES
        index = lax.axis_index("dp")
        self.z = index // (self.rows * CORES)
        self.y = (index // CORES) % self.rows
        self.core = index % CORES
        self.x = lax.axis_index("tensor")
        stride = self.rows * CORES
        self.columns = [[z * stride + i for z in range(PLANES)] for i in range(stride)]

    def move(self, value, target):
        return lax.ppermute(value, "dp", [(d, target(d)) for d in range(self.dp)])

    def across_z(self, value, mask):
        stride = self.rows * CORES
        return self.move(value, lambda d: d ^ (mask * stride))

    def along_y(self, value, steps):
        def target(d):
            y = (d // CORES) % self.rows
            return d + ((y + steps) % self.rows - y) * CORES

        return self.move(value, target)

    def other_core(self, value):
        return self.move(value, lambda d: d ^ 1)

    def other_x(self, value):
        return lax.ppermute(value, "tensor", [(0, 1), (1, 0)])


def product(left_side, right_side, contract):
    return lax.dot_general(
        left_side, right_side, (contract, ((), ())), preferred_element_type=jnp.float32
    )


NN = ((1,), (0,))
NT = ((1,), (1,))
TN = ((0,), (0,))


class Held:
    def __init__(self, place, blocks, sources, which, held, sems):
        self.z, self.y, self.core, self.rows = (place[i] for i in range(4))
        self.blocks, self.sources, self.which = blocks, sources, which
        self.held, self.sems = held, sems
        for i in range(len(which)):
            for n in range(len(blocks)):
                self.copy(i, n).start()

    def copy(self, i, n):
        (mask, back, other), first, counts = self.blocks[n]
        source, within = first, self.which[i]
        for count in counts:
            if within < count:
                break
            source, within = source + 1, within - count
        size = self.sources[source].shape[1]
        chip = (self.z ^ mask) * self.rows + lax.rem(self.y + self.rows - back, self.rows)
        start = pl.multiple_of((chip * CORES + (self.core ^ other)) * size, size)
        return pltpu.make_async_copy(
            self.sources[source].at[within], self.held.at[i, pl.ds(start, size)], self.sems.at[i, n]
        )

    def wait(self, i):
        for n in range(len(self.blocks)):
            self.copy(i, n).wait()


def cost_of(flops, arrays, out_shapes):
    moved = [math.prod(array.shape) * array.dtype.itemsize for array in arrays]
    moved += [math.prod(shape) * jnp.dtype(kind).itemsize for shape, kind in out_shapes]
    return pl.CostEstimate(flops=flops, bytes_accessed=sum(moved), transcendentals=0)


def held_call(at, kernel, weights, which, arrays, out_shapes):
    blocks, sources = [], []
    for key, parts in weights.items():
        blocks.append((key, len(sources), [part.shape[0] for part in parts]))
        sources += parts
    _, size, quarter = sources[0].shape
    place = jnp.stack([at.z, at.y, at.core, jnp.int32(at.rows)]).astype(jnp.int32)
    vmem = pl.BlockSpec(memory_space=pltpu.VMEM)
    low = jnp.bfloat16

    def body(place, *refs):
        ins, refs = refs[: len(arrays)], refs[len(arrays) :]
        given, refs = refs[: len(sources)], refs[len(sources) :]
        outs, (held, sems) = refs[: len(out_shapes)], refs[len(out_shapes) :]
        kernel(Held(place, blocks, given, which, held, sems), ins, outs)

    return pl.pallas_call(
        body,
        in_specs=[pl.BlockSpec(memory_space=pltpu.SMEM)]
        + [vmem] * len(arrays)
        + [pl.BlockSpec(memory_space=pl.ANY)] * len(sources),
        out_specs=[vmem] * len(out_shapes),
        out_shape=[jax.ShapeDtypeStruct(shape, low) for shape in out_shapes],
        scratch_shapes=[
            pltpu.VMEM((len(which), len(blocks) * size, quarter), low),
            pltpu.SemaphoreType.DMA((len(which), len(blocks))),
        ],
        compiler_params=pltpu.CompilerParams(vmem_limit_bytes=56 * 2**20),
        cost_estimate=cost_of(
            6 * out_shapes[0][0] * size * len(blocks) * quarter,
            [*arrays, *sources],
            [(shape, low) for shape in out_shapes],
        ),
    )(place, *arrays, *sources)


def forward(at, weights, normed):
    rows_own, width = normed[0].shape
    quarter = next(iter(weights.values()))[0].shape[-1]
    count = len(normed) // 2
    half = width // 2

    def kernel(held, normed, outs):
        hidden_ref, silu_ref, slope_ref, *out_refs = outs
        for k in range(count):
            here = slice(2 * k * rows_own, 2 * (k + 1) * rows_own)
            own = slice(k * rows_own, (k + 1) * rows_own)
            rows = jnp.concatenate([normed[2 * k][...], normed[2 * k + 1][...]], 0)
            if k == 0:
                held.wait(0)
            gate = product(rows, held.held[0], NN)
            if k == 0:
                held.wait(1)
            up = product(rows, held.held[1], NN)
            sigmoid_gate = jax.nn.sigmoid(gate)
            silu_gate = gate * sigmoid_gate
            hidden = (silu_gate * up).astype(jnp.bfloat16)
            hidden_ref[here] = hidden
            silu_ref[here] = silu_gate.astype(jnp.bfloat16)
            slope = up * sigmoid_gate * (1.0 + gate * (1.0 - sigmoid_gate))
            slope_ref[here] = slope.astype(jnp.bfloat16)
            if k == 0:
                held.wait(2)
            out = product(hidden, held.held[2], NT).astype(jnp.bfloat16)
            for i in range(2):
                columns = slice(i * half, (i + 1) * half)
                out_refs[2 * i][own] = out[:rows_own, columns]
                out_refs[2 * i + 1][own] = out[rows_own:, columns]

    shapes = [(2 * count * rows_own, quarter)] * 3 + [(count * rows_own, half)] * 4
    return held_call(at, kernel, weights, (0, 1, 2), normed, shapes)


def backward(at, weights, grads, silu, slope):
    rows_own, width = grads[0].shape
    count = len(grads) // 2

    def kernel(held, ins, outs):
        *grads, silu, slope = ins
        gate_ref, up_ref, *back = outs
        for k in range(count):
            here = slice(2 * k * rows_own, 2 * (k + 1) * rows_own)
            rows = jnp.concatenate([grads[2 * k][...], grads[2 * k + 1][...]], 0)
            if k == 0:
                held.wait(0)
            grad_hidden = product(rows, held.held[0], NN)
            grad_gate = (grad_hidden * slope[here]).astype(jnp.bfloat16)
            grad_up = (grad_hidden * silu[here]).astype(jnp.bfloat16)
            gate_ref[here] = grad_gate
            up_ref[here] = grad_up
            if k == 0:
                held.wait(1)
            total = product(grad_gate, held.held[1], NT)
            if k == 0:
                held.wait(2)
            total = (total + product(grad_up, held.held[2], NT)).astype(jnp.bfloat16)
            back[2 * k][...] = total[:rows_own]
            back[2 * k + 1][...] = total[rows_own:]

    shapes = [silu.shape] * 2 + [(rows_own, width)] * (2 * count)
    return held_call(at, kernel, weights, (2, 0, 1), [*grads, silu, slope], shapes)


def weight_grad_kernel(place, *refs):
    core = place[0]
    *left, right, own_ref, other_ref = refs
    rows = jnp.concatenate([ref[...] for ref in left], 0)
    total = product(rows, right[...], TN).astype(jnp.bfloat16)
    chips, _, own_features, quarter = own_ref.shape
    total = total.reshape(chips, CORES, own_features, quarter)
    own_ref[:, 0] = jnp.where(core == 0, total[:, 0], total[:, 1])
    other_ref[:, 0] = jnp.where(core == 0, total[:, 1], total[:, 0])


def weight_grad(at, left, right, own_features):
    rows, width = left[0].shape
    quarter = right.shape[-1]
    place = jnp.stack([at.core]).astype(jnp.int32)
    shape = (at.rows, at.planes, own_features, quarter)
    block = (at.rows, 1, own_features, quarter)
    left_spec = pl.BlockSpec((rows, width // at.planes), lambda i, place: (0, i))
    return pl.pallas_call(
        weight_grad_kernel,
        grid_spec=pltpu.PrefetchScalarGridSpec(
            num_scalar_prefetch=1,
            grid=(at.planes,),
            in_specs=[left_spec] * len(left) + [pl.BlockSpec(right.shape, lambda i, place: (0, 0))],
            out_specs=[pl.BlockSpec(block, lambda i, place: (0, i, 0, 0))] * 2,
        ),
        out_shape=[jax.ShapeDtypeStruct(shape, jnp.bfloat16)] * 2,
        compiler_params=pltpu.CompilerParams(vmem_limit_bytes=56 * 2**20),
        cost_estimate=cost_of(
            2 * len(left) * rows * width * quarter,
            [*left, right],
            [(shape, right.dtype)] * 2,
        ),
    )(place, *left, right)


class Rotation:
    def __init__(self, cosine, sine):
        self.cosine, self.sine = cosine[...], sine[...]
        lanes = lax.broadcasted_iota(jnp.int32, self.cosine.shape, 1)
        self.first_half = lax.rem(lanes, HEAD_WIDTH) < HEAD_WIDTH // 2

    def turned(self, pair):
        quarter = HEAD_WIDTH // 2
        return pltpu.roll(pair, 2 * HEAD_WIDTH - quarter, 1), pltpu.roll(pair, quarter, 1)

    def forward(self, pair):
        ahead, behind = self.turned(pair)
        return pair * self.cosine + jnp.where(self.first_half, -ahead, behind) * self.sine

    def backward(self, pair):
        ahead, behind = self.turned(pair * self.sine)
        return pair * self.cosine + jnp.where(self.first_half, ahead, -behind)


class Whole:
    def __init__(self, place, keys, sources, held, sems):
        core, z, y, rows = (place[i] for i in range(1, 5))
        self.held = held
        self.copies = []
        for n, (mask, back, other) in enumerate(keys):
            chip = lax.rem(y + rows - back, rows)
            here = held.at[z ^ mask, chip, core ^ other]
            self.copies.append(pltpu.make_async_copy(sources[n], here, sems.at[n]))
        for copy in self.copies:
            copy.start()

    def wait(self):
        for copy in self.copies:
            copy.wait()

    def columns(self, at_columns):
        part = self.held[:, :, :, :, at_columns]
        return part.reshape(-1, part.shape[-1])


def by_x(x, own, other):
    first = jnp.where(x == 0, own[...], other[...])
    second = jnp.where(x == 0, other[...], own[...])
    return jnp.concatenate([first, second], 0)


def allowed_keys(segment, segment_row, per_group):
    rows = segment.shape[0]
    stacked = (per_group * rows, rows)
    row_ids = lax.rem(lax.broadcasted_iota(jnp.int32, stacked, 0), rows)
    columns = lax.broadcasted_iota(jnp.int32, stacked, 1)
    segments = jnp.concatenate([segment[...]] * per_group, 0)
    return (segments == segment_row[...]) & (columns <= row_ids)


def heads_of(values, group, per_group):
    start = group * per_group
    return jnp.concatenate(
        [
            values[:, (start + i) * HEAD_WIDTH : (start + i + 1) * HEAD_WIDTH]
            for i in range(per_group)
        ],
        0,
    )


def softmax_weights(query, key, allowed):
    scores = jnp.where(allowed, product(query, key, NT) * HEAD_WIDTH ** (-0.5), MASKED)
    exponent = jnp.exp(scores - jnp.max(scores, 1, keepdims=True))
    return exponent / jnp.sum(exponent, 1, keepdims=True)


def attention_kernel(width_kv, keys, place, *refs):
    normed_own, normed_other, segment, segment_row, cosine, sine = refs[:6]
    sources, refs = refs[6 : 6 + len(keys)], refs[6 + len(keys) :]
    query_key, value, attended, branch_own, branch_other, held, sems = refs
    x = place[0]
    low = jnp.bfloat16
    weights_of = Whole(place, keys, sources, held, sems)
    normed = by_x(x, normed_own, normed_other)
    rows_own = normed_own.shape[0]
    rotation = Rotation(cosine, sine)
    width_query = attended.shape[1]
    per_group = width_query // width_kv
    allowed = allowed_keys(segment, segment_row, per_group)
    to_value = slice(width_query + width_kv, width_query + 2 * width_kv)
    to_out = slice(width_query + 2 * width_kv, None)
    weights_of.wait()
    projected = product(normed, weights_of.columns(slice(0, width_query + width_kv)), NN)
    pairs = []
    for start in range(0, projected.shape[1], 2 * HEAD_WIDTH):
        pairs.append(rotation.forward(projected[:, start : start + 2 * HEAD_WIDTH]).astype(low))
    rotated = jnp.concatenate(pairs, 1)
    query_key[...] = rotated
    values = product(normed, weights_of.columns(to_value), NN).astype(low)
    value[...] = values
    heads = []
    for group in range(width_kv // HEAD_WIDTH):
        here = slice(group * HEAD_WIDTH, (group + 1) * HEAD_WIDTH)
        key = rotated[:, width_query:][:, here]
        weights = softmax_weights(heads_of(rotated, group, per_group), key, allowed).astype(low)
        out = product(weights, values[:, here], NN).astype(low)
        rows = rotated.shape[0]
        heads += [out[i * rows : (i + 1) * rows] for i in range(per_group)]
    all_heads = jnp.concatenate(heads, 1)
    attended[...] = all_heads
    branch = product(all_heads, weights_of.columns(to_out), NT)
    first, second = branch[:rows_own], branch[rows_own:]
    branch_own[...] = jnp.where(x == 0, first, second)
    branch_other[...] = jnp.where(x == 0, second, first).astype(low)


def attention_back_kernel(width_kv, keys, place, *refs):
    state_own, state_other, normed_own, normed_other, segment, segment_row, cosine, sine = refs[:8]
    query_key, value, attended = refs[8:11]
    sources, refs = refs[11 : 11 + len(keys)], refs[11 + len(keys) :]
    back_own, back_other, qk_own, qk_other, vo_own, vo_other, held, sems = refs
    x, core = place[0], place[1]
    low = jnp.bfloat16
    weights_of = Whole(place, keys, sources, held, sems)
    scaling = HEAD_WIDTH ** (-0.5)
    state = by_x(x, state_own, state_other)
    normed = by_x(x, normed_own, normed_other)
    rows_own, rows = state_own.shape[0], state.shape[0]
    rotation = Rotation(cosine, sine)
    width_query = attended.shape[1]
    per_group = width_query // width_kv
    allowed = allowed_keys(segment, segment_row, per_group)
    to_value = slice(width_query + width_kv, width_query + 2 * width_kv)
    to_out = slice(width_query + 2 * width_kv, None)
    weights_of.wait()
    grad_attended = product(state, weights_of.columns(to_out), NN).astype(low)

    grad_query, grad_key, grad_value = [], [], []
    for group in range(width_kv // HEAD_WIDTH):
        here = slice(group * HEAD_WIDTH, (group + 1) * HEAD_WIDTH)
        key = query_key[:, width_query:][:, here]
        query, grads = heads_of(query_key, group, per_group), heads_of(grad_attended, group, per_group)
        weights = softmax_weights(query, key, allowed)
        grad_probs = product(grads, value[:, here], NT)
        centered = grad_probs - jnp.sum(weights * grad_probs, 1, keepdims=True)
        grad_scores = (weights * centered).astype(low)
        grad_heads = product(grad_scores, key, NN) * scaling
        grad_query += [grad_heads[i * rows : (i + 1) * rows] for i in range(per_group)]
        grad_key.append(product(grad_scores, query, TN) * scaling)
        grad_value.append(product(weights.astype(low), grads, TN))

    grads = grad_query + grad_key
    grad_qk = jnp.concatenate(
        [
            rotation.backward(jnp.concatenate(grads[n : n + 2], 1)).astype(low)
            for n in range(0, len(grads), 2)
        ],
        1,
    )
    grad_v = jnp.concatenate(grad_value, 1).astype(low)

    own_features = qk_own.shape[1]
    block = max(256, CORES * own_features)
    count = block // (CORES * own_features)
    for start in range(0, normed.shape[1], block):
        features = slice(start, start + block)
        chip = slice(start // (CORES * own_features), start // (CORES * own_features) + count)
        left = normed[:, features]
        for total, own_ref, other_ref, at_columns in (
            (product(left, grad_qk, TN), qk_own, qk_other, slice(None)),
            (product(left, grad_v, TN), vo_own, vo_other, slice(0, width_kv)),
            (product(state[:, features], attended[...], TN), vo_own, vo_other, slice(width_kv, None)),
        ):
            total = total.astype(low).reshape(count, CORES, own_features, total.shape[-1])
            own_ref[chip, :, at_columns] = jnp.where(core == 0, total[:, 0], total[:, 1])
            other_ref[chip, :, at_columns] = jnp.where(core == 0, total[:, 1], total[:, 0])
    back = product(grad_qk, weights_of.columns(slice(0, width_query + width_kv)), NT)
    back = back + product(grad_v, weights_of.columns(to_value), NT)
    first, second = back[:rows_own], back[rows_own:]
    back_own[...] = jnp.where(x == 0, first, second)
    back_other[...] = jnp.where(x == 0, second, first).astype(low)


def attention_call(at, kernel, width_kv, arrays, weights, out_shapes):
    place = jnp.stack([at.x, at.core, at.z, at.y, jnp.int32(at.rows)]).astype(jnp.int32)
    vmem = pl.BlockSpec(memory_space=pltpu.VMEM)
    keys, sources = list(weights), list(weights.values())
    held = pltpu.VMEM((at.planes, at.rows, CORES) + sources[0].shape, sources[0].dtype)
    return pl.pallas_call(
        functools.partial(kernel, width_kv, keys),
        in_specs=[pl.BlockSpec(memory_space=pltpu.SMEM)]
        + [vmem] * len(arrays)
        + [pl.BlockSpec(memory_space=pl.ANY)] * len(sources),
        out_specs=[vmem] * len(out_shapes),
        out_shape=[jax.ShapeDtypeStruct(*shape) for shape in out_shapes],
        scratch_shapes=[held, pltpu.SemaphoreType.DMA((len(keys),))],
        compiler_params=pltpu.CompilerParams(vmem_limit_bytes=56 * 2**20),
        cost_estimate=cost_of(
            2 * len(arrays) * arrays[0].shape[0] * sources[0].size * len(sources) // 2,
            [*arrays, *sources],
            out_shapes,
        ),
    )(place, *arrays, *sources)


def on_device(
    tokens,
    seq_lens,
    norm_gains,
    w_query,
    key_weight,
    value_weight,
    w_out,
    w_gate,
    w_up,
    w_down,
    cotangent,
):
    at = Places(lax.axis_size("dp"))
    rows_own = tokens.shape[0]
    row_count = rows_own * lax.axis_size("tensor")
    width_query = w_query.shape[1]
    width_kv = key_weight.shape[1]
    quarter = w_gate.shape[1] // at.planes
    own_features = w_gate.shape[0]

    row_ids, segment, position, in_use = layout(seq_lens[0], row_count)
    in_use_own = lax.dynamic_slice_in_dim(in_use, at.x * rows_own, rows_own, 0)
    gain_rows = norm_gains.astype(jnp.float32)
    inputs = tokens.astype(jnp.float32)
    scale_one = lax.rsqrt(jnp.mean(inputs * inputs, 1, keepdims=True) + EPSILON)
    normed_own = (inputs * scale_one * gain_rows[0]).astype(jnp.bfloat16)
    normed_other = at.other_x(normed_own)
    grad_mixed = cotangent.astype(jnp.float32) * in_use_own[:, None]
    grad_low_own = grad_mixed.astype(jnp.bfloat16)
    grad_low_mine = lax.all_gather(grad_low_own, "dp", axis_index_groups=at.columns)
    packed = jnp.concatenate([w_query, key_weight, value_weight, w_out], 1)
    others = range(1, at.rows)
    projections = {(0, 0, 0): packed}
    projections[2, 0, 0] = at.across_z(packed, 2)
    projections[1, 0, 0] = at.across_z(packed, 1)
    for j in others:
        projections[0, j, 0] = at.along_y(packed, j)

    stage = [*list(projections.values())[1:], normed_other]
    projections[3, 0, 0] = at.across_z(after(projections[2, 0, 0], *stage), 1)
    for j in others:
        projections[1, j, 0] = at.along_y(after(projections[1, 0, 0], *stage), j)
    grads_low = {(0, 0): grad_low_own, (0, 1): at.other_x(after(grad_low_own, *stage))}
    shares = {}
    for mask in range(at.planes):
        start = (at.z ^ mask) * quarter
        shares[mask] = jnp.stack(
            [lax.dynamic_slice_in_dim(w, start, quarter, 1) for w in (w_gate, w_up, w_down)]
        )
    plane_two = [at.across_z(after(shares[2][:1], *stage), 2)]
    second = [plane_two[0], *(projections[1, j, 0] for j in others)]
    for j in others:
        projections[2, j, 0] = at.along_y(after(projections[2, 0, 0], *second), j)
    plane_two.append(at.across_z(after(shares[2][1:2], *second), 2))
    for mask in (0, 1):
        for j in range(at.rows):
            key = (mask, j, 0)
            if key in projections:
                projections[mask, j, 1] = at.other_core(after(projections[key], *stage))

    stage = [projections[3, 0, 0], grads_low[0, 1], plane_two[1]]
    stage += [projections[2, j, 0] for j in others]
    plane_two.append(at.across_z(after(shares[2][2:], *stage), 2))
    for j in others:
        projections[3, j, 0] = at.along_y(after(projections[3, 0, 0], *stage), j)
    for mask, j in ((1, 1), (2, 0), (2, 1), (3, 0)):
        for back in others if j else (0,):
            if (mask, back, 1) not in projections:
                block = after(projections[mask, back, 0], *stage)
                projections[mask, back, 1] = at.other_core(block)

    stage = [projections[3, j, 0] for j in others] + [plane_two[2]]
    plane_two = jnp.concatenate(plane_two, 0)
    for j in others:
        projections[3, j, 1] = at.other_core(projections[3, j, 0])
    tables = [jnp.concatenate([table, table], 1) for table in rope_tables(position, HEAD_WIDTH)]
    keys_of = [segment[:, None], segment[None, :], *tables]

    weights = {}

    def to_chips(mask, parts, *earlier):
        weights.setdefault((mask, 0, 0), []).extend(parts)
        for j in range(1, at.rows):
            sent = [at.along_y(after(part, *earlier), j) for part in parts]
            weights.setdefault((mask, j, 0), []).extend(sent)
            earlier = tuple(sent)
        return earlier

    plane_three = at.across_z(after(shares[3][:2], plane_two, *stage), 3)
    plane_one = at.across_z(after(shares[1][:2], plane_two, *stage), 1)
    last = to_chips(0, [shares[0]], *stage)

    low = jnp.bfloat16
    query_key, value, attended, branch_own, branch_other = attention_call(
        at,
        attention_kernel,
        width_kv,
        [normed_own, normed_other, *keys_of],
        projections,
        [
            ((row_count, width_query + width_kv), low),
            ((row_count, width_kv), low),
            ((row_count, width_query), low),
            ((rows_own, inputs.shape[1]), jnp.float32),
            ((rows_own, inputs.shape[1]), low),
        ],
    )
    branch_other = after(branch_other, plane_one, plane_three, *last)
    branch = branch_other
    state = inputs + branch_own + at.other_x(branch_other)
    scale_two = lax.rsqrt(jnp.mean(state * state, 1, keepdims=True) + EPSILON)
    normed_two = (state * scale_two * gain_rows[1]).astype(jnp.bfloat16)

    plane_three_last = at.across_z(after(shares[3][2:], branch), 3)
    plane_one_last = at.across_z(after(shares[1][2:], branch), 1)
    last = to_chips(2, [plane_two], *last, branch)

    def to_cores(*keys, earlier):
        for mask, back in keys:
            parts = weights[mask, back, 0]
            weights[mask, back, 1] = [at.other_core(after(part, *earlier)) for part in parts]

    every_row = range(at.rows)
    to_cores(*((0, j) for j in every_row), earlier=[branch])
    stage = [normed_two, plane_three_last, plane_one_last]
    normed = {(0, 0): normed_two, (0, 1): at.other_x(after(normed_two, *stage))}
    normed[2, 0] = at.across_z(after(normed_two, *stage), 2)
    normed[1, 0] = at.across_z(after(normed_two, *stage), 1)
    last = to_chips(1, [plane_one], *last, *stage)
    last = to_chips(3, [plane_three], *last)

    for mask in (1, 2, 3):
        grads_low[mask, 0] = lax.dynamic_index_in_dim(
            grad_low_mine, at.z ^ mask, 0, keepdims=False
        )
    grads_low[1, 1] = at.other_x(after(grads_low[1, 0], *stage))

    stage = [*normed.values(), *last, grads_low[1, 1]]
    normed[3, 0] = at.across_z(after(normed[2, 0], *stage), 1)
    normed[2, 1] = at.other_x(after(normed[2, 0], *stage))
    last = to_chips(1, [plane_one_last], *stage)
    last = to_chips(3, [plane_three_last], *last)
    to_cores(*((2, j) for j in every_row), earlier=stage)

    stage = [normed[3, 0], normed[2, 1], *last]
    normed[3, 1] = at.other_x(after(normed[3, 0], *stage))
    normed[1, 1] = at.across_z(after(normed[0, 1], *stage), 1)
    to_cores(*((1, j) for j in every_row), earlier=stage)
    to_cores(*((3, j) for j in every_row), earlier=stage)
    grads_far = at.other_x(
        after(jnp.stack([grads_low[mask, 0] for mask in (2, 3)]), normed[3, 1])
    )
    grads_low[2, 1], grads_low[3, 1] = grads_far[0], grads_far[1]

    masks = (3, 2, 1, 0)
    normed_rows = [normed[mask, x] for mask in masks for x in range(2)]
    grad_rows = [grads_low[mask, x] for mask in masks for x in range(2)]
    hidden, silu, slope, *outs = forward(at, weights, normed_rows)
    def block_of(value, i):
        return value[i * rows_own : (i + 1) * rows_own]

    def out_block(mine, arrived, i):
        return block_of(mine, i).astype(jnp.float32) + arrived

    def of_chip(own, arrived, j):
        y = (at.y + j) % at.rows
        mine = lax.dynamic_index_in_dim(own, y, 0, keepdims=False)
        theirs = lax.dynamic_index_in_dim(arrived, y, 0, keepdims=False)
        return mine.astype(jnp.float32) + theirs

    def for_chips(own, arrived):
        return [of_chip(own, arrived, j).astype(jnp.bfloat16) for j in range(1, at.rows)]

    def send_chips(away, earlier):
        return [at.along_y(after(a, *earlier), j + 1) for j, a in enumerate(away)]

    def of_plane(terms, mask):
        own, arrived, chips = terms
        size = (1, 1) + own.shape[2:]
        at_plane = (at.y, at.z ^ mask, 0, 0)
        total = lax.dynamic_slice(own, at_plane, size)[0, 0].astype(jnp.float32)
        total = total + lax.dynamic_slice(arrived, at_plane, size)[0, 0]
        for part in chips:
            total = total + lax.dynamic_index_in_dim(part, at.z ^ mask, 0, keepdims=False)
        return total

    def send_planes(terms, wanted, earlier):
        sent = {}
        for mask in wanted:
            piece = of_plane(terms, mask).astype(jnp.bfloat16)
            sent[mask] = at.across_z(after(piece, *earlier), mask)
        return sent

    def all_columns(terms, pieces, *earlier):
        result = jnp.zeros((own_features, at.planes * quarter), jnp.float32)
        own = {0: of_plane(terms, 0)}
        for mask, piece in after({**own, **pieces}, *earlier).items():
            result = lax.dynamic_update_slice(
                result, piece.astype(jnp.float32), (0, (at.z ^ mask) * quarter)
            )
        return result

    grad_gate_in, grad_up_in, *back = backward(at, weights, grad_rows, silu, slope)
    out_first = at.other_x(outs[1])

    def sum_of(i, arrived):
        return back[2 * i].astype(jnp.float32) + arrived

    stage = [out_first, back[0]]
    three = at.other_x(after(back[1], *stage))
    one = at.across_z(after(back[5], *stage), 1)
    gate_own, gate_other = weight_grad(
        at, normed_rows, after(grad_gate_in, *stage), own_features
    )
    first_blocks = [out_block(outs[0], block_of(out_first, i), i) for i in range(4)]
    first_two = at.across_z(after(first_blocks[0].astype(jnp.bfloat16), *stage), 1)

    stage = [three, one, gate_own, first_two]
    to_two = at.across_z(after(sum_of(0, three).astype(jnp.bfloat16), *stage), 1)
    two = at.other_x(after(back[3], *stage))
    gate_arrived = at.other_core(after(gate_other, *stage))
    up_own, up_other = weight_grad(at, normed_rows, after(grad_up_in, *stage), own_features)
    first_zero = (first_blocks[1] + first_two).astype(jnp.bfloat16)
    first_zero = at.across_z(after(first_zero, *stage), 2)

    stage = [to_two, two, gate_arrived, up_own, first_zero]
    for_zero = (sum_of(1, two) + to_two).astype(jnp.bfloat16)
    middle = for_zero.shape[1] // 2
    to_zero_first = at.across_z(after(for_zero[:, :middle], *stage), 2)
    other_zero = (back[7].astype(jnp.float32) + one).astype(jnp.bfloat16)
    zero = at.other_x(after(other_zero, *stage))
    gate_chips = send_chips(for_chips(gate_own, gate_arrived), stage)
    up_arrived = at.other_core(after(up_other, *stage))
    down_own, down_other = weight_grad(at, grad_rows, after(hidden, *stage), own_features)
    first_one = at.across_z(after(first_blocks[2].astype(jnp.bfloat16), *stage), 1)

    stage = [zero, to_zero_first, *gate_chips, up_arrived, down_own, first_one]
    to_zero_second = at.across_z(after(for_zero[:, middle:], *stage), 2)
    from_one = at.across_z(after(back[4], *stage), 1)
    down_arrived = at.other_core(after(down_other, *stage))
    gate_terms = (gate_own, gate_arrived, gate_chips)
    gate_pieces = send_planes(gate_terms, (2,), stage)
    up_chips = send_chips(for_chips(up_own, up_arrived), stage)

    to_zero = jnp.concatenate([to_zero_first, to_zero_second], 1)
    grad_normed_two = sum_of(3, zero) + from_one + to_zero
    hat_two = state * scale_two
    inner_two = grad_normed_two * gain_rows[1]
    grad_state = grad_mixed + scale_two * (
        inner_two - hat_two * jnp.mean(inner_two * hat_two, 1, keepdims=True)
    )
    gain_two = jnp.sum(grad_normed_two * hat_two, 0)
    grad_state_own = grad_state.astype(jnp.bfloat16)

    stage = [grad_state_own, *up_chips, down_arrived, gate_pieces[2]]
    grad_state_other = at.other_x(grad_state_own)
    up_terms = (up_own, up_arrived, up_chips)
    down_chips = send_chips(for_chips(down_own, down_arrived), stage)

    def both(mask):
        return jnp.stack([of_plane(terms, mask).astype(jnp.bfloat16) for terms in (gate_terms, up_terms)])

    up_pieces = send_planes(up_terms, (2,), stage)
    pair_pieces = {mask: at.across_z(after(both(mask), *stage), mask) for mask in (3, 1)}
    out_second = at.other_x(after(outs[3], grad_state_other))
    shape = (at.chips, own_features, width_query + width_kv)
    back_own, back_other, qk_own, qk_other, vo_own, vo_other = attention_call(
        at,
        attention_back_kernel,
        width_kv,
        [
            grad_state_own,
            grad_state_other,
            normed_own,
            normed_other,
            *keys_of,
            query_key,
            value,
            attended,
        ],
        projections,
        [
            ((rows_own, inputs.shape[1]), jnp.float32),
            ((rows_own, inputs.shape[1]), low),
            *[(shape, low)] * 4,
        ],
    )
    stage = [qk_other, out_second, *down_chips, *up_pieces.values(), *pair_pieces.values()]
    for mask, piece in pair_pieces.items():
        gate_pieces[mask], up_pieces[mask] = piece[0], piece[1]

    owns = {"qk": qk_own, "vo": vo_own}
    cores = {
        "qk": at.other_core(after(qk_other, *stage)),
        "vo": at.other_core(after(vo_other, *stage)),
    }
    normed_arrived = at.other_x(after(back_other, *stage))

    def by_place(value):
        return value.reshape(at.planes, at.rows, own_features, -1)

    def for_chip(name, j):
        y = (at.y + j) % at.rows
        parts = [
            lax.dynamic_index_in_dim(by_place(value), y, 1, keepdims=False)
            for value in (owns[name], cores[name])
        ]
        return (parts[0].astype(jnp.float32) + parts[1]).astype(jnp.bfloat16)

    chips = {"qk": [], "vo": []}

    def to_chips_of(name, earlier):
        for j in others:
            chips[name].append(at.along_y(after(for_chip(name, j), *earlier), j))

    def for_plane(name, mask):
        z = at.z ^ mask
        total = 0.0
        for value in (owns[name], cores[name]):
            part = lax.dynamic_slice(by_place(value), (z, at.y, 0, 0), (1, 1) + by_place(value).shape[2:])
            total = total + part[0, 0].astype(jnp.float32)
        for part in chips[name]:
            total = total + lax.dynamic_index_in_dim(part, z, 0, keepdims=False)
        return total

    pairs, quarters = {}, {}

    def to_pair(name, earlier):
        both_planes = jnp.stack([for_plane(name, 1), for_plane(name, 3)]).astype(jnp.bfloat16)
        pairs[name] = at.across_z(after(both_planes, *earlier), 1)

    def to_quarter(name, earlier):
        far = (for_plane(name, 2) + pairs[name][1]).astype(jnp.bfloat16)
        quarters[name] = at.across_z(after(far, *earlier), 2)

    def total_of(name):
        return for_plane(name, 0) + pairs[name][0] + quarters[name]

    down_terms = (down_own, down_arrived, down_chips)
    down_pieces = send_planes(down_terms, (2,), stage)
    second_two = out_block(outs[2], block_of(out_second, 0), 0).astype(jnp.bfloat16)
    second_two = at.across_z(after(second_two, *stage), 1)

    to_chips_of("qk", stage)

    stage = [*chips["qk"], *down_pieces.values(), second_two, normed_arrived]
    to_chips_of("vo", stage)
    to_pair("qk", stage)
    down_pieces.update(send_planes(down_terms, (3,), stage))
    second_zero = out_block(outs[2], block_of(out_second, 1), 1) + second_two
    second_zero = at.across_z(after(second_zero.astype(jnp.bfloat16), *stage), 2)
    grad_normed_one = back_own + normed_arrived
    hat_one = inputs * scale_one
    inner_one = grad_normed_one * gain_rows[0]
    grad_tokens = (
        grad_state
        + scale_one * (inner_one - hat_one * jnp.mean(inner_one * hat_one, 1, keepdims=True))
    ).astype(jnp.bfloat16)
    gain_one = jnp.sum(grad_normed_one * hat_one, 0)
    grad_gains = jnp.stack([gain_one, gain_two])
    grad_gains = grad_gains + at.other_x(grad_gains)
    bits = [1 << i for i in range(at.dp.bit_length() - 1)]
    chip_bits = [bit for bit in bits if CORES <= bit < CORES * at.rows]
    for bit in bits:
        if bit not in chip_bits:
            grad_gains = grad_gains + at.move(grad_gains, lambda d: d ^ bit)

    stage = [*chips["vo"], pairs["qk"], second_zero, grad_gains, *down_pieces.values()]
    down_pieces.update(send_planes(down_terms, (1,), stage))
    to_pair("vo", stage)
    to_quarter("qk", stage)
    second_one = out_block(outs[2], block_of(out_second, 2), 2).astype(jnp.bfloat16)
    second_one = at.across_z(after(second_one, *stage), 1)
    for bit in chip_bits:
        grad_gains = grad_gains + at.move(after(grad_gains, *stage), lambda d: d ^ bit)

    stage = [pairs["vo"], quarters["qk"], second_one]
    to_quarter("vo", stage)
    sum_qk, sum_vo = total_of("qk"), total_of("vo")
    grad_gate = all_columns(gate_terms, gate_pieces, *stage)
    grad_up = all_columns(up_terms, up_pieces, *stage)
    grad_down = all_columns(down_terms, down_pieces, *stage)
    first_sum = first_blocks[3] + first_zero + first_one
    second_sum = out_block(outs[2], block_of(out_second, 3), 3) + second_zero + second_one
    ffn_out = jnp.concatenate([first_sum, second_sum], 1)
    mixed = ((state + ffn_out) * in_use_own[:, None]).astype(jnp.bfloat16)
    return (
        mixed,
        grad_tokens,
        grad_gains,
        sum_qk[:, :width_query],
        sum_qk[:, width_query:],
        sum_vo[:, :width_kv],
        sum_vo[:, width_kv:],
        grad_gate,
        grad_up,
        grad_down,
    )


def solution(mesh):
    in_specs = (
        P(("dp", "tensor"), None),
        P("dp", None),
        P(),
        P("dp", "tensor"),
        P("dp", "tensor"),
        P("dp", "tensor"),
        P("dp", "tensor"),
        P("dp", "tensor"),
        P("dp", "tensor"),
        P("dp", "tensor"),
        P(("dp", "tensor"), None),
    )
    out_specs = (
        P(("dp", "tensor"), None),
        P(("dp", "tensor"), None),
        P(),
        P("dp", "tensor"),
        P("dp", "tensor"),
        P("dp", "tensor"),
        P("dp", "tensor"),
        P("dp", "tensor"),
        P("dp", "tensor"),
        P("dp", "tensor"),
    )
    return jax.shard_map(
        on_device, mesh=mesh, in_specs=in_specs, out_specs=out_specs, check_vma=False
    )
```

time: 615 us -> 593 us (0.964)
  Pallas kernels: 72.4 us -> 108 us
  other arithmetic: 63 us -> 38.3 us
  matrix products: 21.7 us -> 0 us
  local copies, waits for them, and re-layouts: 46.4 us -> 30 us
  waiting for transfers between devices: 270 us -> 281 us
  starting transfers between devices: 120 us -> 111 us
    pallas_call x3 -> x5, Pallas kernels: 28.5 us -> 63.8 us  [the longest x2 37.2 us: attention_call(): pl.pallas_call(functools.partial(kernel, width_kv, keys), in_specs=[pl.Bl...]
    dot_general x33 -> x0, matrix products: 21.7 us -> none  [the longest x3 5.35 us: matrix_product(): return jnp.dot(left_side, right_side, preferred_element_type=jnp.float32)]
    ppermute x14 -> x16, waiting for transfers between devices: 26.5 us -> 41.1 us  [other_x(): return lax.ppermute(value, 'tensor', [(0, 1), (1, 0)])]
    dynamic_update_slice x16 -> x0, local copies, waits for them, and re-layouts: 12.1 us -> none  [ring_gather(): lax.dynamic_update_slice(buffers[way], block[None], (chip, 0, 0))]
    ppermute x77 -> x80, starting transfers between devices: 103 us -> 94.1 us  [move(): return lax.ppermute(value, 'dp', [(d, target(d)) for d in range(self.dp)])]
    convert_element_type x31 -> x15, other arithmetic: 23.4 us -> 16.3 us  [the longest x3 7.18 us: for_chips(): of_chip(own, arrived, j).astype(jnp.bfloat16)]
    squeeze x10 -> x3, local copies, waits for them, and re-layouts: 8.19 us -> 1.14 us  [the longest x1 1.07 us: on_device(): grads_low[2, 1], grads_low[3, 1] = (grads_far[0], grads_far[1])]
    add x6 -> x7, other arithmetic: 0.17 us -> 6.69 us  [the longest x2 3.2 us: of_plane(): total + lax.dynamic_index_in_dim(part, at.z ^ mask, 0, keepdims=False)]
  transfers between devices with their start and end apart: 94 -> 97, of which waited for: 53 -> 40; matrix products, arithmetic and copies ran while one was open for 19% -> 8% of each run, Pallas kernels for 8% -> 18%
where the time goes in v3:
time: 593 us; the launch traced here: 584 us
  waiting for transfers between devices  281 us (47%)
  starting transfers between devices  111 us (19%)
  Pallas kernels  108 us (18%)
  other arithmetic  38.3 us (6%)
  local copies, waits for them, and re-layouts  30 us (5%)
  between operations  15.5 us (3%)
    ppermute x80, waiting for transfers between devices, move(): return lax.ppermute(value, 'dp', [(d, target(d)) for d in range(self.dp)])  240 us
    ppermute x80, starting transfers between devices, move(): return lax.ppermute(value, 'dp', [(d, target(d)) for d in range(self.dp)])  94.1 us
    pallas_call x2, Pallas kernels, held_call(): pl.pallas_call(body, in_specs=[pl.BlockSpec(memory_space=pltpu.SMEM)] + [...  44 us
    ppermute x16, waiting for transfers between devices, other_x(): return lax.ppermute(value, 'tensor', [(0, 1), (1, 0)])  41.1 us
    pallas_call x2, Pallas kernels, attention_call(): pl.pallas_call(functools.partial(kernel, width_kv, keys), in_specs=[pl.Bl...  37.2 us
    pallas_call x3, Pallas kernels, weight_grad(): pl.pallas_call(weight_grad_kernel, grid_spec=pltpu.PrefetchScalarGridSpec...  26.6 us
    ppermute x16, starting transfers between devices, other_x(): return lax.ppermute(value, 'tensor', [(0, 1), (1, 0)])  16.6 us
    unnamed x175, local copies, waits for them, and re-layouts  16.2 us
  transfers between devices with their start and end apart: 97, of which 40 were waited for; matrix products, arithmetic and copies ran while one was open for 8% of the time, Pallas kernels for 18%

profile of v3, /device:TPU:0, one launch (start us, length us, event | category | flops | bytes accessed | tf_op | source)
XLA Modules:
  0.0 583.6 jit_solution(9297408388213795860)
XLA Ops:
  26.6 10.4 %collective-permute-done.refs_1_.refs_3_ = bf16[128,2048]{1,0:T(8,128)(2,1)} collective-permute-done((bf16[128,2048]{1,0:T(8,128)(2,1)}, bf16[128,2048]{1,0:T(8,128)(2,1)}, u32[]{:S(2)}, u32[]{:S(2)}) %collective-permute-start) | collective-permute-done | bytes 524320 | tf_op jit(solution)/shard_map/ppermute | solution.py:85
  37.0 9.9 %collective-permute-done.1.refs_7_.refs_12_ = bf16[128,2560]{1,0:T(8,128)(2,1)} collective-permute-done((bf16[128,2560]{1,0:T(8,128)(2,1)}, bf16[128,2560]{1,0:T(8,128)(2,1)}, u32[]{:S(2)}, u32[]{:S(2)}) %collective-permute-start.1) | collective-permute-done | bytes 655392 | tf_op jit(solution)/shard_map/ppermute | solution.py:68
  54.2 13.5 %collective-permute-done.6 = bf16[1,128,1024]{2,1,0:T(8,128)(2,1)S(1)} collective-permute-done((bf16[1,128,1024]{2,1,0:T(8,128)(2,1)}, bf16[1,128,1024]{2,1,0:T(8,128)(2,1)S(1)}, u32[]{:S(2)}, u32[]{:S(2)}) %collective-permute-start.6) | collective-permute-done | bytes 262176 | tf_op jit(solution)/shard_map/ppermute | solution.py:68
  76.9 19.5 %collective-permute-done.13 = bf16[1,128,1024]{2,1,0:T(8,128)(2,1)S(1)} collective-permute-done((bf16[1,128,1024]{2,1,0:T(8,128)(2,1)S(1)}, bf16[1,128,1024]{2,1,0:T(8,128)(2,1)S(1)}, u32[]{:S(2)}, u32[]{:S(2)}) %collective-permute-start.13) | collective-permute-done | bytes 262176 | tf_op jit(solution)/shard_map/ppermute | solution.py:68
  98.8 24.5 %collective-permute-done.19 = bf16[1,128,1024]{2,1,0:T(8,128)(2,1)S(1)} collective-permute-done((bf16[1,128,1024]{2,1,0:T(8,128)(2,1)S(1)}, bf16[1,128,1024]{2,1,0:T(8,128)(2,1)S(1)}, u32[]{:S(2)}, u32[]{:S(2)}) %collective-permute-start.19) | collective-permute-done | bytes 262176 | tf_op jit(solution)/shard_map/ppermute | solution.py:68
  126.1 5.4 collective-permute-start.20
  137.4 16.1 %shard_map.186 = (bf16[256,1280]{1,0:T(8,128)(2,1)}, bf16[256,256]{1,0:T(8,128)(2,1)}, bf16[256,1024]{1,0:T(8,128)(2,1)}, f32[128,2048]{1,0:T(8,128)}, bf16[128,2048]{1,0:T(8,128)(2,1)}) custom-call(s32[5]{0:T(128)} %stack.118.place, bf16[128,2048]{1,0:T(8,128)(2,1)} %fusion.6.refs_0_.refs_2_, bf16[128,2048]{1,0:T(8,128)(2,1)} %collective-permute-done.refs_1_.refs_3_, ...), custom_call_target="tpu_custom_call" | custom-call | flops 4026531840 | bytes 14682112 | tf_op jit(solution)/shard_map/pallas_call | solution.py:456
  162.7 8.0 %collective-permute-done.23 = bf16[128,2048]{1,0:T(8,128)(2,1)S(1)} collective-permute-done((bf16[128,2048]{1,0:T(8,128)(2,1)}, bf16[128,2048]{1,0:T(8,128)(2,1)S(1)}, u32[]{:S(2)}, u32[]{:S(2)}) %collective-permute-start.23) | collective-permute-done | bytes 524320 | tf_op jit(solution)/shard_map/ppermute | solution.py:85
  172.5 6.2 %collective-permute-done.29.refs_11_.refs_13_ = bf16[3,128,1024]{2,1,0:T(8,128)(2,1)S(1)} collective-permute-done((bf16[3,128,1024]{2,1,0:T(8,128)(2,1)S(1)}, bf16[3,128,1024]{2,1,0:T(8,128)(2,1)S(1)}, u32[]{:S(2)}, u32[]{:S(2)}) %collective-permute-start.29) | collective-permute-done | bytes 786464 | tf_op jit(solution)/shard_map/ppermute | solution.py:68
  193.0 13.3 %collective-permute-done.26.refs_2_ = bf16[128,2048]{1,0:T(8,128)(2,1)S(1)} collective-permute-done((bf16[128,2048]{1,0:T(8,128)(2,1)S(1)}, bf16[128,2048]{1,0:T(8,128)(2,1)S(1)}, u32[]{:S(2)}, u32[]{:S(2)}) %collective-permute-start.26) | collective-permute-done | bytes 524320 | tf_op jit(solution)/shard_map/ppermute | solution.py:68
  214.8 5.4 collective-permute-done.33.refs_0_
  222.0 7.0 %collective-permute-done.36.refs_21_.refs_23_ = bf16[1,128,1024]{2,1,0:T(8,128)(2,1)S(1)} collective-permute-done((bf16[1,128,1024]{2,1,0:T(8,128)(2,1)S(1)}, bf16[1,128,1024]{2,1,0:T(8,128)(2,1)S(1)}, u32[]{:S(2)}, u32[]{:S(2)}) %collective-permute-start.36) | collective-permute-done | bytes 262176 | tf_op jit(solution)/shard_map/ppermute | solution.py:68
  233.0 9.3 %collective-permute-done.37.refs_1_ = bf16[128,2048]{1,0:T(8,128)(2,1)S(1)} collective-permute-done((bf16[128,2048]{1,0:T(8,128)(2,1)S(1)}, bf16[128,2048]{1,0:T(8,128)(2,1)S(1)}, u32[]{:S(2)}, u32[]{:S(2)}) %collective-permute-start.37) | collective-permute-done | bytes 524320 | tf_op jit(solution)/shard_map/ppermute | solution.py:85
  249.6 21.7 %shard_map.187 = (bf16[1024,1024]{1,0:T(8,128)(2,1)}, bf16[1024,1024]{1,0:T(8,128)(2,1)}, bf16[1024,1024]{1,0:T(8,128)(2,1)}, bf16[512,1024]{1,0:T(8,128)(2,1)},...) custom-call(s32[4]{0:T(128)} %pad_add_fusion.1.place, ...), custom_call_target="tpu_custom_call" | custom-call | flops 12884901888 | bytes 27262976 | tf_op jit(solution)/shard_map/pallas_call | solution.py:149
  273.1 22.3 %shard_map.188 = (bf16[1024,1024]{1,0:T(8,128)(2,1)}, bf16[1024,1024]{1,0:T(8,128)(2,1)}, bf16[128,2048]{1,0:T(8,128)(2,1)}, bf16[128,2048]{1,0:T(8,128)(2,1)}, ...) custom-call(s32[4]{0:T(128)} %pad_add_fusion.1.place, ...), custom_call_target="tpu_custom_call" | custom-call | flops 12884901888 | bytes 29360128 | tf_op jit(solution)/shard_map/pallas_call | solution.py:149
  299.2 8.7 %shard_map.189 = (bf16[2,4,128,1024]{3,2,1,0:T(8,128)(2,1)}, bf16[2,4,128,1024]{3,2,1,0:T(8,128)(2,1)}) custom-call(s32[1]{0:T(128)} %bitcast.1.place, bf16[128,2048]{1,0:T(8,128)(2,1)} %copy-done.64, bf16[128,2048]{1,0:T(8,128)(2,1)} %copy-done.66, bf16[128,2048]{1,0:T(8,128)(2,1)} %copy-done.61, bf16[128,2048]{1,0:T(8,128)(2,1)} %copy-done.65, ...), custom_call_target="tpu_custom_call" | custom-call | flops 4294967296 | bytes 10485760 | tf_op jit(solution)/shard_map/pallas_call | solution.py:254
  307.9 7.2 %collective-permute-done.53 = bf16[128,1024]{1,0:T(8,128)(2,1)S(1)} collective-permute-done((bf16[128,1024]{1,0:T(8,128)(2,1)S(1)}, bf16[128,1024]{1,0:T(8,128)(2,1)S(1)}, u32[]{:S(2)}, u32[]{:S(2)}) %collective-permute-start.53) | collective-permute-done | bytes 262176 | tf_op jit(solution)/shard_map/ppermute | solution.py:68
  318.5 8.7 %shard_map.190 = (bf16[2,4,128,1024]{3,2,1,0:T(8,128)(2,1)}, bf16[2,4,128,1024]{3,2,1,0:T(8,128)(2,1)}) custom-call(s32[1]{0:T(128)} %bitcast.1.place, bf16[128,2048]{1,0:T(8,128)(2,1)} %copy-done.64, bf16[128,2048]{1,0:T(8,128)(2,1)} %copy-done.66, bf16[128,2048]{1,0:T(8,128)(2,1)} %copy-done.61, bf16[128,2048]{1,0:T(8,128)(2,1)} %copy-done.65, ...), custom_call_target="tpu_custom_call" | custom-call | flops 4294967296 | bytes 10485760 | tf_op jit(solution)/shard_map/pallas_call | solution.py:254
  327.3 5.9 %collective-permute-done.56 = bf16[128,1024]{1,0:T(8,128)(2,1)S(1)} collective-permute-done((bf16[128,1024]{1,0:T(8,128)(2,1)S(1)}, bf16[128,1024]{1,0:T(8,128)(2,1)S(1)}, u32[]{:S(2)}, u32[]{:S(2)}) %collective-permute-start.56) | collective-permute-done | bytes 262176 | tf_op jit(solution)/shard_map/ppermute | solution.py:68
  344.5 9.1 %shard_map.191 = (bf16[2,4,128,1024]{3,2,1,0:T(8,128)(2,1)}, bf16[2,4,128,1024]{3,2,1,0:T(8,128)(2,1)}) custom-call(s32[1]{0:T(128)} %bitcast.1.place, bf16[128,2048]{1,0:T(8,128)(2,1)} %bitcast.202, bf16[128,2048]{1,0:T(8,128)(2,1)} %get-tuple-element.300.refs_1_, bf16[128,2048]{1,0:T(8,128)(2,1)} %bitcast.200, ...), custom_call_target="tpu_custom_call" | custom-call | flops 4294967296 | bytes 10485760 | tf_op jit(solution)/shard_map/pallas_call | solution.py:254
  356.9 8.5 %collective-permute-done.63 = bf16[4,128,1024]{2,1,0:T(8,128)(2,1)S(1)} collective-permute-done((bf16[4,128,1024]{2,1,0:T(8,128)(2,1)S(1)}, bf16[4,128,1024]{2,1,0:T(8,128)(2,1)S(1)}, u32[]{:S(2)}, u32[]{:S(2)}) %collective-permute-start.63) | collective-permute-done | bytes 1048608 | tf_op jit(solution)/shard_map/ppermute | solution.py:68
  371.9 12.2 %collective-permute-done.66 = bf16[128,1024]{1,0:T(8,128)(2,1)S(1)} collective-permute-done((bf16[128,1024]{1,0:T(8,128)(2,1)}, bf16[128,1024]{1,0:T(8,128)(2,1)S(1)}, u32[]{:S(2)}, u32[]{:S(2)}) %collective-permute-start.66) | collective-permute-done | bytes 262176 | tf_op jit(solution)/shard_map/ppermute | solution.py:68
  393.4 7.3 %collective-permute-done.67.refs_1_ = bf16[128,2048]{1,0:T(8,128)(2,1)} collective-permute-done((bf16[128,2048]{1,0:T(8,128)(2,1)}, bf16[128,2048]{1,0:T(8,128)(2,1)}, u32[]{:S(2)}, u32[]{:S(2)}) %collective-permute-start.67) | collective-permute-done | bytes 524320 | tf_op jit(solution)/shard_map/ppermute | solution.py:85
  411.2 21.1 %shard_map.192 = (f32[128,2048]{1,0:T(8,128)}, bf16[128,2048]{1,0:T(8,128)(2,1)}, bf16[8,128,1280]{2,1,0:T(8,128)(2,1)}, bf16[8,128,1280]{2,1,0:T(8,128)(2,1)}, ...) custom-call(s32[5]{0:T(128)} %stack.118.place, bf16[128,2048]{1,0:T(8,128)(2,1)} %get-tuple-element.272.refs_0_, ...), custom_call_target="tpu_custom_call" | custom-call | flops 7381975040 | bytes 26216448 | tf_op jit(solution)/shard_map/pallas_call | solution.py:456
  432.4 6.1 %collective-permute-done.75 = bf16[2,128,1024]{2,1,0:T(8,128)(2,1)S(1)} collective-permute-done((bf16[2,128,1024]{2,1,0:T(8,128)(2,1)S(1)}, bf16[2,128,1024]{2,1,0:T(8,128)(2,1)S(1)}, u32[]{:S(2)}, u32[]{:S(2)}) %collective-permute-start.75) | collective-permute-done | bytes 524320 | tf_op jit(solution)/shard_map/ppermute | solution.py:68
  443.1 5.0 collective-permute-start.76
  466.5 21.2 %collective-permute-done.78 = bf16[4,128,1280]{2,1,0:T(8,128)(2,1)S(1)} collective-permute-done((bf16[4,128,1280]{2,1,0:T(8,128)(2,1)S(1)}, bf16[4,128,1280]{2,1,0:T(8,128)(2,1)S(1)}, u32[]{:S(2)}, u32[]{:S(2)}) %collective-permute-start.78) | collective-permute-done | bytes 1310752 | tf_op jit(solution)/shard_map/ppermute | solution.py:68
  496.2 10.4 %collective-permute-done.88 = f32[2,2048]{1,0:T(2,128)S(1)} collective-permute-done((f32[2,2048]{1,0:T(2,128)S(1)}, f32[2,2048]{1,0:T(2,128)S(1)}, u32[]{:S(2)}, u32[]{:S(2)}) %collective-permute-start.88) | collective-permute-done | bytes 16416 | tf_op jit(solution)/shard_map/ppermute | solution.py:68
  512.4 13.8 %collective-permute-done.81 = bf16[128,1024]{1,0:T(8,128)(2,1)S(1)} collective-permute-done((bf16[128,1024]{1,0:T(8,128)(2,1)S(1)}, bf16[128,1024]{1,0:T(8,128)(2,1)S(1)}, u32[]{:S(2)}, u32[]{:S(2)}) %collective-permute-start.81) | collective-permute-done | bytes 262176 | tf_op jit(solution)/shard_map/ppermute | solution.py:68
  535.1 8.0 %collective-permute-done.90 = bf16[128,1024]{1,0:T(8,128)(2,1)S(1)} collective-permute-done((bf16[128,1024]{1,0:T(8,128)(2,1)S(1)}, bf16[128,1024]{1,0:T(8,128)(2,1)S(1)}, u32[]{:S(2)}, u32[]{:S(2)}) %collective-permute-start.90) | collective-permute-done | bytes 262176 | tf_op jit(solution)/shard_map/ppermute | solution.py:68
  548.6 13.9 %collective-permute-done.93 = bf16[2,128,1280]{2,1,0:T(8,128)(2,1)S(1)} collective-permute-done((bf16[2,128,1280]{2,1,0:T(8,128)(2,1)S(1)}, bf16[2,128,1280]{2,1,0:T(8,128)(2,1)S(1)}, u32[]{:S(2)}, u32[]{:S(2)}) %collective-permute-start.93) | collective-permute-done | bytes 655392 | tf_op jit(solution)/shard_map/ppermute | solution.py:68
  569.1 5.7 collective-permute-done.94
  (442 shorter events, 202.6 us)
Async XLA Ops:
  7.2 173.7 %all-gather.3.cloned.1.call-start = ((), (), s32[]{:S(2)}) async-start(), calls=%async_computation | async-start | bytes 2621440 | tf_op jit(solution)/shard_map/all_gather | solution.py:503
  13.7 33.2 %collective-permute-start.1 = (bf16[128,2560]{1,0:T(8,128)(2,1)}, bf16[128,2560]{1,0:T(8,128)(2,1)}, u32[]{:S(2)}, u32[]{:S(2)}) collective-permute-start(bf16[128,2560]{1,0:T(8,128)(2,1)} %constant_dynamic-update-slice_fusion.3.refs_6_.refs_11_), channel_id=1, source_target_pairs={{0,16},{2,18},{4,20},{6,22},{8,24},{10,26},{12,28},{14,30},{16,0},... | collective-permute-start | bytes 1966088 | tf_op jit(solution)/shard_map/ppermute | solution.py:68
  17.8 29.4 %collective-permute-start.2 = (bf16[128,2560]{1,0:T(8,128)(2,1)}, bf16[128,2560]{1,0:T(8,128)(2,1)}, u32[]{:S(2)}, u32[]{:S(2)}) collective-permute-start(bf16[128,2560]{1,0:T(8,128)(2,1)} %constant_dynamic-update-slice_fusion.3.refs_6_.refs_11_), channel_id=1, source_target_pairs={{0,8},{2,10},{4,12},{6,14},{8,0},{10,2},{12,4},{14,6},{16,24},{18,... | collective-permute-start | bytes 1966088 | tf_op jit(solution)/shard_map/ppermute | solution.py:68
  19.4 27.8 %collective-permute-start.3 = (bf16[128,2560]{1,0:T(8,128)(2,1)}, bf16[128,2560]{1,0:T(8,128)(2,1)}, u32[]{:S(2)}, u32[]{:S(2)}) collective-permute-start(bf16[128,2560]{1,0:T(8,128)(2,1)} %constant_dynamic-update-slice_fusion.3.refs_6_.refs_11_), channel_id=1, source_target_pairs={{0,4},{2,6},{4,0},{6,2},{8,12},{10,14},{12,8},{14,10},{16,20},{18,... | collective-permute-start | bytes 1966088 | tf_op jit(solution)/shard_map/ppermute | solution.py:68
  47.2 24.8 %collective-permute-start.4 = (bf16[128,2560]{1,0:T(8,128)(2,1)}, bf16[128,2560]{1,0:T(8,128)(2,1)}, u32[]{:S(2)}, u32[]{:S(2)}) collective-permute-start(bf16[128,2560]{1,0:T(8,128)(2,1)} %collective-permute-done.1.refs_7_.refs_12_), channel_id=1, source_target_pairs={{0,8},{2,10},{4,12},{6,14},{8,0},{10,2},{12,4},{14,6},{16,24},{18,... | collective-permute-start | bytes 1966088 | tf_op jit(solution)/shard_map/ppermute | solution.py:68
  67.7 28.7 %collective-permute-start.7 = (bf16[128,2560]{1,0:T(8,128)(2,1)}, bf16[128,2560]{1,0:T(8,128)(2,1)}, u32[]{:S(2)}, u32[]{:S(2)}) collective-permute-start(bf16[128,2560]{1,0:T(8,128)(2,1)} %collective-permute-done.1.refs_7_.refs_12_), channel_id=1, source_target_pairs={{0,4},{2,6},{4,0},{6,2},{8,12},{10,14},{12,8},{14,10},{16,20},{18,... | collective-permute-start | bytes 1966088 | tf_op jit(solution)/shard_map/ppermute | solution.py:68
  71.4 27.4 %collective-permute-start.10 = (bf16[128,2560]{1,0:T(8,128)(2,1)}, bf16[128,2560]{1,0:T(8,128)(2,1)S(1)}, u32[]{:S(2)}, u32[]{:S(2)}) collective-permute-start(bf16[128,2560]{1,0:T(8,128)(2,1)} %collective-permute-done.2.refs_8_.refs_13_), channel_id=1, source_target_pairs={{0,2},{2,0},{4,6},{6,4},{8,10},{10,8},{12,14},{14,12},{16,18},{18,... | collective-permute-start | bytes 1966088 | tf_op jit(solution)/shard_map/ppermute | solution.py:68
  71.4 26.7 %collective-permute-start.8 = (bf16[128,2560]{1,0:T(8,128)(2,1)}, bf16[128,2560]{1,0:T(8,128)(2,1)S(1)}, u32[]{:S(2)}, u32[]{:S(2)}) collective-permute-start(bf16[128,2560]{1,0:T(8,128)(2,1)} %constant_dynamic-update-slice_fusion.3.refs_6_.refs_11_), channel_id=1, source_target_pairs={{0,2},{2,0},{4,6},{6,4},{8,10},{10,8},{12,14},{14,12},{16,18},{18,... | collective-permute-start | bytes 1966088 | tf_op jit(solution)/shard_map/ppermute | solution.py:68
  71.9 26.8 %collective-permute-start.9 = (bf16[128,2560]{1,0:T(8,128)(2,1)}, bf16[128,2560]{1,0:T(8,128)(2,1)S(1)}, u32[]{:S(2)}, u32[]{:S(2)}) collective-permute-start(bf16[128,2560]{1,0:T(8,128)(2,1)} %collective-permute-done.3.refs_9_.refs_14_), channel_id=1, source_target_pairs={{0,2},{2,0},{4,6},{6,4},{8,10},{10,8},{12,14},{14,12},{16,18},{18,... | collective-permute-start | bytes 1966088 | tf_op jit(solution)/shard_map/ppermute | solution.py:68
  96.4 27.2 %collective-permute-start.14 = (bf16[128,2560]{1,0:T(8,128)(2,1)}, bf16[128,2560]{1,0:T(8,128)(2,1)}, u32[]{:S(2)}, u32[]{:S(2)}) collective-permute-start(bf16[128,2560]{1,0:T(8,128)(2,1)} %collective-permute-done.4.refs_10_.refs_15_), channel_id=1, source_target_pairs={{0,4},{2,6},{4,0},{6,2},{8,12},{10,14},{12,8},{14,10},{16,20},{18,... | collective-permute-start | bytes 1966088 | tf_op jit(solution)/shard_map/ppermute | solution.py:68
  97.9 26.0 %collective-permute-start.11 = (bf16[128,2560]{1,0:T(8,128)(2,1)}, bf16[128,2560]{1,0:T(8,128)(2,1)S(1)}, u32[]{:S(2)}, u32[]{:S(2)}) collective-permute-start(bf16[128,2560]{1,0:T(8,128)(2,1)} %collective-permute-done.5.refs_11_.refs_16_), channel_id=1, source_target_pairs={{0,2},{2,0},{4,6},{6,4},{8,10},{10,8},{12,14},{14,12},{16,18},{18,... | collective-permute-start | bytes 1966088 | tf_op jit(solution)/shard_map/ppermute | solution.py:68
  98.1 28.0 %collective-permute-start.15 = (bf16[128,2560]{1,0:T(8,128)(2,1)}, bf16[128,2560]{1,0:T(8,128)(2,1)S(1)}, u32[]{:S(2)}, u32[]{:S(2)}) collective-permute-start(bf16[128,2560]{1,0:T(8,128)(2,1)} %collective-permute-done.1.refs_7_.refs_12_), channel_id=1, source_target_pairs={{0,2},{2,0},{4,6},{6,4},{8,10},{10,8},{12,14},{14,12},{16,18},{18,... | collective-permute-start | bytes 1966088 | tf_op jit(solution)/shard_map/ppermute | solution.py:68
  98.7 32.8 %collective-permute-start.16 = (bf16[128,2560]{1,0:T(8,128)(2,1)}, bf16[128,2560]{1,0:T(8,128)(2,1)S(1)}, u32[]{:S(2)}, u32[]{:S(2)}) collective-permute-start(bf16[128,2560]{1,0:T(8,128)(2,1)} %collective-permute-done.7.refs_12_.refs_17_), channel_id=1, source_target_pairs={{0,2},{2,0},{4,6},{6,4},{8,10},{10,8},{12,14},{14,12},{16,18},{18,... | collective-permute-start | bytes 1966088 | tf_op jit(solution)/shard_map/ppermute | solution.py:68
  98.8 24.6 %collective-permute-start.19 = (bf16[1,128,1024]{2,1,0:T(8,128)(2,1)S(1)}, bf16[1,128,1024]{2,1,0:T(8,128)(2,1)S(1)}, u32[]{:S(2)}, u32[]{:S(2)}) collective-permute-start(bf16[1,128,1024]{2,1,0:T(8,128)(2,1)S(1)} %get-tuple-element.153), channel_id=1, source_target_pairs={{0,16},{2,18},{4,20},{6,22},{8,24},{10,26},{12,28},{14,30},{16,0},... | collective-permute-start | bytes 786440 | tf_op jit(solution)/shard_map/ppermute | solution.py:68
  123.9 33.6 %collective-permute-start.22 = (bf16[3,128,1024]{2,1,0:T(8,128)(2,1)}, bf16[3,128,1024]{2,1,0:T(8,128)(2,1)}, u32[]{:S(2)}, u32[]{:S(2)}) collective-permute-start(bf16[3,128,1024]{2,1,0:T(8,128)(2,1)} %pad_maximum_fusion.1.refs_8_.refs_10_), channel_id=1, source_target_pairs={{0,4},{2,6},{4,0},{6,2},{8,12},{10,14},{12,8},{14,10},{16,20},{18,... | collective-permute-start | bytes 2359304 | tf_op jit(solution)/shard_map/ppermute | solution.py:68
  126.1 27.4 %collective-permute-start.20 = (bf16[2,128,1024]{2,1,0:T(8,128)(2,1)S(1)}, bf16[2,128,1024]{2,1,0:T(8,128)(2,1)}, u32[]{:S(2)}, u32[]{:S(2)}) collective-permute-start(bf16[2,128,1024]{2,1,0:T(8,128)(2,1)S(1)} %get-tuple-element.154), channel_id=1, source_target_pairs={{0,8},{2,10},{4,12},{6,14},{8,0},{10,2},{12,4},{14,6},{16,24},{18,... | collective-permute-start | bytes 1572872 | tf_op jit(solution)/shard_map/ppermute | solution.py:68
  131.5 26.1 %collective-permute-start.21 = (bf16[2,128,1024]{2,1,0:T(8,128)(2,1)S(1)}, bf16[2,128,1024]{2,1,0:T(8,128)(2,1)}, u32[]{:S(2)}, u32[]{:S(2)}) collective-permute-start(bf16[2,128,1024]{2,1,0:T(8,128)(2,1)S(1)} %get-tuple-element.155), channel_id=1, source_target_pairs={{0,24},{2,26},{4,28},{6,30},{8,16},{10,18},{12,20},{14,22},{16,8},... | collective-permute-start | bytes 1572872 | tf_op jit(solution)/shard_map/ppermute | solution.py:68
  245.7 26.3 %collective-permute-start.52 = (bf16[2,128,2048]{2,1,0:T(8,128)(2,1)S(1)}, bf16[2,128,2048]{2,1,0:T(8,128)(2,1)S(1)}, u32[]{:S(2)}, u32[]{:S(2)}) collective-permute-start(bf16[2,128,2048]{2,1,0:T(8,128)(2,1)S(1)} %pad_maximum_fusion), channel_id=1, source_target_pairs={{0,1},{1,0},{2,3},{3,2},{4,5},{5,4},{6,7},{7,6},{8,9},{9,8},{10,11... | collective-permute-start | bytes 3145736 | tf_op jit(solution)/shard_map/ppermute | solution.py:85
  336.9 28.5 %collective-permute-start.64 = (bf16[2,4,128,1024]{3,2,1,0:T(8,128)(2,1)}, bf16[2,4,128,1024]{3,2,1,0:T(8,128)(2,1)}, u32[]{:S(2)}, u32[]{:S(2)}) collective-permute-start(bf16[2,4,128,1024]{3,2,1,0:T(8,128)(2,1)} %get-tuple-element.216), channel_id=1, source_target_pairs={{0,2},{2,0},{4,6},{6,4},{8,10},{10,8},{12,14},{14,12},{16,18},{18,... | collective-permute-start | bytes 6291464 | tf_op jit(solution)/shard_map/ppermute | solution.py:68
  339.9 25.6 %collective-permute-start.63 = (bf16[4,128,1024]{2,1,0:T(8,128)(2,1)S(1)}, bf16[4,128,1024]{2,1,0:T(8,128)(2,1)S(1)}, u32[]{:S(2)}, u32[]{:S(2)}) collective-permute-start(bf16[4,128,1024]{2,1,0:T(8,128)(2,1)S(1)} %fusion.15), channel_id=1, source_target_pairs={{0,4},{2,6},{4,0},{6,2},{8,12},{10,14},{12,8},{14,10},{16,20},{18,... | collective-permute-start | bytes 3145736 | tf_op jit(solution)/shard_map/ppermute | solution.py:68
  367.1 35.6 %collective-permute-start.69 = (bf16[2,4,128,1024]{3,2,1,0:T(8,128)(2,1)}, bf16[2,4,128,1024]{3,2,1,0:T(8,128)(2,1)}, u32[]{:S(2)}, u32[]{:S(2)}) collective-permute-start(bf16[2,4,128,1024]{3,2,1,0:T(8,128)(2,1)} %get-tuple-element.228), channel_id=1, source_target_pairs={{0,2},{2,0},{4,6},{6,4},{8,10},{10,8},{12,14},{14,12},{16,18},{18,... | collective-permute-start | bytes 6291464 | tf_op jit(solution)/shard_map/ppermute | solution.py:68
  371.5 29.8 %collective-permute-start.70 = (bf16[4,128,1024]{2,1,0:T(8,128)(2,1)}, bf16[4,128,1024]{2,1,0:T(8,128)(2,1)}, u32[]{:S(2)}, u32[]{:S(2)}) collective-permute-start(bf16[4,128,1024]{2,1,0:T(8,128)(2,1)} %fusion.17), channel_id=1, source_target_pairs={{0,4},{2,6},{4,0},{6,2},{8,12},{10,14},{12,8},{14,10},{16,20},{18,... | collective-permute-start | bytes 3145736 | tf_op jit(solution)/shard_map/ppermute | solution.py:68
  400.7 31.7 %collective-permute-start.68 = (bf16[512,1024]{1,0:T(8,128)(2,1)}, bf16[512,1024]{1,0:T(8,128)(2,1)}, u32[]{:S(2)}, u32[]{:S(2)}) collective-permute-start(bf16[512,1024]{1,0:T(8,128)(2,1)} %get-tuple-element.222), channel_id=1, source_target_pairs={{0,1},{1,0},{2,3},{3,2},{4,5},{5,4},{6,7},{7,6},{8,9},{9,8},{10,11... | collective-permute-start | bytes 3145736 | tf_op jit(solution)/shard_map/ppermute | solution.py:85
  405.3 33.2 %collective-permute-start.72 = (bf16[4,128,1024]{2,1,0:T(8,128)(2,1)}, bf16[4,128,1024]{2,1,0:T(8,128)(2,1)S(1)}, u32[]{:S(2)}, u32[]{:S(2)}) collective-permute-start(bf16[4,128,1024]{2,1,0:T(8,128)(2,1)} %fusion.16), channel_id=1, source_target_pairs={{0,4},{2,6},{4,0},{6,2},{8,12},{10,14},{12,8},{14,10},{16,20},{18,... | collective-permute-start | bytes 3145736 | tf_op jit(solution)/shard_map/ppermute | solution.py:68
  407.3 25.0 %collective-permute-start.73 = (bf16[128,1024]{1,0:T(8,128)(2,1)S(1)}, bf16[128,1024]{1,0:T(8,128)(2,1)S(1)}, u32[]{:S(2)}, u32[]{:S(2)}) collective-permute-start(bf16[128,1024]{1,0:T(8,128)(2,1)S(1)} %get-tuple-element.232), channel_id=1, source_target_pairs={{0,16},{2,18},{4,20},{6,22},{8,24},{10,26},{12,28},{14,30},{16,0},... | collective-permute-start | bytes 786440 | tf_op jit(solution)/shard_map/ppermute | solution.py:68
  411.2 27.3 %collective-permute-start.75 = (bf16[2,128,1024]{2,1,0:T(8,128)(2,1)S(1)}, bf16[2,128,1024]{2,1,0:T(8,128)(2,1)S(1)}, u32[]{:S(2)}, u32[]{:S(2)}) collective-permute-start(bf16[2,128,1024]{2,1,0:T(8,128)(2,1)S(1)} %pad_maximum_fusion.7), channel_id=1, source_target_pairs={{0,8},{2,10},{4,12},{6,14},{8,0},{10,2},{12,4},{14,6},{16,24},{18,... | collective-permute-start | bytes 1572872 | tf_op jit(solution)/shard_map/ppermute | solution.py:68
  439.9 26.2 %collective-permute-start.82 = (bf16[8,128,1280]{2,1,0:T(8,128)(2,1)}, bf16[8,128,1280]{2,1,0:T(8,128)(2,1)S(1)}, u32[]{:S(2)}, u32[]{:S(2)}) collective-permute-start(bf16[8,128,1280]{2,1,0:T(8,128)(2,1)} %get-tuple-element.245), channel_id=1, source_target_pairs={{0,2},{2,0},{4,6},{6,4},{8,10},{10,8},{12,14},{14,12},{16,18},{18,... | collective-permute-start | bytes 7864328 | tf_op jit(solution)/shard_map/ppermute | solution.py:68
  457.9 29.8 %collective-permute-start.78 = (bf16[4,128,1280]{2,1,0:T(8,128)(2,1)S(1)}, bf16[4,128,1280]{2,1,0:T(8,128)(2,1)S(1)}, u32[]{:S(2)}, u32[]{:S(2)}) collective-permute-start(bf16[4,128,1280]{2,1,0:T(8,128)(2,1)S(1)} %fusion.4), channel_id=1, source_target_pairs={{0,4},{2,6},{4,0},{6,2},{8,12},{10,14},{12,8},{14,10},{16,20},{18,... | collective-permute-start | bytes 3932168 | tf_op jit(solution)/shard_map/ppermute | solution.py:68
  461.2 33.1 %collective-permute-start.87 = (f32[2,2048]{1,0:T(2,128)S(1)}, f32[2,2048]{1,0:T(2,128)S(1)}, u32[]{:S(2)}, u32[]{:S(2)}) collective-permute-start(f32[2,2048]{1,0:T(2,128)S(1)} %fusion.43), channel_id=1, source_target_pairs={{0,8},{2,10},{4,12},{6,14},{8,0},{10,2},{12,4},{14,6},{16,24},{18,... | collective-permute-start | bytes 49160 | tf_op jit(solution)/shard_map/ppermute | solution.py:68
  487.7 38.4 %collective-permute-start.83 = (bf16[4,128,1280]{2,1,0:T(8,128)(2,1)S(1)}, bf16[4,128,1280]{2,1,0:T(8,128)(2,1)S(1)}, u32[]{:S(2)}, u32[]{:S(2)}) collective-permute-start(bf16[4,128,1280]{2,1,0:T(8,128)(2,1)S(1)} %fusion.5), channel_id=1, source_target_pairs={{0,4},{2,6},{4,0},{6,2},{8,12},{10,14},{12,8},{14,10},{16,20},{18,... | collective-permute-start | bytes 3932168 | tf_op jit(solution)/shard_map/ppermute | solution.py:68
  532.0 30.5 %collective-permute-start.93 = (bf16[2,128,1280]{2,1,0:T(8,128)(2,1)S(1)}, bf16[2,128,1280]{2,1,0:T(8,128)(2,1)S(1)}, u32[]{:S(2)}, u32[]{:S(2)}) collective-permute-start(bf16[2,128,1280]{2,1,0:T(8,128)(2,1)S(1)} %pad_maximum_fusion.3), channel_id=1, source_target_pairs={{0,8},{2,10},{4,12},{6,14},{8,0},{10,2},{12,4},{14,6},{16,24},{18,... | collective-permute-start | bytes 1966088 | tf_op jit(solution)/shard_map/ppermute | solution.py:68
  534.1 31.8 %collective-permute-start.95 = (bf16[128,1024]{1,0:T(8,128)(2,1)S(1)}, bf16[128,1024]{1,0:T(8,128)(2,1)S(1)}, u32[]{:S(2)}, u32[]{:S(2)}) collective-permute-start(bf16[128,1024]{1,0:T(8,128)(2,1)S(1)} %get-tuple-element.263), channel_id=1, source_target_pairs={{0,8},{2,10},{4,12},{6,14},{8,0},{10,2},{12,4},{14,6},{16,24},{18,... | collective-permute-start | bytes 786440 | tf_op jit(solution)/shard_map/ppermute | solution.py:68
  (150 other events, 2696.9 us)
Sparse Core Ops, SparseCore 0:
  69.4 63.9 all-gather.2

commit v4 on v3

--- a/solution.py
+++ b/solution.py
@@ -61,8 +61,6 @@
         self.y = (index // CORES) % self.rows
         self.core = index % CORES
         self.x = lax.axis_index("tensor")
-        stride = self.rows * CORES
-        self.columns = [[z * stride + i for z in range(PLANES)] for i in range(stride)]
 
     def move(self, value, target):
         return lax.ppermute(value, "dp", [(d, target(d)) for d in range(self.dp)])
@@ -174,15 +172,13 @@
 
     def kernel(held, normed, outs):
         hidden_ref, silu_ref, slope_ref, *out_refs = outs
-        for k in range(count):
-            here = slice(2 * k * rows_own, 2 * (k + 1) * rows_own)
-            own = slice(k * rows_own, (k + 1) * rows_own)
-            rows = jnp.concatenate([normed[2 * k][...], normed[2 * k + 1][...]], 0)
-            if k == 0:
-                held.wait(0)
+        held.wait(0)
+        held.wait(1)
+
+        def block(k, rows):
+            here = pl.ds(pl.multiple_of(2 * k * rows_own, rows_own), 2 * rows_own)
+            own = pl.ds(pl.multiple_of(k * rows_own, rows_own), rows_own)
             gate = product(rows, held.held[0], NN)
-            if k == 0:
-                held.wait(1)
             up = product(rows, held.held[1], NN)
             sigmoid_gate = jax.nn.sigmoid(gate)
             silu_gate = gate * sigmoid_gate
@@ -191,13 +187,24 @@
             silu_ref[here] = silu_gate.astype(jnp.bfloat16)
             slope = up * sigmoid_gate * (1.0 + gate * (1.0 - sigmoid_gate))
             slope_ref[here] = slope.astype(jnp.bfloat16)
-            if k == 0:
+
+            @pl.when(k == 0)
+            def _():
                 held.wait(2)
+
             out = product(hidden, held.held[2], NT).astype(jnp.bfloat16)
             for i in range(2):
                 columns = slice(i * half, (i + 1) * half)
                 out_refs[2 * i][own] = out[:rows_own, columns]
                 out_refs[2 * i + 1][own] = out[rows_own:, columns]
+
+        @pl.loop(0, count)
+        def _(k):
+            rows = jnp.concatenate([normed[0][...], normed[1][...]], 0)
+            for i in range(1, count):
+                other = jnp.concatenate([normed[2 * i][...], normed[2 * i + 1][...]], 0)
+                rows = jnp.where(k == i, other, rows)
+            block(k, rows)
 
     shapes = [(2 * count * rows_own, quarter)] * 3 + [(count * rows_own, half)] * 4
     return held_call(at, kernel, weights, (0, 1, 2), normed, shapes)
@@ -470,6 +477,24 @@
     )(place, *arrays, *sources)
 
 
+def side_by_side(*arrays):
+    def kernel(*refs):
+        start = 0
+        for ref in refs[:-1]:
+            refs[-1][:, start : start + ref.shape[1]] = ref[...]
+            start += ref.shape[1]
+
+    vmem = pl.BlockSpec(memory_space=pltpu.VMEM)
+    shape = (arrays[0].shape[0], sum(array.shape[1] for array in arrays))
+    return pl.pallas_call(
+        kernel,
+        in_specs=[vmem] * len(arrays),
+        out_specs=vmem,
+        out_shape=jax.ShapeDtypeStruct(shape, arrays[0].dtype),
+        cost_estimate=cost_of(0, arrays, [(shape, arrays[0].dtype)]),
+    )(*arrays)
+
+
 def on_device(
     tokens,
     seq_lens,
@@ -500,8 +525,7 @@
     normed_other = at.other_x(normed_own)
     grad_mixed = cotangent.astype(jnp.float32) * in_use_own[:, None]
     grad_low_own = grad_mixed.astype(jnp.bfloat16)
-    grad_low_mine = lax.all_gather(grad_low_own, "dp", axis_index_groups=at.columns)
-    packed = jnp.concatenate([w_query, key_weight, value_weight, w_out], 1)
+    packed = side_by_side(w_query, key_weight, value_weight, w_out)
     others = range(1, at.rows)
     projections = {(0, 0, 0): packed}
     projections[2, 0, 0] = at.across_z(packed, 2)
@@ -531,9 +555,11 @@
             if key in projections:
                 projections[mask, j, 1] = at.other_core(after(projections[key], *stage))
 
+    middle = grad_low_own.shape[1] // 2
     stage = [projections[3, 0, 0], grads_low[0, 1], plane_two[1]]
     stage += [projections[2, j, 0] for j in others]
     plane_two.append(at.across_z(after(shares[2][2:], *stage), 2))
+    grads_low[1, 0] = at.across_z(after(grad_low_own, *stage), 1)
     for j in others:
         projections[3, j, 0] = at.along_y(after(projections[3, 0, 0], *stage), j)
     for mask, j in ((1, 1), (2, 0), (2, 1), (3, 0)):
@@ -542,8 +568,9 @@
                 block = after(projections[mask, back, 0], *stage)
                 projections[mask, back, 1] = at.other_core(block)
 
-    stage = [projections[3, j, 0] for j in others] + [plane_two[2]]
+    stage = [projections[3, j, 0] for j in others] + [plane_two[2], grads_low[1, 0]]
     plane_two = jnp.concatenate(plane_two, 0)
+    low_first = at.across_z(after(grad_low_own[:, :middle], *stage), 2)
     for j in others:
         projections[3, j, 1] = at.other_core(projections[3, j, 0])
     tables = [jnp.concatenate([table, table], 1) for table in rope_tables(position, HEAD_WIDTH)]
@@ -559,8 +586,9 @@
             earlier = tuple(sent)
         return earlier
 
-    plane_three = at.across_z(after(shares[3][:2], plane_two, *stage), 3)
-    plane_one = at.across_z(after(shares[1][:2], plane_two, *stage), 1)
+    plane_three = at.across_z(after(shares[3][:2], low_first, *stage), 3)
+    plane_one = at.across_z(after(shares[1][:2], low_first, *stage), 1)
+    grads_low[1, 1] = at.other_x(after(grads_low[1, 0], *stage))
     last = to_chips(0, [shares[0]], *stage)
 
     low = jnp.bfloat16
@@ -578,7 +606,7 @@
             ((rows_own, inputs.shape[1]), low),
         ],
     )
-    branch_other = after(branch_other, plane_one, plane_three, *last)
+    branch_other = after(branch_other, plane_one, plane_three, grads_low[1, 1], *last)
     branch = branch_other
     state = inputs + branch_own + at.other_x(branch_other)
     scale_two = lax.rsqrt(jnp.mean(state * state, 1, keepdims=True) + EPSILON)
@@ -586,44 +614,44 @@
 
     plane_three_last = at.across_z(after(shares[3][2:], branch), 3)
     plane_one_last = at.across_z(after(shares[1][2:], branch), 1)
+    low_second = at.across_z(after(grad_low_own[:, middle:], branch), 2)
     last = to_chips(2, [plane_two], *last, branch)
 
-    def to_cores(*keys, earlier):
-        for mask, back in keys:
-            parts = weights[mask, back, 0]
-            weights[mask, back, 1] = [at.other_core(after(part, *earlier)) for part in parts]
-
-    every_row = range(at.rows)
-    to_cores(*((0, j) for j in every_row), earlier=[branch])
-    stage = [normed_two, plane_three_last, plane_one_last]
+    def to_cores(mask, backs, part, *earlier):
+        for back in backs:
+            block = after(weights[mask, back, 0][part], *earlier)
+            weights.setdefault((mask, back, 1), []).append(at.other_core(block))
+
+    to_cores(0, range(at.rows), 0, branch)
+    stage = [normed_two, plane_three_last, plane_one_last, low_second]
+    grads_low[2, 0] = jnp.concatenate([low_first, low_second], 1)
     normed = {(0, 0): normed_two, (0, 1): at.other_x(after(normed_two, *stage))}
     normed[2, 0] = at.across_z(after(normed_two, *stage), 2)
     normed[1, 0] = at.across_z(after(normed_two, *stage), 1)
+    to_cores(2, (0,), 0, *stage)
     last = to_chips(1, [plane_one], *last, *stage)
+    to_cores(1, (0,), 0, *stage)
     last = to_chips(3, [plane_three], *last)
-
-    for mask in (1, 2, 3):
-        grads_low[mask, 0] = lax.dynamic_index_in_dim(
-            grad_low_mine, at.z ^ mask, 0, keepdims=False
-        )
-    grads_low[1, 1] = at.other_x(after(grads_low[1, 0], *stage))
-
-    stage = [*normed.values(), *last, grads_low[1, 1]]
+    to_cores(3, (0,), 0, *stage)
+
+    grads_low[2, 1] = at.other_x(after(grads_low[2, 0], normed[0, 1], *stage))
+
+    stage = [*normed.values(), *last, grads_low[2, 1]]
     normed[3, 0] = at.across_z(after(normed[2, 0], *stage), 1)
     normed[2, 1] = at.other_x(after(normed[2, 0], *stage))
-    last = to_chips(1, [plane_one_last], *stage)
-    last = to_chips(3, [plane_three_last], *last)
-    to_cores(*((2, j) for j in every_row), earlier=stage)
-
-    stage = [normed[3, 0], normed[2, 1], *last]
+    grads_low[3, 0] = at.across_z(after(grads_low[2, 0], *stage), 1)
+    for mask in (2, 1, 3):
+        to_cores(mask, others, 0, *stage)
+    last = to_chips(1, [plane_one_last], *stage) + to_chips(3, [plane_three_last], *stage)
+    for mask in (1, 3):
+        to_cores(mask, (0,), 1, *stage)
+
+    stage = [normed[3, 0], normed[2, 1], grads_low[3, 0], *last]
     normed[3, 1] = at.other_x(after(normed[3, 0], *stage))
     normed[1, 1] = at.across_z(after(normed[0, 1], *stage), 1)
-    to_cores(*((1, j) for j in every_row), earlier=stage)
-    to_cores(*((3, j) for j in every_row), earlier=stage)
-    grads_far = at.other_x(
-        after(jnp.stack([grads_low[mask, 0] for mask in (2, 3)]), normed[3, 1])
-    )
-    grads_low[2, 1], grads_low[3, 1] = grads_far[0], grads_far[1]
+    for mask in (1, 3):
+        to_cores(mask, others, 1, *stage)
+    grads_low[3, 1] = at.other_x(after(grads_low[3, 0], normed[3, 1]))
 
     masks = (3, 2, 1, 0)
     normed_rows = [normed[mask, x] for mask in masks for x in range(2)]
@@ -673,47 +701,46 @@
             )
         return result
 
-    grad_gate_in, grad_up_in, *back = backward(at, weights, grad_rows, silu, slope)
     out_first = at.other_x(outs[1])
+    down_own, down_other = weight_grad(at, grad_rows, hidden, own_features)
+    down_arrived = at.other_core(down_other)
+    down_away = for_chips(down_own, down_arrived)
+    grad_gate_in, grad_up_in, *back = backward(
+        at, weights, grad_rows, after(silu, *down_away), slope
+    )
+    down_terms = (down_own, down_arrived, send_chips(down_away, ()))
 
     def sum_of(i, arrived):
         return back[2 * i].astype(jnp.float32) + arrived
 
-    stage = [out_first, back[0]]
+    stage = [out_first, back[0], *down_terms[2]]
     three = at.other_x(after(back[1], *stage))
     one = at.across_z(after(back[5], *stage), 1)
     gate_own, gate_other = weight_grad(
         at, normed_rows, after(grad_gate_in, *stage), own_features
     )
-    first_blocks = [out_block(outs[0], block_of(out_first, i), i) for i in range(4)]
-    first_two = at.across_z(after(first_blocks[0].astype(jnp.bfloat16), *stage), 1)
-
-    stage = [three, one, gate_own, first_two]
+
+    stage = [three, one, gate_own]
     to_two = at.across_z(after(sum_of(0, three).astype(jnp.bfloat16), *stage), 1)
     two = at.other_x(after(back[3], *stage))
     gate_arrived = at.other_core(after(gate_other, *stage))
     up_own, up_other = weight_grad(at, normed_rows, after(grad_up_in, *stage), own_features)
-    first_zero = (first_blocks[1] + first_two).astype(jnp.bfloat16)
-    first_zero = at.across_z(after(first_zero, *stage), 2)
-
-    stage = [to_two, two, gate_arrived, up_own, first_zero]
+
+    stage = [to_two, two, gate_arrived, up_own]
     for_zero = (sum_of(1, two) + to_two).astype(jnp.bfloat16)
     middle = for_zero.shape[1] // 2
     to_zero_first = at.across_z(after(for_zero[:, :middle], *stage), 2)
     other_zero = (back[7].astype(jnp.float32) + one).astype(jnp.bfloat16)
     zero = at.other_x(after(other_zero, *stage))
-    gate_chips = send_chips(for_chips(gate_own, gate_arrived), stage)
+    gate_away = for_chips(gate_own, gate_arrived)
+    lower = at.planes // 2
+    gate_lower = send_chips([away[:lower] for away in gate_away], stage)
     up_arrived = at.other_core(after(up_other, *stage))
-    down_own, down_other = weight_grad(at, grad_rows, after(hidden, *stage), own_features)
-    first_one = at.across_z(after(first_blocks[2].astype(jnp.bfloat16), *stage), 1)
-
-    stage = [zero, to_zero_first, *gate_chips, up_arrived, down_own, first_one]
+
+    stage = [zero, to_zero_first, *gate_lower, up_arrived]
     to_zero_second = at.across_z(after(for_zero[:, middle:], *stage), 2)
     from_one = at.across_z(after(back[4], *stage), 1)
-    down_arrived = at.other_core(after(down_other, *stage))
-    gate_terms = (gate_own, gate_arrived, gate_chips)
-    gate_pieces = send_planes(gate_terms, (2,), stage)
-    up_chips = send_chips(for_chips(up_own, up_arrived), stage)
+    gate_upper = send_chips([away[lower:] for away in gate_away], stage)
 
     to_zero = jnp.concatenate([to_zero_first, to_zero_second], 1)
     grad_normed_two = sum_of(3, zero) + from_one + to_zero
@@ -725,16 +752,23 @@
     gain_two = jnp.sum(grad_normed_two * hat_two, 0)
     grad_state_own = grad_state.astype(jnp.bfloat16)
 
-    stage = [grad_state_own, *up_chips, down_arrived, gate_pieces[2]]
     grad_state_other = at.other_x(grad_state_own)
+    stage = [grad_state_own, *gate_upper]
+    gate_chips = [jnp.concatenate(parts, 0) for parts in zip(gate_lower, gate_upper, strict=True)]
+    gate_terms = (gate_own, gate_arrived, gate_chips)
+
+    def both(mask):
+        return jnp.stack(
+            [of_plane(terms, mask).astype(jnp.bfloat16) for terms in (gate_terms, down_terms)]
+        )
+
+    down_pieces = send_planes(down_terms, (2,), stage)
+    late = [*stage, grad_state_other, down_pieces[2]]
+    gate_pieces = send_planes(gate_terms, (2,), late)
+    pair_pieces = {mask: at.across_z(after(both(mask), *late), mask) for mask in (3, 1)}
+    up_chips = send_chips(for_chips(up_own, up_arrived), stage)
     up_terms = (up_own, up_arrived, up_chips)
-    down_chips = send_chips(for_chips(down_own, down_arrived), stage)
-
-    def both(mask):
-        return jnp.stack([of_plane(terms, mask).astype(jnp.bfloat16) for terms in (gate_terms, up_terms)])
-
-    up_pieces = send_planes(up_terms, (2,), stage)
-    pair_pieces = {mask: at.across_z(after(both(mask), *stage), mask) for mask in (3, 1)}
+
     out_second = at.other_x(after(outs[3], grad_state_other))
     shape = (at.chips, own_features, width_query + width_kv)
     back_own, back_other, qk_own, qk_other, vo_own, vo_other = attention_call(
@@ -747,7 +781,7 @@
             normed_own,
             normed_other,
             *keys_of,
-            query_key,
+            after(query_key, *late),
             value,
             attended,
         ],
@@ -758,16 +792,25 @@
             *[(shape, low)] * 4,
         ],
     )
-    stage = [qk_other, out_second, *down_chips, *up_pieces.values(), *pair_pieces.values()]
+    stage = [qk_other, out_second, *up_chips, gate_pieces[2], *pair_pieces.values()]
     for mask, piece in pair_pieces.items():
-        gate_pieces[mask], up_pieces[mask] = piece[0], piece[1]
+        gate_pieces[mask], down_pieces[mask] = piece[0], piece[1]
+    out_blocks = [
+        jnp.concatenate(
+            [
+                out_block(outs[2 * n], block_of(arrived, i), i)
+                for n, arrived in enumerate((out_first, out_second))
+            ],
+            1,
+        )
+        for i in range(4)
+    ]
 
     owns = {"qk": qk_own, "vo": vo_own}
     cores = {
         "qk": at.other_core(after(qk_other, *stage)),
         "vo": at.other_core(after(vo_other, *stage)),
     }
-    normed_arrived = at.other_x(after(back_other, *stage))
 
     def by_place(value):
         return value.reshape(at.planes, at.rows, own_features, -1)
@@ -809,20 +852,24 @@
     def total_of(name):
         return for_plane(name, 0) + pairs[name][0] + quarters[name]
 
-    down_terms = (down_own, down_arrived, down_chips)
-    down_pieces = send_planes(down_terms, (2,), stage)
-    second_two = out_block(outs[2], block_of(out_second, 0), 0).astype(jnp.bfloat16)
-    second_two = at.across_z(after(second_two, *stage), 1)
-
-    to_chips_of("qk", stage)
-
-    stage = [*chips["qk"], *down_pieces.values(), second_two, normed_arrived]
+    up_pieces = send_planes(up_terms, (2, 3), stage)
+    out_two = at.across_z(after(out_blocks[0].astype(jnp.bfloat16), *stage), 1)
+    to_chips_of("qk", ())
+
+    out_one = at.across_z(after(out_blocks[2].astype(jnp.bfloat16), *stage), 1)
+
+    stage = [*chips["qk"], *up_pieces.values(), out_two, out_one]
+    normed_arrived = at.other_x(after(back_other, *stage))
     to_chips_of("vo", stage)
     to_pair("qk", stage)
-    down_pieces.update(send_planes(down_terms, (3,), stage))
-    second_zero = out_block(outs[2], block_of(out_second, 1), 1) + second_two
-    second_zero = at.across_z(after(second_zero.astype(jnp.bfloat16), *stage), 2)
-    grad_normed_one = back_own + normed_arrived
+    up_pieces.update(send_planes(up_terms, (1,), stage))
+    out_zero = (out_blocks[1] + out_two).astype(jnp.bfloat16)
+    out_zero = at.across_z(after(out_zero, *stage), 2)
+
+    stage = [*chips["vo"], pairs["qk"], out_zero, normed_arrived, up_pieces[1]]
+    to_pair("vo", stage)
+    to_quarter("qk", stage)
+    grad_normed_one = back_own + after(normed_arrived, *stage)
     hat_one = inputs * scale_one
     inner_one = grad_normed_one * gain_rows[0]
     grad_tokens = (
@@ -833,29 +880,23 @@
     grad_gains = jnp.stack([gain_one, gain_two])
     grad_gains = grad_gains + at.other_x(grad_gains)
     bits = [1 << i for i in range(at.dp.bit_length() - 1)]
-    chip_bits = [bit for bit in bits if CORES <= bit < CORES * at.rows]
     for bit in bits:
-        if bit not in chip_bits:
+        if bit < CORES * at.rows:
             grad_gains = grad_gains + at.move(grad_gains, lambda d: d ^ bit)
 
-    stage = [*chips["vo"], pairs["qk"], second_zero, grad_gains, *down_pieces.values()]
-    down_pieces.update(send_planes(down_terms, (1,), stage))
-    to_pair("vo", stage)
-    to_quarter("qk", stage)
-    second_one = out_block(outs[2], block_of(out_second, 2), 2).astype(jnp.bfloat16)
-    second_one = at.across_z(after(second_one, *stage), 1)
-    for bit in chip_bits:
-        grad_gains = grad_gains + at.move(after(grad_gains, *stage), lambda d: d ^ bit)
-
-    stage = [pairs["vo"], quarters["qk"], second_one]
+    stage = [pairs["vo"], quarters["qk"], grad_gains]
     to_quarter("vo", stage)
+    for bit in bits:
+        if bit >= CORES * at.rows:
+            grad_gains = grad_gains + at.move(after(grad_gains, *stage), lambda d: d ^ bit)
+    grad_gate = all_columns(gate_terms, gate_pieces, *stage)
+    grad_up = all_columns(up_terms, up_pieces, *stage)
+    grad_down = all_columns(down_terms, down_pieces, *stage)
     sum_qk, sum_vo = total_of("qk"), total_of("vo")
     grad_gate = all_columns(gate_terms, gate_pieces, *stage)
     grad_up = all_columns(up_terms, up_pieces, *stage)
     grad_down = all_columns(down_terms, down_pieces, *stage)
-    first_sum = first_blocks[3] + first_zero + first_one
-    second_sum = out_block(outs[2], block_of(out_second, 3), 3) + second_zero + second_one
-    ffn_out = jnp.concatenate([first_sum, second_sum], 1)
+    ffn_out = out_blocks[3] + out_zero + out_one
     mixed = ((state + ffn_out) * in_use_own[:, None]).astype(jnp.bfloat16)
     return (
         mixed,

time: 593 us -> 553 us (0.933)
  between operations: 15.5 us -> 2.49 us
  starting transfers between devices: 111 us -> 101 us
  local copies, waits for them, and re-layouts: 30 us -> 20.7 us
  other arithmetic: 38.3 us -> 32.3 us
    ppermute x80 -> x82, starting transfers between devices: 94.1 us -> 81.5 us  [move(): return lax.ppermute(value, 'dp', [(d, target(d)) for d in range(self.dp)])]
    ppermute x80 -> x82, waiting for transfers between devices: 240 us -> 231 us  [move(): return lax.ppermute(value, 'dp', [(d, target(d)) for d in range(self.dp)])]
    unnamed x175 -> x198, local copies, waits for them, and re-layouts: 16.2 us -> 10.5 us
    ppermute x16 -> x17, waiting for transfers between devices: 41.1 us -> 45 us  [other_x(): return lax.ppermute(value, 'tensor', [(0, 1), (1, 0)])]
    ppermute x16 -> x17, starting transfers between devices: 16.6 us -> 19.1 us  [other_x(): return lax.ppermute(value, 'tensor', [(0, 1), (1, 0)])]
  transfers between devices with their start and end apart: 97 -> 99, of which waited for: 40 -> 47; matrix products, arithmetic and copies ran while one was open for 8% -> 7% of each run, Pallas kernels for 18% -> 19%
where the time goes in v4:
time: 553 us; the launch traced here: 544 us
  waiting for transfers between devices  276 us (50%)
  Pallas kernels  112 us (20%)
  starting transfers between devices  101 us (18%)
  other arithmetic  32.3 us (6%)
  local copies, waits for them, and re-layouts  20.7 us (4%)
    ppermute x82, waiting for transfers between devices, move(): return lax.ppermute(value, 'dp', [(d, target(d)) for d in range(self.dp)])  231 us
    ppermute x82, starting transfers between devices, move(): return lax.ppermute(value, 'dp', [(d, target(d)) for d in range(self.dp)])  81.5 us
    pallas_call x2, Pallas kernels, held_call(): pl.pallas_call(body, in_specs=[pl.BlockSpec(memory_space=pltpu.SMEM)] + [...  46.1 us
    ppermute x17, waiting for transfers between devices, other_x(): return lax.ppermute(value, 'tensor', [(0, 1), (1, 0)])  45 us
    pallas_call x2, Pallas kernels, attention_call(): pl.pallas_call(functools.partial(kernel, width_kv, keys), in_specs=[pl.Bl...  37.3 us
    pallas_call x3, Pallas kernels, weight_grad(): pl.pallas_call(weight_grad_kernel, grid_spec=pltpu.PrefetchScalarGridSpec...  26.8 us
    ppermute x17, starting transfers between devices, other_x(): return lax.ppermute(value, 'tensor', [(0, 1), (1, 0)])  19.1 us
  transfers between devices with their start and end apart: 99, of which 47 were waited for; matrix products, arithmetic and copies ran while one was open for 7% of the time, Pallas kernels for 19%

profile of v4, /device:TPU:0, one launch (start us, length us, event | category | flops | bytes accessed | tf_op | source)
XLA Modules:
  0.0 544.3 jit_solution(10043493296145737621)
XLA Ops:
  14.8 11.3 %collective-permute-done.refs_1_.refs_3_ = bf16[128,2048]{1,0:T(8,128)(2,1)} collective-permute-done((bf16[128,2048]{1,0:T(8,128)(2,1)}, bf16[128,2048]{1,0:T(8,128)(2,1)}, u32[]{:S(2)}, u32[]{:S(2)}) %collective-permute-start) | collective-permute-done | bytes 524320 | tf_op jit(solution)/shard_map/ppermute | solution.py:83
  26.1 9.9 %collective-permute-done.1.refs_7_.refs_12_ = bf16[128,2560]{1,0:T(8,128)(2,1)} collective-permute-done((bf16[128,2560]{1,0:T(8,128)(2,1)}, bf16[128,2560]{1,0:T(8,128)(2,1)}, u32[]{:S(2)}, u32[]{:S(2)}) %collective-permute-start.1) | collective-permute-done | bytes 655392 | tf_op jit(solution)/shard_map/ppermute | solution.py:66
  43.4 7.8 %collective-permute-done.6 = bf16[1,128,1024]{2,1,0:T(8,128)(2,1)S(1)} collective-permute-done((bf16[1,128,1024]{2,1,0:T(8,128)(2,1)S(1)}, bf16[1,128,1024]{2,1,0:T(8,128)(2,1)S(1)}, u32[]{:S(2)}, u32[]{:S(2)}) %collective-permute-start.6) | collective-permute-done | bytes 262176 | tf_op jit(solution)/shard_map/ppermute | solution.py:66
  55.4 10.0 %collective-permute-done.4.refs_10_.refs_15_ = bf16[128,2560]{1,0:T(8,128)(2,1)S(1)} collective-permute-done((bf16[128,2560]{1,0:T(8,128)(2,1)}, bf16[128,2560]{1,0:T(8,128)(2,1)S(1)}, u32[]{:S(2)}, u32[]{:S(2)}) %collective-permute-start.4) | collective-permute-done | bytes 655392 | tf_op jit(solution)/shard_map/ppermute | solution.py:66
  77.6 9.9 %collective-permute-done.19 = bf16[1,128,1024]{2,1,0:T(8,128)(2,1)S(1)} collective-permute-done((bf16[1,128,1024]{2,1,0:T(8,128)(2,1)S(1)}, bf16[1,128,1024]{2,1,0:T(8,128)(2,1)S(1)}, u32[]{:S(2)}, u32[]{:S(2)}) %collective-permute-start.19) | collective-permute-done | bytes 262176 | tf_op jit(solution)/shard_map/ppermute | solution.py:66
  92.6 12.3 %collective-permute-done.21 = bf16[128,1024]{1,0:T(8,128)(2,1)S(1)} collective-permute-done((bf16[128,1024]{1,0:T(8,128)(2,1)S(1)}, bf16[128,1024]{1,0:T(8,128)(2,1)S(1)}, u32[]{:S(2)}, u32[]{:S(2)}) %collective-permute-start.21) | collective-permute-done | bytes 262176 | tf_op jit(solution)/shard_map/ppermute | solution.py:66
  114.1 16.1 %shard_map.187 = (bf16[256,1280]{1,0:T(8,128)(2,1)}, bf16[256,256]{1,0:T(8,128)(2,1)}, bf16[256,1024]{1,0:T(8,128)(2,1)}, f32[128,2048]{1,0:T(8,128)}, bf16[128,2048]{1,0:T(8,128)(2,1)}) custom-call(s32[5]{0:T(128)} %stack.113.place, bf16[128,2048]{1,0:T(8,128)(2,1)} %fusion.6.refs_0_.refs_2_, bf16[128,2048]{1,0:T(8,128)(2,1)} %collective-permute-done.refs_1_.refs_3_, ...), custom_call_target="tpu_custom_call" | custom-call | flops 4026531840 | bytes 14682112 | tf_op jit(solution)/shard_map/pallas_call | solution.py:463
  139.8 7.6 %collective-permute-done.26 = bf16[128,2048]{1,0:T(8,128)(2,1)S(1)} collective-permute-done((bf16[128,2048]{1,0:T(8,128)(2,1)}, bf16[128,2048]{1,0:T(8,128)(2,1)S(1)}, u32[]{:S(2)}, u32[]{:S(2)}) %collective-permute-start.26) | collective-permute-done | bytes 524320 | tf_op jit(solution)/shard_map/ppermute | solution.py:83
  148.1 6.2 %collective-permute-done.29 = bf16[128,1024]{1,0:T(8,128)(2,1)S(1)} collective-permute-done((bf16[128,1024]{1,0:T(8,128)(2,1)S(1)}, bf16[128,1024]{1,0:T(8,128)(2,1)S(1)}, u32[]{:S(2)}, u32[]{:S(2)}) %collective-permute-start.29) | collective-permute-done | bytes 262176 | tf_op jit(solution)/shard_map/ppermute | solution.py:66
  163.3 4.9 collective-permute-done.31.refs_7_
  170.7 14.3 %collective-permute-done.30.refs_2_ = bf16[128,2048]{1,0:T(8,128)(2,1)S(1)} collective-permute-done((bf16[128,2048]{1,0:T(8,128)(2,1)S(1)}, bf16[128,2048]{1,0:T(8,128)(2,1)S(1)}, u32[]{:S(2)}, u32[]{:S(2)}) %collective-permute-start.30) | collective-permute-done | bytes 524320 | tf_op jit(solution)/shard_map/ppermute | solution.py:66
  191.3 5.8 %collective-permute-done.41.refs_24_.refs_26_ = bf16[1,128,1024]{2,1,0:T(8,128)(2,1)S(1)} collective-permute-done((bf16[1,128,1024]{2,1,0:T(8,128)(2,1)S(1)}, bf16[1,128,1024]{2,1,0:T(8,128)(2,1)S(1)}, u32[]{:S(2)}, u32[]{:S(2)}) %collective-permute-start.41) | collective-permute-done | bytes 262176 | tf_op jit(solution)/shard_map/ppermute | solution.py:66
  201.3 8.3 %collective-permute-done.37.refs_0_ = bf16[128,2048]{1,0:T(8,128)(2,1)S(1)} collective-permute-done((bf16[128,2048]{1,0:T(8,128)(2,1)S(1)}, bf16[128,2048]{1,0:T(8,128)(2,1)S(1)}, u32[]{:S(2)}, u32[]{:S(2)}) %collective-permute-start.37) | collective-permute-done | bytes 524320 | tf_op jit(solution)/shard_map/ppermute | solution.py:66
  217.0 10.3 %collective-permute-done.42.refs_1_ = bf16[128,2048]{1,0:T(8,128)(2,1)S(1)} collective-permute-done((bf16[128,2048]{1,0:T(8,128)(2,1)S(1)}, bf16[128,2048]{1,0:T(8,128)(2,1)S(1)}, u32[]{:S(2)}, u32[]{:S(2)}) %collective-permute-start.42) | collective-permute-done | bytes 524320 | tf_op jit(solution)/shard_map/ppermute | solution.py:83
  232.1 23.9 %shard_map.188 = (bf16[1024,1024]{1,0:T(8,128)(2,1)}, bf16[1024,1024]{1,0:T(8,128)(2,1)}, bf16[1024,1024]{1,0:T(8,128)(2,1)}, bf16[512,1024]{1,0:T(8,128)(2,1)},...) custom-call(s32[4]{0:T(128)} %pad_add_fusion.1.place, ...), custom_call_target="tpu_custom_call" | custom-call | flops 12884901888 | bytes 27262976 | tf_op jit(solution)/shard_map/pallas_call | solution.py:147
  256.0 9.2 %shard_map.189 = (bf16[2,4,128,1024]{3,2,1,0:T(8,128)(2,1)}, bf16[2,4,128,1024]{3,2,1,0:T(8,128)(2,1)}) custom-call(s32[1]{0:T(128)} %bitcast.1.place, bf16[128,2048]{1,0:T(8,128)(2,1)} %collective-permute-done.39.refs_0_, bf16[128,2048]{1,0:T(8,128)(2,1)} %collective-permute-done.57.refs_1_, bf16[128,2048]{1,0:T(8,128)(2,1)} %copy-done.52, ...), custom_call_target="tpu_custom_call" | custom-call | flops 4294967296 | bytes 10485760 | tf_op jit(solution)/shard_map/pallas_call | solution.py:261
  273.3 22.2 %shard_map.190 = (bf16[1024,1024]{1,0:T(8,128)(2,1)}, bf16[1024,1024]{1,0:T(8,128)(2,1)}, bf16[128,2048]{1,0:T(8,128)(2,1)}, bf16[128,2048]{1,0:T(8,128)(2,1)}, ...) custom-call(s32[4]{0:T(128)} %pad_add_fusion.1.place, ...), custom_call_target="tpu_custom_call" | custom-call | flops 12884901888 | bytes 29360128 | tf_op jit(solution)/shard_map/pallas_call | solution.py:147
  300.0 8.8 %shard_map.191 = (bf16[2,4,128,1024]{3,2,1,0:T(8,128)(2,1)}, bf16[2,4,128,1024]{3,2,1,0:T(8,128)(2,1)}) custom-call(s32[1]{0:T(128)} %bitcast.1.place, bf16[128,2048]{1,0:T(8,128)(2,1)} %copy-done.75, bf16[128,2048]{1,0:T(8,128)(2,1)} %copy-done.80, bf16[128,2048]{1,0:T(8,128)(2,1)} %copy-done.73, bf16[128,2048]{1,0:T(8,128)(2,1)} %copy-done.76, ...), custom_call_target="tpu_custom_call" | custom-call | flops 4294967296 | bytes 10485760 | tf_op jit(solution)/shard_map/pallas_call | solution.py:261
  313.7 8.8 %shard_map.192 = (bf16[2,4,128,1024]{3,2,1,0:T(8,128)(2,1)}, bf16[2,4,128,1024]{3,2,1,0:T(8,128)(2,1)}) custom-call(s32[1]{0:T(128)} %bitcast.1.place, bf16[128,2048]{1,0:T(8,128)(2,1)} %copy-done.75, bf16[128,2048]{1,0:T(8,128)(2,1)} %copy-done.80, bf16[128,2048]{1,0:T(8,128)(2,1)} %copy-done.73, bf16[128,2048]{1,0:T(8,128)(2,1)} %copy-done.76, ...), custom_call_target="tpu_custom_call" | custom-call | flops 4294967296 | bytes 10485760 | tf_op jit(solution)/shard_map/pallas_call | solution.py:261
  335.9 11.9 %collective-permute-done.66 = bf16[128,1024]{1,0:T(8,128)(2,1)S(1)} collective-permute-done((bf16[128,1024]{1,0:T(8,128)(2,1)S(1)}, bf16[128,1024]{1,0:T(8,128)(2,1)S(1)}, u32[]{:S(2)}, u32[]{:S(2)}) %collective-permute-start.66) | collective-permute-done | bytes 262176 | tf_op jit(solution)/shard_map/ppermute | solution.py:66
  354.1 12.0 %collective-permute-done.70 = bf16[128,1024]{1,0:T(8,128)(2,1)} collective-permute-done((bf16[128,1024]{1,0:T(8,128)(2,1)}, bf16[128,1024]{1,0:T(8,128)(2,1)}, u32[]{:S(2)}, u32[]{:S(2)}) %collective-permute-start.70) | collective-permute-done | bytes 262176 | tf_op jit(solution)/shard_map/ppermute | solution.py:66
  379.7 5.2 collective-permute-done.71.refs_1_
  393.7 21.1 %shard_map.193 = (f32[128,2048]{1,0:T(8,128)}, bf16[128,2048]{1,0:T(8,128)(2,1)}, bf16[8,128,1280]{2,1,0:T(8,128)(2,1)}, bf16[8,128,1280]{2,1,0:T(8,128)(2,1)}, ...) custom-call(s32[5]{0:T(128)} %stack.113.place, bf16[128,2048]{1,0:T(8,128)(2,1)} %copy-done.30, ...), custom_call_target="tpu_custom_call" | custom-call | flops 7381975040 | bytes 26216448 | tf_op jit(solution)/shard_map/pallas_call | solution.py:463
  414.8 13.1 %collective-permute-done.76 = bf16[128,1024]{1,0:T(8,128)(2,1)S(1)} collective-permute-done((bf16[128,1024]{1,0:T(8,128)(2,1)S(1)}, bf16[128,1024]{1,0:T(8,128)(2,1)S(1)}, u32[]{:S(2)}, u32[]{:S(2)}) %collective-permute-start.76) | collective-permute-done | bytes 262176 | tf_op jit(solution)/shard_map/ppermute | solution.py:66
  438.1 14.1 %collective-permute-done.79 = bf16[128,2048]{1,0:T(8,128)(2,1)S(1)} collective-permute-done((bf16[128,2048]{1,0:T(8,128)(2,1)S(1)}, bf16[128,2048]{1,0:T(8,128)(2,1)S(1)}, u32[]{:S(2)}, u32[]{:S(2)}) %collective-permute-start.79) | collective-permute-done | bytes 524320 | tf_op jit(solution)/shard_map/ppermute | solution.py:66
  452.7 8.4 %collective-permute-done.82 = bf16[128,1024]{1,0:T(8,128)(2,1)S(1)} collective-permute-done((bf16[128,1024]{1,0:T(8,128)(2,1)S(1)}, bf16[128,1024]{1,0:T(8,128)(2,1)S(1)}, u32[]{:S(2)}, u32[]{:S(2)}) %collective-permute-start.82) | collective-permute-done | bytes 262176 | tf_op jit(solution)/shard_map/ppermute | solution.py:66
  461.1 9.2 %collective-permute-done.84 = bf16[128,2048]{1,0:T(8,128)(2,1)S(1)} collective-permute-done((bf16[128,2048]{1,0:T(8,128)(2,1)S(1)}, bf16[128,2048]{1,0:T(8,128)(2,1)S(1)}, u32[]{:S(2)}, u32[]{:S(2)}) %collective-permute-start.84) | collective-permute-done | bytes 524320 | tf_op jit(solution)/shard_map/ppermute | solution.py:66
  474.5 19.9 %collective-permute-done.85 = bf16[128,2048]{1,0:T(8,128)(2,1)S(1)} collective-permute-done((bf16[128,2048]{1,0:T(8,128)(2,1)S(1)}, bf16[128,2048]{1,0:T(8,128)(2,1)S(1)}, u32[]{:S(2)}, u32[]{:S(2)}) %collective-permute-start.85) | collective-permute-done | bytes 524320 | tf_op jit(solution)/shard_map/ppermute | solution.py:66
  495.5 4.6 collective-permute-done.89
  513.2 4.9 collective-permute-done.95
  519.9 7.1 %collective-permute-done.94 = bf16[2,128,1280]{2,1,0:T(8,128)(2,1)S(1)} collective-permute-done((bf16[2,128,1280]{2,1,0:T(8,128)(2,1)S(1)}, bf16[2,128,1280]{2,1,0:T(8,128)(2,1)S(1)}, u32[]{:S(2)}, u32[]{:S(2)}) %collective-permute-start.94) | collective-permute-done | bytes 655392 | tf_op jit(solution)/shard_map/ppermute | solution.py:66
  535.2 6.4 %collective-permute-done.97 = f32[2,2048]{1,0:T(2,128)S(1)} collective-permute-done((f32[2,2048]{1,0:T(2,128)S(1)}, f32[2,2048]{1,0:T(2,128)S(1)}, u32[]{:S(2)}, u32[]{:S(2)}) %collective-permute-start.97) | collective-permute-done | bytes 16416 | tf_op jit(solution)/shard_map/ppermute | solution.py:66
  (468 shorter events, 196.4 us)
Async XLA Ops:
  2.8 33.2 %collective-permute-start.1 = (bf16[128,2560]{1,0:T(8,128)(2,1)}, bf16[128,2560]{1,0:T(8,128)(2,1)}, u32[]{:S(2)}, u32[]{:S(2)}) collective-permute-start(bf16[128,2560]{1,0:T(8,128)(2,1)} %shard_map.186.refs_6_.refs_11_), channel_id=1, source_target_pairs={{0,16},{2,18},{4,20},{6,22},{8,24},{10,26},{12,28},{14,30},{16,0},... | collective-permute-start | bytes 1966088 | tf_op jit(solution)/shard_map/ppermute | solution.py:66
  6.8 29.4 %collective-permute-start.2 = (bf16[128,2560]{1,0:T(8,128)(2,1)}, bf16[128,2560]{1,0:T(8,128)(2,1)}, u32[]{:S(2)}, u32[]{:S(2)}) collective-permute-start(bf16[128,2560]{1,0:T(8,128)(2,1)} %shard_map.186.refs_6_.refs_11_), channel_id=1, source_target_pairs={{0,8},{2,10},{4,12},{6,14},{8,0},{10,2},{12,4},{14,6},{16,24},{18,... | collective-permute-start | bytes 1966088 | tf_op jit(solution)/shard_map/ppermute | solution.py:66
  8.4 27.8 %collective-permute-start.3 = (bf16[128,2560]{1,0:T(8,128)(2,1)}, bf16[128,2560]{1,0:T(8,128)(2,1)}, u32[]{:S(2)}, u32[]{:S(2)}) collective-permute-start(bf16[128,2560]{1,0:T(8,128)(2,1)} %shard_map.186.refs_6_.refs_11_), channel_id=1, source_target_pairs={{0,4},{2,6},{4,0},{6,2},{8,12},{10,14},{12,8},{14,10},{16,20},{18,... | collective-permute-start | bytes 1966088 | tf_op jit(solution)/shard_map/ppermute | solution.py:66
  41.0 24.4 %collective-permute-start.4 = (bf16[128,2560]{1,0:T(8,128)(2,1)}, bf16[128,2560]{1,0:T(8,128)(2,1)S(1)}, u32[]{:S(2)}, u32[]{:S(2)}) collective-permute-start(bf16[128,2560]{1,0:T(8,128)(2,1)} %collective-permute-done.1.refs_7_.refs_12_), channel_id=1, source_target_pairs={{0,8},{2,10},{4,12},{6,14},{8,0},{10,2},{12,4},{14,6},{16,24},{18,... | collective-permute-start | bytes 1966088 | tf_op jit(solution)/shard_map/ppermute | solution.py:66
  87.5 22.7 %collective-permute-start.17 = (bf16[128,2560]{1,0:T(8,128)(2,1)S(1)}, bf16[128,2560]{1,0:T(8,128)(2,1)S(1)}, u32[]{:S(2)}, u32[]{:S(2)}) collective-permute-start(bf16[128,2560]{1,0:T(8,128)(2,1)S(1)} %collective-permute-done.4.refs_10_.refs_15_), channel_id=1, source_target_pairs={{0,2},{2,0},{4,6},{6,4},{8,10},{10,8},{12,14},{14,12},{16,18},{18,... | collective-permute-start | bytes 1966088 | tf_op jit(solution)/shard_map/ppermute | solution.py:66
  92.4 21.7 %collective-permute-start.18 = (bf16[128,2560]{1,0:T(8,128)(2,1)}, bf16[128,2560]{1,0:T(8,128)(2,1)}, u32[]{:S(2)}, u32[]{:S(2)}) collective-permute-start(bf16[128,2560]{1,0:T(8,128)(2,1)} %collective-permute-done.14.refs_17_.refs_22_), channel_id=1, source_target_pairs={{0,2},{2,0},{4,6},{6,4},{8,10},{10,8},{12,14},{14,12},{16,18},{18,... | collective-permute-start | bytes 1966088 | tf_op jit(solution)/shard_map/ppermute | solution.py:66
  104.9 25.3 %collective-permute-start.25 = (bf16[3,128,1024]{2,1,0:T(8,128)(2,1)S(1)}, bf16[3,128,1024]{2,1,0:T(8,128)(2,1)}, u32[]{:S(2)}, u32[]{:S(2)}) collective-permute-start(bf16[3,128,1024]{2,1,0:T(8,128)(2,1)S(1)} %pad_maximum_fusion.refs_8_.refs_10_), channel_id=1, source_target_pairs={{0,4},{2,6},{4,0},{6,2},{8,12},{10,14},{12,8},{14,10},{16,20},{18,... | collective-permute-start | bytes 2359304 | tf_op jit(solution)/shard_map/ppermute | solution.py:66
  105.7 24.5 %collective-permute-start.24 = (bf16[128,2048]{1,0:T(8,128)(2,1)}, bf16[128,2048]{1,0:T(8,128)(2,1)}, u32[]{:S(2)}, u32[]{:S(2)}) collective-permute-start(bf16[128,2048]{1,0:T(8,128)(2,1)} %collective-permute-done.20.refs_4_), channel_id=1, source_target_pairs={{0,1},{1,0},{2,3},{3,2},{4,5},{5,4},{6,7},{7,6},{8,9},{9,8},{10,11... | collective-permute-start | bytes 1572872 | tf_op jit(solution)/shard_map/ppermute | solution.py:83
  107.0 23.2 %collective-permute-start.23 = (bf16[2,128,1024]{2,1,0:T(8,128)(2,1)S(1)}, bf16[2,128,1024]{2,1,0:T(8,128)(2,1)}, u32[]{:S(2)}, u32[]{:S(2)}) collective-permute-start(bf16[2,128,1024]{2,1,0:T(8,128)(2,1)S(1)} %get-tuple-element.158), channel_id=1, source_target_pairs={{0,24},{2,26},{4,28},{6,30},{8,16},{10,18},{12,20},{14,22},{16,8},... | collective-permute-start | bytes 1572872 | tf_op jit(solution)/shard_map/ppermute | solution.py:66
  110.2 23.0 %collective-permute-start.22 = (bf16[2,128,1024]{2,1,0:T(8,128)(2,1)S(1)}, bf16[2,128,1024]{2,1,0:T(8,128)(2,1)}, u32[]{:S(2)}, u32[]{:S(2)}) collective-permute-start(bf16[2,128,1024]{2,1,0:T(8,128)(2,1)S(1)} %get-tuple-element.157), channel_id=1, source_target_pairs={{0,8},{2,10},{4,12},{6,14},{8,0},{10,2},{12,4},{14,6},{16,24},{18,... | collective-permute-start | bytes 1572872 | tf_op jit(solution)/shard_map/ppermute | solution.py:66
  158.4 26.6 %collective-permute-start.30 = (bf16[128,2048]{1,0:T(8,128)(2,1)S(1)}, bf16[128,2048]{1,0:T(8,128)(2,1)S(1)}, u32[]{:S(2)}, u32[]{:S(2)}) collective-permute-start(bf16[128,2048]{1,0:T(8,128)(2,1)S(1)} %multiply_convert_fusion.refs_6_), channel_id=1, source_target_pairs={{0,16},{2,18},{4,20},{6,22},{8,24},{10,26},{12,28},{14,30},{16,0},... | collective-permute-start | bytes 1572872 | tf_op jit(solution)/shard_map/ppermute | solution.py:66
  162.2 22.8 %collective-permute-start.32 = (bf16[128,2048]{1,0:T(8,128)(2,1)S(1)}, bf16[128,2048]{1,0:T(8,128)(2,1)S(1)}, u32[]{:S(2)}, u32[]{:S(2)}) collective-permute-start(bf16[128,2048]{1,0:T(8,128)(2,1)S(1)} %multiply_convert_fusion.refs_6_), channel_id=1, source_target_pairs={{0,8},{2,10},{4,12},{6,14},{8,0},{10,2},{12,4},{14,6},{16,24},{18,... | collective-permute-start | bytes 1572872 | tf_op jit(solution)/shard_map/ppermute | solution.py:66
  228.7 27.3 %collective-permute-start.57 = (bf16[128,2048]{1,0:T(8,128)(2,1)}, bf16[128,2048]{1,0:T(8,128)(2,1)}, u32[]{:S(2)}, u32[]{:S(2)}) collective-permute-start(bf16[128,2048]{1,0:T(8,128)(2,1)} %collective-permute-done.39.refs_0_), channel_id=1, source_target_pairs={{0,1},{1,0},{2,3},{3,2},{4,5},{5,4},{6,7},{7,6},{8,9},{9,8},{10,11... | collective-permute-start | bytes 1572872 | tf_op jit(solution)/shard_map/ppermute | solution.py:83
  265.6 29.9 %collective-permute-start.56 = (bf16[512,1024]{1,0:T(8,128)(2,1)S(1)}, bf16[512,1024]{1,0:T(8,128)(2,1)S(1)}, u32[]{:S(2)}, u32[]{:S(2)}) collective-permute-start(bf16[512,1024]{1,0:T(8,128)(2,1)S(1)} %copy-done.55), channel_id=1, source_target_pairs={{0,1},{1,0},{2,3},{3,2},{4,5},{5,4},{6,7},{7,6},{8,9},{9,8},{10,11... | collective-permute-start | bytes 3145736 | tf_op jit(solution)/shard_map/ppermute | solution.py:83
  271.8 25.3 %collective-permute-start.59 = (bf16[4,128,1024]{2,1,0:T(8,128)(2,1)S(1)}, bf16[4,128,1024]{2,1,0:T(8,128)(2,1)S(1)}, u32[]{:S(2)}, u32[]{:S(2)}) collective-permute-start(bf16[4,128,1024]{2,1,0:T(8,128)(2,1)S(1)} %fusion.15), channel_id=1, source_target_pairs={{0,4},{2,6},{4,0},{6,2},{8,12},{10,14},{12,8},{14,10},{16,20},{18,... | collective-permute-start | bytes 3145736 | tf_op jit(solution)/shard_map/ppermute | solution.py:66
  327.6 21.0 %collective-permute-start.68 = (bf16[2,4,128,1024]{3,2,1,0:T(8,128)(2,1)}, bf16[2,4,128,1024]{3,2,1,0:T(8,128)(2,1)}, u32[]{:S(2)}, u32[]{:S(2)}) collective-permute-start(bf16[2,4,128,1024]{3,2,1,0:T(8,128)(2,1)} %get-tuple-element.221), channel_id=1, source_target_pairs={{0,2},{2,0},{4,6},{6,4},{8,10},{10,8},{12,14},{14,12},{16,18},{18,... | collective-permute-start | bytes 6291464 | tf_op jit(solution)/shard_map/ppermute | solution.py:66
  352.8 24.7 %collective-permute-start.73 = (bf16[2,128,1024]{2,1,0:T(8,128)(2,1)S(1)}, bf16[2,128,1024]{2,1,0:T(8,128)(2,1)S(1)}, u32[]{:S(2)}, u32[]{:S(2)}) collective-permute-start(bf16[2,128,1024]{2,1,0:T(8,128)(2,1)S(1)} %copy-done.40), channel_id=1, source_target_pairs={{0,4},{2,6},{4,0},{6,2},{8,12},{10,14},{12,8},{14,10},{16,20},{18,... | collective-permute-start | bytes 1572872 | tf_op jit(solution)/shard_map/ppermute | solution.py:66
  378.7 49.2 %collective-permute-start.75 = (bf16[4,128,1024]{2,1,0:T(8,128)(2,1)}, bf16[4,128,1024]{2,1,0:T(8,128)(2,1)}, u32[]{:S(2)}, u32[]{:S(2)}) collective-permute-start(bf16[4,128,1024]{2,1,0:T(8,128)(2,1)} %fusion.16), channel_id=1, source_target_pairs={{0,4},{2,6},{4,0},{6,2},{8,12},{10,14},{12,8},{14,10},{16,20},{18,... | collective-permute-start | bytes 3145736 | tf_op jit(solution)/shard_map/ppermute | solution.py:66
  384.9 43.0 %collective-permute-start.72 = (bf16[512,1024]{1,0:T(8,128)(2,1)}, bf16[512,1024]{1,0:T(8,128)(2,1)S(1)}, u32[]{:S(2)}, u32[]{:S(2)}) collective-permute-start(bf16[512,1024]{1,0:T(8,128)(2,1)} %get-tuple-element.224), channel_id=1, source_target_pairs={{0,1},{1,0},{2,3},{3,2},{4,5},{5,4},{6,7},{7,6},{8,9},{9,8},{10,11... | collective-permute-start | bytes 3145736 | tf_op jit(solution)/shard_map/ppermute | solution.py:83
  390.2 37.7 %collective-permute-start.78 = (bf16[2,128,1024]{2,1,0:T(8,128)(2,1)}, bf16[2,128,1024]{2,1,0:T(8,128)(2,1)S(1)}, u32[]{:S(2)}, u32[]{:S(2)}) collective-permute-start(bf16[2,128,1024]{2,1,0:T(8,128)(2,1)} %pad_maximum_fusion.7), channel_id=1, source_target_pairs={{0,8},{2,10},{4,12},{6,14},{8,0},{10,2},{12,4},{14,6},{16,24},{18,... | collective-permute-start | bytes 1572872 | tf_op jit(solution)/shard_map/ppermute | solution.py:66
  390.2 37.7 %collective-permute-start.77 = (bf16[2,128,1024]{2,1,0:T(8,128)(2,1)}, bf16[2,128,1024]{2,1,0:T(8,128)(2,1)S(1)}, u32[]{:S(2)}, u32[]{:S(2)}) collective-permute-start(bf16[2,128,1024]{2,1,0:T(8,128)(2,1)} %pad_maximum_fusion.6), channel_id=1, source_target_pairs={{0,24},{2,26},{4,28},{6,30},{8,16},{10,18},{12,20},{14,22},{16,8},... | collective-permute-start | bytes 1572872 | tf_op jit(solution)/shard_map/ppermute | solution.py:66
  391.2 36.7 %collective-permute-start.76 = (bf16[128,1024]{1,0:T(8,128)(2,1)S(1)}, bf16[128,1024]{1,0:T(8,128)(2,1)S(1)}, u32[]{:S(2)}, u32[]{:S(2)}) collective-permute-start(bf16[128,1024]{1,0:T(8,128)(2,1)S(1)} %get-tuple-element.233), channel_id=1, source_target_pairs={{0,16},{2,18},{4,20},{6,22},{8,24},{10,26},{12,28},{14,30},{16,0},... | collective-permute-start | bytes 786440 | tf_op jit(solution)/shard_map/ppermute | solution.py:66
  429.1 23.2 %collective-permute-start.87 = (bf16[8,128,1280]{2,1,0:T(8,128)(2,1)}, bf16[8,128,1280]{2,1,0:T(8,128)(2,1)S(1)}, u32[]{:S(2)}, u32[]{:S(2)}) collective-permute-start(bf16[8,128,1280]{2,1,0:T(8,128)(2,1)} %get-tuple-element.248), channel_id=1, source_target_pairs={{0,2},{2,0},{4,6},{6,4},{8,10},{10,8},{12,14},{14,12},{16,18},{18,... | collective-permute-start | bytes 7864328 | tf_op jit(solution)/shard_map/ppermute | solution.py:66
  431.2 21.0 %collective-permute-start.79 = (bf16[128,2048]{1,0:T(8,128)(2,1)S(1)}, bf16[128,2048]{1,0:T(8,128)(2,1)S(1)}, u32[]{:S(2)}, u32[]{:S(2)}) collective-permute-start(bf16[128,2048]{1,0:T(8,128)(2,1)S(1)} %pad_maximum_fusion.5), channel_id=1, source_target_pairs={{0,8},{2,10},{4,12},{6,14},{8,0},{10,2},{12,4},{14,6},{16,24},{18,... | collective-permute-start | bytes 1572872 | tf_op jit(solution)/shard_map/ppermute | solution.py:66
  433.5 36.8 %collective-permute-start.81 = (bf16[4,128,1280]{2,1,0:T(8,128)(2,1)S(1)}, bf16[4,128,1280]{2,1,0:T(8,128)(2,1)S(1)}, u32[]{:S(2)}, u32[]{:S(2)}) collective-permute-start(bf16[4,128,1280]{2,1,0:T(8,128)(2,1)S(1)} %fusion.4), channel_id=1, source_target_pairs={{0,4},{2,6},{4,0},{6,2},{8,12},{10,14},{12,8},{14,10},{16,20},{18,... | collective-permute-start | bytes 3932168 | tf_op jit(solution)/shard_map/ppermute | solution.py:66
  437.9 23.2 %collective-permute-start.82 = (bf16[128,1024]{1,0:T(8,128)(2,1)S(1)}, bf16[128,1024]{1,0:T(8,128)(2,1)S(1)}, u32[]{:S(2)}, u32[]{:S(2)}) collective-permute-start(bf16[128,1024]{1,0:T(8,128)(2,1)S(1)} %get-tuple-element.239), channel_id=1, source_target_pairs={{0,16},{2,18},{4,20},{6,22},{8,24},{10,26},{12,28},{14,30},{16,0},... | collective-permute-start | bytes 786440 | tf_op jit(solution)/shard_map/ppermute | solution.py:66
  470.2 33.0 %collective-permute-start.88 = (bf16[4,128,1280]{2,1,0:T(8,128)(2,1)S(1)}, bf16[4,128,1280]{2,1,0:T(8,128)(2,1)S(1)}, u32[]{:S(2)}, u32[]{:S(2)}) collective-permute-start(bf16[4,128,1280]{2,1,0:T(8,128)(2,1)S(1)} %fusion.5), channel_id=1, source_target_pairs={{0,4},{2,6},{4,0},{6,2},{8,12},{10,14},{12,8},{14,10},{16,20},{18,... | collective-permute-start | bytes 3932168 | tf_op jit(solution)/shard_map/ppermute | solution.py:66
  470.9 23.5 %collective-permute-start.85 = (bf16[128,2048]{1,0:T(8,128)(2,1)S(1)}, bf16[128,2048]{1,0:T(8,128)(2,1)S(1)}, u32[]{:S(2)}, u32[]{:S(2)}) collective-permute-start(bf16[128,2048]{1,0:T(8,128)(2,1)S(1)} %fusion.21), channel_id=1, source_target_pairs={{0,16},{2,18},{4,20},{6,22},{8,24},{10,26},{12,28},{14,30},{16,0},... | collective-permute-start | bytes 1572872 | tf_op jit(solution)/shard_map/ppermute | solution.py:66
  471.2 28.9 %collective-permute-start.89 = (bf16[2,128,1280]{2,1,0:T(8,128)(2,1)S(1)}, bf16[2,128,1280]{2,1,0:T(8,128)(2,1)S(1)}, u32[]{:S(2)}, u32[]{:S(2)}) collective-permute-start(bf16[2,128,1280]{2,1,0:T(8,128)(2,1)S(1)} %pad_maximum_fusion.1), channel_id=1, source_target_pairs={{0,8},{2,10},{4,12},{6,14},{8,0},{10,2},{12,4},{14,6},{16,24},{18,... | collective-permute-start | bytes 1966088 | tf_op jit(solution)/shard_map/ppermute | solution.py:66
  473.3 29.9 %collective-permute-start.90 = (bf16[128,1024]{1,0:T(8,128)(2,1)S(1)}, bf16[128,1024]{1,0:T(8,128)(2,1)S(1)}, u32[]{:S(2)}, u32[]{:S(2)}) collective-permute-start(bf16[128,1024]{1,0:T(8,128)(2,1)S(1)} %get-tuple-element.251), channel_id=1, source_target_pairs={{0,8},{2,10},{4,12},{6,14},{8,0},{10,2},{12,4},{14,6},{16,24},{18,... | collective-permute-start | bytes 786440 | tf_op jit(solution)/shard_map/ppermute | solution.py:66
  473.4 29.8 %collective-permute-start.86 = (bf16[128,2048]{1,0:T(8,128)(2,1)S(1)}, bf16[128,2048]{1,0:T(8,128)(2,1)S(1)}, u32[]{:S(2)}, u32[]{:S(2)}) collective-permute-start(bf16[128,2048]{1,0:T(8,128)(2,1)S(1)} %copy-done.81), channel_id=1, source_target_pairs={{0,1},{1,0},{2,3},{3,2},{4,5},{5,4},{6,7},{7,6},{8,9},{9,8},{10,11... | collective-permute-start | bytes 1572872 | tf_op jit(solution)/shard_map/ppermute | solution.py:83
  505.5 21.4 %collective-permute-start.94 = (bf16[2,128,1280]{2,1,0:T(8,128)(2,1)S(1)}, bf16[2,128,1280]{2,1,0:T(8,128)(2,1)S(1)}, u32[]{:S(2)}, u32[]{:S(2)}) collective-permute-start(bf16[2,128,1280]{2,1,0:T(8,128)(2,1)S(1)} %pad_maximum_fusion.2), channel_id=1, source_target_pairs={{0,8},{2,10},{4,12},{6,14},{8,0},{10,2},{12,4},{14,6},{16,24},{18,... | collective-permute-start | bytes 1966088 | tf_op jit(solution)/shard_map/ppermute | solution.py:66
  (164 other events, 2847.6 us)

commit v5 on v4

--- a/solution.py
+++ b/solution.py
@@ -586,8 +586,8 @@
             earlier = tuple(sent)
         return earlier
 
-    plane_three = at.across_z(after(shares[3][:2], low_first, *stage), 3)
-    plane_one = at.across_z(after(shares[1][:2], low_first, *stage), 1)
+    plane_three = at.across_z(after(shares[3][:2], *stage), 3)
+    plane_one = at.across_z(after(shares[1][:2], *stage), 1)
     grads_low[1, 1] = at.other_x(after(grads_low[1, 0], *stage))
     last = to_chips(0, [shares[0]], *stage)
 
@@ -606,7 +606,9 @@
             ((rows_own, inputs.shape[1]), low),
         ],
     )
-    branch_other = after(branch_other, plane_one, plane_three, grads_low[1, 1], *last)
+    branch_other = after(
+        branch_other, plane_one, plane_three, low_first, grads_low[1, 1], *last
+    )
     branch = branch_other
     state = inputs + branch_own + at.other_x(branch_other)
     scale_two = lax.rsqrt(jnp.mean(state * state, 1, keepdims=True) + EPSILON)
@@ -757,15 +759,15 @@
     gate_chips = [jnp.concatenate(parts, 0) for parts in zip(gate_lower, gate_upper, strict=True)]
     gate_terms = (gate_own, gate_arrived, gate_chips)
 
-    def both(mask):
-        return jnp.stack(
-            [of_plane(terms, mask).astype(jnp.bfloat16) for terms in (gate_terms, down_terms)]
-        )
+    def both(mask, *pair):
+        return jnp.stack([of_plane(terms, mask).astype(jnp.bfloat16) for terms in pair])
 
     down_pieces = send_planes(down_terms, (2,), stage)
-    late = [*stage, grad_state_other, down_pieces[2]]
-    gate_pieces = send_planes(gate_terms, (2,), late)
-    pair_pieces = {mask: at.across_z(after(both(mask), *late), mask) for mask in (3, 1)}
+    first_one = out_block(outs[0], block_of(out_first, 2), 2).astype(jnp.bfloat16)
+    first_one = at.across_z(after(first_one, *stage), 1)
+    late = [*stage, grad_state_other, down_pieces[2], first_one]
+    gate_pieces = send_planes(gate_terms, (2, 3), late)
+    gate_down = at.across_z(after(both(1, gate_terms, down_terms), *late), 1)
     up_chips = send_chips(for_chips(up_own, up_arrived), stage)
     up_terms = (up_own, up_arrived, up_chips)
 
@@ -792,9 +794,8 @@
             *[(shape, low)] * 4,
         ],
     )
-    stage = [qk_other, out_second, *up_chips, gate_pieces[2], *pair_pieces.values()]
-    for mask, piece in pair_pieces.items():
-        gate_pieces[mask], down_pieces[mask] = piece[0], piece[1]
+    stage = [qk_other, out_second, *up_chips, *gate_pieces.values(), gate_down]
+    gate_pieces[1], down_pieces[1] = gate_down[0], gate_down[1]
     out_blocks = [
         jnp.concatenate(
             [
@@ -852,13 +853,17 @@
     def total_of(name):
         return for_plane(name, 0) + pairs[name][0] + quarters[name]
 
-    up_pieces = send_planes(up_terms, (2, 3), stage)
+    up_pieces = send_planes(up_terms, (2,), stage)
+    up_down = at.across_z(after(both(3, up_terms, down_terms), *stage), 3)
+    up_pieces[3], down_pieces[3] = up_down[0], up_down[1]
     out_two = at.across_z(after(out_blocks[0].astype(jnp.bfloat16), *stage), 1)
     to_chips_of("qk", ())
 
-    out_one = at.across_z(after(out_blocks[2].astype(jnp.bfloat16), *stage), 1)
-
-    stage = [*chips["qk"], *up_pieces.values(), out_two, out_one]
+    middle = out_blocks[2].shape[1] // 2
+    second_one = at.across_z(after(out_blocks[2][:, middle:].astype(jnp.bfloat16), *stage), 1)
+    out_one = jnp.concatenate([first_one, second_one], 1)
+
+    stage = [*chips["qk"], up_pieces[2], up_down, out_two, second_one]
     normed_arrived = at.other_x(after(back_other, *stage))
     to_chips_of("vo", stage)
     to_pair("qk", stage)

time: 553 us -> 547 us (0.989)
  waiting for transfers between devices: 276 us -> 265 us
    ppermute x82 -> x83, waiting for transfers between devices: 231 us -> 216 us  [move(): return lax.ppermute(value, 'dp', [(d, target(d)) for d in range(self.dp)])]
    unnamed x198 -> x202, local copies, waits for them, and re-layouts: 10.5 us -> 13.8 us
    ppermute x82 -> x83, starting transfers between devices: 81.5 us -> 79.1 us  [move(): return lax.ppermute(value, 'dp', [(d, target(d)) for d in range(self.dp)])]
  transfers between devices with their start and end apart: 99 -> 100, of which waited for: 47 -> 49; matrix products, arithmetic and copies ran while one was open for 7% -> 9% of each run, Pallas kernels for 19% -> 19%
where the time goes in v5:
time: 547 us; the launch traced here: 537 us
  waiting for transfers between devices  265 us (48%)
  Pallas kernels  112 us (20%)
  starting transfers between devices  97.9 us (18%)
  other arithmetic  35.5 us (6%)
  local copies, waits for them, and re-layouts  24.9 us (5%)
    ppermute x83, waiting for transfers between devices, move(): return lax.ppermute(value, 'dp', [(d, target(d)) for d in range(self.dp)])  216 us
    ppermute x83, starting transfers between devices, move(): return lax.ppermute(value, 'dp', [(d, target(d)) for d in range(self.dp)])  79.1 us
    ppermute x17, waiting for transfers between devices, other_x(): return lax.ppermute(value, 'tensor', [(0, 1), (1, 0)])  48.8 us
    pallas_call x2, Pallas kernels, held_call(): pl.pallas_call(body, in_specs=[pl.BlockSpec(memory_space=pltpu.SMEM)] + [...  46 us
    pallas_call x2, Pallas kernels, attention_call(): pl.pallas_call(functools.partial(kernel, width_kv, keys), in_specs=[pl.Bl...  37.2 us
    pallas_call x3, Pallas kernels, weight_grad(): pl.pallas_call(weight_grad_kernel, grid_spec=pltpu.PrefetchScalarGridSpec...  26.8 us
    ppermute x17, starting transfers between devices, other_x(): return lax.ppermute(value, 'tensor', [(0, 1), (1, 0)])  18.8 us
    unnamed x202, local copies, waits for them, and re-layouts  13.8 us
  transfers between devices with their start and end apart: 100, of which 49 were waited for; matrix products, arithmetic and copies ran while one was open for 9% of the time, Pallas kernels for 19%

profile of v5, /device:TPU:0, one launch (start us, length us, event | category | flops | bytes accessed | tf_op | source)
XLA Modules:
  0.0 537.5 jit_solution(11498298066926817300)
XLA Ops:
  2.8 4.0 collective-permute-start.1
  14.4 11.3 %collective-permute-done.refs_1_.refs_3_ = bf16[128,2048]{1,0:T(8,128)(2,1)S(1)} collective-permute-done((bf16[128,2048]{1,0:T(8,128)(2,1)S(1)}, bf16[128,2048]{1,0:T(8,128)(2,1)S(1)}, u32[]{:S(2)}, u32[]{:S(2)}) %collective-permute-start) | collective-permute-done | bytes 524320 | tf_op jit(solution)/shard_map/ppermute | solution.py:83
  26.6 9.4 %collective-permute-done.1.refs_7_.refs_12_ = bf16[128,2560]{1,0:T(8,128)(2,1)} collective-permute-done((bf16[128,2560]{1,0:T(8,128)(2,1)}, bf16[128,2560]{1,0:T(8,128)(2,1)}, u32[]{:S(2)}, u32[]{:S(2)}) %collective-permute-start.1) | collective-permute-done | bytes 655392 | tf_op jit(solution)/shard_map/ppermute | solution.py:66
  42.8 9.7 %collective-permute-done.6 = bf16[1,128,1024]{2,1,0:T(8,128)(2,1)} collective-permute-done((bf16[1,128,1024]{2,1,0:T(8,128)(2,1)}, bf16[1,128,1024]{2,1,0:T(8,128)(2,1)}, u32[]{:S(2)}, u32[]{:S(2)}) %collective-permute-start.6) | collective-permute-done | bytes 262176 | tf_op jit(solution)/shard_map/ppermute | solution.py:66
  57.0 8.4 %collective-permute-done.12.refs_7_ = bf16[128,2048]{1,0:T(8,128)(2,1)} collective-permute-done((bf16[128,2048]{1,0:T(8,128)(2,1)S(1)}, bf16[128,2048]{1,0:T(8,128)(2,1)}, u32[]{:S(2)}, u32[]{:S(2)}) %collective-permute-start.12) | collective-permute-done | bytes 524320 | tf_op jit(solution)/shard_map/ppermute | solution.py:83
  65.9 4.8 collective-permute-done.13
  79.1 9.1 %collective-permute-done.19 = bf16[1,128,1024]{2,1,0:T(8,128)(2,1)S(1)} collective-permute-done((bf16[1,128,1024]{2,1,0:T(8,128)(2,1)S(1)}, bf16[1,128,1024]{2,1,0:T(8,128)(2,1)S(1)}, u32[]{:S(2)}, u32[]{:S(2)}) %collective-permute-start.19) | collective-permute-done | bytes 262176 | tf_op jit(solution)/shard_map/ppermute | solution.py:66
  100.9 16.1 %shard_map.187 = (bf16[256,1280]{1,0:T(8,128)(2,1)}, bf16[256,256]{1,0:T(8,128)(2,1)}, bf16[256,1024]{1,0:T(8,128)(2,1)}, f32[128,2048]{1,0:T(8,128)}, bf16[128,2048]{1,0:T(8,128)(2,1)}) custom-call(s32[5]{0:T(128)} %stack.113.place, bf16[128,2048]{1,0:T(8,128)(2,1)} %copy-done.41, bf16[128,2048]{1,0:T(8,128)(2,1)} %copy-done.74, ...), custom_call_target="tpu_custom_call" | custom-call | flops 4026531840 | bytes 14682112 | tf_op jit(solution)/shard_map/pallas_call | solution.py:463
  117.0 14.2 %collective-permute-done.23 = bf16[128,1024]{1,0:T(8,128)(2,1)S(1)} collective-permute-done((bf16[128,1024]{1,0:T(8,128)(2,1)S(1)}, bf16[128,1024]{1,0:T(8,128)(2,1)S(1)}, u32[]{:S(2)}, u32[]{:S(2)}) %collective-permute-start.23) | collective-permute-done | bytes 262176 | tf_op jit(solution)/shard_map/ppermute | solution.py:66
  138.5 6.8 %collective-permute-done.26 = bf16[128,2048]{1,0:T(8,128)(2,1)S(1)} collective-permute-done((bf16[128,2048]{1,0:T(8,128)(2,1)}, bf16[128,2048]{1,0:T(8,128)(2,1)S(1)}, u32[]{:S(2)}, u32[]{:S(2)}) %collective-permute-start.26) | collective-permute-done | bytes 524320 | tf_op jit(solution)/shard_map/ppermute | solution.py:83
  146.1 5.8 %collective-permute-done.29 = bf16[128,1024]{1,0:T(8,128)(2,1)S(1)} collective-permute-done((bf16[128,1024]{1,0:T(8,128)(2,1)}, bf16[128,1024]{1,0:T(8,128)(2,1)S(1)}, u32[]{:S(2)}, u32[]{:S(2)}) %collective-permute-start.29) | collective-permute-done | bytes 262176 | tf_op jit(solution)/shard_map/ppermute | solution.py:66
  156.6 4.8 collective-permute-start.30
  161.3 4.5 collective-permute-done.31.refs_7_
  168.3 15.8 %collective-permute-done.30.refs_2_ = bf16[128,2048]{1,0:T(8,128)(2,1)S(1)} collective-permute-done((bf16[128,2048]{1,0:T(8,128)(2,1)S(1)}, bf16[128,2048]{1,0:T(8,128)(2,1)S(1)}, u32[]{:S(2)}, u32[]{:S(2)}) %collective-permute-start.30) | collective-permute-done | bytes 524320 | tf_op jit(solution)/shard_map/ppermute | solution.py:66
  189.5 5.6 %collective-permute-done.41.refs_24_.refs_26_ = bf16[1,128,1024]{2,1,0:T(8,128)(2,1)S(1)} collective-permute-done((bf16[1,128,1024]{2,1,0:T(8,128)(2,1)S(1)}, bf16[1,128,1024]{2,1,0:T(8,128)(2,1)S(1)}, u32[]{:S(2)}, u32[]{:S(2)}) %collective-permute-start.41) | collective-permute-done | bytes 262176 | tf_op jit(solution)/shard_map/ppermute | solution.py:66
  199.4 8.7 %collective-permute-done.37.refs_0_ = bf16[128,2048]{1,0:T(8,128)(2,1)S(1)} collective-permute-done((bf16[128,2048]{1,0:T(8,128)(2,1)S(1)}, bf16[128,2048]{1,0:T(8,128)(2,1)S(1)}, u32[]{:S(2)}, u32[]{:S(2)}) %collective-permute-start.37) | collective-permute-done | bytes 524320 | tf_op jit(solution)/shard_map/ppermute | solution.py:66
  215.5 10.2 %collective-permute-done.42.refs_1_ = bf16[128,2048]{1,0:T(8,128)(2,1)S(1)} collective-permute-done((bf16[128,2048]{1,0:T(8,128)(2,1)S(1)}, bf16[128,2048]{1,0:T(8,128)(2,1)S(1)}, u32[]{:S(2)}, u32[]{:S(2)}) %collective-permute-start.42) | collective-permute-done | bytes 524320 | tf_op jit(solution)/shard_map/ppermute | solution.py:83
  230.7 23.9 %shard_map.188 = (bf16[1024,1024]{1,0:T(8,128)(2,1)}, bf16[1024,1024]{1,0:T(8,128)(2,1)}, bf16[1024,1024]{1,0:T(8,128)(2,1)}, bf16[512,1024]{1,0:T(8,128)(2,1)},...) custom-call(s32[4]{0:T(128)} %pad_add_fusion.1.place, ...), custom_call_target="tpu_custom_call" | custom-call | flops 12884901888 | bytes 27262976 | tf_op jit(solution)/shard_map/pallas_call | solution.py:147
  254.6 9.2 %shard_map.189 = (bf16[2,4,128,1024]{3,2,1,0:T(8,128)(2,1)}, bf16[2,4,128,1024]{3,2,1,0:T(8,128)(2,1)}) custom-call(s32[1]{0:T(128)} %bitcast.1.place, bf16[128,2048]{1,0:T(8,128)(2,1)} %collective-permute-done.39.refs_0_, bf16[128,2048]{1,0:T(8,128)(2,1)} %collective-permute-done.57.refs_1_, bf16[128,2048]{1,0:T(8,128)(2,1)} %copy-done.56, ...), custom_call_target="tpu_custom_call" | custom-call | flops 4294967296 | bytes 10485760 | tf_op jit(solution)/shard_map/pallas_call | solution.py:261
  272.0 22.1 %shard_map.190 = (bf16[1024,1024]{1,0:T(8,128)(2,1)}, bf16[1024,1024]{1,0:T(8,128)(2,1)}, bf16[128,2048]{1,0:T(8,128)(2,1)}, bf16[128,2048]{1,0:T(8,128)(2,1)}, ...) custom-call(s32[4]{0:T(128)} %pad_add_fusion.1.place, ...), custom_call_target="tpu_custom_call" | custom-call | flops 12884901888 | bytes 29360128 | tf_op jit(solution)/shard_map/pallas_call | solution.py:147
  298.0 8.8 %shard_map.191 = (bf16[2,4,128,1024]{3,2,1,0:T(8,128)(2,1)}, bf16[2,4,128,1024]{3,2,1,0:T(8,128)(2,1)}) custom-call(s32[1]{0:T(128)} %bitcast.1.place, bf16[128,2048]{1,0:T(8,128)(2,1)} %copy-done.78, bf16[128,2048]{1,0:T(8,128)(2,1)} %copy-done.83, bf16[128,2048]{1,0:T(8,128)(2,1)} %copy-done.76, bf16[128,2048]{1,0:T(8,128)(2,1)} %copy-done.79, ...), custom_call_target="tpu_custom_call" | custom-call | flops 4294967296 | bytes 10485760 | tf_op jit(solution)/shard_map/pallas_call | solution.py:261
  312.3 8.8 %shard_map.192 = (bf16[2,4,128,1024]{3,2,1,0:T(8,128)(2,1)}, bf16[2,4,128,1024]{3,2,1,0:T(8,128)(2,1)}) custom-call(s32[1]{0:T(128)} %bitcast.1.place, bf16[128,2048]{1,0:T(8,128)(2,1)} %copy-done.78, bf16[128,2048]{1,0:T(8,128)(2,1)} %copy-done.83, bf16[128,2048]{1,0:T(8,128)(2,1)} %copy-done.76, bf16[128,2048]{1,0:T(8,128)(2,1)} %copy-done.79, ...), custom_call_target="tpu_custom_call" | custom-call | flops 4294967296 | bytes 10485760 | tf_op jit(solution)/shard_map/pallas_call | solution.py:261
  332.7 13.6 %collective-permute-done.66 = bf16[128,1024]{1,0:T(8,128)(2,1)S(1)} collective-permute-done((bf16[128,1024]{1,0:T(8,128)(2,1)S(1)}, bf16[128,1024]{1,0:T(8,128)(2,1)S(1)}, u32[]{:S(2)}, u32[]{:S(2)}) %collective-permute-start.66) | collective-permute-done | bytes 262176 | tf_op jit(solution)/shard_map/ppermute | solution.py:66
  352.3 12.2 %collective-permute-done.70 = bf16[128,1024]{1,0:T(8,128)(2,1)S(1)} collective-permute-done((bf16[128,1024]{1,0:T(8,128)(2,1)}, bf16[128,1024]{1,0:T(8,128)(2,1)S(1)}, u32[]{:S(2)}, u32[]{:S(2)}) %collective-permute-start.70) | collective-permute-done | bytes 262176 | tf_op jit(solution)/shard_map/ppermute | solution.py:66
  394.8 21.1 %shard_map.193 = (f32[128,2048]{1,0:T(8,128)}, bf16[128,2048]{1,0:T(8,128)(2,1)}, bf16[8,128,1280]{2,1,0:T(8,128)(2,1)}, bf16[8,128,1280]{2,1,0:T(8,128)(2,1)}, ...) custom-call(s32[5]{0:T(128)} %stack.113.place, bf16[128,2048]{1,0:T(8,128)(2,1)} %copy-done.33, ...), custom_call_target="tpu_custom_call" | custom-call | flops 7381975040 | bytes 26216448 | tf_op jit(solution)/shard_map/pallas_call | solution.py:463
  428.7 5.3 collective-permute-done.80
  439.3 24.2 %collective-permute-done.83 = bf16[128,1024]{1,0:T(8,128)(2,1)S(1)} collective-permute-done((bf16[128,1024]{1,0:T(8,128)(2,1)S(1)}, bf16[128,1024]{1,0:T(8,128)(2,1)S(1)}, u32[]{:S(2)}, u32[]{:S(2)}) %collective-permute-start.83) | collective-permute-done | bytes 262176 | tf_op jit(solution)/shard_map/ppermute | solution.py:66
  468.2 20.0 %collective-permute-done.86 = bf16[128,2048]{1,0:T(8,128)(2,1)S(1)} collective-permute-done((bf16[128,2048]{1,0:T(8,128)(2,1)S(1)}, bf16[128,2048]{1,0:T(8,128)(2,1)S(1)}, u32[]{:S(2)}, u32[]{:S(2)}) %collective-permute-start.86) | collective-permute-done | bytes 524320 | tf_op jit(solution)/shard_map/ppermute | solution.py:66
  489.3 4.8 collective-permute-done.90
  506.6 4.7 collective-permute-done.96
  513.0 6.7 %collective-permute-done.95 = bf16[2,128,1280]{2,1,0:T(8,128)(2,1)S(1)} collective-permute-done((bf16[2,128,1280]{2,1,0:T(8,128)(2,1)S(1)}, bf16[2,128,1280]{2,1,0:T(8,128)(2,1)S(1)}, u32[]{:S(2)}, u32[]{:S(2)}) %collective-permute-start.95) | collective-permute-done | bytes 655392 | tf_op jit(solution)/shard_map/ppermute | solution.py:66
  528.3 6.4 %collective-permute-done.98 = f32[2,2048]{1,0:T(2,128)S(1)} collective-permute-done((f32[2,2048]{1,0:T(2,128)S(1)}, f32[2,2048]{1,0:T(2,128)S(1)}, u32[]{:S(2)}, u32[]{:S(2)}) %collective-permute-start.98) | collective-permute-done | bytes 16416 | tf_op jit(solution)/shard_map/ppermute | solution.py:66
  (474 shorter events, 193.8 us)
Async XLA Ops:
  2.8 33.2 %collective-permute-start.1 = (bf16[128,2560]{1,0:T(8,128)(2,1)}, bf16[128,2560]{1,0:T(8,128)(2,1)}, u32[]{:S(2)}, u32[]{:S(2)}) collective-permute-start(bf16[128,2560]{1,0:T(8,128)(2,1)} %shard_map.186.refs_6_.refs_11_), channel_id=1, source_target_pairs={{0,16},{2,18},{4,20},{6,22},{8,24},{10,26},{12,28},{14,30},{16,0},... | collective-permute-start | bytes 1966088 | tf_op jit(solution)/shard_map/ppermute | solution.py:66
  6.8 29.4 %collective-permute-start.2 = (bf16[128,2560]{1,0:T(8,128)(2,1)}, bf16[128,2560]{1,0:T(8,128)(2,1)}, u32[]{:S(2)}, u32[]{:S(2)}) collective-permute-start(bf16[128,2560]{1,0:T(8,128)(2,1)} %shard_map.186.refs_6_.refs_11_), channel_id=1, source_target_pairs={{0,8},{2,10},{4,12},{6,14},{8,0},{10,2},{12,4},{14,6},{16,24},{18,... | collective-permute-start | bytes 1966088 | tf_op jit(solution)/shard_map/ppermute | solution.py:66
  8.4 27.8 %collective-permute-start.3 = (bf16[128,2560]{1,0:T(8,128)(2,1)}, bf16[128,2560]{1,0:T(8,128)(2,1)}, u32[]{:S(2)}, u32[]{:S(2)}) collective-permute-start(bf16[128,2560]{1,0:T(8,128)(2,1)} %shard_map.186.refs_6_.refs_11_), channel_id=1, source_target_pairs={{0,4},{2,6},{4,0},{6,2},{8,12},{10,14},{12,8},{14,10},{16,20},{18,... | collective-permute-start | bytes 1966088 | tf_op jit(solution)/shard_map/ppermute | solution.py:66
  40.3 25.0 %collective-permute-start.4 = (bf16[128,2560]{1,0:T(8,128)(2,1)}, bf16[128,2560]{1,0:T(8,128)(2,1)S(1)}, u32[]{:S(2)}, u32[]{:S(2)}) collective-permute-start(bf16[128,2560]{1,0:T(8,128)(2,1)} %collective-permute-done.1.refs_7_.refs_12_), channel_id=1, source_target_pairs={{0,8},{2,10},{4,12},{6,14},{8,0},{10,2},{12,4},{14,6},{16,24},{18,... | collective-permute-start | bytes 1966088 | tf_op jit(solution)/shard_map/ppermute | solution.py:66
  55.2 20.5 %collective-permute-start.8 = (bf16[128,2560]{1,0:T(8,128)(2,1)}, bf16[128,2560]{1,0:T(8,128)(2,1)S(1)}, u32[]{:S(2)}, u32[]{:S(2)}) collective-permute-start(bf16[128,2560]{1,0:T(8,128)(2,1)} %shard_map.186.refs_6_.refs_11_), channel_id=1, source_target_pairs={{0,2},{2,0},{4,6},{6,4},{8,10},{10,8},{12,14},{14,12},{16,18},{18,... | collective-permute-start | bytes 1966088 | tf_op jit(solution)/shard_map/ppermute | solution.py:66
  91.7 39.5 %collective-permute-start.25 = (bf16[3,128,1024]{2,1,0:T(8,128)(2,1)S(1)}, bf16[3,128,1024]{2,1,0:T(8,128)(2,1)}, u32[]{:S(2)}, u32[]{:S(2)}) collective-permute-start(bf16[3,128,1024]{2,1,0:T(8,128)(2,1)S(1)} %pad_maximum_fusion.refs_8_.refs_10_), channel_id=1, source_target_pairs={{0,4},{2,6},{4,0},{6,2},{8,12},{10,14},{12,8},{14,10},{16,20},{18,... | collective-permute-start | bytes 2359304 | tf_op jit(solution)/shard_map/ppermute | solution.py:66
  92.5 38.7 %collective-permute-start.24 = (bf16[128,2048]{1,0:T(8,128)(2,1)}, bf16[128,2048]{1,0:T(8,128)(2,1)}, u32[]{:S(2)}, u32[]{:S(2)}) collective-permute-start(bf16[128,2048]{1,0:T(8,128)(2,1)} %collective-permute-done.20.refs_4_), channel_id=1, source_target_pairs={{0,1},{1,0},{2,3},{3,2},{4,5},{5,4},{6,7},{7,6},{8,9},{9,8},{10,11... | collective-permute-start | bytes 1572872 | tf_op jit(solution)/shard_map/ppermute | solution.py:83
  93.1 38.1 %collective-permute-start.22 = (bf16[2,128,1024]{2,1,0:T(8,128)(2,1)}, bf16[2,128,1024]{2,1,0:T(8,128)(2,1)}, u32[]{:S(2)}, u32[]{:S(2)}) collective-permute-start(bf16[2,128,1024]{2,1,0:T(8,128)(2,1)} %get-tuple-element.158), channel_id=1, source_target_pairs={{0,24},{2,26},{4,28},{6,30},{8,16},{10,18},{12,20},{14,22},{16,8},... | collective-permute-start | bytes 1572872 | tf_op jit(solution)/shard_map/ppermute | solution.py:66
  96.2 35.0 %collective-permute-start.21 = (bf16[2,128,1024]{2,1,0:T(8,128)(2,1)S(1)}, bf16[2,128,1024]{2,1,0:T(8,128)(2,1)}, u32[]{:S(2)}, u32[]{:S(2)}) collective-permute-start(bf16[2,128,1024]{2,1,0:T(8,128)(2,1)S(1)} %get-tuple-element.157), channel_id=1, source_target_pairs={{0,8},{2,10},{4,12},{6,14},{8,0},{10,2},{12,4},{14,6},{16,24},{18,... | collective-permute-start | bytes 1572872 | tf_op jit(solution)/shard_map/ppermute | solution.py:66
  100.0 31.2 %collective-permute-start.23 = (bf16[128,1024]{1,0:T(8,128)(2,1)S(1)}, bf16[128,1024]{1,0:T(8,128)(2,1)S(1)}, u32[]{:S(2)}, u32[]{:S(2)}) collective-permute-start(bf16[128,1024]{1,0:T(8,128)(2,1)S(1)} %get-tuple-element.159), channel_id=1, source_target_pairs={{0,16},{2,18},{4,20},{6,22},{8,24},{10,26},{12,28},{14,30},{16,0},... | collective-permute-start | bytes 786440 | tf_op jit(solution)/shard_map/ppermute | solution.py:66
  156.6 27.5 %collective-permute-start.30 = (bf16[128,2048]{1,0:T(8,128)(2,1)S(1)}, bf16[128,2048]{1,0:T(8,128)(2,1)S(1)}, u32[]{:S(2)}, u32[]{:S(2)}) collective-permute-start(bf16[128,2048]{1,0:T(8,128)(2,1)S(1)} %multiply_convert_fusion.refs_6_), channel_id=1, source_target_pairs={{0,16},{2,18},{4,20},{6,22},{8,24},{10,26},{12,28},{14,30},{16,0},... | collective-permute-start | bytes 1572872 | tf_op jit(solution)/shard_map/ppermute | solution.py:66
  161.3 23.0 %collective-permute-start.32 = (bf16[128,2048]{1,0:T(8,128)(2,1)S(1)}, bf16[128,2048]{1,0:T(8,128)(2,1)S(1)}, u32[]{:S(2)}, u32[]{:S(2)}) collective-permute-start(bf16[128,2048]{1,0:T(8,128)(2,1)S(1)} %multiply_convert_fusion.refs_6_), channel_id=1, source_target_pairs={{0,8},{2,10},{4,12},{6,14},{8,0},{10,2},{12,4},{14,6},{16,24},{18,... | collective-permute-start | bytes 1572872 | tf_op jit(solution)/shard_map/ppermute | solution.py:66
  188.5 19.7 %collective-permute-start.38 = (bf16[128,2048]{1,0:T(8,128)(2,1)S(1)}, bf16[128,2048]{1,0:T(8,128)(2,1)S(1)}, u32[]{:S(2)}, u32[]{:S(2)}) collective-permute-start(bf16[128,2048]{1,0:T(8,128)(2,1)S(1)} %collective-permute-done.30.refs_2_), channel_id=1, source_target_pairs={{0,1},{1,0},{2,3},{3,2},{4,5},{5,4},{6,7},{7,6},{8,9},{9,8},{10,11... | collective-permute-start | bytes 1572872 | tf_op jit(solution)/shard_map/ppermute | solution.py:83
  227.2 27.4 %collective-permute-start.57 = (bf16[128,2048]{1,0:T(8,128)(2,1)}, bf16[128,2048]{1,0:T(8,128)(2,1)}, u32[]{:S(2)}, u32[]{:S(2)}) collective-permute-start(bf16[128,2048]{1,0:T(8,128)(2,1)} %collective-permute-done.39.refs_0_), channel_id=1, source_target_pairs={{0,1},{1,0},{2,3},{3,2},{4,5},{5,4},{6,7},{7,6},{8,9},{9,8},{10,11... | collective-permute-start | bytes 1572872 | tf_op jit(solution)/shard_map/ppermute | solution.py:83
  264.1 30.1 %collective-permute-start.56 = (bf16[512,1024]{1,0:T(8,128)(2,1)S(1)}, bf16[512,1024]{1,0:T(8,128)(2,1)S(1)}, u32[]{:S(2)}, u32[]{:S(2)}) collective-permute-start(bf16[512,1024]{1,0:T(8,128)(2,1)S(1)} %copy-done.59), channel_id=1, source_target_pairs={{0,1},{1,0},{2,3},{3,2},{4,5},{5,4},{6,7},{7,6},{8,9},{9,8},{10,11... | collective-permute-start | bytes 3145736 | tf_op jit(solution)/shard_map/ppermute | solution.py:83
  270.3 25.3 %collective-permute-start.59 = (bf16[4,128,1024]{2,1,0:T(8,128)(2,1)S(1)}, bf16[4,128,1024]{2,1,0:T(8,128)(2,1)S(1)}, u32[]{:S(2)}, u32[]{:S(2)}) collective-permute-start(bf16[4,128,1024]{2,1,0:T(8,128)(2,1)S(1)} %fusion.15), channel_id=1, source_target_pairs={{0,4},{2,6},{4,0},{6,2},{8,12},{10,14},{12,8},{14,10},{16,20},{18,... | collective-permute-start | bytes 3145736 | tf_op jit(solution)/shard_map/ppermute | solution.py:66
  325.6 21.5 %collective-permute-start.68 = (bf16[2,4,128,1024]{3,2,1,0:T(8,128)(2,1)}, bf16[2,4,128,1024]{3,2,1,0:T(8,128)(2,1)}, u32[]{:S(2)}, u32[]{:S(2)}) collective-permute-start(bf16[2,4,128,1024]{3,2,1,0:T(8,128)(2,1)} %get-tuple-element.222), channel_id=1, source_target_pairs={{0,2},{2,0},{4,6},{6,4},{8,10},{10,8},{12,14},{14,12},{16,18},{18,... | collective-permute-start | bytes 6291464 | tf_op jit(solution)/shard_map/ppermute | solution.py:66
  350.9 26.5 %collective-permute-start.73 = (bf16[2,128,1024]{2,1,0:T(8,128)(2,1)S(1)}, bf16[2,128,1024]{2,1,0:T(8,128)(2,1)S(1)}, u32[]{:S(2)}, u32[]{:S(2)}) collective-permute-start(bf16[2,128,1024]{2,1,0:T(8,128)(2,1)S(1)} %copy-done.42), channel_id=1, source_target_pairs={{0,4},{2,6},{4,0},{6,2},{8,12},{10,14},{12,8},{14,10},{16,20},{18,... | collective-permute-start | bytes 1572872 | tf_op jit(solution)/shard_map/ppermute | solution.py:66
  379.3 36.6 %collective-permute-start.76 = (bf16[4,128,1024]{2,1,0:T(8,128)(2,1)}, bf16[4,128,1024]{2,1,0:T(8,128)(2,1)}, u32[]{:S(2)}, u32[]{:S(2)}) collective-permute-start(bf16[4,128,1024]{2,1,0:T(8,128)(2,1)} %fusion.16), channel_id=1, source_target_pairs={{0,4},{2,6},{4,0},{6,2},{8,12},{10,14},{12,8},{14,10},{16,20},{18,... | collective-permute-start | bytes 3145736 | tf_op jit(solution)/shard_map/ppermute | solution.py:66
  383.0 32.9 %collective-permute-start.72 = (bf16[512,1024]{1,0:T(8,128)(2,1)}, bf16[512,1024]{1,0:T(8,128)(2,1)S(1)}, u32[]{:S(2)}, u32[]{:S(2)}) collective-permute-start(bf16[512,1024]{1,0:T(8,128)(2,1)} %get-tuple-element.225), channel_id=1, source_target_pairs={{0,1},{1,0},{2,3},{3,2},{4,5},{5,4},{6,7},{7,6},{8,9},{9,8},{10,11... | collective-permute-start | bytes 3145736 | tf_op jit(solution)/shard_map/ppermute | solution.py:83
  391.3 24.6 %collective-permute-start.79 = (bf16[2,128,1024]{2,1,0:T(8,128)(2,1)}, bf16[2,128,1024]{2,1,0:T(8,128)(2,1)S(1)}, u32[]{:S(2)}, u32[]{:S(2)}) collective-permute-start(bf16[2,128,1024]{2,1,0:T(8,128)(2,1)} %pad_maximum_fusion.6), channel_id=1, source_target_pairs={{0,8},{2,10},{4,12},{6,14},{8,0},{10,2},{12,4},{14,6},{16,24},{18,... | collective-permute-start | bytes 1572872 | tf_op jit(solution)/shard_map/ppermute | solution.py:66
  391.5 24.3 %collective-permute-start.78 = (bf16[128,1024]{1,0:T(8,128)(2,1)}, bf16[128,1024]{1,0:T(8,128)(2,1)S(1)}, u32[]{:S(2)}, u32[]{:S(2)}) collective-permute-start(bf16[128,1024]{1,0:T(8,128)(2,1)} %get-tuple-element.236), channel_id=1, source_target_pairs={{0,24},{2,26},{4,28},{6,30},{8,16},{10,18},{12,20},{14,22},{16,8},... | collective-permute-start | bytes 786440 | tf_op jit(solution)/shard_map/ppermute | solution.py:66
  393.6 22.2 %collective-permute-start.77 = (bf16[128,1024]{1,0:T(8,128)(2,1)S(1)}, bf16[128,1024]{1,0:T(8,128)(2,1)S(1)}, u32[]{:S(2)}, u32[]{:S(2)}) collective-permute-start(bf16[128,1024]{1,0:T(8,128)(2,1)S(1)} %get-tuple-element.235), channel_id=1, source_target_pairs={{0,16},{2,18},{4,20},{6,22},{8,24},{10,26},{12,28},{14,30},{16,0},... | collective-permute-start | bytes 786440 | tf_op jit(solution)/shard_map/ppermute | solution.py:66
  421.4 42.1 %collective-permute-start.82 = (bf16[4,128,1280]{2,1,0:T(8,128)(2,1)S(1)}, bf16[4,128,1280]{2,1,0:T(8,128)(2,1)S(1)}, u32[]{:S(2)}, u32[]{:S(2)}) collective-permute-start(bf16[4,128,1280]{2,1,0:T(8,128)(2,1)S(1)} %fusion.4), channel_id=1, source_target_pairs={{0,4},{2,6},{4,0},{6,2},{8,12},{10,14},{12,8},{14,10},{16,20},{18,... | collective-permute-start | bytes 3932168 | tf_op jit(solution)/shard_map/ppermute | solution.py:66
  427.0 36.4 %collective-permute-start.84 = (bf16[2,128,1024]{2,1,0:T(8,128)(2,1)S(1)}, bf16[2,128,1024]{2,1,0:T(8,128)(2,1)S(1)}, u32[]{:S(2)}, u32[]{:S(2)}) collective-permute-start(bf16[2,128,1024]{2,1,0:T(8,128)(2,1)S(1)} %pad_maximum_fusion.7), channel_id=1, source_target_pairs={{0,24},{2,26},{4,28},{6,30},{8,16},{10,18},{12,20},{14,22},{16,8},... | collective-permute-start | bytes 1572872 | tf_op jit(solution)/shard_map/ppermute | solution.py:66
  434.0 29.5 %collective-permute-start.83 = (bf16[128,1024]{1,0:T(8,128)(2,1)S(1)}, bf16[128,1024]{1,0:T(8,128)(2,1)S(1)}, u32[]{:S(2)}, u32[]{:S(2)}) collective-permute-start(bf16[128,1024]{1,0:T(8,128)(2,1)S(1)} %get-tuple-element.241), channel_id=1, source_target_pairs={{0,16},{2,18},{4,20},{6,22},{8,24},{10,26},{12,28},{14,30},{16,0},... | collective-permute-start | bytes 786440 | tf_op jit(solution)/shard_map/ppermute | solution.py:66
  463.5 33.7 %collective-permute-start.89 = (bf16[4,128,1280]{2,1,0:T(8,128)(2,1)S(1)}, bf16[4,128,1280]{2,1,0:T(8,128)(2,1)S(1)}, u32[]{:S(2)}, u32[]{:S(2)}) collective-permute-start(bf16[4,128,1280]{2,1,0:T(8,128)(2,1)S(1)} %fusion.5), channel_id=1, source_target_pairs={{0,4},{2,6},{4,0},{6,2},{8,12},{10,14},{12,8},{14,10},{16,20},{18,... | collective-permute-start | bytes 3932168 | tf_op jit(solution)/shard_map/ppermute | solution.py:66
  464.0 24.2 %collective-permute-start.86 = (bf16[128,2048]{1,0:T(8,128)(2,1)S(1)}, bf16[128,2048]{1,0:T(8,128)(2,1)S(1)}, u32[]{:S(2)}, u32[]{:S(2)}) collective-permute-start(bf16[128,2048]{1,0:T(8,128)(2,1)S(1)} %fusion.21), channel_id=1, source_target_pairs={{0,16},{2,18},{4,20},{6,22},{8,24},{10,26},{12,28},{14,30},{16,0},... | collective-permute-start | bytes 1572872 | tf_op jit(solution)/shard_map/ppermute | solution.py:66
  464.4 29.8 %collective-permute-start.90 = (bf16[2,128,1280]{2,1,0:T(8,128)(2,1)S(1)}, bf16[2,128,1280]{2,1,0:T(8,128)(2,1)S(1)}, u32[]{:S(2)}, u32[]{:S(2)}) collective-permute-start(bf16[2,128,1280]{2,1,0:T(8,128)(2,1)S(1)} %pad_maximum_fusion.1), channel_id=1, source_target_pairs={{0,8},{2,10},{4,12},{6,14},{8,0},{10,2},{12,4},{14,6},{16,24},{18,... | collective-permute-start | bytes 1966088 | tf_op jit(solution)/shard_map/ppermute | solution.py:66
  467.4 29.8 %collective-permute-start.91 = (bf16[128,1024]{1,0:T(8,128)(2,1)S(1)}, bf16[128,1024]{1,0:T(8,128)(2,1)S(1)}, u32[]{:S(2)}, u32[]{:S(2)}) collective-permute-start(bf16[128,1024]{1,0:T(8,128)(2,1)S(1)} %get-tuple-element.253), channel_id=1, source_target_pairs={{0,8},{2,10},{4,12},{6,14},{8,0},{10,2},{12,4},{14,6},{16,24},{18,... | collective-permute-start | bytes 786440 | tf_op jit(solution)/shard_map/ppermute | solution.py:66
  467.5 29.7 %collective-permute-start.87 = (bf16[128,2048]{1,0:T(8,128)(2,1)S(1)}, bf16[128,2048]{1,0:T(8,128)(2,1)S(1)}, u32[]{:S(2)}, u32[]{:S(2)}) collective-permute-start(bf16[128,2048]{1,0:T(8,128)(2,1)S(1)} %copy-done.85), channel_id=1, source_target_pairs={{0,1},{1,0},{2,3},{3,2},{4,5},{5,4},{6,7},{7,6},{8,9},{9,8},{10,11... | collective-permute-start | bytes 1572872 | tf_op jit(solution)/shard_map/ppermute | solution.py:83
  498.7 21.0 %collective-permute-start.95 = (bf16[2,128,1280]{2,1,0:T(8,128)(2,1)S(1)}, bf16[2,128,1280]{2,1,0:T(8,128)(2,1)S(1)}, u32[]{:S(2)}, u32[]{:S(2)}) collective-permute-start(bf16[2,128,1280]{2,1,0:T(8,128)(2,1)S(1)} %pad_maximum_fusion.2), channel_id=1, source_target_pairs={{0,8},{2,10},{4,12},{6,14},{8,0},{10,2},{12,4},{14,6},{16,24},{18,... | collective-permute-start | bytes 1966088 | tf_op jit(solution)/shard_map/ppermute | solution.py:66
  (167 other events, 2752.0 us)

commit v6 on v5

--- a/solution.py
+++ b/solution.py
@@ -730,21 +730,13 @@
 
     stage = [to_two, two, gate_arrived, up_own]
     for_zero = (sum_of(1, two) + to_two).astype(jnp.bfloat16)
-    middle = for_zero.shape[1] // 2
-    to_zero_first = at.across_z(after(for_zero[:, :middle], *stage), 2)
+    to_zero = at.across_z(after(for_zero, *stage), 2)
     other_zero = (back[7].astype(jnp.float32) + one).astype(jnp.bfloat16)
     zero = at.other_x(after(other_zero, *stage))
-    gate_away = for_chips(gate_own, gate_arrived)
-    lower = at.planes // 2
-    gate_lower = send_chips([away[:lower] for away in gate_away], stage)
+    from_one = at.across_z(after(back[4], *stage), 1)
+    gate_chips = send_chips(for_chips(gate_own, gate_arrived), stage)
     up_arrived = at.other_core(after(up_other, *stage))
 
-    stage = [zero, to_zero_first, *gate_lower, up_arrived]
-    to_zero_second = at.across_z(after(for_zero[:, middle:], *stage), 2)
-    from_one = at.across_z(after(back[4], *stage), 1)
-    gate_upper = send_chips([away[lower:] for away in gate_away], stage)
-
-    to_zero = jnp.concatenate([to_zero_first, to_zero_second], 1)
     grad_normed_two = sum_of(3, zero) + from_one + to_zero
     hat_two = state * scale_two
     inner_two = grad_normed_two * gain_rows[1]
@@ -755,8 +747,7 @@
     grad_state_own = grad_state.astype(jnp.bfloat16)
 
     grad_state_other = at.other_x(grad_state_own)
-    stage = [grad_state_own, *gate_upper]
-    gate_chips = [jnp.concatenate(parts, 0) for parts in zip(gate_lower, gate_upper, strict=True)]
+    stage = [grad_state_own, *gate_chips]
     gate_terms = (gate_own, gate_arrived, gate_chips)
 
     def both(mask, *pair):

time: 547 us -> 529 us (0.967)
  waiting for transfers between devices: 265 us -> 255 us
  local copies, waits for them, and re-layouts: 24.9 us -> 15.2 us
    ppermute x83 -> x81, waiting for transfers between devices: 216 us -> 199 us  [move(): return lax.ppermute(value, 'dp', [(d, target(d)) for d in range(self.dp)])]
    unnamed x202 -> x189, local copies, waits for them, and re-layouts: 13.8 us -> 5.26 us
    ppermute x17, waiting for transfers between devices: 48.8 us -> 57 us  [other_x(): return lax.ppermute(value, 'tensor', [(0, 1), (1, 0)])]
    ppermute x83 -> x81, starting transfers between devices: 79.1 us -> 77.1 us  [move(): return lax.ppermute(value, 'dp', [(d, target(d)) for d in range(self.dp)])]
  transfers between devices with their start and end apart: 100 -> 98, of which waited for: 49 -> 47; matrix products, arithmetic and copies ran while one was open for 9% -> 9% of each run, Pallas kernels for 19% -> 19%
where the time goes in v6:
time: 529 us; the launch traced here: 520 us
  waiting for transfers between devices  255 us (48%)
  Pallas kernels  112 us (21%)
  starting transfers between devices  94.7 us (18%)
  other arithmetic  39.6 us (7%)
  local copies, waits for them, and re-layouts  15.2 us (3%)
    ppermute x81, waiting for transfers between devices, move(): return lax.ppermute(value, 'dp', [(d, target(d)) for d in range(self.dp)])  199 us
    ppermute x81, starting transfers between devices, move(): return lax.ppermute(value, 'dp', [(d, target(d)) for d in range(self.dp)])  77.1 us
    ppermute x17, waiting for transfers between devices, other_x(): return lax.ppermute(value, 'tensor', [(0, 1), (1, 0)])  57 us
    pallas_call x2, Pallas kernels, held_call(): pl.pallas_call(body, in_specs=[pl.BlockSpec(memory_space=pltpu.SMEM)] + [...  46 us
    pallas_call x2, Pallas kernels, attention_call(): pl.pallas_call(functools.partial(kernel, width_kv, keys), in_specs=[pl.Bl...  37.2 us
    pallas_call x3, Pallas kernels, weight_grad(): pl.pallas_call(weight_grad_kernel, grid_spec=pltpu.PrefetchScalarGridSpec...  26.8 us
    ppermute x17, starting transfers between devices, other_x(): return lax.ppermute(value, 'tensor', [(0, 1), (1, 0)])  17.6 us
  transfers between devices with their start and end apart: 98, of which 47 were waited for; matrix products, arithmetic and copies ran while one was open for 9% of the time, Pallas kernels for 19%

profile of v6, /device:TPU:0, one launch (start us, length us, event | category | flops | bytes accessed | tf_op | source)
XLA Modules:
  0.0 519.6 jit_solution(432198990052335909)
XLA Ops:
  14.4 11.3 %collective-permute-done.refs_1_.refs_3_ = bf16[128,2048]{1,0:T(8,128)(2,1)S(1)} collective-permute-done((bf16[128,2048]{1,0:T(8,128)(2,1)S(1)}, bf16[128,2048]{1,0:T(8,128)(2,1)S(1)}, u32[]{:S(2)}, u32[]{:S(2)}) %collective-permute-start) | collective-permute-done | bytes 524320 | tf_op jit(solution)/shard_map/ppermute | solution.py:83
  25.8 10.1 %collective-permute-done.1.refs_7_.refs_12_ = bf16[128,2560]{1,0:T(8,128)(2,1)S(1)} collective-permute-done((bf16[128,2560]{1,0:T(8,128)(2,1)}, bf16[128,2560]{1,0:T(8,128)(2,1)S(1)}, u32[]{:S(2)}, u32[]{:S(2)}) %collective-permute-start.1) | collective-permute-done | bytes 655392 | tf_op jit(solution)/shard_map/ppermute | solution.py:66
  42.1 9.4 %collective-permute-done.6 = bf16[1,128,1024]{2,1,0:T(8,128)(2,1)S(1)} collective-permute-done((bf16[1,128,1024]{2,1,0:T(8,128)(2,1)S(1)}, bf16[1,128,1024]{2,1,0:T(8,128)(2,1)S(1)}, u32[]{:S(2)}, u32[]{:S(2)}) %collective-permute-start.6) | collective-permute-done | bytes 262176 | tf_op jit(solution)/shard_map/ppermute | solution.py:66
  58.2 6.7 %collective-permute-done.12.refs_7_ = bf16[128,2048]{1,0:T(8,128)(2,1)S(1)} collective-permute-done((bf16[128,2048]{1,0:T(8,128)(2,1)S(1)}, bf16[128,2048]{1,0:T(8,128)(2,1)S(1)}, u32[]{:S(2)}, u32[]{:S(2)}) %collective-permute-start.12) | collective-permute-done | bytes 524320 | tf_op jit(solution)/shard_map/ppermute | solution.py:83
  65.6 6.2 %collective-permute-done.13 = bf16[1,128,1024]{2,1,0:T(8,128)(2,1)S(1)} collective-permute-done((bf16[1,128,1024]{2,1,0:T(8,128)(2,1)S(1)}, bf16[1,128,1024]{2,1,0:T(8,128)(2,1)S(1)}, u32[]{:S(2)}, u32[]{:S(2)}) %collective-permute-start.13) | collective-permute-done | bytes 262176 | tf_op jit(solution)/shard_map/ppermute | solution.py:66
  79.6 9.2 %collective-permute-done.19 = bf16[1,128,1024]{2,1,0:T(8,128)(2,1)S(1)} collective-permute-done((bf16[1,128,1024]{2,1,0:T(8,128)(2,1)S(1)}, bf16[1,128,1024]{2,1,0:T(8,128)(2,1)S(1)}, u32[]{:S(2)}, u32[]{:S(2)}) %collective-permute-start.19) | collective-permute-done | bytes 262176 | tf_op jit(solution)/shard_map/ppermute | solution.py:66
  101.4 16.1 %shard_map.187 = (bf16[256,1280]{1,0:T(8,128)(2,1)}, bf16[256,256]{1,0:T(8,128)(2,1)}, bf16[256,1024]{1,0:T(8,128)(2,1)}, f32[128,2048]{1,0:T(8,128)}, bf16[128,2048]{1,0:T(8,128)(2,1)}) custom-call(s32[5]{0:T(128)} %stack.113.place, bf16[128,2048]{1,0:T(8,128)(2,1)} %copy-done.27, bf16[128,2048]{1,0:T(8,128)(2,1)} %copy-done.63, ...), custom_call_target="tpu_custom_call" | custom-call | flops 4026531840 | bytes 14682112 | tf_op jit(solution)/shard_map/pallas_call | solution.py:463
  117.6 14.3 %collective-permute-done.23 = bf16[128,1024]{1,0:T(8,128)(2,1)S(1)} collective-permute-done((bf16[128,1024]{1,0:T(8,128)(2,1)S(1)}, bf16[128,1024]{1,0:T(8,128)(2,1)S(1)}, u32[]{:S(2)}, u32[]{:S(2)}) %collective-permute-start.23) | collective-permute-done | bytes 262176 | tf_op jit(solution)/shard_map/ppermute | solution.py:66
  138.0 7.7 %collective-permute-done.26 = bf16[128,2048]{1,0:T(8,128)(2,1)S(1)} collective-permute-done((bf16[128,2048]{1,0:T(8,128)(2,1)}, bf16[128,2048]{1,0:T(8,128)(2,1)S(1)}, u32[]{:S(2)}, u32[]{:S(2)}) %collective-permute-start.26) | collective-permute-done | bytes 524320 | tf_op jit(solution)/shard_map/ppermute | solution.py:83
  146.5 4.5 collective-permute-done.29
  156.0 5.0 collective-permute-start.30
  167.8 15.8 %collective-permute-done.30.refs_2_ = bf16[128,2048]{1,0:T(8,128)(2,1)S(1)} collective-permute-done((bf16[128,2048]{1,0:T(8,128)(2,1)S(1)}, bf16[128,2048]{1,0:T(8,128)(2,1)S(1)}, u32[]{:S(2)}, u32[]{:S(2)}) %collective-permute-start.30) | collective-permute-done | bytes 524320 | tf_op jit(solution)/shard_map/ppermute | solution.py:66
  189.1 5.3 %collective-permute-done.41.refs_24_.refs_26_ = bf16[1,128,1024]{2,1,0:T(8,128)(2,1)S(1)} collective-permute-done((bf16[1,128,1024]{2,1,0:T(8,128)(2,1)S(1)}, bf16[1,128,1024]{2,1,0:T(8,128)(2,1)S(1)}, u32[]{:S(2)}, u32[]{:S(2)}) %collective-permute-start.41) | collective-permute-done | bytes 262176 | tf_op jit(solution)/shard_map/ppermute | solution.py:66
  198.7 8.7 %collective-permute-done.37.refs_0_ = bf16[128,2048]{1,0:T(8,128)(2,1)S(1)} collective-permute-done((bf16[128,2048]{1,0:T(8,128)(2,1)S(1)}, bf16[128,2048]{1,0:T(8,128)(2,1)S(1)}, u32[]{:S(2)}, u32[]{:S(2)}) %collective-permute-start.37) | collective-permute-done | bytes 524320 | tf_op jit(solution)/shard_map/ppermute | solution.py:66
  214.2 10.8 %collective-permute-done.42.refs_1_ = bf16[128,2048]{1,0:T(8,128)(2,1)S(1)} collective-permute-done((bf16[128,2048]{1,0:T(8,128)(2,1)S(1)}, bf16[128,2048]{1,0:T(8,128)(2,1)S(1)}, u32[]{:S(2)}, u32[]{:S(2)}) %collective-permute-start.42) | collective-permute-done | bytes 524320 | tf_op jit(solution)/shard_map/ppermute | solution.py:83
  228.7 23.9 %shard_map.188 = (bf16[1024,1024]{1,0:T(8,128)(2,1)}, bf16[1024,1024]{1,0:T(8,128)(2,1)}, bf16[1024,1024]{1,0:T(8,128)(2,1)}, bf16[512,1024]{1,0:T(8,128)(2,1)},...) custom-call(s32[4]{0:T(128)} %pad_add_fusion.1.place, ...), custom_call_target="tpu_custom_call" | custom-call | flops 12884901888 | bytes 27262976 | tf_op jit(solution)/shard_map/pallas_call | solution.py:147
  252.6 9.2 %shard_map.189 = (bf16[2,4,128,1024]{3,2,1,0:T(8,128)(2,1)}, bf16[2,4,128,1024]{3,2,1,0:T(8,128)(2,1)}) custom-call(s32[1]{0:T(128)} %bitcast.1.place, bf16[128,2048]{1,0:T(8,128)(2,1)} %collective-permute-done.39.refs_0_, bf16[128,2048]{1,0:T(8,128)(2,1)} %collective-permute-done.57.refs_1_, bf16[128,2048]{1,0:T(8,128)(2,1)} %copy-done.41, ...), custom_call_target="tpu_custom_call" | custom-call | flops 4294967296 | bytes 10485760 | tf_op jit(solution)/shard_map/pallas_call | solution.py:261
  269.0 22.2 %shard_map.190 = (bf16[1024,1024]{1,0:T(8,128)(2,1)}, bf16[1024,1024]{1,0:T(8,128)(2,1)}, bf16[128,2048]{1,0:T(8,128)(2,1)}, bf16[128,2048]{1,0:T(8,128)(2,1)}, ...) custom-call(s32[4]{0:T(128)} %pad_add_fusion.1.place, ...), custom_call_target="tpu_custom_call" | custom-call | flops 12884901888 | bytes 29360128 | tf_op jit(solution)/shard_map/pallas_call | solution.py:147
  295.7 8.8 %shard_map.191 = (bf16[2,4,128,1024]{3,2,1,0:T(8,128)(2,1)}, bf16[2,4,128,1024]{3,2,1,0:T(8,128)(2,1)}) custom-call(s32[1]{0:T(128)} %bitcast.1.place, bf16[128,2048]{1,0:T(8,128)(2,1)} %copy-done.71, bf16[128,2048]{1,0:T(8,128)(2,1)} %copy-done.76, bf16[128,2048]{1,0:T(8,128)(2,1)} %copy-done.69, bf16[128,2048]{1,0:T(8,128)(2,1)} %copy-done.72, ...), custom_call_target="tpu_custom_call" | custom-call | flops 4294967296 | bytes 10485760 | tf_op jit(solution)/shard_map/pallas_call | solution.py:261
  309.8 8.8 %shard_map.192 = (bf16[2,4,128,1024]{3,2,1,0:T(8,128)(2,1)}, bf16[2,4,128,1024]{3,2,1,0:T(8,128)(2,1)}) custom-call(s32[1]{0:T(128)} %bitcast.1.place, bf16[128,2048]{1,0:T(8,128)(2,1)} %copy-done.71, bf16[128,2048]{1,0:T(8,128)(2,1)} %copy-done.76, bf16[128,2048]{1,0:T(8,128)(2,1)} %copy-done.69, bf16[128,2048]{1,0:T(8,128)(2,1)} %copy-done.72, ...), custom_call_target="tpu_custom_call" | custom-call | flops 4294967296 | bytes 10485760 | tf_op jit(solution)/shard_map/pallas_call | solution.py:261
  330.3 7.2 %collective-permute-done.65 = bf16[128,2048]{1,0:T(8,128)(2,1)S(1)} collective-permute-done((bf16[128,2048]{1,0:T(8,128)(2,1)}, bf16[128,2048]{1,0:T(8,128)(2,1)S(1)}, u32[]{:S(2)}, u32[]{:S(2)}) %collective-permute-start.65) | collective-permute-done | bytes 524320 | tf_op jit(solution)/shard_map/ppermute | solution.py:83
  337.5 11.5 %collective-permute-done.66 = bf16[128,2048]{1,0:T(8,128)(2,1)} collective-permute-done((bf16[128,2048]{1,0:T(8,128)(2,1)}, bf16[128,2048]{1,0:T(8,128)(2,1)}, u32[]{:S(2)}, u32[]{:S(2)}) %collective-permute-start.66) | collective-permute-done | bytes 524320 | tf_op jit(solution)/shard_map/ppermute | solution.py:66
  362.1 4.9 collective-permute-done.68.refs_1_
  379.1 21.0 %shard_map.193 = (f32[128,2048]{1,0:T(8,128)}, bf16[128,2048]{1,0:T(8,128)(2,1)}, bf16[8,128,1280]{2,1,0:T(8,128)(2,1)}, bf16[8,128,1280]{2,1,0:T(8,128)(2,1)}, ...) custom-call(s32[5]{0:T(128)} %stack.113.place, bf16[128,2048]{1,0:T(8,128)(2,1)} %copy-done.23, ...), custom_call_target="tpu_custom_call" | custom-call | flops 7381975040 | bytes 26216448 | tf_op jit(solution)/shard_map/pallas_call | solution.py:463
  412.9 4.8 collective-permute-done.78
  419.7 4.6 collective-permute-done.83
  424.2 21.2 %collective-permute-done.81 = bf16[128,1024]{1,0:T(8,128)(2,1)S(1)} collective-permute-done((bf16[128,1024]{1,0:T(8,128)(2,1)S(1)}, bf16[128,1024]{1,0:T(8,128)(2,1)S(1)}, u32[]{:S(2)}, u32[]{:S(2)}) %collective-permute-start.81) | collective-permute-done | bytes 262176 | tf_op jit(solution)/shard_map/ppermute | solution.py:66
  450.0 20.0 %collective-permute-done.84 = bf16[128,2048]{1,0:T(8,128)(2,1)S(1)} collective-permute-done((bf16[128,2048]{1,0:T(8,128)(2,1)S(1)}, bf16[128,2048]{1,0:T(8,128)(2,1)S(1)}, u32[]{:S(2)}, u32[]{:S(2)}) %collective-permute-start.84) | collective-permute-done | bytes 524320 | tf_op jit(solution)/shard_map/ppermute | solution.py:66
  471.2 4.8 collective-permute-done.88
  488.7 5.1 collective-permute-done.94
  495.4 6.7 %collective-permute-done.93 = bf16[2,128,1280]{2,1,0:T(8,128)(2,1)S(1)} collective-permute-done((bf16[2,128,1280]{2,1,0:T(8,128)(2,1)S(1)}, bf16[2,128,1280]{2,1,0:T(8,128)(2,1)S(1)}, u32[]{:S(2)}, u32[]{:S(2)}) %collective-permute-start.93) | collective-permute-done | bytes 655392 | tf_op jit(solution)/shard_map/ppermute | solution.py:66
  511.4 5.5 %collective-permute-done.96 = f32[2,2048]{1,0:T(2,128)S(1)} collective-permute-done((f32[2,2048]{1,0:T(2,128)S(1)}, f32[2,2048]{1,0:T(2,128)S(1)}, u32[]{:S(2)}, u32[]{:S(2)}) %collective-permute-start.96) | collective-permute-done | bytes 16416 | tf_op jit(solution)/shard_map/ppermute | solution.py:66
  (454 shorter events, 185.7 us)
Async XLA Ops:
  2.8 33.1 %collective-permute-start.1 = (bf16[128,2560]{1,0:T(8,128)(2,1)}, bf16[128,2560]{1,0:T(8,128)(2,1)S(1)}, u32[]{:S(2)}, u32[]{:S(2)}) collective-permute-start(bf16[128,2560]{1,0:T(8,128)(2,1)} %shard_map.186.refs_6_.refs_11_), channel_id=1, source_target_pairs={{0,16},{2,18},{4,20},{6,22},{8,24},{10,26},{12,28},{14,30},{16,0},... | collective-permute-start | bytes 1966088 | tf_op jit(solution)/shard_map/ppermute | solution.py:66
  6.8 29.4 %collective-permute-start.2 = (bf16[128,2560]{1,0:T(8,128)(2,1)}, bf16[128,2560]{1,0:T(8,128)(2,1)}, u32[]{:S(2)}, u32[]{:S(2)}) collective-permute-start(bf16[128,2560]{1,0:T(8,128)(2,1)} %shard_map.186.refs_6_.refs_11_), channel_id=1, source_target_pairs={{0,8},{2,10},{4,12},{6,14},{8,0},{10,2},{12,4},{14,6},{16,24},{18,... | collective-permute-start | bytes 1966088 | tf_op jit(solution)/shard_map/ppermute | solution.py:66
  8.4 27.8 %collective-permute-start.3 = (bf16[128,2560]{1,0:T(8,128)(2,1)}, bf16[128,2560]{1,0:T(8,128)(2,1)S(1)}, u32[]{:S(2)}, u32[]{:S(2)}) collective-permute-start(bf16[128,2560]{1,0:T(8,128)(2,1)} %shard_map.186.refs_6_.refs_11_), channel_id=1, source_target_pairs={{0,4},{2,6},{4,0},{6,2},{8,12},{10,14},{12,8},{14,10},{16,20},{18,... | collective-permute-start | bytes 1966088 | tf_op jit(solution)/shard_map/ppermute | solution.py:66
  39.7 25.3 %collective-permute-start.4 = (bf16[128,2560]{1,0:T(8,128)(2,1)}, bf16[128,2560]{1,0:T(8,128)(2,1)S(1)}, u32[]{:S(2)}, u32[]{:S(2)}) collective-permute-start(bf16[128,2560]{1,0:T(8,128)(2,1)} %copy-done.50), channel_id=1, source_target_pairs={{0,8},{2,10},{4,12},{6,14},{8,0},{10,2},{12,4},{14,6},{16,24},{18,... | collective-permute-start | bytes 1966088 | tf_op jit(solution)/shard_map/ppermute | solution.py:66
  92.5 39.5 %collective-permute-start.25 = (bf16[3,128,1024]{2,1,0:T(8,128)(2,1)S(1)}, bf16[3,128,1024]{2,1,0:T(8,128)(2,1)}, u32[]{:S(2)}, u32[]{:S(2)}) collective-permute-start(bf16[3,128,1024]{2,1,0:T(8,128)(2,1)S(1)} %pad_maximum_fusion.refs_8_.refs_10_), channel_id=1, source_target_pairs={{0,4},{2,6},{4,0},{6,2},{8,12},{10,14},{12,8},{14,10},{16,20},{18,... | collective-permute-start | bytes 2359304 | tf_op jit(solution)/shard_map/ppermute | solution.py:66
  93.3 38.6 %collective-permute-start.24 = (bf16[128,2048]{1,0:T(8,128)(2,1)}, bf16[128,2048]{1,0:T(8,128)(2,1)S(1)}, u32[]{:S(2)}, u32[]{:S(2)}) collective-permute-start(bf16[128,2048]{1,0:T(8,128)(2,1)} %collective-permute-done.20.refs_4_), channel_id=1, source_target_pairs={{0,1},{1,0},{2,3},{3,2},{4,5},{5,4},{6,7},{7,6},{8,9},{9,8},{10,11... | collective-permute-start | bytes 1572872 | tf_op jit(solution)/shard_map/ppermute | solution.py:83
  94.0 37.9 %collective-permute-start.22 = (bf16[2,128,1024]{2,1,0:T(8,128)(2,1)}, bf16[2,128,1024]{2,1,0:T(8,128)(2,1)S(1)}, u32[]{:S(2)}, u32[]{:S(2)}) collective-permute-start(bf16[2,128,1024]{2,1,0:T(8,128)(2,1)} %get-tuple-element.156), channel_id=1, source_target_pairs={{0,24},{2,26},{4,28},{6,30},{8,16},{10,18},{12,20},{14,22},{16,8},... | collective-permute-start | bytes 1572872 | tf_op jit(solution)/shard_map/ppermute | solution.py:66
  97.2 34.8 %collective-permute-start.21 = (bf16[2,128,1024]{2,1,0:T(8,128)(2,1)}, bf16[2,128,1024]{2,1,0:T(8,128)(2,1)}, u32[]{:S(2)}, u32[]{:S(2)}) collective-permute-start(bf16[2,128,1024]{2,1,0:T(8,128)(2,1)} %get-tuple-element.155), channel_id=1, source_target_pairs={{0,8},{2,10},{4,12},{6,14},{8,0},{10,2},{12,4},{14,6},{16,24},{18,... | collective-permute-start | bytes 1572872 | tf_op jit(solution)/shard_map/ppermute | solution.py:66
  100.9 31.0 %collective-permute-start.23 = (bf16[128,1024]{1,0:T(8,128)(2,1)S(1)}, bf16[128,1024]{1,0:T(8,128)(2,1)S(1)}, u32[]{:S(2)}, u32[]{:S(2)}) collective-permute-start(bf16[128,1024]{1,0:T(8,128)(2,1)S(1)} %get-tuple-element.157), channel_id=1, source_target_pairs={{0,16},{2,18},{4,20},{6,22},{8,24},{10,26},{12,28},{14,30},{16,0},... | collective-permute-start | bytes 786440 | tf_op jit(solution)/shard_map/ppermute | solution.py:66
  156.0 27.6 %collective-permute-start.30 = (bf16[128,2048]{1,0:T(8,128)(2,1)S(1)}, bf16[128,2048]{1,0:T(8,128)(2,1)S(1)}, u32[]{:S(2)}, u32[]{:S(2)}) collective-permute-start(bf16[128,2048]{1,0:T(8,128)(2,1)S(1)} %multiply_convert_fusion.refs_6_), channel_id=1, source_target_pairs={{0,16},{2,18},{4,20},{6,22},{8,24},{10,26},{12,28},{14,30},{16,0},... | collective-permute-start | bytes 1572872 | tf_op jit(solution)/shard_map/ppermute | solution.py:66
  161.0 22.6 %collective-permute-start.32 = (bf16[128,2048]{1,0:T(8,128)(2,1)S(1)}, bf16[128,2048]{1,0:T(8,128)(2,1)S(1)}, u32[]{:S(2)}, u32[]{:S(2)}) collective-permute-start(bf16[128,2048]{1,0:T(8,128)(2,1)S(1)} %multiply_convert_fusion.refs_6_), channel_id=1, source_target_pairs={{0,8},{2,10},{4,12},{6,14},{8,0},{10,2},{12,4},{14,6},{16,24},{18,... | collective-permute-start | bytes 1572872 | tf_op jit(solution)/shard_map/ppermute | solution.py:66
  225.7 26.9 %collective-permute-start.57 = (bf16[128,2048]{1,0:T(8,128)(2,1)}, bf16[128,2048]{1,0:T(8,128)(2,1)}, u32[]{:S(2)}, u32[]{:S(2)}) collective-permute-start(bf16[128,2048]{1,0:T(8,128)(2,1)} %collective-permute-done.39.refs_0_), channel_id=1, source_target_pairs={{0,1},{1,0},{2,3},{3,2},{4,5},{5,4},{6,7},{7,6},{8,9},{9,8},{10,11... | collective-permute-start | bytes 1572872 | tf_op jit(solution)/shard_map/ppermute | solution.py:83
  262.1 29.1 %collective-permute-start.56 = (bf16[512,1024]{1,0:T(8,128)(2,1)S(1)}, bf16[512,1024]{1,0:T(8,128)(2,1)S(1)}, u32[]{:S(2)}, u32[]{:S(2)}) collective-permute-start(bf16[512,1024]{1,0:T(8,128)(2,1)S(1)} %copy-done.44), channel_id=1, source_target_pairs={{0,1},{1,0},{2,3},{3,2},{4,5},{5,4},{6,7},{7,6},{8,9},{9,8},{10,11... | collective-permute-start | bytes 3145736 | tf_op jit(solution)/shard_map/ppermute | solution.py:83
  268.4 25.3 %collective-permute-start.59 = (bf16[4,128,1024]{2,1,0:T(8,128)(2,1)S(1)}, bf16[4,128,1024]{2,1,0:T(8,128)(2,1)S(1)}, u32[]{:S(2)}, u32[]{:S(2)}) collective-permute-start(bf16[4,128,1024]{2,1,0:T(8,128)(2,1)S(1)} %fusion.15), channel_id=1, source_target_pairs={{0,4},{2,6},{4,0},{6,2},{8,12},{10,14},{12,8},{14,10},{16,20},{18,... | collective-permute-start | bytes 3145736 | tf_op jit(solution)/shard_map/ppermute | solution.py:66
  325.5 23.5 %collective-permute-start.66 = (bf16[128,2048]{1,0:T(8,128)(2,1)}, bf16[128,2048]{1,0:T(8,128)(2,1)}, u32[]{:S(2)}, u32[]{:S(2)}) collective-permute-start(bf16[128,2048]{1,0:T(8,128)(2,1)} %get-tuple-element.216), channel_id=1, source_target_pairs={{0,8},{2,10},{4,12},{6,14},{8,0},{10,2},{12,4},{14,6},{16,24},{18,... | collective-permute-start | bytes 1572872 | tf_op jit(solution)/shard_map/ppermute | solution.py:66
  326.3 25.2 %collective-permute-start.67 = (bf16[128,2048]{1,0:T(8,128)(2,1)}, bf16[128,2048]{1,0:T(8,128)(2,1)}, u32[]{:S(2)}, u32[]{:S(2)}) collective-permute-start(bf16[128,2048]{1,0:T(8,128)(2,1)} %add_convert_fusion.5), channel_id=1, source_target_pairs={{0,16},{2,18},{4,20},{6,22},{8,24},{10,26},{12,28},{14,30},{16,0},... | collective-permute-start | bytes 1572872 | tf_op jit(solution)/shard_map/ppermute | solution.py:66
  327.9 39.8 %collective-permute-start.73 = (bf16[2,4,128,1024]{3,2,1,0:T(8,128)(2,1)}, bf16[2,4,128,1024]{3,2,1,0:T(8,128)(2,1)}, u32[]{:S(2)}, u32[]{:S(2)}) collective-permute-start(bf16[2,4,128,1024]{3,2,1,0:T(8,128)(2,1)} %get-tuple-element.229), channel_id=1, source_target_pairs={{0,2},{2,0},{4,6},{6,4},{8,10},{10,8},{12,14},{14,12},{16,18},{18,... | collective-permute-start | bytes 6291464 | tf_op jit(solution)/shard_map/ppermute | solution.py:66
  329.8 30.1 %collective-permute-start.70 = (bf16[4,128,1024]{2,1,0:T(8,128)(2,1)S(1)}, bf16[4,128,1024]{2,1,0:T(8,128)(2,1)S(1)}, u32[]{:S(2)}, u32[]{:S(2)}) collective-permute-start(bf16[4,128,1024]{2,1,0:T(8,128)(2,1)S(1)} %fusion.16), channel_id=1, source_target_pairs={{0,4},{2,6},{4,0},{6,2},{8,12},{10,14},{12,8},{14,10},{16,20},{18,... | collective-permute-start | bytes 3145736 | tf_op jit(solution)/shard_map/ppermute | solution.py:66
  367.1 33.2 %collective-permute-start.69 = (bf16[512,1024]{1,0:T(8,128)(2,1)}, bf16[512,1024]{1,0:T(8,128)(2,1)}, u32[]{:S(2)}, u32[]{:S(2)}) collective-permute-start(bf16[512,1024]{1,0:T(8,128)(2,1)} %get-tuple-element.219), channel_id=1, source_target_pairs={{0,1},{1,0},{2,3},{3,2},{4,5},{5,4},{6,7},{7,6},{8,9},{9,8},{10,11... | collective-permute-start | bytes 3145736 | tf_op jit(solution)/shard_map/ppermute | solution.py:83
  370.3 29.9 %collective-permute-start.74 = (bf16[4,128,1024]{2,1,0:T(8,128)(2,1)}, bf16[4,128,1024]{2,1,0:T(8,128)(2,1)}, u32[]{:S(2)}, u32[]{:S(2)}) collective-permute-start(bf16[4,128,1024]{2,1,0:T(8,128)(2,1)} %fusion.17), channel_id=1, source_target_pairs={{0,4},{2,6},{4,0},{6,2},{8,12},{10,14},{12,8},{14,10},{16,20},{18,... | collective-permute-start | bytes 3145736 | tf_op jit(solution)/shard_map/ppermute | solution.py:66
  375.6 24.6 %collective-permute-start.77 = (bf16[2,128,1024]{2,1,0:T(8,128)(2,1)}, bf16[2,128,1024]{2,1,0:T(8,128)(2,1)S(1)}, u32[]{:S(2)}, u32[]{:S(2)}) collective-permute-start(bf16[2,128,1024]{2,1,0:T(8,128)(2,1)} %pad_maximum_fusion.6), channel_id=1, source_target_pairs={{0,8},{2,10},{4,12},{6,14},{8,0},{10,2},{12,4},{14,6},{16,24},{18,... | collective-permute-start | bytes 1572872 | tf_op jit(solution)/shard_map/ppermute | solution.py:66
  375.6 24.5 %collective-permute-start.76 = (bf16[128,1024]{1,0:T(8,128)(2,1)}, bf16[128,1024]{1,0:T(8,128)(2,1)}, u32[]{:S(2)}, u32[]{:S(2)}) collective-permute-start(bf16[128,1024]{1,0:T(8,128)(2,1)} %get-tuple-element.232), channel_id=1, source_target_pairs={{0,24},{2,26},{4,28},{6,30},{8,16},{10,18},{12,20},{14,22},{16,8},... | collective-permute-start | bytes 786440 | tf_op jit(solution)/shard_map/ppermute | solution.py:66
  377.6 22.6 %collective-permute-start.75 = (bf16[128,1024]{1,0:T(8,128)(2,1)S(1)}, bf16[128,1024]{1,0:T(8,128)(2,1)}, u32[]{:S(2)}, u32[]{:S(2)}) collective-permute-start(bf16[128,1024]{1,0:T(8,128)(2,1)S(1)} %get-tuple-element.231), channel_id=1, source_target_pairs={{0,16},{2,18},{4,20},{6,22},{8,24},{10,26},{12,28},{14,30},{16,0},... | collective-permute-start | bytes 786440 | tf_op jit(solution)/shard_map/ppermute | solution.py:66
  405.7 39.7 %collective-permute-start.80 = (bf16[4,128,1280]{2,1,0:T(8,128)(2,1)S(1)}, bf16[4,128,1280]{2,1,0:T(8,128)(2,1)S(1)}, u32[]{:S(2)}, u32[]{:S(2)}) collective-permute-start(bf16[4,128,1280]{2,1,0:T(8,128)(2,1)S(1)} %fusion.4), channel_id=1, source_target_pairs={{0,4},{2,6},{4,0},{6,2},{8,12},{10,14},{12,8},{14,10},{16,20},{18,... | collective-permute-start | bytes 3932168 | tf_op jit(solution)/shard_map/ppermute | solution.py:66
  409.0 36.4 %collective-permute-start.82 = (bf16[2,128,1024]{2,1,0:T(8,128)(2,1)S(1)}, bf16[2,128,1024]{2,1,0:T(8,128)(2,1)S(1)}, u32[]{:S(2)}, u32[]{:S(2)}) collective-permute-start(bf16[2,128,1024]{2,1,0:T(8,128)(2,1)S(1)} %pad_maximum_fusion.7), channel_id=1, source_target_pairs={{0,24},{2,26},{4,28},{6,30},{8,16},{10,18},{12,20},{14,22},{16,8},... | collective-permute-start | bytes 1572872 | tf_op jit(solution)/shard_map/ppermute | solution.py:66
  417.7 27.8 %collective-permute-start.81 = (bf16[128,1024]{1,0:T(8,128)(2,1)S(1)}, bf16[128,1024]{1,0:T(8,128)(2,1)S(1)}, u32[]{:S(2)}, u32[]{:S(2)}) collective-permute-start(bf16[128,1024]{1,0:T(8,128)(2,1)S(1)} %get-tuple-element.237), channel_id=1, source_target_pairs={{0,16},{2,18},{4,20},{6,22},{8,24},{10,26},{12,28},{14,30},{16,0},... | collective-permute-start | bytes 786440 | tf_op jit(solution)/shard_map/ppermute | solution.py:66
  445.5 33.5 %collective-permute-start.87 = (bf16[4,128,1280]{2,1,0:T(8,128)(2,1)S(1)}, bf16[4,128,1280]{2,1,0:T(8,128)(2,1)S(1)}, u32[]{:S(2)}, u32[]{:S(2)}) collective-permute-start(bf16[4,128,1280]{2,1,0:T(8,128)(2,1)S(1)} %fusion.5), channel_id=1, source_target_pairs={{0,4},{2,6},{4,0},{6,2},{8,12},{10,14},{12,8},{14,10},{16,20},{18,... | collective-permute-start | bytes 3932168 | tf_op jit(solution)/shard_map/ppermute | solution.py:66
  446.6 23.5 %collective-permute-start.84 = (bf16[128,2048]{1,0:T(8,128)(2,1)S(1)}, bf16[128,2048]{1,0:T(8,128)(2,1)S(1)}, u32[]{:S(2)}, u32[]{:S(2)}) collective-permute-start(bf16[128,2048]{1,0:T(8,128)(2,1)S(1)} %fusion.22), channel_id=1, source_target_pairs={{0,16},{2,18},{4,20},{6,22},{8,24},{10,26},{12,28},{14,30},{16,0},... | collective-permute-start | bytes 1572872 | tf_op jit(solution)/shard_map/ppermute | solution.py:66
  446.9 29.1 %collective-permute-start.88 = (bf16[2,128,1280]{2,1,0:T(8,128)(2,1)S(1)}, bf16[2,128,1280]{2,1,0:T(8,128)(2,1)S(1)}, u32[]{:S(2)}, u32[]{:S(2)}) collective-permute-start(bf16[2,128,1280]{2,1,0:T(8,128)(2,1)S(1)} %pad_maximum_fusion.1), channel_id=1, source_target_pairs={{0,8},{2,10},{4,12},{6,14},{8,0},{10,2},{12,4},{14,6},{16,24},{18,... | collective-permute-start | bytes 1966088 | tf_op jit(solution)/shard_map/ppermute | solution.py:66
  449.2 29.8 %collective-permute-start.89 = (bf16[128,1024]{1,0:T(8,128)(2,1)S(1)}, bf16[128,1024]{1,0:T(8,128)(2,1)S(1)}, u32[]{:S(2)}, u32[]{:S(2)}) collective-permute-start(bf16[128,1024]{1,0:T(8,128)(2,1)S(1)} %get-tuple-element.249), channel_id=1, source_target_pairs={{0,8},{2,10},{4,12},{6,14},{8,0},{10,2},{12,4},{14,6},{16,24},{18,... | collective-permute-start | bytes 786440 | tf_op jit(solution)/shard_map/ppermute | solution.py:66
  449.3 29.7 %collective-permute-start.85 = (bf16[128,2048]{1,0:T(8,128)(2,1)S(1)}, bf16[128,2048]{1,0:T(8,128)(2,1)S(1)}, u32[]{:S(2)}, u32[]{:S(2)}) collective-permute-start(bf16[128,2048]{1,0:T(8,128)(2,1)S(1)} %copy-done.77), channel_id=1, source_target_pairs={{0,1},{1,0},{2,3},{3,2},{4,5},{5,4},{6,7},{7,6},{8,9},{9,8},{10,11... | collective-permute-start | bytes 1572872 | tf_op jit(solution)/shard_map/ppermute | solution.py:83
  480.8 21.3 %collective-permute-start.93 = (bf16[2,128,1280]{2,1,0:T(8,128)(2,1)S(1)}, bf16[2,128,1280]{2,1,0:T(8,128)(2,1)S(1)}, u32[]{:S(2)}, u32[]{:S(2)}) collective-permute-start(bf16[2,128,1280]{2,1,0:T(8,128)(2,1)S(1)} %pad_maximum_fusion.2), channel_id=1, source_target_pairs={{0,8},{2,10},{4,12},{6,14},{8,0},{10,2},{12,4},{14,6},{16,24},{18,... | collective-permute-start | bytes 1966088 | tf_op jit(solution)/shard_map/ppermute | solution.py:66
  (159 other events, 2816.3 us)

commit v7 on v6

--- a/solution.py
+++ b/solution.py
@@ -641,14 +641,14 @@
     stage = [*normed.values(), *last, grads_low[2, 1]]
     normed[3, 0] = at.across_z(after(normed[2, 0], *stage), 1)
     normed[2, 1] = at.other_x(after(normed[2, 0], *stage))
-    grads_low[3, 0] = at.across_z(after(grads_low[2, 0], *stage), 1)
     for mask in (2, 1, 3):
         to_cores(mask, others, 0, *stage)
     last = to_chips(1, [plane_one_last], *stage) + to_chips(3, [plane_three_last], *stage)
     for mask in (1, 3):
         to_cores(mask, (0,), 1, *stage)
 
-    stage = [normed[3, 0], normed[2, 1], grads_low[3, 0], *last]
+    stage = [normed[3, 0], normed[2, 1], *last]
+    grads_low[3, 0] = at.across_z(after(grads_low[2, 0], *stage), 1)
     normed[3, 1] = at.other_x(after(normed[3, 0], *stage))
     normed[1, 1] = at.across_z(after(normed[0, 1], *stage), 1)
     for mask in (1, 3):

time: 529 us -> 536 us (1.013)
  starting transfers between devices: 94.7 us -> 104 us
    ppermute x17, waiting for transfers between devices: 57 us -> 45.5 us  [other_x(): return lax.ppermute(value, 'tensor', [(0, 1), (1, 0)])]
    ppermute x81, waiting for transfers between devices: 199 us -> 209 us  [move(): return lax.ppermute(value, 'dp', [(d, target(d)) for d in range(self.dp)])]
  transfers between devices with their start and end apart: 98 -> 98, of which waited for: 47 -> 48; matrix products, arithmetic and copies ran while one was open for 9% -> 9% of each run, Pallas kernels for 19% -> 19%
where the time goes in v7:
time: 536 us; the launch traced here: 527 us
  waiting for transfers between devices  255 us (48%)
  Pallas kernels  112 us (21%)
  starting transfers between devices  104 us (19%)
  other arithmetic  39.6 us (7%)
  local copies, waits for them, and re-layouts  14.5 us (3%)
    ppermute x81, waiting for transfers between devices, move(): return lax.ppermute(value, 'dp', [(d, target(d)) for d in range(self.dp)])  209 us
    ppermute x81, starting transfers between devices, move(): return lax.ppermute(value, 'dp', [(d, target(d)) for d in range(self.dp)])  81.9 us
    pallas_call x2, Pallas kernels, held_call(): pl.pallas_call(body, in_specs=[pl.BlockSpec(memory_space=pltpu.SMEM)] + [...  46.1 us
    ppermute x17, waiting for transfers between devices, other_x(): return lax.ppermute(value, 'tensor', [(0, 1), (1, 0)])  45.5 us
    pallas_call x2, Pallas kernels, attention_call(): pl.pallas_call(functools.partial(kernel, width_kv, keys), in_specs=[pl.Bl...  37.2 us
    pallas_call x3, Pallas kernels, weight_grad(): pl.pallas_call(weight_grad_kernel, grid_spec=pltpu.PrefetchScalarGridSpec...  26.8 us
    ppermute x17, starting transfers between devices, other_x(): return lax.ppermute(value, 'tensor', [(0, 1), (1, 0)])  21.7 us
  transfers between devices with their start and end apart: 98, of which 48 were waited for; matrix products, arithmetic and copies ran while one was open for 9% of the time, Pallas kernels for 19%

profile of v7, /device:TPU:0, one launch (start us, length us, event | category | flops | bytes accessed | tf_op | source)
XLA Modules:
  0.0 527.1 jit_solution(14305807671750654293)
XLA Ops:
  14.4 11.3 %collective-permute-done.refs_1_.refs_3_ = bf16[128,2048]{1,0:T(8,128)(2,1)S(1)} collective-permute-done((bf16[128,2048]{1,0:T(8,128)(2,1)S(1)}, bf16[128,2048]{1,0:T(8,128)(2,1)S(1)}, u32[]{:S(2)}, u32[]{:S(2)}) %collective-permute-start) | collective-permute-done | bytes 524320 | tf_op jit(solution)/shard_map/ppermute | solution.py:83
  25.8 10.1 %collective-permute-done.1.refs_7_.refs_12_ = bf16[128,2560]{1,0:T(8,128)(2,1)S(1)} collective-permute-done((bf16[128,2560]{1,0:T(8,128)(2,1)}, bf16[128,2560]{1,0:T(8,128)(2,1)S(1)}, u32[]{:S(2)}, u32[]{:S(2)}) %collective-permute-start.1) | collective-permute-done | bytes 655392 | tf_op jit(solution)/shard_map/ppermute | solution.py:66
  42.1 9.4 %collective-permute-done.6 = bf16[1,128,1024]{2,1,0:T(8,128)(2,1)S(1)} collective-permute-done((bf16[1,128,1024]{2,1,0:T(8,128)(2,1)S(1)}, bf16[1,128,1024]{2,1,0:T(8,128)(2,1)S(1)}, u32[]{:S(2)}, u32[]{:S(2)}) %collective-permute-start.6) | collective-permute-done | bytes 262176 | tf_op jit(solution)/shard_map/ppermute | solution.py:66
  58.2 6.8 %collective-permute-done.12.refs_7_ = bf16[128,2048]{1,0:T(8,128)(2,1)S(1)} collective-permute-done((bf16[128,2048]{1,0:T(8,128)(2,1)S(1)}, bf16[128,2048]{1,0:T(8,128)(2,1)S(1)}, u32[]{:S(2)}, u32[]{:S(2)}) %collective-permute-start.12) | collective-permute-done | bytes 524320 | tf_op jit(solution)/shard_map/ppermute | solution.py:83
  65.6 6.2 %collective-permute-done.13 = bf16[1,128,1024]{2,1,0:T(8,128)(2,1)S(1)} collective-permute-done((bf16[1,128,1024]{2,1,0:T(8,128)(2,1)S(1)}, bf16[1,128,1024]{2,1,0:T(8,128)(2,1)S(1)}, u32[]{:S(2)}, u32[]{:S(2)}) %collective-permute-start.13) | collective-permute-done | bytes 262176 | tf_op jit(solution)/shard_map/ppermute | solution.py:66
  79.6 9.2 %collective-permute-done.19 = bf16[1,128,1024]{2,1,0:T(8,128)(2,1)S(1)} collective-permute-done((bf16[1,128,1024]{2,1,0:T(8,128)(2,1)S(1)}, bf16[1,128,1024]{2,1,0:T(8,128)(2,1)S(1)}, u32[]{:S(2)}, u32[]{:S(2)}) %collective-permute-start.19) | collective-permute-done | bytes 262176 | tf_op jit(solution)/shard_map/ppermute | solution.py:66
  101.4 16.1 %shard_map.187 = (bf16[256,1280]{1,0:T(8,128)(2,1)}, bf16[256,256]{1,0:T(8,128)(2,1)}, bf16[256,1024]{1,0:T(8,128)(2,1)}, f32[128,2048]{1,0:T(8,128)}, bf16[128,2048]{1,0:T(8,128)(2,1)}) custom-call(s32[5]{0:T(128)} %stack.113.place, bf16[128,2048]{1,0:T(8,128)(2,1)} %copy-done.27, bf16[128,2048]{1,0:T(8,128)(2,1)} %copy-done.63, ...), custom_call_target="tpu_custom_call" | custom-call | flops 4026531840 | bytes 14682112 | tf_op jit(solution)/shard_map/pallas_call | solution.py:463
  117.6 14.3 %collective-permute-done.23 = bf16[128,1024]{1,0:T(8,128)(2,1)S(1)} collective-permute-done((bf16[128,1024]{1,0:T(8,128)(2,1)S(1)}, bf16[128,1024]{1,0:T(8,128)(2,1)S(1)}, u32[]{:S(2)}, u32[]{:S(2)}) %collective-permute-start.23) | collective-permute-done | bytes 262176 | tf_op jit(solution)/shard_map/ppermute | solution.py:66
  138.0 7.7 %collective-permute-done.26 = bf16[128,2048]{1,0:T(8,128)(2,1)S(1)} collective-permute-done((bf16[128,2048]{1,0:T(8,128)(2,1)}, bf16[128,2048]{1,0:T(8,128)(2,1)S(1)}, u32[]{:S(2)}, u32[]{:S(2)}) %collective-permute-start.26) | collective-permute-done | bytes 524320 | tf_op jit(solution)/shard_map/ppermute | solution.py:83
  146.5 4.6 collective-permute-done.29
  155.9 4.9 collective-permute-start.30
  165.1 6.0 %collective-permute-start.32 = (bf16[128,2048]{1,0:T(8,128)(2,1)S(1)}, bf16[128,2048]{1,0:T(8,128)(2,1)}, u32[]{:S(2)}, u32[]{:S(2)}) collective-permute-start(bf16[128,2048]{1,0:T(8,128)(2,1)S(1)} %multiply_convert_fusion.refs_6_), channel_id=1, source_target_pairs={{0,8},{2,10},{4,12},{6,14},{8,0},{10,2},{12,4},{14,6},{16,24},{18,... | collective-permute-start | bytes 1572872 | tf_op jit(solution)/shard_map/ppermute | solution.py:66
  172.6 10.8 %collective-permute-done.30.refs_2_ = bf16[128,2048]{1,0:T(8,128)(2,1)S(1)} collective-permute-done((bf16[128,2048]{1,0:T(8,128)(2,1)S(1)}, bf16[128,2048]{1,0:T(8,128)(2,1)S(1)}, u32[]{:S(2)}, u32[]{:S(2)}) %collective-permute-start.30) | collective-permute-done | bytes 524320 | tf_op jit(solution)/shard_map/ppermute | solution.py:66
  184.5 7.8 %collective-permute-done.32.refs_4_ = bf16[128,2048]{1,0:T(8,128)(2,1)} collective-permute-done((bf16[128,2048]{1,0:T(8,128)(2,1)S(1)}, bf16[128,2048]{1,0:T(8,128)(2,1)}, u32[]{:S(2)}, u32[]{:S(2)}) %collective-permute-start.32) | collective-permute-done | bytes 524320 | tf_op jit(solution)/shard_map/ppermute | solution.py:66
  199.4 5.2 collective-permute-done.40.refs_24_.refs_26_
  214.0 10.5 %collective-permute-done.56.refs_0_ = bf16[128,2048]{1,0:T(8,128)(2,1)} collective-permute-done((bf16[128,2048]{1,0:T(8,128)(2,1)S(1)}, bf16[128,2048]{1,0:T(8,128)(2,1)}, u32[]{:S(2)}, u32[]{:S(2)}) %collective-permute-start.56) | collective-permute-done | bytes 524320 | tf_op jit(solution)/shard_map/ppermute | solution.py:66
  228.6 6.7 %collective-permute-done.42.refs_5_ = bf16[128,2048]{1,0:T(8,128)(2,1)} collective-permute-done((bf16[128,2048]{1,0:T(8,128)(2,1)S(1)}, bf16[128,2048]{1,0:T(8,128)(2,1)}, u32[]{:S(2)}, u32[]{:S(2)}) %collective-permute-start.42) | collective-permute-done | bytes 524320 | tf_op jit(solution)/shard_map/ppermute | solution.py:66
  235.3 24.0 %shard_map.188 = (bf16[1024,1024]{1,0:T(8,128)(2,1)}, bf16[1024,1024]{1,0:T(8,128)(2,1)}, bf16[1024,1024]{1,0:T(8,128)(2,1)}, bf16[512,1024]{1,0:T(8,128)(2,1)},...) custom-call(s32[4]{0:T(128)} %pad_add_fusion.1.place, ...), custom_call_target="tpu_custom_call" | custom-call | flops 12884901888 | bytes 27262976 | tf_op jit(solution)/shard_map/pallas_call | solution.py:147
  259.3 9.2 %shard_map.189 = (bf16[2,4,128,1024]{3,2,1,0:T(8,128)(2,1)}, bf16[2,4,128,1024]{3,2,1,0:T(8,128)(2,1)}) custom-call(s32[1]{0:T(128)} %bitcast.1.place, bf16[128,2048]{1,0:T(8,128)(2,1)} %collective-permute-done.56.refs_0_, bf16[128,2048]{1,0:T(8,128)(2,1)} %collective-permute-done.57.refs_1_, bf16[128,2048]{1,0:T(8,128)(2,1)} %copy-done.41, ...), custom_call_target="tpu_custom_call" | custom-call | flops 4294967296 | bytes 10485760 | tf_op jit(solution)/shard_map/pallas_call | solution.py:261
  276.2 22.1 %shard_map.190 = (bf16[1024,1024]{1,0:T(8,128)(2,1)}, bf16[1024,1024]{1,0:T(8,128)(2,1)}, bf16[128,2048]{1,0:T(8,128)(2,1)}, bf16[128,2048]{1,0:T(8,128)(2,1)}, ...) custom-call(s32[4]{0:T(128)} %pad_add_fusion.1.place, ...), custom_call_target="tpu_custom_call" | custom-call | flops 12884901888 | bytes 29360128 | tf_op jit(solution)/shard_map/pallas_call | solution.py:147
  303.0 8.8 %shard_map.191 = (bf16[2,4,128,1024]{3,2,1,0:T(8,128)(2,1)}, bf16[2,4,128,1024]{3,2,1,0:T(8,128)(2,1)}) custom-call(s32[1]{0:T(128)} %bitcast.1.place, bf16[128,2048]{1,0:T(8,128)(2,1)} %copy-done.70, bf16[128,2048]{1,0:T(8,128)(2,1)} %copy-done.75, bf16[128,2048]{1,0:T(8,128)(2,1)} %copy-done.69, bf16[128,2048]{1,0:T(8,128)(2,1)} %copy-done.71, ...), custom_call_target="tpu_custom_call" | custom-call | flops 4294967296 | bytes 10485760 | tf_op jit(solution)/shard_map/pallas_call | solution.py:261
  317.0 8.7 %shard_map.192 = (bf16[2,4,128,1024]{3,2,1,0:T(8,128)(2,1)}, bf16[2,4,128,1024]{3,2,1,0:T(8,128)(2,1)}) custom-call(s32[1]{0:T(128)} %bitcast.1.place, bf16[128,2048]{1,0:T(8,128)(2,1)} %copy-done.70, bf16[128,2048]{1,0:T(8,128)(2,1)} %copy-done.75, bf16[128,2048]{1,0:T(8,128)(2,1)} %copy-done.69, bf16[128,2048]{1,0:T(8,128)(2,1)} %copy-done.71, ...), custom_call_target="tpu_custom_call" | custom-call | flops 4294967296 | bytes 10485760 | tf_op jit(solution)/shard_map/pallas_call | solution.py:261
  337.5 7.3 %collective-permute-done.65 = bf16[128,2048]{1,0:T(8,128)(2,1)S(1)} collective-permute-done((bf16[128,2048]{1,0:T(8,128)(2,1)}, bf16[128,2048]{1,0:T(8,128)(2,1)S(1)}, u32[]{:S(2)}, u32[]{:S(2)}) %collective-permute-start.65) | collective-permute-done | bytes 524320 | tf_op jit(solution)/shard_map/ppermute | solution.py:83
  344.8 10.9 %collective-permute-done.66 = bf16[128,2048]{1,0:T(8,128)(2,1)} collective-permute-done((bf16[128,2048]{1,0:T(8,128)(2,1)}, bf16[128,2048]{1,0:T(8,128)(2,1)}, u32[]{:S(2)}, u32[]{:S(2)}) %collective-permute-start.66) | collective-permute-done | bytes 524320 | tf_op jit(solution)/shard_map/ppermute | solution.py:66
  368.8 4.7 collective-permute-done.68.refs_1_
  385.7 21.1 %shard_map.193 = (f32[128,2048]{1,0:T(8,128)}, bf16[128,2048]{1,0:T(8,128)(2,1)}, bf16[8,128,1280]{2,1,0:T(8,128)(2,1)}, bf16[8,128,1280]{2,1,0:T(8,128)(2,1)}, ...) custom-call(s32[5]{0:T(128)} %stack.113.place, bf16[128,2048]{1,0:T(8,128)(2,1)} %copy-done.23, ...), custom_call_target="tpu_custom_call" | custom-call | flops 7381975040 | bytes 26216448 | tf_op jit(solution)/shard_map/pallas_call | solution.py:463
  429.3 23.4 %collective-permute-done.81 = bf16[128,1024]{1,0:T(8,128)(2,1)S(1)} collective-permute-done((bf16[128,1024]{1,0:T(8,128)(2,1)S(1)}, bf16[128,1024]{1,0:T(8,128)(2,1)S(1)}, u32[]{:S(2)}, u32[]{:S(2)}) %collective-permute-start.81) | collective-permute-done | bytes 262176 | tf_op jit(solution)/shard_map/ppermute | solution.py:66
  457.4 19.5 %collective-permute-done.84 = bf16[128,2048]{1,0:T(8,128)(2,1)S(1)} collective-permute-done((bf16[128,2048]{1,0:T(8,128)(2,1)S(1)}, bf16[128,2048]{1,0:T(8,128)(2,1)S(1)}, u32[]{:S(2)}, u32[]{:S(2)}) %collective-permute-start.84) | collective-permute-done | bytes 524320 | tf_op jit(solution)/shard_map/ppermute | solution.py:66
  478.0 4.8 collective-permute-done.88
  495.7 4.6 collective-permute-done.94
  502.0 7.4 %collective-permute-done.93 = bf16[2,128,1280]{2,1,0:T(8,128)(2,1)S(1)} collective-permute-done((bf16[2,128,1280]{2,1,0:T(8,128)(2,1)S(1)}, bf16[2,128,1280]{2,1,0:T(8,128)(2,1)S(1)}, u32[]{:S(2)}, u32[]{:S(2)}) %collective-permute-start.93) | collective-permute-done | bytes 655392 | tf_op jit(solution)/shard_map/ppermute | solution.py:66
  518.7 5.7 %collective-permute-done.96 = f32[2,2048]{1,0:T(2,128)S(1)} collective-permute-done((f32[2,2048]{1,0:T(2,128)S(1)}, f32[2,2048]{1,0:T(2,128)S(1)}, u32[]{:S(2)}, u32[]{:S(2)}) %collective-permute-start.96) | collective-permute-done | bytes 16416 | tf_op jit(solution)/shard_map/ppermute | solution.py:66
  (450 shorter events, 194.7 us)
Async XLA Ops:
  2.8 33.1 %collective-permute-start.1 = (bf16[128,2560]{1,0:T(8,128)(2,1)}, bf16[128,2560]{1,0:T(8,128)(2,1)S(1)}, u32[]{:S(2)}, u32[]{:S(2)}) collective-permute-start(bf16[128,2560]{1,0:T(8,128)(2,1)} %shard_map.186.refs_6_.refs_11_), channel_id=1, source_target_pairs={{0,16},{2,18},{4,20},{6,22},{8,24},{10,26},{12,28},{14,30},{16,0},... | collective-permute-start | bytes 1966088 | tf_op jit(solution)/shard_map/ppermute | solution.py:66
  6.8 29.4 %collective-permute-start.2 = (bf16[128,2560]{1,0:T(8,128)(2,1)}, bf16[128,2560]{1,0:T(8,128)(2,1)}, u32[]{:S(2)}, u32[]{:S(2)}) collective-permute-start(bf16[128,2560]{1,0:T(8,128)(2,1)} %shard_map.186.refs_6_.refs_11_), channel_id=1, source_target_pairs={{0,8},{2,10},{4,12},{6,14},{8,0},{10,2},{12,4},{14,6},{16,24},{18,... | collective-permute-start | bytes 1966088 | tf_op jit(solution)/shard_map/ppermute | solution.py:66
  8.4 27.8 %collective-permute-start.3 = (bf16[128,2560]{1,0:T(8,128)(2,1)}, bf16[128,2560]{1,0:T(8,128)(2,1)S(1)}, u32[]{:S(2)}, u32[]{:S(2)}) collective-permute-start(bf16[128,2560]{1,0:T(8,128)(2,1)} %shard_map.186.refs_6_.refs_11_), channel_id=1, source_target_pairs={{0,4},{2,6},{4,0},{6,2},{8,12},{10,14},{12,8},{14,10},{16,20},{18,... | collective-permute-start | bytes 1966088 | tf_op jit(solution)/shard_map/ppermute | solution.py:66
  39.7 25.3 %collective-permute-start.4 = (bf16[128,2560]{1,0:T(8,128)(2,1)}, bf16[128,2560]{1,0:T(8,128)(2,1)S(1)}, u32[]{:S(2)}, u32[]{:S(2)}) collective-permute-start(bf16[128,2560]{1,0:T(8,128)(2,1)} %copy-done.50), channel_id=1, source_target_pairs={{0,8},{2,10},{4,12},{6,14},{8,0},{10,2},{12,4},{14,6},{16,24},{18,... | collective-permute-start | bytes 1966088 | tf_op jit(solution)/shard_map/ppermute | solution.py:66
  92.4 39.5 %collective-permute-start.25 = (bf16[3,128,1024]{2,1,0:T(8,128)(2,1)S(1)}, bf16[3,128,1024]{2,1,0:T(8,128)(2,1)}, u32[]{:S(2)}, u32[]{:S(2)}) collective-permute-start(bf16[3,128,1024]{2,1,0:T(8,128)(2,1)S(1)} %pad_maximum_fusion.refs_8_.refs_10_), channel_id=1, source_target_pairs={{0,4},{2,6},{4,0},{6,2},{8,12},{10,14},{12,8},{14,10},{16,20},{18,... | collective-permute-start | bytes 2359304 | tf_op jit(solution)/shard_map/ppermute | solution.py:66
  93.3 38.6 %collective-permute-start.24 = (bf16[128,2048]{1,0:T(8,128)(2,1)}, bf16[128,2048]{1,0:T(8,128)(2,1)S(1)}, u32[]{:S(2)}, u32[]{:S(2)}) collective-permute-start(bf16[128,2048]{1,0:T(8,128)(2,1)} %collective-permute-done.20.refs_4_), channel_id=1, source_target_pairs={{0,1},{1,0},{2,3},{3,2},{4,5},{5,4},{6,7},{7,6},{8,9},{9,8},{10,11... | collective-permute-start | bytes 1572872 | tf_op jit(solution)/shard_map/ppermute | solution.py:83
  94.0 37.9 %collective-permute-start.22 = (bf16[2,128,1024]{2,1,0:T(8,128)(2,1)}, bf16[2,128,1024]{2,1,0:T(8,128)(2,1)S(1)}, u32[]{:S(2)}, u32[]{:S(2)}) collective-permute-start(bf16[2,128,1024]{2,1,0:T(8,128)(2,1)} %get-tuple-element.156), channel_id=1, source_target_pairs={{0,24},{2,26},{4,28},{6,30},{8,16},{10,18},{12,20},{14,22},{16,8},... | collective-permute-start | bytes 1572872 | tf_op jit(solution)/shard_map/ppermute | solution.py:66
  97.1 34.8 %collective-permute-start.21 = (bf16[2,128,1024]{2,1,0:T(8,128)(2,1)}, bf16[2,128,1024]{2,1,0:T(8,128)(2,1)}, u32[]{:S(2)}, u32[]{:S(2)}) collective-permute-start(bf16[2,128,1024]{2,1,0:T(8,128)(2,1)} %get-tuple-element.155), channel_id=1, source_target_pairs={{0,8},{2,10},{4,12},{6,14},{8,0},{10,2},{12,4},{14,6},{16,24},{18,... | collective-permute-start | bytes 1572872 | tf_op jit(solution)/shard_map/ppermute | solution.py:66
  100.9 31.0 %collective-permute-start.23 = (bf16[128,1024]{1,0:T(8,128)(2,1)S(1)}, bf16[128,1024]{1,0:T(8,128)(2,1)S(1)}, u32[]{:S(2)}, u32[]{:S(2)}) collective-permute-start(bf16[128,1024]{1,0:T(8,128)(2,1)S(1)} %get-tuple-element.157), channel_id=1, source_target_pairs={{0,16},{2,18},{4,20},{6,22},{8,24},{10,26},{12,28},{14,30},{16,0},... | collective-permute-start | bytes 786440 | tf_op jit(solution)/shard_map/ppermute | solution.py:66
  155.9 27.5 %collective-permute-start.30 = (bf16[128,2048]{1,0:T(8,128)(2,1)S(1)}, bf16[128,2048]{1,0:T(8,128)(2,1)S(1)}, u32[]{:S(2)}, u32[]{:S(2)}) collective-permute-start(bf16[128,2048]{1,0:T(8,128)(2,1)S(1)} %multiply_convert_fusion.refs_6_), channel_id=1, source_target_pairs={{0,16},{2,18},{4,20},{6,22},{8,24},{10,26},{12,28},{14,30},{16,0},... | collective-permute-start | bytes 1572872 | tf_op jit(solution)/shard_map/ppermute | solution.py:66
  160.9 37.1 %collective-permute-start.44 = (bf16[3,128,1024]{2,1,0:T(8,128)(2,1)}, bf16[3,128,1024]{2,1,0:T(8,128)(2,1)S(1)}, u32[]{:S(2)}, u32[]{:S(2)}) collective-permute-start(bf16[3,128,1024]{2,1,0:T(8,128)(2,1)} %collective-permute-done.25.refs_9_.refs_11_), channel_id=1, source_target_pairs={{0,2},{2,0},{4,6},{6,4},{8,10},{10,8},{12,14},{14,12},{16,18},{18,... | collective-permute-start | bytes 2359304 | tf_op jit(solution)/shard_map/ppermute | solution.py:66
  160.9 37.2 %collective-permute-start.43 = (bf16[3,128,1024]{2,1,0:T(8,128)(2,1)S(1)}, bf16[3,128,1024]{2,1,0:T(8,128)(2,1)S(1)}, u32[]{:S(2)}, u32[]{:S(2)}) collective-permute-start(bf16[3,128,1024]{2,1,0:T(8,128)(2,1)S(1)} %copy-done.22), channel_id=1, source_target_pairs={{0,2},{2,0},{4,6},{6,4},{8,10},{10,8},{12,14},{14,12},{16,18},{18,... | collective-permute-start | bytes 2359304 | tf_op jit(solution)/shard_map/ppermute | solution.py:66
  165.1 27.2 %collective-permute-start.32 = (bf16[128,2048]{1,0:T(8,128)(2,1)S(1)}, bf16[128,2048]{1,0:T(8,128)(2,1)}, u32[]{:S(2)}, u32[]{:S(2)}) collective-permute-start(bf16[128,2048]{1,0:T(8,128)(2,1)S(1)} %multiply_convert_fusion.refs_6_), channel_id=1, source_target_pairs={{0,8},{2,10},{4,12},{6,14},{8,0},{10,2},{12,4},{14,6},{16,24},{18,... | collective-permute-start | bytes 1572872 | tf_op jit(solution)/shard_map/ppermute | solution.py:66
  226.5 32.8 %collective-permute-start.57 = (bf16[128,2048]{1,0:T(8,128)(2,1)}, bf16[128,2048]{1,0:T(8,128)(2,1)}, u32[]{:S(2)}, u32[]{:S(2)}) collective-permute-start(bf16[128,2048]{1,0:T(8,128)(2,1)} %collective-permute-done.56.refs_0_), channel_id=1, source_target_pairs={{0,1},{1,0},{2,3},{3,2},{4,5},{5,4},{6,7},{7,6},{8,9},{9,8},{10,11... | collective-permute-start | bytes 1572872 | tf_op jit(solution)/shard_map/ppermute | solution.py:83
  268.6 29.7 %collective-permute-start.55 = (bf16[512,1024]{1,0:T(8,128)(2,1)S(1)}, bf16[512,1024]{1,0:T(8,128)(2,1)S(1)}, u32[]{:S(2)}, u32[]{:S(2)}) collective-permute-start(bf16[512,1024]{1,0:T(8,128)(2,1)S(1)} %copy-done.44), channel_id=1, source_target_pairs={{0,1},{1,0},{2,3},{3,2},{4,5},{5,4},{6,7},{7,6},{8,9},{9,8},{10,11... | collective-permute-start | bytes 3145736 | tf_op jit(solution)/shard_map/ppermute | solution.py:83
  275.1 25.3 %collective-permute-start.59 = (bf16[4,128,1024]{2,1,0:T(8,128)(2,1)S(1)}, bf16[4,128,1024]{2,1,0:T(8,128)(2,1)S(1)}, u32[]{:S(2)}, u32[]{:S(2)}) collective-permute-start(bf16[4,128,1024]{2,1,0:T(8,128)(2,1)S(1)} %fusion.15), channel_id=1, source_target_pairs={{0,4},{2,6},{4,0},{6,2},{8,12},{10,14},{12,8},{14,10},{16,20},{18,... | collective-permute-start | bytes 3145736 | tf_op jit(solution)/shard_map/ppermute | solution.py:66
  332.1 23.7 %collective-permute-start.66 = (bf16[128,2048]{1,0:T(8,128)(2,1)}, bf16[128,2048]{1,0:T(8,128)(2,1)}, u32[]{:S(2)}, u32[]{:S(2)}) collective-permute-start(bf16[128,2048]{1,0:T(8,128)(2,1)} %get-tuple-element.216), channel_id=1, source_target_pairs={{0,8},{2,10},{4,12},{6,14},{8,0},{10,2},{12,4},{14,6},{16,24},{18,... | collective-permute-start | bytes 1572872 | tf_op jit(solution)/shard_map/ppermute | solution.py:66
  332.8 25.2 %collective-permute-start.67 = (bf16[128,2048]{1,0:T(8,128)(2,1)}, bf16[128,2048]{1,0:T(8,128)(2,1)}, u32[]{:S(2)}, u32[]{:S(2)}) collective-permute-start(bf16[128,2048]{1,0:T(8,128)(2,1)} %add_convert_fusion.5), channel_id=1, source_target_pairs={{0,16},{2,18},{4,20},{6,22},{8,24},{10,26},{12,28},{14,30},{16,0},... | collective-permute-start | bytes 1572872 | tf_op jit(solution)/shard_map/ppermute | solution.py:66
  334.4 40.5 %collective-permute-start.73 = (bf16[2,4,128,1024]{3,2,1,0:T(8,128)(2,1)}, bf16[2,4,128,1024]{3,2,1,0:T(8,128)(2,1)}, u32[]{:S(2)}, u32[]{:S(2)}) collective-permute-start(bf16[2,4,128,1024]{3,2,1,0:T(8,128)(2,1)} %get-tuple-element.229), channel_id=1, source_target_pairs={{0,2},{2,0},{4,6},{6,4},{8,10},{10,8},{12,14},{14,12},{16,18},{18,... | collective-permute-start | bytes 6291464 | tf_op jit(solution)/shard_map/ppermute | solution.py:66
  336.3 30.1 %collective-permute-start.70 = (bf16[4,128,1024]{2,1,0:T(8,128)(2,1)S(1)}, bf16[4,128,1024]{2,1,0:T(8,128)(2,1)S(1)}, u32[]{:S(2)}, u32[]{:S(2)}) collective-permute-start(bf16[4,128,1024]{2,1,0:T(8,128)(2,1)S(1)} %fusion.16), channel_id=1, source_target_pairs={{0,4},{2,6},{4,0},{6,2},{8,12},{10,14},{12,8},{14,10},{16,20},{18,... | collective-permute-start | bytes 3145736 | tf_op jit(solution)/shard_map/ppermute | solution.py:66
  373.6 33.2 %collective-permute-start.69 = (bf16[512,1024]{1,0:T(8,128)(2,1)}, bf16[512,1024]{1,0:T(8,128)(2,1)}, u32[]{:S(2)}, u32[]{:S(2)}) collective-permute-start(bf16[512,1024]{1,0:T(8,128)(2,1)} %get-tuple-element.219), channel_id=1, source_target_pairs={{0,1},{1,0},{2,3},{3,2},{4,5},{5,4},{6,7},{7,6},{8,9},{9,8},{10,11... | collective-permute-start | bytes 3145736 | tf_op jit(solution)/shard_map/ppermute | solution.py:83
  377.5 29.3 %collective-permute-start.74 = (bf16[4,128,1024]{2,1,0:T(8,128)(2,1)}, bf16[4,128,1024]{2,1,0:T(8,128)(2,1)}, u32[]{:S(2)}, u32[]{:S(2)}) collective-permute-start(bf16[4,128,1024]{2,1,0:T(8,128)(2,1)} %fusion.17), channel_id=1, source_target_pairs={{0,4},{2,6},{4,0},{6,2},{8,12},{10,14},{12,8},{14,10},{16,20},{18,... | collective-permute-start | bytes 3145736 | tf_op jit(solution)/shard_map/ppermute | solution.py:66
  382.1 24.6 %collective-permute-start.77 = (bf16[2,128,1024]{2,1,0:T(8,128)(2,1)}, bf16[2,128,1024]{2,1,0:T(8,128)(2,1)S(1)}, u32[]{:S(2)}, u32[]{:S(2)}) collective-permute-start(bf16[2,128,1024]{2,1,0:T(8,128)(2,1)} %pad_maximum_fusion.6), channel_id=1, source_target_pairs={{0,8},{2,10},{4,12},{6,14},{8,0},{10,2},{12,4},{14,6},{16,24},{18,... | collective-permute-start | bytes 1572872 | tf_op jit(solution)/shard_map/ppermute | solution.py:66
  382.2 24.5 %collective-permute-start.76 = (bf16[128,1024]{1,0:T(8,128)(2,1)}, bf16[128,1024]{1,0:T(8,128)(2,1)}, u32[]{:S(2)}, u32[]{:S(2)}) collective-permute-start(bf16[128,1024]{1,0:T(8,128)(2,1)} %get-tuple-element.232), channel_id=1, source_target_pairs={{0,24},{2,26},{4,28},{6,30},{8,16},{10,18},{12,20},{14,22},{16,8},... | collective-permute-start | bytes 786440 | tf_op jit(solution)/shard_map/ppermute | solution.py:66
  412.3 40.4 %collective-permute-start.80 = (bf16[4,128,1280]{2,1,0:T(8,128)(2,1)S(1)}, bf16[4,128,1280]{2,1,0:T(8,128)(2,1)S(1)}, u32[]{:S(2)}, u32[]{:S(2)}) collective-permute-start(bf16[4,128,1280]{2,1,0:T(8,128)(2,1)S(1)} %fusion.4), channel_id=1, source_target_pairs={{0,4},{2,6},{4,0},{6,2},{8,12},{10,14},{12,8},{14,10},{16,20},{18,... | collective-permute-start | bytes 3932168 | tf_op jit(solution)/shard_map/ppermute | solution.py:66
  416.3 36.4 %collective-permute-start.82 = (bf16[2,128,1024]{2,1,0:T(8,128)(2,1)S(1)}, bf16[2,128,1024]{2,1,0:T(8,128)(2,1)S(1)}, u32[]{:S(2)}, u32[]{:S(2)}) collective-permute-start(bf16[2,128,1024]{2,1,0:T(8,128)(2,1)S(1)} %pad_maximum_fusion.7), channel_id=1, source_target_pairs={{0,24},{2,26},{4,28},{6,30},{8,16},{10,18},{12,20},{14,22},{16,8},... | collective-permute-start | bytes 1572872 | tf_op jit(solution)/shard_map/ppermute | solution.py:66
  424.3 28.4 %collective-permute-start.81 = (bf16[128,1024]{1,0:T(8,128)(2,1)S(1)}, bf16[128,1024]{1,0:T(8,128)(2,1)S(1)}, u32[]{:S(2)}, u32[]{:S(2)}) collective-permute-start(bf16[128,1024]{1,0:T(8,128)(2,1)S(1)} %get-tuple-element.237), channel_id=1, source_target_pairs={{0,16},{2,18},{4,20},{6,22},{8,24},{10,26},{12,28},{14,30},{16,0},... | collective-permute-start | bytes 786440 | tf_op jit(solution)/shard_map/ppermute | solution.py:66
  452.7 33.1 %collective-permute-start.87 = (bf16[4,128,1280]{2,1,0:T(8,128)(2,1)S(1)}, bf16[4,128,1280]{2,1,0:T(8,128)(2,1)S(1)}, u32[]{:S(2)}, u32[]{:S(2)}) collective-permute-start(bf16[4,128,1280]{2,1,0:T(8,128)(2,1)S(1)} %fusion.5), channel_id=1, source_target_pairs={{0,4},{2,6},{4,0},{6,2},{8,12},{10,14},{12,8},{14,10},{16,20},{18,... | collective-permute-start | bytes 3932168 | tf_op jit(solution)/shard_map/ppermute | solution.py:66
  453.1 23.7 %collective-permute-start.84 = (bf16[128,2048]{1,0:T(8,128)(2,1)S(1)}, bf16[128,2048]{1,0:T(8,128)(2,1)S(1)}, u32[]{:S(2)}, u32[]{:S(2)}) collective-permute-start(bf16[128,2048]{1,0:T(8,128)(2,1)S(1)} %fusion.22), channel_id=1, source_target_pairs={{0,16},{2,18},{4,20},{6,22},{8,24},{10,26},{12,28},{14,30},{16,0},... | collective-permute-start | bytes 1572872 | tf_op jit(solution)/shard_map/ppermute | solution.py:66
  453.4 29.3 %collective-permute-start.88 = (bf16[2,128,1280]{2,1,0:T(8,128)(2,1)S(1)}, bf16[2,128,1280]{2,1,0:T(8,128)(2,1)S(1)}, u32[]{:S(2)}, u32[]{:S(2)}) collective-permute-start(bf16[2,128,1280]{2,1,0:T(8,128)(2,1)S(1)} %pad_maximum_fusion.1), channel_id=1, source_target_pairs={{0,8},{2,10},{4,12},{6,14},{8,0},{10,2},{12,4},{14,6},{16,24},{18,... | collective-permute-start | bytes 1966088 | tf_op jit(solution)/shard_map/ppermute | solution.py:66
  456.0 29.8 %collective-permute-start.89 = (bf16[128,1024]{1,0:T(8,128)(2,1)S(1)}, bf16[128,1024]{1,0:T(8,128)(2,1)S(1)}, u32[]{:S(2)}, u32[]{:S(2)}) collective-permute-start(bf16[128,1024]{1,0:T(8,128)(2,1)S(1)} %get-tuple-element.249), channel_id=1, source_target_pairs={{0,8},{2,10},{4,12},{6,14},{8,0},{10,2},{12,4},{14,6},{16,24},{18,... | collective-permute-start | bytes 786440 | tf_op jit(solution)/shard_map/ppermute | solution.py:66
  456.1 29.7 %collective-permute-start.85 = (bf16[128,2048]{1,0:T(8,128)(2,1)S(1)}, bf16[128,2048]{1,0:T(8,128)(2,1)S(1)}, u32[]{:S(2)}, u32[]{:S(2)}) collective-permute-start(bf16[128,2048]{1,0:T(8,128)(2,1)S(1)} %copy-done.76), channel_id=1, source_target_pairs={{0,1},{1,0},{2,3},{3,2},{4,5},{5,4},{6,7},{7,6},{8,9},{9,8},{10,11... | collective-permute-start | bytes 1572872 | tf_op jit(solution)/shard_map/ppermute | solution.py:83
  (157 other events, 2784.3 us)
